TPU v7x, 128 devices: a whole 4x4x4 slice. The times are simulated.
128 devices in a mesh: row: 8 (over y_hi, z), col: 16 (over y_lo, x, core).
Axes of the slice: x: 4, y: 4 (y_hi: 2, y_lo: 2; y = y_hi * 2 + y_lo), z: 4, core: 2. Of those that a mesh axis runs over, the one named last changes fastest.
Arguments:
- entries: float32 [8192, 8192], P('row', 'col'), may hold values from 0.01 to 1
- pattern: int32 [32, 32], P('row', 'col'), may hold values 0 or 1
- prune: int32 [32, 32], P('row', 'col'), may hold values 0 or 1
Outputs:
- result: float32 [8192, 8192], P('row', 'col')
All inputs are finite; a program needn't handle non-finite values. No bound on the sum of `pattern` or of `prune` on one device may be relied on, other than what follows from the above.
Results may differ from a plain program's by a relative error of at most 0.00038.
Values may be sent and summed in bfloat16 or wider, within the bound.
No kernel may reach another device: no remote copies, remote signals or barrier semaphores. Data moves between devices by JAX's collectives and lax.ppermute only.
A program may use at most 128 MiB of HBM per device.

v0:
```python
import jax
import jax.numpy as jnp
from jax import lax
from jax.sharding import PartitionSpec as P


def tile_keep(flags):
    tile_rows, tile_cols = flags.shape
    first_row = lax.axis_index("row") * tile_rows
    first_col = lax.axis_index("col") * tile_cols
    row_ids = first_row + jnp.arange(tile_rows, dtype=jnp.int32)
    col_ids = first_col + jnp.arange(tile_cols, dtype=jnp.int32)
    diagonal = (row_ids[:, None] == col_ids[None, :]).astype(jnp.int32)
    return jnp.maximum(flags, diagonal).astype(jnp.float32)


def spread(block, keep):
    tile_rows, tile_cols = keep.shape
    height, width = block.shape
    shaped = block.reshape(tile_rows, height // tile_rows, tile_cols, width // tile_cols)
    return (shaped * keep[:, None, :, None]).reshape(height, width)


def shards(entries, pattern, prune):
    masked = spread(entries, tile_keep(pattern))
    colsum = lax.psum(jnp.sum(masked, axis=0), "row")
    stoch = (masked / colsum[None, :]).astype(jnp.bfloat16)
    height, width = stoch.shape
    right = lax.all_gather(stoch, "row", axis=0, tiled=True)
    product = jnp.dot(
        lax.all_gather(stoch, "col", axis=1, tiled=True), right, preferred_element_type=jnp.float32
    )
    inflated = spread(product * product, tile_keep(prune))
    total = lax.psum(jnp.sum(inflated, axis=0), "row")
    order = float(height * lax.axis_size("row"))
    return order * inflated / total[None, :]


def solution(mesh):
    return jax.shard_map(
        shards,
        mesh=mesh,
        in_specs=(P("row", "col"), P("row", "col"), P("row", "col")),
        out_specs=P("row", "col"),
        check_vma=False,
    )
```

profile of v0, /device:TPU:0, one launch (start us, length us, event | category | flops | bytes accessed | tf_op | source)
XLA Modules:
  0.0 282.2 jit_solution(7082363152708476003)
XLA Ops:
  6.5 0.0 all-gather.5.cloned.1.call-start
  6.5 0.8 fusion.2
  7.3 0.1 copy.4
  7.4 0.6 mul.41
  8.0 0.0 copy-start
  8.0 0.2 copy.6
  8.2 1.4 copy-done
  9.6 0.5 fusion.4
  10.1 25.7 %psum.14 = f32[512]{0:T(512)S(1)} all-reduce(f32[512]{0:T(512)S(1)} %get-tuple-element.5), channel_id=1, replica_groups=mesh['row'=8,'col'=16] {'row'}, use_global_device_ids=true, to_apply=%region_1.0 | all-reduce | flops 512 | bytes 4096 | tf_op jit(solution)/shard_map/psum | solution.py:26
  35.9 1.3 divide_convert_fusion
  37.1 0.0 all-gather.5.cloned.1.call-update
  37.2 0.0 all-gather.3.cloned.1.call-start
  37.2 0.7 all-gather.3.cloned.1.call-update
  37.9 0.1 copy.5
  38.0 0.6 mul.45
  38.6 0.2 copy.7
  38.8 102.5 %all-gather.5.cloned.1.call-done = bf16[8192,512]{1,0:T(8,128)(2,1)} async-done(((bf16[1024,512]{1,0:T(8,128)(2,1)}), bf16[8192,512]{1,0:T(8,128)(2,1)}) %all-gather.5.cloned.1.call-update) | async-done | bytes 8388624 | tf_op jit(solution)/shard_map/all_gather | solution.py:29
  141.3 91.0 %all-gather.3.cloned.1.call-done = bf16[1024,8192]{1,0:T(8,128)(2,1)} async-done(((bf16[1024,512]{1,0:T(8,128)(2,1)}), bf16[1024,8192]{1,0:T(8,128)(2,1)}) %all-gather.3.cloned.1.call-update) | async-done | bytes 16777232 | tf_op jit(solution)/shard_map/all_gather | solution.py:31
  232.3 15.7 %fusion.5 = (f32[512]{0:T(512)S(1)}, f32[1024,512]{1,0:T(8,128)}) fusion(f32[1024,512]{1,0:T(8,128)S(1)} %bitcast.11, bf16[1024,8192]{1,0:T(8,128)(2,1)} %all-gather.3.cloned.1.call-done, bf16[8192,512]{1,0:T(8,128)(2,1)} %all-gather.5.cloned.1.call-done), kind=kOutput, calls=%fused_computation.11 | convolution fusion | flops 8591507456 | bytes 29362176 | tf_op jit(solution)/shard_map/dot_general | solution.py:30
  248.0 24.2 %psum.15 = f32[512]{0:T(512)S(1)} all-reduce(f32[512]{0:T(512)S(1)} %get-tuple-element.9), channel_id=1, replica_groups=mesh['row'=8,'col'=16] {'row'}, use_global_device_ids=true, to_apply=%region_3.0 | all-reduce | flops 512 | bytes 4096 | tf_op jit(solution)/shard_map/psum | solution.py:34
  272.2 3.2 %multiply_divide_fusion = f32[1024,512]{1,0:T(8,128)} fusion(f32[1024,512]{1,0:T(8,128)} %get-tuple-element.10, f32[512]{0:T(512)S(1)} %psum.15), kind=kLoop, calls=%fused_computation | loop fusion | flops 1048576 | bytes 4196352 | tf_op jit(solution)/shard_map/div | solution.py:36
  (2 shorter events, 0.0 us)
Async XLA Ops:
  6.5 134.8 %all-gather.5.cloned.1.call-start = ((), (), s32[]{:S(2)}) async-start(), calls=%async_computation.1 | async-start | bytes 9437184 | tf_op jit(solution)/shard_map/all_gather | solution.py:29
  8.0 1.6 copy-start
  37.2 195.1 %all-gather.3.cloned.1.call-start = ((), (), s32[]{:S(2)}) async-start(), calls=%async_computation | async-start | bytes 17825792 | tf_op jit(solution)/shard_map/all_gather | solution.py:31
Sparse Core Ops, SparseCore 0:
  37.3 104.0 all-gather.4
  143.0 89.2 all-gather.2
where the time goes:
time: 282 us
  waiting for transfers between devices  194 us (69%)
  blocking collectives  49.9 us (18%)
  matrix products  15.7 us (6%)
  between operations  13.4 us (5%)
  other arithmetic  5.76 us (2%)
  local copies, waits for them, and re-layouts  3.16 us (1%)
    all_gather x1, waiting for transfers between devices, shards(): right = lax.all_gather(stoch, 'row', axis=0, tiled=True)  103 us
    all_gather x1, waiting for transfers between devices, shards(): lax.all_gather(stoch, 'col', axis=1, tiled=True)  91 us
    psum x1, blocking collectives, shards(): colsum = lax.psum(jnp.sum(masked, axis=0), 'row')  25.7 us
    psum x1, blocking collectives, shards(): total = lax.psum(jnp.sum(inflated, axis=0), 'row')  24.2 us
    dot_general x1, matrix products, shards(): jnp.dot(lax.all_gather(stoch, 'col', axis=1, tiled=True), right, preferre...  15.7 us
  transfers between devices with their start and end apart: 2, of which 2 were waited for; matrix products, arithmetic and copies ran while one was open for 0% of the time, Pallas kernels for 0%

commit v1 on v0

v1 whole, which is shorter than its diff:
```python
import functools
import jax
import jax.numpy as jnp
from jax import lax
from jax.experimental import pallas as pl
from jax.experimental.pallas import tpu as pltpu
from jax.sharding import PartitionSpec as P

AXES = ("row", "col")
YH, NZ, YL, NX, NC = 2, 4, 2, 4, 2
F32 = jnp.float32
BF16 = jnp.bfloat16
I32 = jnp.int32


def place(yh, z, yl, x, c):
    return (yh * NZ + z) * (YL * NX * NC) + (yl * NX + x) * NC + c


def pairs(step):
    return [
        (place(yh, z, yl, x, c), place(*step(yh, z, yl, x, c)))
        for yh in range(YH)
        for z in range(NZ)
        for yl in range(YL)
        for x in range(NX)
        for c in range(NC)
    ]


RING_X = pairs(lambda yh, z, yl, x, c: (yh, z, yl, (x + 1 - 2 * c) % NX, c))
RING_Z = pairs(lambda yh, z, yl, x, c: (yh, (z + 1 - 2 * c) % NZ, yl, x, c))
SWAP_CORE = pairs(lambda yh, z, yl, x, c: (yh, z, yl, x, 1 - c))
SWAP_YL = pairs(lambda yh, z, yl, x, c: (yh, z, 1 - yl, x, c))
SWAP_YH = pairs(lambda yh, z, yl, x, c: (1 - yh, z, yl, x, c))
Z_NEAR = pairs(lambda yh, z, yl, x, c: (yh, z ^ 1, yl, x, c))
Z_FAR = pairs(lambda yh, z, yl, x, c: (yh, 3 - z, yl, x, c))
X_NEAR = pairs(lambda yh, z, yl, x, c: (yh, z, yl, x ^ 1, c))
X_FAR = pairs(lambda yh, z, yl, x, c: (yh, z, yl, 3 - x, c))


def move(value, perm):
    return lax.ppermute(value, AXES, perm)


def add_up(value, perms):
    for perm in perms:
        value = value + move(value, perm)
    return value


def scale_kernel(keep_ref, entries_ref, colsum_ref, out_ref):
    keep = keep_ref[pl.program_id(0), pl.program_id(1)].astype(F32)
    out_ref[0] = (entries_ref[...] * keep / colsum_ref[...]).astype(BF16)


def scaled_tiles(entries, keep, colsum):
    rows, cols = keep.shape
    tall, wide = entries.shape[0] // rows, entries.shape[1] // cols
    return pl.pallas_call(
        scale_kernel,
        grid=(rows, cols),
        out_shape=jax.ShapeDtypeStruct((rows * cols, tall, wide), BF16),
        in_specs=[
            pl.BlockSpec(memory_space=pltpu.SMEM),
            pl.BlockSpec((tall, wide), lambda i, j: (i, j)),
            pl.BlockSpec((1, wide), lambda i, j: (0, j)),
        ],
        out_specs=pl.BlockSpec((1, tall, wide), lambda i, j: (i * cols + j, 0, 0)),
        name="scale",
    )(keep, entries, colsum[None, :])


def product_kernel(n_a, n_b, rows, cols, grid, *refs):
    base_a, base_b, need_a, need_b, count, order = refs[:6]
    a_in = refs[6:6 + n_a]
    b_in = refs[6 + n_a:6 + n_a + n_b]
    out_ref, sum_ref, a_buf, b_buf, acc, a_sem, b_sem = refs[6 + n_a + n_b:]

    def each(act):
        def a_tile(u, t):
            slot = base_a[u] + (t // cols) * grid + t % cols

            @pl.when(need_a[slot] > 0)
            def _():
                act(pltpu.make_async_copy(a_in[u].at[t], a_buf.at[slot], a_sem.at[slot]))

        def b_tile(u, t):
            slot = base_b[u] + t

            @pl.when(need_b[slot] > 0)
            def _():
                act(pltpu.make_async_copy(b_in[u].at[t], b_buf.at[slot], b_sem.at[slot]))

        for u in range(n_a):
            lax.fori_loop(0, rows * cols, lambda t, _, u=u: (a_tile(u, t), 0)[1], 0)
        for u in range(n_b):
            lax.fori_loop(0, rows * cols, lambda t, _, u=u: (b_tile(u, t), 0)[1], 0)

    each(lambda copy: copy.start())
    each(lambda copy: copy.wait())

    tile = acc.shape[0]
    for j in range(cols):
        total = jnp.zeros((1, tile), F32)
        for i in range(rows):
            acc[...] = jnp.zeros_like(acc)

            def step(n, _, i=i, j=j):
                k = order[i * cols + j, n]
                acc[...] += jnp.dot(
                    a_buf[i * grid + k], b_buf[k * cols + j], preferred_element_type=F32
                )
                return 0

            lax.fori_loop(0, count[i * cols + j], step, 0)
            square = acc[...] * acc[...]
            out_ref[i * tile:(i + 1) * tile, j * tile:(j + 1) * tile] = square
            total = total + jnp.sum(square, axis=0, keepdims=True)
        sum_ref[:, j * tile:(j + 1) * tile] = total


def product(a_units, b_units, base_a, base_b, left, right, keep_out):
    rows, cols = keep_out.shape
    grid = left.shape[1]
    tile = a_units[0].shape[1]
    used = left[:, None, :] * right.T[None, :, :] * keep_out[:, :, None]
    need_a = jnp.max(used, axis=1).reshape(-1)
    need_b = jnp.max(used, axis=0).T.reshape(-1)
    used = used.reshape(rows * cols, grid)
    count = jnp.sum(used, axis=1)
    rank = jnp.cumsum(used, axis=1) - 1
    ids = jnp.arange(grid, dtype=I32)
    hit = (rank[:, :, None] == ids[None, None, :]) & (used[:, :, None] > 0)
    order = jnp.sum(jnp.where(hit, ids[None, :, None], 0), axis=1)
    smem = pl.BlockSpec(memory_space=pltpu.SMEM)
    return pl.pallas_call(
        functools.partial(product_kernel, len(a_units), len(b_units), rows, cols, grid),
        out_shape=(
            jax.ShapeDtypeStruct((rows * tile, cols * tile), F32),
            jax.ShapeDtypeStruct((1, cols * tile), F32),
        ),
        in_specs=[smem] * 6 + [pl.BlockSpec(memory_space=pl.ANY)] * (len(a_units) + len(b_units)),
        out_specs=(
            pl.BlockSpec(memory_space=pltpu.VMEM),
            pl.BlockSpec(memory_space=pltpu.VMEM),
        ),
        scratch_shapes=[
            pltpu.VMEM((rows * grid, tile, tile), BF16),
            pltpu.VMEM((cols * grid, tile, tile), BF16),
            pltpu.VMEM((tile, tile), F32),
            pltpu.SemaphoreType.DMA((rows * grid,)),
            pltpu.SemaphoreType.DMA((cols * grid,)),
        ],
        compiler_params=pltpu.CompilerParams(vmem_limit_bytes=40 * 1024 * 1024),
        name="product",
    )(base_a, base_b, need_a, need_b, count, order, *a_units, *b_units)


def tile_keep(flags):
    tile_rows, tile_cols = flags.shape
    row_ids = lax.axis_index("row") * tile_rows + jnp.arange(tile_rows, dtype=I32)
    col_ids = lax.axis_index("col") * tile_cols + jnp.arange(tile_cols, dtype=I32)
    diagonal = (row_ids[:, None] == col_ids[None, :]).astype(I32)
    return jnp.maximum(flags, diagonal)


def shards(entries, pattern, prune):
    row, col = lax.axis_index("row"), lax.axis_index("col")
    rows, cols = pattern.shape
    height, width = entries.shape
    grid = rows * lax.axis_size("row")
    yh, z = row // NZ, row % NZ
    yl, x, c = col // (NX * NC), (col // NC) % NX, col % NC

    keep = tile_keep(pattern)
    keep_out = tile_keep(prune)
    keep_f = keep.astype(F32)
    masked = (
        entries.reshape(rows, height // rows, cols, width // cols) * keep_f[:, None, :, None]
    ).reshape(height, width)

    flags = lax.dynamic_update_slice(jnp.zeros((grid, cols), F32), keep_f, (row * rows, 0))
    sums = jnp.concatenate([jnp.sum(masked, axis=0), flags.reshape(-1)])
    sums = add_up(sums, (Z_NEAR, Z_FAR, SWAP_YH))
    colsum = sums[:width]
    right = sums[width:].reshape(grid, cols).astype(I32)

    own = scaled_tiles(entries, keep, colsum)

    left = lax.dynamic_update_slice(jnp.zeros((rows, grid), F32), keep_f, (0, col * cols))
    left = add_up(left.reshape(-1), (SWAP_CORE, SWAP_YL, X_NEAR, X_FAR)).reshape(rows, grid).astype(I32)

    other = move(own, SWAP_CORE)
    xa = move(own, RING_X)
    za = move(own, RING_Z)
    px = move(own, SWAP_YL)
    pz = move(own, SWAP_YH)
    xb = move(other, RING_X)
    zb = move(other, RING_Z)
    xc = move(xa, RING_X)
    zc = move(za, RING_Z)
    px_o = move(px, SWAP_CORE)
    pz_o = move(pz, SWAP_CORE)
    pxa = move(px, RING_X)
    pxb = move(px_o, RING_X)
    pxc = move(pxa, RING_X)
    pza = move(pz, RING_Z)
    pzb = move(pz_o, RING_Z)
    pzc = move(pza, RING_Z)
    swap = lambda v: move(v, SWAP_CORE)

    near, back = (x - 1 + 2 * c) % NX, (x + 1 - 2 * c) % NX
    far = (x + 2) % NX
    a_units, base_a = [], []

    def a_unit(value, yl_of, x_of, core_of):
        a_units.append(value)
        base_a.append(((yl_of * NX + x_of) * NC + core_of) * cols)

    d = 1 - c
    for y, (u0, u1), (ua, ub, uc) in (
        (yl, (own, other), (xa, xb, xc)),
        (1 - yl, (px, px_o), (pxa, pxb, pxc)),
    ):
        a_unit(u0, y, x, c)
        a_unit(u1, y, x, d)
        a_unit(ua, y, near, c)
        a_unit(ub, y, near, d)
        a_unit(swap(ua), y, back, d)
        a_unit(swap(ub), y, back, c)
        a_unit(uc, y, far, c)
        a_unit(swap(uc), y, far, d)

    near, back = (z - 1 + 2 * c) % NZ, (z + 1 - 2 * c) % NZ
    far = (z + 2) % NZ
    b_units, base_b = [], []

    def b_unit(value, yh_of, z_of):
        b_units.append(value)
        base_b.append((yh_of * NZ + z_of) * rows * cols)

    for y, u0, (ua, ub, uc) in ((yh, own, (za, zb, zc)), (1 - yh, pz, (pza, pzb, pzc))):
        b_unit(u0, y, z)
        b_unit(ua, y, near)
        b_unit(swap(ub), y, back)
        b_unit(uc, y, far)

    inflated, total = product(
        a_units, b_units, jnp.stack(base_a).astype(I32), jnp.stack(base_b).astype(I32), left, right, keep_out
    )
    total = add_up(total[0], (Z_NEAR, Z_FAR, SWAP_YH))
    order = float(height * lax.axis_size("row"))
    return order * inflated / total[None, :]


def solution(mesh):
    return jax.shard_map(
        shards,
        mesh=mesh,
        in_specs=(P("row", "col"), P("row", "col"), P("row", "col")),
        out_specs=P("row", "col"),
        check_vma=False,
    )
```

time: 282 us -> 191 us (0.68)
  waiting for transfers between devices: 194 us -> 111 us
  blocking collectives: 49.9 us -> 0 us
  starting transfers between devices: 0.04 us -> 32.7 us
  Pallas kernels: 0 us -> 30.2 us
  matrix products: 15.7 us -> 0 us
  between operations: 13.4 us -> 0.21 us
  local copies, waits for them, and re-layouts: 3.16 us -> 12.1 us
    all_gather x2 -> x0, waiting for transfers between devices: 193 us -> none  [the longest x1 103 us: shards(): right = lax.all_gather(stoch, 'row', axis=0, tiled=True)]
    ppermute x0 -> x35, waiting for transfers between devices: none -> 111 us  [move(): return lax.ppermute(value, AXES, perm)]
    psum x2 -> x0, blocking collectives: 49.9 us -> none  [the longest x1 25.7 us: shards(): colsum = lax.psum(jnp.sum(masked, axis=0), 'row')]
    ppermute x0 -> x35, starting transfers between devices: none -> 32.7 us  [move(): return lax.ppermute(value, AXES, perm)]
    pallas_call x0 -> x2, Pallas kernels: none -> 30.2 us  [the longest x1 24.7 us: product(): pl.pallas_call(functools.partial(product_kernel, len(a_units), len(b_unit...]
    dot_general x1 -> x0, matrix products: 15.7 us -> none  [shards(): jnp.dot(lax.all_gather(stoch, 'col', axis=1, tiled=True), right, preferre...]
    unnamed x4 -> x27, local copies, waits for them, and re-layouts: 1.75 us -> 9.75 us
  transfers between devices with their start and end apart: 2 -> 35, of which waited for: 2 -> 20; matrix products, arithmetic and copies ran while one was open for 0% -> 1% of each run, Pallas kernels for 0% -> 3%
where the time goes in v1:
time: 191 us
  waiting for transfers between devices  111 us (58%)
  starting transfers between devices  32.7 us (17%)
  Pallas kernels  30.2 us (16%)
  local copies, waits for them, and re-layouts  12.1 us (6%)
  other arithmetic  4.54 us (2%)
    ppermute x35, waiting for transfers between devices, move(): return lax.ppermute(value, AXES, perm)  111 us
    ppermute x35, starting transfers between devices, move(): return lax.ppermute(value, AXES, perm)  32.7 us
    pallas_call x1, Pallas kernels, product(): pl.pallas_call(functools.partial(product_kernel, len(a_units), len(b_unit...  24.7 us
    unnamed x27, local copies, waits for them, and re-layouts  9.75 us
    pallas_call x1, Pallas kernels, scaled_tiles(): pl.pallas_call(scale_kernel, grid=(rows, cols), out_shape=jax.ShapeDtypeS...  5.5 us
  transfers between devices with their start and end apart: 35, of which 20 were waited for; matrix products, arithmetic and copies ran while one was open for 1% of the time, Pallas kernels for 3%

profile of v1, /device:TPU:0, one launch (start us, length us, event | category | flops | bytes accessed | tf_op | source)
XLA Modules:
  0.0 191.2 jit_solution(939620254414940961)
XLA Ops:
  0.0 0.8 copy.14
  0.8 0.8 copy.16
  1.6 0.1 reshape.122
  1.7 0.6 mul.269
  2.4 0.2 copy.18
  2.5 1.4 copy-done.5
  3.9 0.6 multiply_reduce_fusion
  4.5 2.1 %collective-permute-start.4 = (f32[576]{0:T(1024)S(1)}, f32[576]{0:T(1024)S(1)}, u32[]{:S(2)}, u32[]{:S(2)}) collective-permute-start(f32[576]{0:T(1024)S(1)} %pad_maximum_fusion), channel_id=1, source_target_pairs={{0,16},{1,17},{2,18},{3,19},{4,20},{5,21},{6,22},{7,23},{8,24},{9,... | collective-permute-start | bytes 6920 | tf_op jit(solution)/shard_map/ppermute | solution.py:43
  6.6 1.6 collective-permute-done.4
  8.2 4.1 %collective-permute-start.5 = (f32[576]{0:T(1024)S(1)}, f32[576]{0:T(1024)S(1)}, u32[]{:S(2)}, u32[]{:S(2)}) collective-permute-start(f32[576]{0:T(1024)S(1)} %fusion.1), channel_id=1, source_target_pairs={{0,48},{1,49},{2,50},{3,51},{4,52},{5,53},{6,54},{7,55},{8,56},{9,... | collective-permute-start | bytes 6920 | tf_op jit(solution)/shard_map/ppermute | solution.py:43
  12.3 1.6 collective-permute-done.5
  13.9 3.2 %collective-permute-start.6 = (f32[576]{0:T(1024)S(1)}, f32[576]{0:T(1024)S(1)}, u32[]{:S(2)}, u32[]{:S(2)}) collective-permute-start(f32[576]{0:T(1024)S(1)} %add.278), channel_id=1, source_target_pairs={{0,64},{1,65},{2,66},{3,67},{4,68},{5,69},{6,70},{7,71},{8,72},{9,... | collective-permute-start | bytes 6920 | tf_op jit(solution)/shard_map/ppermute | solution.py:43
  17.3 1.1 collective-permute-done
  18.4 0.8 collective-permute-start.1
  19.2 2.8 %collective-permute-done.1 = f32[128]{0:T(128)S(1)} collective-permute-done((f32[128]{0:T(128)S(1)}, f32[128]{0:T(128)S(1)}, u32[]{:S(2)}, u32[]{:S(2)}) %collective-permute-start.1) | collective-permute-done | bytes 544 | tf_op jit(solution)/shard_map/ppermute | solution.py:43
  22.0 1.6 collective-permute-start.2
  23.6 1.9 %collective-permute-done.2 = f32[128]{0:T(128)S(1)} collective-permute-done((f32[128]{0:T(128)S(1)}, f32[128]{0:T(128)S(1)}, u32[]{:S(2)}, u32[]{:S(2)}) %collective-permute-start.2) | collective-permute-done | bytes 544 | tf_op jit(solution)/shard_map/ppermute | solution.py:43
  25.5 2.9 %collective-permute-start.3 = (f32[128]{0:T(128)S(1)}, f32[128]{0:T(128)S(1)}, u32[]{:S(2)}, u32[]{:S(2)}) collective-permute-start(f32[128]{0:T(128)S(1)} %add.274), channel_id=1, source_target_pairs={{0,6},{1,7},{2,4},{3,5},{4,2},{5,3},{6,0},{7,1},{8,14},{9,15},{10,... | collective-permute-start | bytes 1544 | tf_op jit(solution)/shard_map/ppermute | solution.py:43
  28.4 0.6 slice.15
  28.9 5.5 %scale.1.refs_6_.refs_22_ = bf16[8,256,256]{2,1,0:T(8,128)(2,1)} custom-call(s32[4,2]{1,0:T(4,128)} %copy-done.9, f32[1024,512]{1,0:T(8,128)} %entries_ref.1, f32[1,512]{1,0:T(1,128)} %bitcast.38), custom_call_target="tpu_custom_call" | custom-call | tf_op jit(solution)/shard_map/scale/pallas_call | solution.py:60
  34.4 0.5 collective-permute-start.26
  34.9 1.4 collective-permute-start.14
  36.4 0.2 collective-permute-start.8
  36.6 25.7 %collective-permute-done.26.refs_26_ = bf16[8,256,256]{2,1,0:T(8,128)(2,1)S(1)} collective-permute-done((bf16[8,256,256]{2,1,0:T(8,128)(2,1)}, bf16[8,256,256]{2,1,0:T(8,128)(2,1)S(1)}, u32[]{:S(2)}, u32[]{:S(2)}) %collective-permute-start.26) | collective-permute-done | bytes 1048608 | tf_op jit(solution)/shard_map/ppermute | solution.py:43
  62.4 17.3 %collective-permute-done.14.refs_14_ = bf16[8,256,256]{2,1,0:T(8,128)(2,1)S(1)} collective-permute-done((bf16[8,256,256]{2,1,0:T(8,128)(2,1)}, bf16[8,256,256]{2,1,0:T(8,128)(2,1)S(1)}, u32[]{:S(2)}, u32[]{:S(2)}) %collective-permute-start.14) | collective-permute-done | bytes 1048608 | tf_op jit(solution)/shard_map/ppermute | solution.py:43
  79.7 0.2 collective-permute-start.16
  79.9 1.3 collective-permute-start.12
  81.2 2.0 %collective-permute-start.10 = (bf16[8,256,256]{2,1,0:T(8,128)(2,1)S(1)}, bf16[8,256,256]{2,1,0:T(8,128)(2,1)S(1)}, u32[]{:S(2)}, u32[]{:S(2)}) collective-permute-start(bf16[8,256,256]{2,1,0:T(8,128)(2,1)S(1)} %collective-permute-done.8.refs_8_), channel_id=1, source_target_pairs={{0,1},{1,0},{2,3},{3,2},{4,5},{5,4},{6,7},{7,6},{8,9},{9,8},{10,11... | collective-permute-start | bytes 3145736 | tf_op jit(solution)/shard_map/ppermute | solution.py:43
  83.2 12.5 %collective-permute-done.25.refs_25_ = bf16[8,256,256]{2,1,0:T(8,128)(2,1)S(1)} collective-permute-done((bf16[8,256,256]{2,1,0:T(8,128)(2,1)S(1)}, bf16[8,256,256]{2,1,0:T(8,128)(2,1)S(1)}, u32[]{:S(2)}, u32[]{:S(2)}) %collective-permute-start.25) | collective-permute-done | bytes 1048608 | tf_op jit(solution)/shard_map/ppermute | solution.py:43
  95.7 0.1 collective-permute-done.16.refs_16_
  95.8 0.2 collective-permute-start.9
  96.0 1.6 collective-permute-start.29
  97.7 9.4 %collective-permute-done.12.refs_12_ = bf16[8,256,256]{2,1,0:T(8,128)(2,1)} collective-permute-done((bf16[8,256,256]{2,1,0:T(8,128)(2,1)S(1)}, bf16[8,256,256]{2,1,0:T(8,128)(2,1)}, u32[]{:S(2)}, u32[]{:S(2)}) %collective-permute-start.12) | collective-permute-done | bytes 1048608 | tf_op jit(solution)/shard_map/ppermute | solution.py:43
  107.1 1.8 collective-permute-start.31
  108.9 1.0 copy-done.1
  109.9 1.8 collective-permute-done.23
  111.7 6.5 %collective-permute-done.9.refs_9_ = bf16[8,256,256]{2,1,0:T(8,128)(2,1)S(1)} collective-permute-done((bf16[8,256,256]{2,1,0:T(8,128)(2,1)S(1)}, bf16[8,256,256]{2,1,0:T(8,128)(2,1)S(1)}, u32[]{:S(2)}, u32[]{:S(2)}) %collective-permute-start.9) | collective-permute-done | bytes 1048608 | tf_op jit(solution)/shard_map/ppermute | solution.py:43
  118.2 1.0 copy-done.3
  119.2 3.8 %collective-permute-done.29 = bf16[8,256,256]{2,1,0:T(8,128)(2,1)S(1)} collective-permute-done((bf16[8,256,256]{2,1,0:T(8,128)(2,1)S(1)}, bf16[8,256,256]{2,1,0:T(8,128)(2,1)S(1)}, u32[]{:S(2)}, u32[]{:S(2)}) %collective-permute-start.29) | collective-permute-done | bytes 1048608 | tf_op jit(solution)/shard_map/ppermute | solution.py:43
  123.0 1.0 copy-done.11
  124.1 0.1 stack.94.refs_0_
  124.2 10.1 %collective-permute-done.31.refs_29_ = bf16[8,256,256]{2,1,0:T(8,128)(2,1)} collective-permute-done((bf16[8,256,256]{2,1,0:T(8,128)(2,1)}, bf16[8,256,256]{2,1,0:T(8,128)(2,1)}, u32[]{:S(2)}, u32[]{:S(2)}) %collective-permute-start.31) | collective-permute-done | bytes 1048608 | tf_op jit(solution)/shard_map/ppermute | solution.py:43
  134.3 0.5 collective-permute-start.11
  134.9 5.9 %collective-permute-done.17.refs_17_ = bf16[8,256,256]{2,1,0:T(8,128)(2,1)} collective-permute-done((bf16[8,256,256]{2,1,0:T(8,128)(2,1)}, bf16[8,256,256]{2,1,0:T(8,128)(2,1)}, u32[]{:S(2)}, u32[]{:S(2)}) %collective-permute-start.17) | collective-permute-done | bytes 1048608 | tf_op jit(solution)/shard_map/ppermute | solution.py:43
  140.8 0.5 collective-permute-start.19
  141.4 0.1 convert_element_type.28
  141.6 0.2 multiply_reduce_fusion.1
  142.0 0.2 reduce_window_sum.11
  142.2 0.1 copy.17
  142.3 0.1 reshape.124.refs_3_
  142.4 0.1 select_reduce_fusion.refs_5_
  142.6 1.2 collective-permute-done.21.refs_21_
  143.8 1.5 collective-permute-done.19.refs_19_
  145.3 1.2 copy-done
  146.5 1.2 copy-done.2
  147.7 1.2 copy-done.4
  148.9 24.7 %product.1 = (f32[1024,512]{1,0:T(8,128)}, f32[1,512]{1,0:T(1,128)S(1)}) custom-call(s32[16]{0:T(128)S(1)} %stack.94.refs_0_, s32[8]{0:T(128)S(1)} %stack.103.refs_1_, s32[128]{0:T(128)S(1)} %reshape.123.refs_2_, s32[64]{0:T(128)S(1)} %reshape.124.refs_3_, s32[8]{0:T(128)S(1)} %reduce_sum.31.refs_4_, s32[8,32]{1,0:T(8,128)S(1)} %select_reduce_fusion.refs_5_, ...), custom_call_target="tpu_custom_call" | custom-call | tf_op jit(solution)/shard_map/product/pallas_call | solution.py:137
  173.7 0.1 collective-permute-start.32
  173.8 3.6 %collective-permute-done.32 = f32[512]{0:T(512)S(1)} collective-permute-done((f32[512]{0:T(512)S(1)}, f32[512]{0:T(512)S(1)}, u32[]{:S(2)}, u32[]{:S(2)}) %collective-permute-start.32) | collective-permute-done | bytes 2080 | tf_op jit(solution)/shard_map/ppermute | solution.py:43
  177.4 3.9 %collective-permute-start.33 = (f32[512]{0:T(512)S(1)}, f32[512]{0:T(512)S(1)}, u32[]{:S(2)}, u32[]{:S(2)}) collective-permute-start(f32[512]{0:T(512)S(1)} %add.280), channel_id=1, source_target_pairs={{0,48},{1,49},{2,50},{3,51},{4,52},{5,53},{6,54},{7,55},{8,56},{9,... | collective-permute-start | bytes 6152 | tf_op jit(solution)/shard_map/ppermute | solution.py:43
  181.2 1.6 collective-permute-done.33
  182.8 3.6 %collective-permute-start.34 = (f32[512]{0:T(512)S(1)}, f32[512]{0:T(512)S(1)}, u32[]{:S(2)}, u32[]{:S(2)}) collective-permute-start(f32[512]{0:T(512)S(1)} %add.281), channel_id=1, source_target_pairs={{0,64},{1,65},{2,66},{3,67},{4,68},{5,69},{6,70},{7,71},{8,72},{9,... | collective-permute-start | bytes 6152 | tf_op jit(solution)/shard_map/ppermute | solution.py:43
  186.4 1.6 collective-permute-done.34
  188.0 3.2 %multiply_divide_fusion = f32[1024,512]{1,0:T(8,128)} fusion(f32[1024,512]{1,0:T(8,128)} %get-tuple-element.7, f32[512]{0:T(512)S(1)} %add.282), kind=kLoop, calls=%fused_computation | loop fusion | flops 1048576 | bytes 4196352 | tf_op jit(solution)/shard_map/div | solution.py:254
  (75 shorter events, 1.2 us)
Async XLA Ops:
  1.6 0.9 copy-start.9
  2.3 1.6 copy-start.5
  4.5 3.7 %collective-permute-start.4 = (f32[576]{0:T(1024)S(1)}, f32[576]{0:T(1024)S(1)}, u32[]{:S(2)}, u32[]{:S(2)}) collective-permute-start(f32[576]{0:T(1024)S(1)} %pad_maximum_fusion), channel_id=1, source_target_pairs={{0,16},{1,17},{2,18},{3,19},{4,20},{5,21},{6,22},{7,23},{8,24},{9,... | collective-permute-start | bytes 6920 | tf_op jit(solution)/shard_map/ppermute | solution.py:43
  8.2 5.7 %collective-permute-start.5 = (f32[576]{0:T(1024)S(1)}, f32[576]{0:T(1024)S(1)}, u32[]{:S(2)}, u32[]{:S(2)}) collective-permute-start(f32[576]{0:T(1024)S(1)} %fusion.1), channel_id=1, source_target_pairs={{0,48},{1,49},{2,50},{3,51},{4,52},{5,53},{6,54},{7,55},{8,56},{9,... | collective-permute-start | bytes 6920 | tf_op jit(solution)/shard_map/ppermute | solution.py:43
  13.9 14.5 %collective-permute-start.6 = (f32[576]{0:T(1024)S(1)}, f32[576]{0:T(1024)S(1)}, u32[]{:S(2)}, u32[]{:S(2)}) collective-permute-start(f32[576]{0:T(1024)S(1)} %add.278), channel_id=1, source_target_pairs={{0,64},{1,65},{2,66},{3,67},{4,68},{5,69},{6,70},{7,71},{8,72},{9,... | collective-permute-start | bytes 6920 | tf_op jit(solution)/shard_map/ppermute | solution.py:43
  17.3 1.1 collective-permute-start
  18.4 3.5 %collective-permute-start.1 = (f32[128]{0:T(128)S(1)}, f32[128]{0:T(128)S(1)}, u32[]{:S(2)}, u32[]{:S(2)}) collective-permute-start(f32[128]{0:T(128)S(1)} %add.272), channel_id=1, source_target_pairs={{0,8},{1,9},{2,10},{3,11},{4,12},{5,13},{6,14},{7,15},{8,0},{9,1},... | collective-permute-start | bytes 1544 | tf_op jit(solution)/shard_map/ppermute | solution.py:43
  22.0 3.5 %collective-permute-start.2 = (f32[128]{0:T(128)S(1)}, f32[128]{0:T(128)S(1)}, u32[]{:S(2)}, u32[]{:S(2)}) collective-permute-start(f32[128]{0:T(128)S(1)} %add.273), channel_id=1, source_target_pairs={{0,2},{1,3},{2,0},{3,1},{4,6},{5,7},{6,4},{7,5},{8,10},{9,11},{10,... | collective-permute-start | bytes 1544 | tf_op jit(solution)/shard_map/ppermute | solution.py:43
  25.5 11.1 %collective-permute-start.3 = (f32[128]{0:T(128)S(1)}, f32[128]{0:T(128)S(1)}, u32[]{:S(2)}, u32[]{:S(2)}) collective-permute-start(f32[128]{0:T(128)S(1)} %add.274), channel_id=1, source_target_pairs={{0,6},{1,7},{2,4},{3,5},{4,2},{5,3},{6,0},{7,1},{8,14},{9,15},{10,... | collective-permute-start | bytes 1544 | tf_op jit(solution)/shard_map/ppermute | solution.py:43
  34.4 27.8 %collective-permute-start.26 = (bf16[8,256,256]{2,1,0:T(8,128)(2,1)}, bf16[8,256,256]{2,1,0:T(8,128)(2,1)S(1)}, u32[]{:S(2)}, u32[]{:S(2)}) collective-permute-start(bf16[8,256,256]{2,1,0:T(8,128)(2,1)} %scale.1.refs_6_.refs_22_), channel_id=1, source_target_pairs={{0,64},{1,65},{2,66},{3,67},{4,68},{5,69},{6,70},{7,71},{8,72},{9,... | collective-permute-start | bytes 3145736 | tf_op jit(solution)/shard_map/ppermute | solution.py:43
  34.9 27.3 %collective-permute-start.22 = (bf16[8,256,256]{2,1,0:T(8,128)(2,1)}, bf16[8,256,256]{2,1,0:T(8,128)(2,1)S(1)}, u32[]{:S(2)}, u32[]{:S(2)}) collective-permute-start(bf16[8,256,256]{2,1,0:T(8,128)(2,1)} %scale.1.refs_6_.refs_22_), channel_id=1, source_target_pairs={{0,16},{1,49},{2,18},{3,51},{4,20},{5,53},{6,22},{7,55},{8,24},{9,... | collective-permute-start | bytes 3145736 | tf_op jit(solution)/shard_map/ppermute | solution.py:43
  34.9 44.8 %collective-permute-start.14 = (bf16[8,256,256]{2,1,0:T(8,128)(2,1)}, bf16[8,256,256]{2,1,0:T(8,128)(2,1)S(1)}, u32[]{:S(2)}, u32[]{:S(2)}) collective-permute-start(bf16[8,256,256]{2,1,0:T(8,128)(2,1)} %scale.1.refs_6_.refs_22_), channel_id=1, source_target_pairs={{0,8},{1,9},{2,10},{3,11},{4,12},{5,13},{6,14},{7,15},{8,0},{9,1},... | collective-permute-start | bytes 3145736 | tf_op jit(solution)/shard_map/ppermute | solution.py:43
  36.4 43.4 %collective-permute-start.8 = (bf16[8,256,256]{2,1,0:T(8,128)(2,1)}, bf16[8,256,256]{2,1,0:T(8,128)(2,1)S(1)}, u32[]{:S(2)}, u32[]{:S(2)}) collective-permute-start(bf16[8,256,256]{2,1,0:T(8,128)(2,1)} %scale.1.refs_6_.refs_22_), channel_id=1, source_target_pairs={{0,2},{1,7},{2,4},{3,1},{4,6},{5,3},{6,0},{7,5},{8,10},{9,15},{10,... | collective-permute-start | bytes 3145736 | tf_op jit(solution)/shard_map/ppermute | solution.py:43
  36.6 43.4 %collective-permute-start.7 = (bf16[8,256,256]{2,1,0:T(8,128)(2,1)}, bf16[8,256,256]{2,1,0:T(8,128)(2,1)S(1)}, u32[]{:S(2)}, u32[]{:S(2)}) collective-permute-start(bf16[8,256,256]{2,1,0:T(8,128)(2,1)} %scale.1.refs_6_.refs_22_), channel_id=1, source_target_pairs={{0,1},{1,0},{2,3},{3,2},{4,5},{5,4},{6,7},{7,6},{8,9},{9,8},{10,11... | collective-permute-start | bytes 3145736 | tf_op jit(solution)/shard_map/ppermute | solution.py:43
  62.3 19.0 %copy-start.6 = (bf16[8,256,256]{2,1,0:T(8,128)(2,1)}, bf16[8,256,256]{2,1,0:T(8,128)(2,1)S(1)}, u32[]{:S(2)}) copy-start(bf16[8,256,256]{2,1,0:T(8,128)(2,1)S(1)} %collective-permute-done.26.refs_26_) | copy-start | bytes 3145732
  62.3 17.7 %collective-permute-start.28 = (bf16[8,256,256]{2,1,0:T(8,128)(2,1)S(1)}, bf16[8,256,256]{2,1,0:T(8,128)(2,1)S(1)}, u32[]{:S(2)}, u32[]{:S(2)}) collective-permute-start(bf16[8,256,256]{2,1,0:T(8,128)(2,1)S(1)} %collective-permute-done.26.refs_26_), channel_id=1, source_target_pairs={{0,1},{1,0},{2,3},{3,2},{4,5},{5,4},{6,7},{7,6},{8,9},{9,8},{10,11... | collective-permute-start | bytes 3145736 | tf_op jit(solution)/shard_map/ppermute | solution.py:43
  62.3 33.4 %copy-start.7 = (bf16[8,256,256]{2,1,0:T(8,128)(2,1)}, bf16[8,256,256]{2,1,0:T(8,128)(2,1)S(1)}, u32[]{:S(2)}) copy-start(bf16[8,256,256]{2,1,0:T(8,128)(2,1)S(1)} %collective-permute-done.22.refs_23_) | copy-start | bytes 3145732
  62.3 18.9 %collective-permute-start.27 = (bf16[8,256,256]{2,1,0:T(8,128)(2,1)S(1)}, bf16[8,256,256]{2,1,0:T(8,128)(2,1)}, u32[]{:S(2)}, u32[]{:S(2)}) collective-permute-start(bf16[8,256,256]{2,1,0:T(8,128)(2,1)S(1)} %collective-permute-done.26.refs_26_), channel_id=1, source_target_pairs={{0,16},{1,49},{2,18},{3,51},{4,20},{5,53},{6,22},{7,55},{8,24},{9,... | collective-permute-start | bytes 3145736 | tf_op jit(solution)/shard_map/ppermute | solution.py:43
  79.7 16.0 %collective-permute-start.25 = (bf16[8,256,256]{2,1,0:T(8,128)(2,1)S(1)}, bf16[8,256,256]{2,1,0:T(8,128)(2,1)S(1)}, u32[]{:S(2)}, u32[]{:S(2)}) collective-permute-start(bf16[8,256,256]{2,1,0:T(8,128)(2,1)S(1)} %collective-permute-done.22.refs_23_), channel_id=1, source_target_pairs={{0,16},{1,49},{2,18},{3,51},{4,20},{5,53},{6,22},{7,55},{8,24},{9,... | collective-permute-start | bytes 3145736 | tf_op jit(solution)/shard_map/ppermute | solution.py:43
  79.7 16.1 %collective-permute-start.16 = (bf16[8,256,256]{2,1,0:T(8,128)(2,1)S(1)}, bf16[8,256,256]{2,1,0:T(8,128)(2,1)}, u32[]{:S(2)}, u32[]{:S(2)}) collective-permute-start(bf16[8,256,256]{2,1,0:T(8,128)(2,1)S(1)} %collective-permute-done.14.refs_14_), channel_id=1, source_target_pairs={{0,2},{1,7},{2,4},{3,1},{4,6},{5,3},{6,0},{7,5},{8,10},{9,15},{10,... | collective-permute-start | bytes 3145736 | tf_op jit(solution)/shard_map/ppermute | solution.py:43
  79.9 16.1 %collective-permute-start.15 = (bf16[8,256,256]{2,1,0:T(8,128)(2,1)S(1)}, bf16[8,256,256]{2,1,0:T(8,128)(2,1)}, u32[]{:S(2)}, u32[]{:S(2)}) collective-permute-start(bf16[8,256,256]{2,1,0:T(8,128)(2,1)S(1)} %collective-permute-done.14.refs_14_), channel_id=1, source_target_pairs={{0,1},{1,0},{2,3},{3,2},{4,5},{5,4},{6,7},{7,6},{8,9},{9,8},{10,11... | collective-permute-start | bytes 3145736 | tf_op jit(solution)/shard_map/ppermute | solution.py:43
  79.9 27.1 %collective-permute-start.12 = (bf16[8,256,256]{2,1,0:T(8,128)(2,1)S(1)}, bf16[8,256,256]{2,1,0:T(8,128)(2,1)}, u32[]{:S(2)}, u32[]{:S(2)}) collective-permute-start(bf16[8,256,256]{2,1,0:T(8,128)(2,1)S(1)} %collective-permute-done.8.refs_8_), channel_id=1, source_target_pairs={{0,2},{1,7},{2,4},{3,1},{4,6},{5,3},{6,0},{7,5},{8,10},{9,15},{10,... | collective-permute-start | bytes 3145736 | tf_op jit(solution)/shard_map/ppermute | solution.py:43
  81.2 27.7 %collective-permute-start.10 = (bf16[8,256,256]{2,1,0:T(8,128)(2,1)S(1)}, bf16[8,256,256]{2,1,0:T(8,128)(2,1)S(1)}, u32[]{:S(2)}, u32[]{:S(2)}) collective-permute-start(bf16[8,256,256]{2,1,0:T(8,128)(2,1)S(1)} %collective-permute-done.8.refs_8_), channel_id=1, source_target_pairs={{0,1},{1,0},{2,3},{3,2},{4,5},{5,4},{6,7},{7,6},{8,9},{9,8},{10,11... | collective-permute-start | bytes 3145736 | tf_op jit(solution)/shard_map/ppermute | solution.py:43
  95.7 23.5 %copy-start.8 = (bf16[8,256,256]{2,1,0:T(8,128)(2,1)}, bf16[8,256,256]{2,1,0:T(8,128)(2,1)S(1)}, u32[]{:S(2)}) copy-start(bf16[8,256,256]{2,1,0:T(8,128)(2,1)S(1)} %collective-permute-done.25.refs_25_) | copy-start | bytes 3145732
  95.7 16.0 %collective-permute-start.23 = (bf16[8,256,256]{2,1,0:T(8,128)(2,1)S(1)}, bf16[8,256,256]{2,1,0:T(8,128)(2,1)S(1)}, u32[]{:S(2)}, u32[]{:S(2)}) collective-permute-start(bf16[8,256,256]{2,1,0:T(8,128)(2,1)S(1)} %collective-permute-done.7.refs_7_), channel_id=1, source_target_pairs={{0,16},{1,49},{2,18},{3,51},{4,20},{5,53},{6,22},{7,55},{8,24},{9,... | collective-permute-start | bytes 3145736 | tf_op jit(solution)/shard_map/ppermute | solution.py:43
  95.8 22.4 %collective-permute-start.9 = (bf16[8,256,256]{2,1,0:T(8,128)(2,1)S(1)}, bf16[8,256,256]{2,1,0:T(8,128)(2,1)S(1)}, u32[]{:S(2)}, u32[]{:S(2)}) collective-permute-start(bf16[8,256,256]{2,1,0:T(8,128)(2,1)S(1)} %collective-permute-done.7.refs_7_), channel_id=1, source_target_pairs={{0,2},{1,7},{2,4},{3,1},{4,6},{5,3},{6,0},{7,5},{8,10},{9,15},{10,... | collective-permute-start | bytes 3145736 | tf_op jit(solution)/shard_map/ppermute | solution.py:43
  96.0 26.9 %collective-permute-start.29 = (bf16[8,256,256]{2,1,0:T(8,128)(2,1)S(1)}, bf16[8,256,256]{2,1,0:T(8,128)(2,1)S(1)}, u32[]{:S(2)}, u32[]{:S(2)}) collective-permute-start(bf16[8,256,256]{2,1,0:T(8,128)(2,1)S(1)} %collective-permute-done.28), channel_id=1, source_target_pairs={{0,16},{1,49},{2,18},{3,51},{4,20},{5,53},{6,22},{7,55},{8,24},{9,... | collective-permute-start | bytes 3145736 | tf_op jit(solution)/shard_map/ppermute | solution.py:43
  107.1 27.2 %collective-permute-start.31 = (bf16[8,256,256]{2,1,0:T(8,128)(2,1)}, bf16[8,256,256]{2,1,0:T(8,128)(2,1)}, u32[]{:S(2)}, u32[]{:S(2)}) collective-permute-start(bf16[8,256,256]{2,1,0:T(8,128)(2,1)} %collective-permute-done.27.refs_27_), channel_id=1, source_target_pairs={{0,16},{1,49},{2,18},{3,51},{4,20},{5,53},{6,22},{7,55},{8,24},{9,... | collective-permute-start | bytes 3145736 | tf_op jit(solution)/shard_map/ppermute | solution.py:43
  108.9 1.0 copy-start.1
  109.9 24.4 %collective-permute-start.20 = (bf16[8,256,256]{2,1,0:T(8,128)(2,1)}, bf16[8,256,256]{2,1,0:T(8,128)(2,1)}, u32[]{:S(2)}, u32[]{:S(2)}) collective-permute-start(bf16[8,256,256]{2,1,0:T(8,128)(2,1)} %collective-permute-done.16.refs_16_), channel_id=1, source_target_pairs={{0,2},{1,7},{2,4},{3,1},{4,6},{5,3},{6,0},{7,5},{8,10},{9,15},{10,... | collective-permute-start | bytes 3145736 | tf_op jit(solution)/shard_map/ppermute | solution.py:43
  111.7 11.2 %copy-start.10 = (bf16[8,256,256]{2,1,0:T(8,128)(2,1)}, bf16[8,256,256]{2,1,0:T(8,128)(2,1)S(1)}, u32[]{:S(2)}) copy-start(bf16[8,256,256]{2,1,0:T(8,128)(2,1)S(1)} %collective-permute-done.23) | copy-start | bytes 3145732
  111.7 23.1 %collective-permute-start.18 = (bf16[8,256,256]{2,1,0:T(8,128)(2,1)}, bf16[8,256,256]{2,1,0:T(8,128)(2,1)}, u32[]{:S(2)}, u32[]{:S(2)}) collective-permute-start(bf16[8,256,256]{2,1,0:T(8,128)(2,1)} %collective-permute-done.16.refs_16_), channel_id=1, source_target_pairs={{0,1},{1,0},{2,3},{3,2},{4,5},{5,4},{6,7},{7,6},{8,9},{9,8},{10,11... | collective-permute-start | bytes 3145736 | tf_op jit(solution)/shard_map/ppermute | solution.py:43
  118.2 1.0 copy-start.3
  119.2 21.6 %collective-permute-start.17 = (bf16[8,256,256]{2,1,0:T(8,128)(2,1)}, bf16[8,256,256]{2,1,0:T(8,128)(2,1)}, u32[]{:S(2)}, u32[]{:S(2)}) collective-permute-start(bf16[8,256,256]{2,1,0:T(8,128)(2,1)} %collective-permute-done.15.refs_15_), channel_id=1, source_target_pairs={{0,2},{1,7},{2,4},{3,1},{4,6},{5,3},{6,0},{7,5},{8,10},{9,15},{10,... | collective-permute-start | bytes 3145736 | tf_op jit(solution)/shard_map/ppermute | solution.py:43
  123.0 1.0 copy-start.11
  123.9 16.8 %collective-permute-start.13 = (bf16[8,256,256]{2,1,0:T(8,128)(2,1)}, bf16[8,256,256]{2,1,0:T(8,128)(2,1)}, u32[]{:S(2)}, u32[]{:S(2)}) collective-permute-start(bf16[8,256,256]{2,1,0:T(8,128)(2,1)} %collective-permute-done.12.refs_12_), channel_id=1, source_target_pairs={{0,1},{1,0},{2,3},{3,2},{4,5},{5,4},{6,7},{7,6},{8,9},{9,8},{10,11... | collective-permute-start | bytes 3145736 | tf_op jit(solution)/shard_map/ppermute | solution.py:43
  134.3 8.3 %collective-permute-start.24 = (bf16[8,256,256]{2,1,0:T(8,128)(2,1)}, bf16[8,256,256]{2,1,0:T(8,128)(2,1)}, u32[]{:S(2)}, u32[]{:S(2)}) collective-permute-start(bf16[8,256,256]{2,1,0:T(8,128)(2,1)} %copy-done.10), channel_id=1, source_target_pairs={{0,1},{1,0},{2,3},{3,2},{4,5},{5,4},{6,7},{7,6},{8,9},{9,8},{10,11... | collective-permute-start | bytes 3145736 | tf_op jit(solution)/shard_map/ppermute | solution.py:43
  134.3 8.3 %collective-permute-start.11 = (bf16[8,256,256]{2,1,0:T(8,128)(2,1)}, bf16[8,256,256]{2,1,0:T(8,128)(2,1)}, u32[]{:S(2)}, u32[]{:S(2)}) collective-permute-start(bf16[8,256,256]{2,1,0:T(8,128)(2,1)} %copy-done.3), channel_id=1, source_target_pairs={{0,1},{1,0},{2,3},{3,2},{4,5},{5,4},{6,7},{7,6},{8,9},{9,8},{10,11... | collective-permute-start | bytes 3145736 | tf_op jit(solution)/shard_map/ppermute | solution.py:43
  134.8 7.8 %collective-permute-start.30 = (bf16[8,256,256]{2,1,0:T(8,128)(2,1)}, bf16[8,256,256]{2,1,0:T(8,128)(2,1)}, u32[]{:S(2)}, u32[]{:S(2)}) collective-permute-start(bf16[8,256,256]{2,1,0:T(8,128)(2,1)} %copy-done.11), channel_id=1, source_target_pairs={{0,1},{1,0},{2,3},{3,2},{4,5},{5,4},{6,7},{7,6},{8,9},{9,8},{10,11... | collective-permute-start | bytes 3145736 | tf_op jit(solution)/shard_map/ppermute | solution.py:43
  140.8 3.0 %collective-permute-start.21 = (bf16[8,256,256]{2,1,0:T(8,128)(2,1)}, bf16[8,256,256]{2,1,0:T(8,128)(2,1)}, u32[]{:S(2)}, u32[]{:S(2)}) collective-permute-start(bf16[8,256,256]{2,1,0:T(8,128)(2,1)} %collective-permute-done.20.refs_20_), channel_id=1, source_target_pairs={{0,1},{1,0},{2,3},{3,2},{4,5},{5,4},{6,7},{7,6},{8,9},{9,8},{10,11... | collective-permute-start | bytes 3145736 | tf_op jit(solution)/shard_map/ppermute | solution.py:43
  140.8 4.5 %collective-permute-start.19 = (bf16[8,256,256]{2,1,0:T(8,128)(2,1)}, bf16[8,256,256]{2,1,0:T(8,128)(2,1)}, u32[]{:S(2)}, u32[]{:S(2)}) collective-permute-start(bf16[8,256,256]{2,1,0:T(8,128)(2,1)} %collective-permute-done.17.refs_17_), channel_id=1, source_target_pairs={{0,1},{1,0},{2,3},{3,2},{4,5},{5,4},{6,7},{7,6},{8,9},{9,8},{10,11... | collective-permute-start | bytes 3145736 | tf_op jit(solution)/shard_map/ppermute | solution.py:43
  145.3 1.2 copy-start
  146.5 1.2 copy-start.2
  147.7 1.2 copy-start.4
  173.7 3.7 %collective-permute-start.32 = (f32[512]{0:T(512)S(1)}, f32[512]{0:T(512)S(1)}, u32[]{:S(2)}, u32[]{:S(2)}) collective-permute-start(f32[512]{0:T(512)S(1)} %bitcast.32), channel_id=1, source_target_pairs={{0,16},{1,17},{2,18},{3,19},{4,20},{5,21},{6,22},{7,23},{8,24},{9,... | collective-permute-start | bytes 6152 | tf_op jit(solution)/shard_map/ppermute | solution.py:43
  177.4 5.4 %collective-permute-start.33 = (f32[512]{0:T(512)S(1)}, f32[512]{0:T(512)S(1)}, u32[]{:S(2)}, u32[]{:S(2)}) collective-permute-start(f32[512]{0:T(512)S(1)} %add.280), channel_id=1, source_target_pairs={{0,48},{1,49},{2,50},{3,51},{4,52},{5,53},{6,54},{7,55},{8,56},{9,... | collective-permute-start | bytes 6152 | tf_op jit(solution)/shard_map/ppermute | solution.py:43
  182.8 5.2 %collective-permute-start.34 = (f32[512]{0:T(512)S(1)}, f32[512]{0:T(512)S(1)}, u32[]{:S(2)}, u32[]{:S(2)}) collective-permute-start(f32[512]{0:T(512)S(1)} %add.281), channel_id=1, source_target_pairs={{0,64},{1,65},{2,66},{3,67},{4,68},{5,69},{6,70},{7,71},{8,72},{9,... | collective-permute-start | bytes 6152 | tf_op jit(solution)/shard_map/ppermute | solution.py:43

commit v2 on v0

v2 whole, which is shorter than its diff:
```python
import functools
import jax
import jax.numpy as jnp
from jax import lax
from jax.experimental import pallas as pl
from jax.experimental.pallas import tpu as pltpu
from jax.sharding import PartitionSpec as P

AXES = ("row", "col")
YH, NZ, YL, NX, NC = 2, 4, 2, 4, 2
F32 = jnp.float32
BF16 = jnp.bfloat16
I32 = jnp.int32
GROUP = 4


def place(yh, z, yl, x, c):
    return (yh * NZ + z) * (YL * NX * NC) + (yl * NX + x) * NC + c


def pairs(step):
    return [
        (place(yh, z, yl, x, c), place(*step(yh, z, yl, x, c)))
        for yh in range(YH)
        for z in range(NZ)
        for yl in range(YL)
        for x in range(NX)
        for c in range(NC)
    ]


X_UP = pairs(lambda yh, z, yl, x, c: (yh, z, yl, (x + 1) % NX, c))
X_DOWN = pairs(lambda yh, z, yl, x, c: (yh, z, yl, (x - 1) % NX, c))
Z_UP = pairs(lambda yh, z, yl, x, c: (yh, (z + 1) % NZ, yl, x, c))
Z_DOWN = pairs(lambda yh, z, yl, x, c: (yh, (z - 1) % NZ, yl, x, c))
SWAP_CORE = pairs(lambda yh, z, yl, x, c: (yh, z, yl, x, 1 - c))
SWAP_YL = pairs(lambda yh, z, yl, x, c: (yh, z, 1 - yl, x, c))
SWAP_YH = pairs(lambda yh, z, yl, x, c: (1 - yh, z, yl, x, c))
Z_TURNS = [pairs(lambda yh, z, yl, x, c, d=d: (yh, (z + d) % NZ, yl, x, c)) for d in range(1, NZ)]
X_TURNS = [pairs(lambda yh, z, yl, x, c, d=d: (yh, z, yl, (x + d) % NX, c)) for d in range(1, NX)]


def move(value, perm):
    return lax.ppermute(value, AXES, perm)


def turn_sum(value, turns):
    return value + sum(move(value, turn) for turn in turns)


def row_sum(value):
    value = turn_sum(value, Z_TURNS)
    return value + move(value, SWAP_YH)


def after(value, *deps):
    return lax.optimization_barrier((value, *deps))[0]


def product_kernel(n_a, n_b, shape, cols_out, begun, *refs):
    rows, cols, grid, tile = shape
    base_a, base_b, todo_a, todo_b, n_todo_a, n_todo_b, count, order = refs[:8]
    refs = refs[8:]
    if begun:
        start_ref, refs = refs[0], refs[1:]
    a_in, b_in, refs = refs[:n_a], refs[n_a:n_a + n_b], refs[n_a + n_b:]
    out_ref, a_buf, b_buf, acc, a_sem, b_sem = refs
    no_a, no_b = rows * grid, cols * grid
    deep = a_in[0].shape[1] // tile

    def tile_at(ref, i, j):
        return ref.at[pl.ds(pl.multiple_of(i * tile, tile), tile), pl.ds(pl.multiple_of(j * tile, tile), tile)]

    def each(act):
        for u in range(n_a):
            def a_tile(n, _, u=u):
                t = todo_a[u, n]
                i, j = t // deep, t % deep
                slot = base_a[u] + i * grid + j
                act(pltpu.make_async_copy(tile_at(a_in[u], i, j), a_buf.at[slot], a_sem.at[slot]))
                return 0

            lax.fori_loop(0, n_todo_a[u], a_tile, 0)
        for u in range(n_b):
            def b_tile(n, _, u=u):
                t = todo_b[u, n]
                slot = base_b[u] * cols + t
                act(pltpu.make_async_copy(tile_at(b_in[u], t // cols, t % cols), b_buf.at[slot], b_sem.at[slot]))
                return 0

            lax.fori_loop(0, n_todo_b[u], b_tile, 0)

    each(lambda copy: copy.start())
    a_buf[no_a] = jnp.zeros((tile, tile), BF16)
    b_buf[no_b] = jnp.zeros((tile, tile), BF16)
    each(lambda copy: copy.wait())

    for n_out, j in enumerate(cols_out):
        for i in range(rows):
            down = slice(i * tile, (i + 1) * tile)
            if begun:
                acc[...] = start_ref[down, j * tile:(j + 1) * tile]
            else:
                acc[...] = jnp.zeros_like(acc)

            def step(n, _, i=i, j=j):
                part = None
                for g in range(GROUP):
                    k = order[i * cols + j, n * GROUP + g]
                    a_tile = a_buf[jnp.where(k < grid, i * grid + k, no_a)]
                    b_tile = b_buf[jnp.where(k < grid, k * cols + j, no_b)]
                    dot = jnp.dot(a_tile, b_tile, preferred_element_type=F32)
                    part = dot if part is None else part + dot
                acc[...] += part
                return 0

            lax.fori_loop(0, (count[i * cols + j] + GROUP - 1) // GROUP, step, 0)
            out_ref[down, n_out * tile:(n_out + 1) * tile] = acc[...]


def listed(flags):
    size = flags.shape[1]
    ids = jnp.arange(size, dtype=I32)
    count = jnp.sum(flags, axis=1)
    rank = jnp.cumsum(flags, axis=1) - 1
    hit = (rank[:, :, None] == ids[None, None, :]) & (flags[:, :, None] > 0)
    order = jnp.sum(jnp.where(hit, ids[None, :, None], 0), axis=1)
    return jnp.where(ids[None, :] < count[:, None], order, size).astype(I32), count.astype(I32)


def product(a_units, b_units, used, cols_out, start=None):
    rows, cols, grid = used.shape
    begun = start is not None
    tile = a_units[0][0].shape[0] // rows
    deep = a_units[0][0].shape[1] // tile
    wanted = jnp.stack([used[:, j] if j in cols_out else jnp.zeros_like(used[:, j]) for j in range(cols)], axis=1)
    need_a = jnp.max(wanted, axis=1)
    need_b = jnp.max(wanted, axis=0).T
    base_a = jnp.stack([base for _, base in a_units]).astype(I32)
    base_b = jnp.stack([base for _, base in b_units]).astype(I32)
    todo_a, n_todo_a = listed(
        jnp.stack([lax.dynamic_slice(need_a, (0, base), (rows, deep)).reshape(-1) for _, base in a_units])
    )
    todo_b, n_todo_b = listed(
        jnp.stack([lax.dynamic_slice(need_b, (base, 0), (deep, cols)).reshape(-1) for _, base in b_units])
    )
    order, count = listed(wanted.reshape(rows * cols, grid))
    order = jnp.pad(order, ((0, 0), (0, GROUP - 1)), constant_values=grid)
    smem = pl.BlockSpec(memory_space=pltpu.SMEM)
    vmem = pl.BlockSpec(memory_space=pltpu.VMEM)
    return pl.pallas_call(
        functools.partial(product_kernel, len(a_units), len(b_units), (rows, cols, grid, tile), cols_out, begun),
        out_shape=jax.ShapeDtypeStruct((rows * tile, len(cols_out) * tile), F32),
        in_specs=[smem] * 8
        + [vmem] * begun
        + [pl.BlockSpec(memory_space=pl.ANY)] * (len(a_units) + len(b_units)),
        out_specs=vmem,
        scratch_shapes=[
            pltpu.VMEM((rows * grid + 1, tile, tile), BF16),
            pltpu.VMEM((cols * grid + 1, tile, tile), BF16),
            pltpu.VMEM((tile, tile), F32),
            pltpu.SemaphoreType.DMA((rows * grid,)),
            pltpu.SemaphoreType.DMA((cols * grid,)),
        ],
        compiler_params=pltpu.CompilerParams(vmem_limit_bytes=40 * 1024 * 1024),
        cost_estimate=pl.CostEstimate(flops=4 * 10**9, bytes_accessed=16 * 2**20, transcendentals=0),
        name="finish" if begun else "begin",
    )(
        base_a, base_b, todo_a, todo_b, n_todo_a, n_todo_b, count, order,
        *([start] if begun else []),
        *[value for value, _ in a_units],
        *[value for value, _ in b_units],
    )


def tile_keep(flags):
    tile_rows, tile_cols = flags.shape
    row_ids = lax.axis_index("row") * tile_rows + jnp.arange(tile_rows, dtype=I32)
    col_ids = lax.axis_index("col") * tile_cols + jnp.arange(tile_cols, dtype=I32)
    diagonal = (row_ids[:, None] == col_ids[None, :]).astype(I32)
    return jnp.maximum(flags, diagonal)


def shards(entries, pattern, prune):
    row, col = lax.axis_index("row"), lax.axis_index("col")
    rows, cols = pattern.shape
    height, width = entries.shape
    grid = rows * lax.axis_size("row")
    yh, z = row // NZ, row % NZ
    yl, x, c = col // (NX * NC), (col // NC) % NX, col % NC

    keep = tile_keep(pattern)
    keep_out = tile_keep(prune)
    keep_f = keep.astype(F32)
    masked = (
        entries.reshape(rows, height // rows, cols, width // cols) * keep_f[:, None, :, None]
    ).reshape(height, width)

    left = lax.dynamic_update_slice(jnp.zeros((rows, grid), F32), keep_f, (0, col * cols)).reshape(-1)
    left = turn_sum(left, X_TURNS)
    left = left + move(left, SWAP_YL)

    flags = lax.dynamic_update_slice(jnp.zeros((grid, cols), F32), keep_f, (row * rows, 0))
    sums = jnp.concatenate([jnp.sum(masked, axis=0), flags.reshape(-1)])
    sums = row_sum(sums)
    colsum, right = sums[:width], sums[width:]
    a = (masked / colsum[None, :]).astype(BF16)
    a, left = lax.optimization_barrier((a, left))

    half = height // 2
    mine = lax.dynamic_slice(a, (c * half, 0), (half, width))
    theirs = lax.dynamic_slice(a, ((1 - c) * half, 0), (half, width))
    b = jnp.concatenate([mine, move(theirs, SWAP_CORE)], axis=1)
    notes = jnp.concatenate([left, right, keep_out.astype(F32).reshape(-1)])
    notes_o = move(notes, SWAP_CORE)

    xl, xr, pa = move(a, X_UP), move(a, X_DOWN), move(a, SWAP_YL)
    zl, zr = move(b, Z_UP), move(b, Z_DOWN)
    a, b, xl, xr, pa, zl, zr = lax.optimization_barrier((a, b, xl, xr, pa, zl, zr))
    pxl, pxr = move(pa, X_UP), move(pa, X_DOWN)
    zf, pb = move(zl, Z_UP), move(b, SWAP_YH)
    a, b, xl, xr, pa, zl, zr, pxl, pxr, zf, pb, notes_o, left, right = lax.optimization_barrier(
        (a, b, xl, xr, pa, zl, zr, pxl, pxr, zf, pb, notes_o, left, right)
    )
    xf, pxf = move(xl, X_UP), move(pxr, X_DOWN)
    pzl, pzr, pzf = move(pb, Z_UP), move(pb, Z_DOWN), move(zf, SWAP_YH)

    n_left, n_right = rows * grid, grid * cols
    left = (left + notes_o[:n_left]).reshape(rows, -1, NC, cols)
    left = lax.dynamic_index_in_dim(left, c, 2, False).reshape(rows, -1)
    right = jnp.concatenate(
        [right.reshape(grid, cols), notes_o[n_left:n_left + n_right].reshape(grid, cols)], axis=1
    )
    right = lax.dynamic_index_in_dim(right.reshape(-1, NC, cols, NC * cols), c, 1, False).reshape(-1, NC * cols)
    out = jnp.concatenate([keep_out.astype(F32), notes_o[n_left + n_right:].reshape(rows, cols)], axis=1)
    used = (left[:, None, :] * right.T[None, :, :] * out[:, :, None]).astype(I32)

    a_unit = lambda value, y, dx: (value, (y * NX + (x + dx) % NX) * cols)
    b_unit = lambda value, y, dz: (value, (y * NZ + (z + dz) % NZ) * cols)
    py, ph = 1 - yl, 1 - yh
    a_early = [
        a_unit(a, yl, 0), a_unit(xl, yl, NX - 1), a_unit(xr, yl, 1),
        a_unit(pa, py, 0), a_unit(pxl, py, NX - 1), a_unit(pxr, py, 1),
    ]
    a_late = [a_unit(xf, yl, 2), a_unit(pxf, py, 2)]
    b_early = [
        b_unit(b, yh, 0), b_unit(zl, yh, NZ - 1), b_unit(zr, yh, 1), b_unit(zf, yh, 2), b_unit(pb, ph, 0),
    ]
    b_late = [b_unit(pzl, ph, NZ - 1), b_unit(pzr, ph, 1), b_unit(pzf, ph, 2)]

    ids = jnp.arange(used.shape[2], dtype=I32)
    late = functools.reduce(
        jnp.logical_or, [(ids >= base) & (ids < base + cols) for _, base in a_late + b_late]
    ).astype(I32)[None, None, :]
    own_cols, other_cols = tuple(range(cols)), tuple(range(cols, NC * cols))
    begun = product(a_early, b_early, used * (1 - late), own_cols + other_cols)
    a_units, b_units, used = a_early + a_late, b_early + b_late, used * late
    part_o = product(a_units, b_units, used, other_cols, begun)
    got = move(part_o, SWAP_CORE)
    part = product(a_units, b_units, used, own_cols, begun)
    full = part + got
    inflated = full * full
    total = row_sum(jnp.sum(inflated, axis=0))
    order = float(height * lax.axis_size("row"))
    return inflated * (order / total)[None, :]


def solution(mesh):
    return jax.shard_map(
        shards,
        mesh=mesh,
        in_specs=(P("row", "col"), P("row", "col"), P("row", "col")),
        out_specs=P("row", "col"),
        check_vma=False,
    )
```

time: 282 us -> 161 us (0.57)
  waiting for transfers between devices: 194 us -> 64.8 us
  blocking collectives: 49.9 us -> 0 us
  starting transfers between devices: 0.04 us -> 37.9 us
  Pallas kernels: 0 us -> 25.1 us
  local copies, waits for them, and re-layouts: 3.16 us -> 20.7 us
  matrix products: 15.7 us -> 0 us
  between operations: 13.4 us -> 0.5 us
  other arithmetic: 5.76 us -> 11.9 us
    all_gather x2 -> x0, waiting for transfers between devices: 193 us -> none  [the longest x1 103 us: shards(): right = lax.all_gather(stoch, 'row', axis=0, tiled=True)]
    ppermute x0 -> x29, waiting for transfers between devices: none -> 64.8 us  [move(): return lax.ppermute(value, AXES, perm)]
    psum x2 -> x0, blocking collectives: 49.9 us -> none  [the longest x1 25.7 us: shards(): colsum = lax.psum(jnp.sum(masked, axis=0), 'row')]
    ppermute x0 -> x29, starting transfers between devices: none -> 37.9 us  [move(): return lax.ppermute(value, AXES, perm)]
    pallas_call x0 -> x3, Pallas kernels: none -> 25.1 us  [product(): pl.pallas_call(functools.partial(product_kernel, len(a_units), len(b_unit...]
    dot_general x1 -> x0, matrix products: 15.7 us -> none  [shards(): jnp.dot(lax.all_gather(stoch, 'col', axis=1, tiled=True), right, preferre...]
    unnamed x4 -> x33, local copies, waits for them, and re-layouts: 1.75 us -> 11.9 us
    reduce_sum x1 -> x19, other arithmetic: 0.53 us -> 5.35 us  [the longest x1 2.66 us: shards(): total = row_sum(jnp.sum(inflated, axis=0))]
  transfers between devices with their start and end apart: 2 -> 29, of which waited for: 2 -> 17; matrix products, arithmetic and copies ran while one was open for 0% -> 4% of each run, Pallas kernels for 0% -> 11%
where the time goes in v2:
time: 161 us
  waiting for transfers between devices  64.8 us (40%)
  starting transfers between devices  37.9 us (24%)
  Pallas kernels  25.1 us (16%)
  local copies, waits for them, and re-layouts  20.7 us (13%)
  other arithmetic  11.9 us (7%)
    ppermute x29, waiting for transfers between devices, move(): return lax.ppermute(value, AXES, perm)  64.8 us
    ppermute x29, starting transfers between devices, move(): return lax.ppermute(value, AXES, perm)  37.9 us
    pallas_call x3, Pallas kernels, product(): pl.pallas_call(functools.partial(product_kernel, len(a_units), len(b_unit...  25.1 us
    unnamed x33, local copies, waits for them, and re-layouts  11.9 us
    mul x1, other arithmetic, shards(): return inflated * (order / total)[None, :]  3.42 us
  transfers between devices with their start and end apart: 29, of which 17 were waited for; matrix products, arithmetic and copies ran while one was open for 4% of the time, Pallas kernels for 11%

profile of v2, /device:TPU:0, one launch (start us, length us, event | category | flops | bytes accessed | tf_op | source)
XLA Modules:
  0.0 161.0 jit_solution(14672028541552062350)
XLA Ops:
  0.0 0.8 copy.40
  1.0 0.6 mul.250
  1.6 0.2 copy.66
  1.8 1.4 copy-done.12
  3.2 0.5 fusion.46
  3.7 4.2 %collective-permute-start.2 = (f32[576]{0:T(1024)S(1)}, f32[576]{0:T(1024)S(1)}, u32[]{:S(2)}, u32[]{:S(2)}) collective-permute-start(f32[576]{0:T(1024)S(1)} %pad_maximum_fusion.1), channel_id=1, source_target_pairs={{0,48},{1,49},{2,50},{3,51},{4,52},{5,53},{6,54},{7,55},{8,56},{9,... | collective-permute-start | bytes 6920 | tf_op jit(solution)/shard_map/ppermute | solution.py:44
  7.9 1.3 collective-permute-start
  9.3 2.9 %collective-permute-start.6 = (f32[128]{0:T(128)S(1)}, f32[128]{0:T(128)S(1)}, u32[]{:S(2)}, u32[]{:S(2)}) collective-permute-start(f32[128]{0:T(128)S(1)} %reshape.772), channel_id=1, source_target_pairs={{0,6},{1,7},{2,0},{3,1},{4,2},{5,3},{6,4},{7,5},{8,14},{9,15},{10,... | collective-permute-start | bytes 1544 | tf_op jit(solution)/shard_map/ppermute | solution.py:44
  12.2 0.8 collective-permute-start.5
  13.0 0.9 collective-permute-start.4
  13.9 3.3 %collective-permute-start.3 = (f32[576]{0:T(1024)S(1)}, f32[576]{0:T(1024)S(1)}, u32[]{:S(2)}, u32[]{:S(2)}) collective-permute-start(f32[576]{0:T(1024)S(1)} %add_add_fusion), channel_id=1, source_target_pairs={{0,64},{1,65},{2,66},{3,67},{4,68},{5,69},{6,70},{7,71},{8,72},{9,... | collective-permute-start | bytes 6920 | tf_op jit(solution)/shard_map/ppermute | solution.py:44
  17.2 0.5 collective-permute-done.4
  17.8 1.6 collective-permute-start.7
  19.3 2.0 %collective-permute-done.7 = f32[128]{0:T(128)S(1)} collective-permute-done((f32[128]{0:T(128)S(1)}, f32[128]{0:T(128)S(1)}, u32[]{:S(2)}, u32[]{:S(2)}) %collective-permute-start.7) | collective-permute-done | bytes 544 | tf_op jit(solution)/shard_map/ppermute | solution.py:44
  21.3 0.3 divide_convert_fusion.refs_8_.refs_9_
  21.8 1.7 %collective-permute-start.11 = (bf16[1024,512]{1,0:T(8,128)(2,1)S(1)}, bf16[1024,512]{1,0:T(8,128)(2,1)S(1)}, u32[]{:S(2)}, u32[]{:S(2)}) collective-permute-start(bf16[1024,512]{1,0:T(8,128)(2,1)S(1)} %divide_convert_fusion.refs_8_.refs_9_), channel_id=1, source_target_pairs={{0,8},{1,9},{2,10},{3,11},{4,12},{5,13},{6,14},{7,15},{8,0},{9,1},... | collective-permute-start | bytes 3145736 | tf_op jit(solution)/shard_map/ppermute | solution.py:44
  23.5 1.0 collective-permute-start.10
  24.4 1.0 collective-permute-start.9
  25.6 2.0 %collective-permute-start.13 = (bf16[512,1024]{1,0:T(8,128)(2,1)S(1)}, bf16[512,1024]{1,0:T(8,128)(2,1)S(1)}, u32[]{:S(2)}, u32[]{:S(2)}) collective-permute-start(bf16[512,1024]{1,0:T(8,128)(2,1)S(1)} %pad_maximum_fusion.refs_14_.refs_17_), channel_id=1, source_target_pairs={{0,48},{1,49},{2,50},{3,51},{4,52},{5,53},{6,54},{7,55},{8,56},{9,... | collective-permute-start | bytes 3145736 | tf_op jit(solution)/shard_map/ppermute | solution.py:44
  27.7 0.3 collective-permute-start.12
  28.0 19.4 %collective-permute-done.11.refs_11_.refs_12_ = bf16[1024,512]{1,0:T(8,128)(2,1)S(1)} collective-permute-done((bf16[1024,512]{1,0:T(8,128)(2,1)S(1)}, bf16[1024,512]{1,0:T(8,128)(2,1)S(1)}, u32[]{:S(2)}, u32[]{:S(2)}) %collective-permute-start.11) | collective-permute-done | bytes 1048608 | tf_op jit(solution)/shard_map/ppermute | solution.py:44
  47.4 1.3 collective-permute-done.10.refs_10_.refs_11_
  48.7 1.0 copy-done
  49.7 0.9 collective-permute-done.9.refs_9_.refs_10_
  50.6 0.2 collective-permute-done.13.refs_16_.refs_19_
  50.8 1.1 copy-done.8
  51.9 1.4 collective-permute-done.12.refs_15_.refs_18_
  53.4 2.9 %collective-permute-start.17 = (bf16[512,1024]{1,0:T(8,128)(2,1)S(1)}, bf16[512,1024]{1,0:T(8,128)(2,1)}, u32[]{:S(2)}, u32[]{:S(2)}) collective-permute-start(bf16[512,1024]{1,0:T(8,128)(2,1)S(1)} %pad_maximum_fusion.refs_14_.refs_17_), channel_id=1, source_target_pairs={{0,64},{1,65},{2,66},{3,67},{4,68},{5,69},{6,70},{7,71},{8,72},{9,... | collective-permute-start | bytes 3145736 | tf_op jit(solution)/shard_map/ppermute | solution.py:44
  56.3 0.2 collective-permute-start.16
  56.5 1.6 collective-permute-start.15
  58.1 0.4 collective-permute-start.14
  59.4 0.8 collective-permute-done.18
  60.2 18.3 %collective-permute-done.17.refs_18_.refs_21_ = bf16[512,1024]{1,0:T(8,128)(2,1)} collective-permute-done((bf16[512,1024]{1,0:T(8,128)(2,1)S(1)}, bf16[512,1024]{1,0:T(8,128)(2,1)}, u32[]{:S(2)}, u32[]{:S(2)}) %collective-permute-start.17) | collective-permute-done | bytes 1048608 | tf_op jit(solution)/shard_map/ppermute | solution.py:44
  78.4 2.5 %collective-permute-done.16.refs_17_.refs_20_ = bf16[512,1024]{1,0:T(8,128)(2,1)} collective-permute-done((bf16[512,1024]{1,0:T(8,128)(2,1)}, bf16[512,1024]{1,0:T(8,128)(2,1)}, u32[]{:S(2)}, u32[]{:S(2)}) %collective-permute-start.16) | collective-permute-done | bytes 1048608 | tf_op jit(solution)/shard_map/ppermute | solution.py:44
  81.0 1.6 collective-permute-done.14.refs_12_.refs_13_
  83.3 0.2 reshape.774
  83.7 0.3 fusion.14
  85.9 0.2 reduce_window_sum.79
  88.9 0.2 reduce_window_sum.83
  89.1 2.5 %collective-permute-start.22 = (bf16[512,1024]{1,0:T(8,128)(2,1)}, bf16[512,1024]{1,0:T(8,128)(2,1)}, u32[]{:S(2)}, u32[]{:S(2)}) collective-permute-start(bf16[512,1024]{1,0:T(8,128)(2,1)} %collective-permute-done.17.refs_18_.refs_21_), channel_id=1, source_target_pairs={{0,48},{1,49},{2,50},{3,51},{4,52},{5,53},{6,54},{7,55},{8,56},{9,... | collective-permute-start | bytes 3145736 | tf_op jit(solution)/shard_map/ppermute | solution.py:44
  91.8 0.2 reduce_window_sum.85
  92.0 0.2 reduce_window_sum.81
  92.4 3.2 %collective-permute-start.20 = (bf16[1024,512]{1,0:T(8,128)(2,1)}, bf16[1024,512]{1,0:T(8,128)(2,1)}, u32[]{:S(2)}, u32[]{:S(2)}) collective-permute-start(bf16[1024,512]{1,0:T(8,128)(2,1)} %collective-permute-done.15.refs_13_.refs_14_), channel_id=1, source_target_pairs={{0,6},{1,7},{2,0},{3,1},{4,2},{5,3},{6,4},{7,5},{8,14},{9,15},{10,... | collective-permute-start | bytes 3145736 | tf_op jit(solution)/shard_map/ppermute | solution.py:44
  95.6 1.2 collective-permute-start.23
  97.9 0.2 reduce_window_sum.78
  98.3 1.2 copy-done.1
  99.5 1.2 copy-done.5
  100.7 1.2 copy-done.9
  101.9 9.1 %begin.1.refs_8_ = f32[1024,1024]{1,0:T(8,128)} custom-call(s32[6]{0:T(128)S(1)} %stack.141.refs_0_, s32[5]{0:T(128)S(1)} %stack.142.refs_1_, s32[6,8]{1,0:T(8,128)S(1)} %fusion.19.refs_2_, s32[5,8]{1,0:T(8,128)S(1)} %fusion.20.refs_3_, s32[6]{0:T(128)S(1)} %reduce_sum.194.refs_4_, s32[5]{0:T(128)S(1)} %reduce_sum.196.refs_5_, s32[16]{0:T(128)S(1)} %reduce_sum.199.refs_6_, ...), custom_call_target="tpu_custom_call" | custom-call | flops 4000000000 | bytes 16777216 | tf_op jit(solution)/shard_map/begin/pallas_call | solution.py:151
  111.0 4.3 %collective-permute-done.19.refs_15_ = bf16[1024,512]{1,0:T(8,128)(2,1)} collective-permute-done((bf16[1024,512]{1,0:T(8,128)(2,1)}, bf16[1024,512]{1,0:T(8,128)(2,1)}, u32[]{:S(2)}, u32[]{:S(2)}) %collective-permute-start.19) | collective-permute-done | bytes 1048608 | tf_op jit(solution)/shard_map/ppermute | solution.py:44
  115.3 3.0 %collective-permute-done.23.refs_24_ = bf16[512,1024]{1,0:T(8,128)(2,1)} collective-permute-done((bf16[512,1024]{1,0:T(8,128)(2,1)}, bf16[512,1024]{1,0:T(8,128)(2,1)}, u32[]{:S(2)}, u32[]{:S(2)}) %collective-permute-start.23) | collective-permute-done | bytes 1048608 | tf_op jit(solution)/shard_map/ppermute | solution.py:44
  118.3 7.6 %finish.3 = f32[1024,512]{1,0:T(8,128)} custom-call(s32[8]{0:T(128)S(1)} %stack.127.refs_0_, s32[8]{0:T(128)S(1)} %stack.136.refs_1_, s32[8,8]{1,0:T(8,128)S(1)} %fusion.21.refs_2_, s32[8,8]{1,0:T(8,128)S(1)} %fusion.22.refs_3_, s32[8]{0:T(128)S(1)} %reduce_sum.201.refs_4_, s32[8]{0:T(128)S(1)} %reduce_sum.203.refs_5_, s32[16]{0:T(128)S(1)} %reduce_sum.206.refs_6_, ...), custom_call_target="tpu_custom_call" | custom-call | flops 4000000000 | bytes 16777216 | tf_op jit(solution)/shard_map/finish/pallas_call | solution.py:151
  129.5 1.2 copy-done.3
  130.7 1.2 copy-done.7
  131.9 1.2 copy-done.10
  133.2 8.5 %finish.2 = f32[1024,512]{1,0:T(8,128)} custom-call(s32[8]{0:T(128)S(1)} %stack.127.refs_0_, s32[8]{0:T(128)S(1)} %stack.136.refs_1_, s32[8,8]{1,0:T(8,128)S(1)} %fusion.17.refs_2_, s32[8,8]{1,0:T(8,128)S(1)} %fusion.18.refs_3_, s32[8]{0:T(128)S(1)} %reduce_sum.187.refs_4_, s32[8]{0:T(128)S(1)} %reduce_sum.189.refs_5_, s32[16]{0:T(128)S(1)} %reduce_sum.192.refs_6_, ...), custom_call_target="tpu_custom_call" | custom-call | flops 4000000000 | bytes 16777216 | tf_op jit(solution)/shard_map/finish/pallas_call | solution.py:151
  141.6 2.7 %fusion = f32[512]{0:T(512)S(1)} fusion(f32[1024,512]{1,0:T(8,128)} %finish.2, f32[1024,512]{1,0:T(8,128)} %collective-permute-done.24), kind=kLoop, calls=%fused_computation.4 | loop fusion | flops 1572352 | bytes 4196352 | tf_op jit(solution)/shard_map/reduce_sum | solution.py:263
  144.3 1.0 collective-permute-start.27
  145.3 2.3 %collective-permute-start.26 = (f32[512]{0:T(512)S(1)}, f32[512]{0:T(512)S(1)}, u32[]{:S(2)}, u32[]{:S(2)}) collective-permute-start(f32[512]{0:T(512)S(1)} %fusion), channel_id=1, source_target_pairs={{0,32},{1,33},{2,34},{3,35},{4,36},{5,37},{6,38},{7,39},{8,40},{9,... | collective-permute-start | bytes 6152 | tf_op jit(solution)/shard_map/ppermute | solution.py:44
  147.6 1.3 collective-permute-start.25
  149.0 1.4 collective-permute-done.26
  150.4 2.0 %collective-permute-done.25 = f32[512]{0:T(512)S(1)} collective-permute-done((f32[512]{0:T(512)S(1)}, f32[512]{0:T(512)S(1)}, u32[]{:S(2)}, u32[]{:S(2)}) %collective-permute-start.25) | collective-permute-done | bytes 2080 | tf_op jit(solution)/shard_map/ppermute | solution.py:44
  152.5 5.1 %collective-permute-done.28 = f32[512]{0:T(512)S(1)} collective-permute-done((f32[512]{0:T(512)S(1)}, f32[512]{0:T(512)S(1)}, u32[]{:S(2)}, u32[]{:S(2)}) %collective-permute-start.28) | collective-permute-done | bytes 2080 | tf_op jit(solution)/shard_map/ppermute | solution.py:44
  157.5 3.4 %broadcast_multiply_fusion = f32[1024,512]{1,0:T(8,128)} fusion(f32[512]{0:T(512)S(1)} %add_divide_fusion, f32[1024,512]{1,0:T(8,128)S(1)} %copy-done.11, f32[1024,512]{1,0:T(8,128)} %collective-permute-done.24), kind=kLoop, calls=%fused_computation.3 | loop fusion | flops 1572864 | bytes 6293504 | tf_op jit(solution)/shard_map/mul | solution.py:265
  (212 shorter events, 12.4 us)
Async XLA Ops:
  1.6 1.6 copy-start.12
  3.7 9.3 %collective-permute-start.2 = (f32[576]{0:T(1024)S(1)}, f32[576]{0:T(1024)S(1)}, u32[]{:S(2)}, u32[]{:S(2)}) collective-permute-start(f32[576]{0:T(1024)S(1)} %pad_maximum_fusion.1), channel_id=1, source_target_pairs={{0,48},{1,49},{2,50},{3,51},{4,52},{5,53},{6,54},{7,55},{8,56},{9,... | collective-permute-start | bytes 6920 | tf_op jit(solution)/shard_map/ppermute | solution.py:44
  7.9 6.0 %collective-permute-start.1 = (f32[576]{0:T(1024)S(1)}, f32[576]{0:T(1024)S(1)}, u32[]{:S(2)}, u32[]{:S(2)}) collective-permute-start(f32[576]{0:T(1024)S(1)} %pad_maximum_fusion.1), channel_id=1, source_target_pairs={{0,32},{1,33},{2,34},{3,35},{4,36},{5,37},{6,38},{7,39},{8,40},{9,... | collective-permute-start | bytes 6920 | tf_op jit(solution)/shard_map/ppermute | solution.py:44
  7.9 6.0 %collective-permute-start = (f32[576]{0:T(1024)S(1)}, f32[576]{0:T(1024)S(1)}, u32[]{:S(2)}, u32[]{:S(2)}) collective-permute-start(f32[576]{0:T(1024)S(1)} %pad_maximum_fusion.1), channel_id=1, source_target_pairs={{0,16},{1,17},{2,18},{3,19},{4,20},{5,21},{6,22},{7,23},{8,24},{9,... | collective-permute-start | bytes 6920 | tf_op jit(solution)/shard_map/ppermute | solution.py:44
  9.3 7.9 %collective-permute-start.6 = (f32[128]{0:T(128)S(1)}, f32[128]{0:T(128)S(1)}, u32[]{:S(2)}, u32[]{:S(2)}) collective-permute-start(f32[128]{0:T(128)S(1)} %reshape.772), channel_id=1, source_target_pairs={{0,6},{1,7},{2,0},{3,1},{4,2},{5,3},{6,4},{7,5},{8,14},{9,15},{10,... | collective-permute-start | bytes 1544 | tf_op jit(solution)/shard_map/ppermute | solution.py:44
  12.2 5.0 %collective-permute-start.5 = (f32[128]{0:T(128)S(1)}, f32[128]{0:T(128)S(1)}, u32[]{:S(2)}, u32[]{:S(2)}) collective-permute-start(f32[128]{0:T(128)S(1)} %reshape.772), channel_id=1, source_target_pairs={{0,4},{1,5},{2,6},{3,7},{4,0},{5,1},{6,2},{7,3},{8,12},{9,13},{10,... | collective-permute-start | bytes 1544 | tf_op jit(solution)/shard_map/ppermute | solution.py:44
  13.0 4.8 %collective-permute-start.4 = (f32[128]{0:T(128)S(1)}, f32[128]{0:T(128)S(1)}, u32[]{:S(2)}, u32[]{:S(2)}) collective-permute-start(f32[128]{0:T(128)S(1)} %reshape.772), channel_id=1, source_target_pairs={{0,2},{1,3},{2,4},{3,5},{4,6},{5,7},{6,0},{7,1},{8,10},{9,11},{10,... | collective-permute-start | bytes 1544 | tf_op jit(solution)/shard_map/ppermute | solution.py:44
  13.9 7.4 %collective-permute-start.3 = (f32[576]{0:T(1024)S(1)}, f32[576]{0:T(1024)S(1)}, u32[]{:S(2)}, u32[]{:S(2)}) collective-permute-start(f32[576]{0:T(1024)S(1)} %add_add_fusion), channel_id=1, source_target_pairs={{0,64},{1,65},{2,66},{3,67},{4,68},{5,69},{6,70},{7,71},{8,72},{9,... | collective-permute-start | bytes 6920 | tf_op jit(solution)/shard_map/ppermute | solution.py:44
  17.8 3.5 %collective-permute-start.7 = (f32[128]{0:T(128)S(1)}, f32[128]{0:T(128)S(1)}, u32[]{:S(2)}, u32[]{:S(2)}) collective-permute-start(f32[128]{0:T(128)S(1)} %add_add_fusion.2), channel_id=1, source_target_pairs={{0,8},{1,9},{2,10},{3,11},{4,12},{5,13},{6,14},{7,15},{8,0},{9,1},... | collective-permute-start | bytes 1544 | tf_op jit(solution)/shard_map/ppermute | solution.py:44
  21.6 36.9 %copy-start.14 = (pred[4]{0:T(512)(128)(4,1)S(1)}, pred[4]{0:T(512)(128)(4,1)}, u32[]{:S(2)}) copy-start(pred[4]{0:T(512)(128)(4,1)} %constant.180.clone.1) | copy-start | bytes 16
  21.6 37.0 %copy-start.13 = (s32[4,2]{0,1:T(2,128)S(1)}, s32[4,2]{0,1:T(2,128)}, u32[]{:S(2)}) copy-start(s32[4,2]{0,1:T(2,128)} %param.5) | copy-start | bytes 100
  21.7 3.8 %collective-permute-start.8 = (bf16[512,512]{1,0:T(8,128)(2,1)S(1)}, bf16[512,512]{1,0:T(8,128)(2,1)S(1)}, u32[]{:S(2)}, u32[]{:S(2)}) collective-permute-start(bf16[512,512]{1,0:T(8,128)(2,1)S(1)} %get-tuple-element.73), channel_id=1, source_target_pairs={{0,1},{1,0},{2,3},{3,2},{4,5},{5,4},{6,7},{7,6},{8,9},{9,8},{10,11... | collective-permute-start | bytes 1572872 | tf_op jit(solution)/shard_map/ppermute | solution.py:44
  21.8 25.6 %collective-permute-start.11 = (bf16[1024,512]{1,0:T(8,128)(2,1)S(1)}, bf16[1024,512]{1,0:T(8,128)(2,1)S(1)}, u32[]{:S(2)}, u32[]{:S(2)}) collective-permute-start(bf16[1024,512]{1,0:T(8,128)(2,1)S(1)} %divide_convert_fusion.refs_8_.refs_9_), channel_id=1, source_target_pairs={{0,8},{1,9},{2,10},{3,11},{4,12},{5,13},{6,14},{7,15},{8,0},{9,1},... | collective-permute-start | bytes 3145736 | tf_op jit(solution)/shard_map/ppermute | solution.py:44
  23.5 25.2 %collective-permute-start.10 = (bf16[1024,512]{1,0:T(8,128)(2,1)S(1)}, bf16[1024,512]{1,0:T(8,128)(2,1)S(1)}, u32[]{:S(2)}, u32[]{:S(2)}) collective-permute-start(bf16[1024,512]{1,0:T(8,128)(2,1)S(1)} %divide_convert_fusion.refs_8_.refs_9_), channel_id=1, source_target_pairs={{0,6},{1,7},{2,0},{3,1},{4,2},{5,3},{6,4},{7,5},{8,14},{9,15},{10,... | collective-permute-start | bytes 3145736 | tf_op jit(solution)/shard_map/ppermute | solution.py:44
  24.4 26.1 %collective-permute-start.9 = (bf16[1024,512]{1,0:T(8,128)(2,1)S(1)}, bf16[1024,512]{1,0:T(8,128)(2,1)S(1)}, u32[]{:S(2)}, u32[]{:S(2)}) collective-permute-start(bf16[1024,512]{1,0:T(8,128)(2,1)S(1)} %divide_convert_fusion.refs_8_.refs_9_), channel_id=1, source_target_pairs={{0,2},{1,3},{2,4},{3,5},{4,6},{5,7},{6,0},{7,1},{8,10},{9,11},{10,... | collective-permute-start | bytes 3145736 | tf_op jit(solution)/shard_map/ppermute | solution.py:44
  25.6 25.2 %collective-permute-start.13 = (bf16[512,1024]{1,0:T(8,128)(2,1)S(1)}, bf16[512,1024]{1,0:T(8,128)(2,1)S(1)}, u32[]{:S(2)}, u32[]{:S(2)}) collective-permute-start(bf16[512,1024]{1,0:T(8,128)(2,1)S(1)} %pad_maximum_fusion.refs_14_.refs_17_), channel_id=1, source_target_pairs={{0,48},{1,49},{2,50},{3,51},{4,52},{5,53},{6,54},{7,55},{8,56},{9,... | collective-permute-start | bytes 3145736 | tf_op jit(solution)/shard_map/ppermute | solution.py:44
  27.7 25.7 %collective-permute-start.12 = (bf16[512,1024]{1,0:T(8,128)(2,1)S(1)}, bf16[512,1024]{1,0:T(8,128)(2,1)}, u32[]{:S(2)}, u32[]{:S(2)}) collective-permute-start(bf16[512,1024]{1,0:T(8,128)(2,1)S(1)} %pad_maximum_fusion.refs_14_.refs_17_), channel_id=1, source_target_pairs={{0,16},{1,17},{2,18},{3,19},{4,20},{5,21},{6,22},{7,23},{8,24},{9,... | collective-permute-start | bytes 3145736 | tf_op jit(solution)/shard_map/ppermute | solution.py:44
  48.7 1.0 copy-start
  50.6 5.9 %copy-start.4 = (bf16[1024,512]{1,0:T(8,128)(2,1)}, bf16[1024,512]{1,0:T(8,128)(2,1)S(1)}, u32[]{:S(2)}) copy-start(bf16[1024,512]{1,0:T(8,128)(2,1)S(1)} %collective-permute-done.9.refs_9_.refs_10_) | copy-start | bytes 3145732
  50.8 1.1 copy-start.8
  53.4 25.1 %collective-permute-start.17 = (bf16[512,1024]{1,0:T(8,128)(2,1)S(1)}, bf16[512,1024]{1,0:T(8,128)(2,1)}, u32[]{:S(2)}, u32[]{:S(2)}) collective-permute-start(bf16[512,1024]{1,0:T(8,128)(2,1)S(1)} %pad_maximum_fusion.refs_14_.refs_17_), channel_id=1, source_target_pairs={{0,64},{1,65},{2,66},{3,67},{4,68},{5,69},{6,70},{7,71},{8,72},{9,... | collective-permute-start | bytes 3145736 | tf_op jit(solution)/shard_map/ppermute | solution.py:44
  56.3 24.7 %collective-permute-start.16 = (bf16[512,1024]{1,0:T(8,128)(2,1)}, bf16[512,1024]{1,0:T(8,128)(2,1)}, u32[]{:S(2)}, u32[]{:S(2)}) collective-permute-start(bf16[512,1024]{1,0:T(8,128)(2,1)} %collective-permute-done.12.refs_15_.refs_18_), channel_id=1, source_target_pairs={{0,16},{1,17},{2,18},{3,19},{4,20},{5,21},{6,22},{7,23},{8,24},{9,... | collective-permute-start | bytes 3145736 | tf_op jit(solution)/shard_map/ppermute | solution.py:44
  56.5 24.5 %collective-permute-start.15 = (bf16[1024,512]{1,0:T(8,128)(2,1)S(1)}, bf16[1024,512]{1,0:T(8,128)(2,1)}, u32[]{:S(2)}, u32[]{:S(2)}) collective-permute-start(bf16[1024,512]{1,0:T(8,128)(2,1)S(1)} %collective-permute-done.11.refs_11_.refs_12_), channel_id=1, source_target_pairs={{0,6},{1,7},{2,0},{3,1},{4,2},{5,3},{6,4},{7,5},{8,14},{9,15},{10,... | collective-permute-start | bytes 3145736 | tf_op jit(solution)/shard_map/ppermute | solution.py:44
  58.1 24.5 %collective-permute-start.14 = (bf16[1024,512]{1,0:T(8,128)(2,1)S(1)}, bf16[1024,512]{1,0:T(8,128)(2,1)}, u32[]{:S(2)}, u32[]{:S(2)}) collective-permute-start(bf16[1024,512]{1,0:T(8,128)(2,1)S(1)} %collective-permute-done.11.refs_11_.refs_12_), channel_id=1, source_target_pairs={{0,2},{1,3},{2,4},{3,5},{4,6},{5,7},{6,0},{7,1},{8,10},{9,11},{10,... | collective-permute-start | bytes 3145736 | tf_op jit(solution)/shard_map/ppermute | solution.py:44
  59.0 1.2 collective-permute-start.18
  89.1 29.2 %collective-permute-start.22 = (bf16[512,1024]{1,0:T(8,128)(2,1)}, bf16[512,1024]{1,0:T(8,128)(2,1)}, u32[]{:S(2)}, u32[]{:S(2)}) collective-permute-start(bf16[512,1024]{1,0:T(8,128)(2,1)} %collective-permute-done.17.refs_18_.refs_21_), channel_id=1, source_target_pairs={{0,48},{1,49},{2,50},{3,51},{4,52},{5,53},{6,54},{7,55},{8,56},{9,... | collective-permute-start | bytes 3145736 | tf_op jit(solution)/shard_map/ppermute | solution.py:44
  91.6 26.7 %collective-permute-start.21 = (bf16[512,1024]{1,0:T(8,128)(2,1)}, bf16[512,1024]{1,0:T(8,128)(2,1)}, u32[]{:S(2)}, u32[]{:S(2)}) collective-permute-start(bf16[512,1024]{1,0:T(8,128)(2,1)} %collective-permute-done.17.refs_18_.refs_21_), channel_id=1, source_target_pairs={{0,16},{1,17},{2,18},{3,19},{4,20},{5,21},{6,22},{7,23},{8,24},{9,... | collective-permute-start | bytes 3145736 | tf_op jit(solution)/shard_map/ppermute | solution.py:44
  92.3 23.0 %collective-permute-start.19 = (bf16[1024,512]{1,0:T(8,128)(2,1)}, bf16[1024,512]{1,0:T(8,128)(2,1)}, u32[]{:S(2)}, u32[]{:S(2)}) collective-permute-start(bf16[1024,512]{1,0:T(8,128)(2,1)} %copy-done.4), channel_id=1, source_target_pairs={{0,2},{1,3},{2,4},{3,5},{4,6},{5,7},{6,0},{7,1},{8,10},{9,11},{10,... | collective-permute-start | bytes 3145736 | tf_op jit(solution)/shard_map/ppermute | solution.py:44
  92.4 22.9 %collective-permute-start.20 = (bf16[1024,512]{1,0:T(8,128)(2,1)}, bf16[1024,512]{1,0:T(8,128)(2,1)}, u32[]{:S(2)}, u32[]{:S(2)}) collective-permute-start(bf16[1024,512]{1,0:T(8,128)(2,1)} %collective-permute-done.15.refs_13_.refs_14_), channel_id=1, source_target_pairs={{0,6},{1,7},{2,0},{3,1},{4,2},{5,3},{6,4},{7,5},{8,14},{9,15},{10,... | collective-permute-start | bytes 3145736 | tf_op jit(solution)/shard_map/ppermute | solution.py:44
  95.6 22.7 %collective-permute-start.23 = (bf16[512,1024]{1,0:T(8,128)(2,1)}, bf16[512,1024]{1,0:T(8,128)(2,1)}, u32[]{:S(2)}, u32[]{:S(2)}) collective-permute-start(bf16[512,1024]{1,0:T(8,128)(2,1)} %collective-permute-done.16.refs_17_.refs_20_), channel_id=1, source_target_pairs={{0,64},{1,65},{2,66},{3,67},{4,68},{5,69},{6,70},{7,71},{8,72},{9,... | collective-permute-start | bytes 3145736 | tf_op jit(solution)/shard_map/ppermute | solution.py:44
  98.3 1.2 copy-start.1
  99.5 1.2 copy-start.5
  100.7 1.2 copy-start.9
  101.9 16.4 %copy-start.2 = (bf16[1024,512]{1,0:T(8,128)(2,1)S(1)}, bf16[1024,512]{1,0:T(8,128)(2,1)}, u32[]{:S(2)}) copy-start(bf16[1024,512]{1,0:T(8,128)(2,1)} %copy-done) | copy-start | bytes 3145732
  101.9 16.4 %copy-start.6 = (bf16[1024,512]{1,0:T(8,128)(2,1)S(1)}, bf16[1024,512]{1,0:T(8,128)(2,1)}, u32[]{:S(2)}) copy-start(bf16[1024,512]{1,0:T(8,128)(2,1)} %copy-done.4) | copy-start | bytes 3145732
  125.9 15.7 %collective-permute-start.24 = (f32[1024,512]{1,0:T(8,128)}, f32[1024,512]{1,0:T(8,128)}, u32[]{:S(2)}, u32[]{:S(2)}) collective-permute-start(f32[1024,512]{1,0:T(8,128)} %finish.3), channel_id=1, source_target_pairs={{0,1},{1,0},{2,3},{3,2},{4,5},{5,4},{6,7},{7,6},{8,9},{9,8},{10,11... | collective-permute-start | bytes 6291464 | tf_op jit(solution)/shard_map/ppermute | solution.py:44
  129.5 1.2 copy-start.3
  130.7 1.2 copy-start.7
  131.9 1.2 copy-start.10
  141.6 15.9 %copy-start.11 = (f32[1024,512]{1,0:T(8,128)S(1)}, f32[1024,512]{1,0:T(8,128)}, u32[]{:S(2)}) copy-start(f32[1024,512]{1,0:T(8,128)} %finish.2) | copy-start | bytes 6291460
  144.3 4.7 %collective-permute-start.27 = (f32[512]{0:T(512)S(1)}, f32[512]{0:T(512)S(1)}, u32[]{:S(2)}, u32[]{:S(2)}) collective-permute-start(f32[512]{0:T(512)S(1)} %fusion), channel_id=1, source_target_pairs={{0,48},{1,49},{2,50},{3,51},{4,52},{5,53},{6,54},{7,55},{8,56},{9,... | collective-permute-start | bytes 6152 | tf_op jit(solution)/shard_map/ppermute | solution.py:44
  145.3 5.1 %collective-permute-start.26 = (f32[512]{0:T(512)S(1)}, f32[512]{0:T(512)S(1)}, u32[]{:S(2)}, u32[]{:S(2)}) collective-permute-start(f32[512]{0:T(512)S(1)} %fusion), channel_id=1, source_target_pairs={{0,32},{1,33},{2,34},{3,35},{4,36},{5,37},{6,38},{7,39},{8,40},{9,... | collective-permute-start | bytes 6152 | tf_op jit(solution)/shard_map/ppermute | solution.py:44
  147.6 4.8 %collective-permute-start.25 = (f32[512]{0:T(512)S(1)}, f32[512]{0:T(512)S(1)}, u32[]{:S(2)}, u32[]{:S(2)}) collective-permute-start(f32[512]{0:T(512)S(1)} %fusion), channel_id=1, source_target_pairs={{0,16},{1,17},{2,18},{3,19},{4,20},{5,21},{6,22},{7,23},{8,24},{9,... | collective-permute-start | bytes 6152 | tf_op jit(solution)/shard_map/ppermute | solution.py:44
  152.4 5.1 %collective-permute-start.28 = (f32[512]{0:T(512)S(1)}, f32[512]{0:T(512)S(1)}, u32[]{:S(2)}, u32[]{:S(2)}) collective-permute-start(f32[512]{0:T(512)S(1)} %add_add_fusion.1), channel_id=1, source_target_pairs={{0,64},{1,65},{2,66},{3,67},{4,68},{5,69},{6,70},{7,71},{8,72},{9,... | collective-permute-start | bytes 6152 | tf_op jit(solution)/shard_map/ppermute | solution.py:44

commit v3 on v2

v3 whole, which is shorter than its diff:
```python
import functools
import jax
import jax.numpy as jnp
from jax import lax
from jax.experimental import pallas as pl
from jax.experimental.pallas import tpu as pltpu
from jax.sharding import PartitionSpec as P

AXES = ("row", "col")
YH, NZ, YL, NX, NC = 2, 4, 2, 4, 2
F32 = jnp.float32
BF16 = jnp.bfloat16
I32 = jnp.int32
GROUP = 2


def place(yh, z, yl, x, c):
    return (yh * NZ + z) * (YL * NX * NC) + (yl * NX + x) * NC + c


def pairs(step):
    return [
        (place(yh, z, yl, x, c), place(*step(yh, z, yl, x, c)))
        for yh in range(YH)
        for z in range(NZ)
        for yl in range(YL)
        for x in range(NX)
        for c in range(NC)
    ]


X_UP = pairs(lambda yh, z, yl, x, c: (yh, z, yl, (x + 1) % NX, c))
X_DOWN = pairs(lambda yh, z, yl, x, c: (yh, z, yl, (x - 1) % NX, c))
Z_UP = pairs(lambda yh, z, yl, x, c: (yh, (z + 1) % NZ, yl, x, c))
Z_DOWN = pairs(lambda yh, z, yl, x, c: (yh, (z - 1) % NZ, yl, x, c))
SWAP_CORE = pairs(lambda yh, z, yl, x, c: (yh, z, yl, x, 1 - c))
SWAP_YL = pairs(lambda yh, z, yl, x, c: (yh, z, 1 - yl, x, c))
SWAP_YH = pairs(lambda yh, z, yl, x, c: (1 - yh, z, yl, x, c))
Z_TURNS = [pairs(lambda yh, z, yl, x, c, d=d: (yh, (z + d) % NZ, yl, x, c)) for d in range(1, NZ)]
X_TURNS = [pairs(lambda yh, z, yl, x, c, d=d: (yh, z, yl, (x + d) % NX, c)) for d in range(1, NX)]


def move(value, perm):
    return lax.ppermute(value, AXES, perm)


def turn_sum(value, turns):
    return value + sum(move(value, turn) for turn in turns)


def row_sum(value):
    value = turn_sum(value, Z_TURNS)
    return value + move(value, SWAP_YH)


def after(value, *deps):
    return lax.optimization_barrier((value, *deps))[0]


def vmem_limit(mib):
    return pltpu.CompilerParams(vmem_limit_bytes=mib * 2**20)


VMEM = pl.BlockSpec(memory_space=pltpu.VMEM)
SMEM = pl.BlockSpec(memory_space=pltpu.SMEM)
ANY = pl.BlockSpec(memory_space=pl.ANY)


def mask_kernel(keep_ref, entries_ref, masked_ref, sum_ref):
    rows, cols = keep_ref.shape
    tall, wide = entries_ref.shape[0] // rows, entries_ref.shape[1] // cols
    for j in range(cols):
        right = slice(j * wide, (j + 1) * wide)
        total = jnp.zeros((1, wide), F32)
        for i in range(rows):
            down = slice(i * tall, (i + 1) * tall)
            masked = entries_ref[down, right] * keep_ref[i, j].astype(F32)
            masked_ref[down, right] = masked
            total = total + jnp.sum(masked, axis=0, keepdims=True)
        sum_ref[:, right] = total


def mask(keep, entries):
    return pl.pallas_call(
        mask_kernel,
        out_shape=(
            jax.ShapeDtypeStruct(entries.shape, F32),
            jax.ShapeDtypeStruct((1, entries.shape[1]), F32),
        ),
        in_specs=[SMEM, VMEM],
        out_specs=(VMEM, VMEM),
        compiler_params=vmem_limit(16),
        name="mask",
    )(keep, entries)


def square_kernel(mine_ref, got_ref, out_ref, sum_ref):
    rows = out_ref.shape[0]
    step = rows // 4
    total = jnp.zeros(sum_ref.shape, F32)
    for r in range(0, rows, step):
        full = mine_ref[r:r + step, :] + got_ref[r:r + step, :]
        square = full * full
        out_ref[r:r + step, :] = square
        total = total + jnp.sum(square, axis=0, keepdims=True)
    sum_ref[...] = total


def squared(mine, got):
    return pl.pallas_call(
        square_kernel,
        out_shape=(
            jax.ShapeDtypeStruct(mine.shape, F32),
            jax.ShapeDtypeStruct((1, mine.shape[1]), F32),
        ),
        in_specs=[VMEM, VMEM],
        out_specs=(VMEM, VMEM),
        compiler_params=vmem_limit(16),
        name="square",
    )(mine, got)


def rescale_kernel(order, value_ref, total_ref, out_ref):
    factor = order / total_ref[...]
    rows = out_ref.shape[0]
    step = rows // 4
    for r in range(0, rows, step):
        out_ref[r:r + step, :] = value_ref[r:r + step, :] * factor


def rescaled(order, value, total):
    return pl.pallas_call(
        functools.partial(rescale_kernel, order),
        out_shape=jax.ShapeDtypeStruct(value.shape, F32),
        in_specs=[VMEM, VMEM],
        out_specs=VMEM,
        compiler_params=vmem_limit(16),
        name="rescale",
    )(value, total)


PLAN_LEFT, PLAN_RIGHT, PLAN_OUT, PLAN_LATE, PLAN_A, PLAN_B, PLAN_SIZE = 0, 4, 8, 24, 25, 33, 48
A_PLACES = [(0, 0), (0, NX - 1), (0, 1), (1, 0), (1, NX - 1), (1, 1), (0, 2), (1, 2)]
B_PLACES = [(0, 0), (0, NZ - 1), (0, 1), (0, 2), (1, 0), (1, NZ - 1), (1, 1), (1, 2)]
A_LATE, B_LATE = (6, 7), (5, 6, 7)


def plan_kernel(rows, cols, left_ref, right_ref, out_ref, other_ref, plan_ref):
    row, col = lax.axis_index("row"), lax.axis_index("col")
    yh, z = row // NZ, row % NZ
    yl, x, c = col // (NX * NC), (col // NC) % NX, col % NC
    parts = YL * NX
    grid = parts * NC * cols
    n_left, n_right = rows * grid, grid * cols

    for i in range(rows):
        def add(q, m, i=i):
            for j in range(cols):
                at = i * grid + (q * NC + c) * cols + j
                flag = ((left_ref[at] + other_ref[at]) > 0.5).astype(I32)
                m = m + flag * (1 << (q * cols + j))
            return m

        plan_ref[PLAN_LEFT + i] = functools.reduce(lambda m, q: add(q, m), range(parts), jnp.int32(0))
    for j in range(NC * cols):
        m = jnp.int32(0)
        for q in range(parts):
            for i in range(cols):
                at = ((q * NC + c) * cols + i) * cols + j % cols
                flag = right_ref[at] if j < cols else other_ref[n_left + at]
                m = m + (flag > 0.5).astype(I32) * (1 << (q * cols + i))
        plan_ref[PLAN_RIGHT + j] = m
    for i in range(rows):
        for j in range(NC * cols):
            if j < cols:
                flag = out_ref[i * cols + j]
            else:
                flag = other_ref[n_left + n_right + i * cols + j - cols]
            plan_ref[PLAN_OUT + i * NC * cols + j] = (flag > 0.5).astype(I32)
    late = jnp.int32(0)
    whole = (1 << cols) - 1
    for u, (dy, dx) in enumerate(A_PLACES):
        base = ((yl + dy) % YL * NX + (x + dx) % NX) * cols
        plan_ref[PLAN_A + u] = base
        if u in A_LATE:
            late = late | lax.shift_left(jnp.int32(whole), base)
    for u, (dy, dz) in enumerate(B_PLACES):
        base = ((yh + dy) % YH * NZ + (z + dz) % NZ) * cols
        plan_ref[PLAN_B + u] = base
        if u in B_LATE:
            late = late | lax.shift_left(jnp.int32(whole), base)
    plan_ref[PLAN_LATE] = late


def planned(rows, cols, left, right, keep_out, other):
    return pl.pallas_call(
        functools.partial(plan_kernel, rows, cols),
        out_shape=jax.ShapeDtypeStruct((PLAN_SIZE,), I32),
        in_specs=[SMEM] * 4,
        out_specs=SMEM,
        name="plan",
    )(left, right, keep_out, other)


def product_kernel(n_a, n_b, shape, cols_out, begun, *refs):
    rows, cols, grid, tile = shape
    plan, refs = refs[0], refs[1:]
    if begun:
        start_ref, refs = refs[0], refs[1:]
    a_in, b_in, refs = refs[:n_a], refs[n_a:n_a + n_b], refs[n_a + n_b:]
    n_out = 1 if begun else 2
    out_refs, (a_buf, b_buf, acc, order, a_sem, b_sem) = refs[:n_out], refs[n_out:]
    wide = len(cols_out)
    no_a, no_b = rows * grid, wide * grid
    deep = a_in[0].shape[1] // tile

    when = plan[PLAN_LATE] if begun else ~plan[PLAN_LATE]
    used = {}
    for i in range(rows):
        for j in cols_out:
            pair = plan[PLAN_LEFT + i] & plan[PLAN_RIGHT + j] & when
            used[i, j] = jnp.where(plan[PLAN_OUT + i * cols + j] > 0, pair, 0)
    need_a = [functools.reduce(jnp.bitwise_or, [used[i, j] for j in cols_out]) for i in range(rows)]
    need_b = [functools.reduce(jnp.bitwise_or, [used[i, j] for i in range(rows)]) for j in cols_out]

    def tile_at(ref, i, j):
        return ref.at[pl.ds(i * tile, tile), pl.ds(j * tile, tile)]

    def each(act):
        for u in range(n_a):
            base = plan[PLAN_A + u]
            for i in range(rows):
                bits = lax.shift_right_logical(need_a[i], base)
                for k in range(deep):
                    @pl.when(bits & (1 << k) > 0)
                    def _(u=u, i=i, k=k, base=base):
                        slot = i * grid + base + k
                        act(pltpu.make_async_copy(tile_at(a_in[u], i, k), a_buf.at[slot], a_sem.at[slot]))
        for u in range(n_b):
            base = plan[PLAN_B + u]
            for n, j in enumerate(cols_out):
                bits = lax.shift_right_logical(need_b[n], base)
                for k in range(deep):
                    @pl.when(bits & (1 << k) > 0)
                    def _(u=u, n=n, j=j, k=k, base=base):
                        slot = n * grid + base + k
                        act(pltpu.make_async_copy(tile_at(b_in[u], k, j), b_buf.at[slot], b_sem.at[slot]))

    each(lambda copy: copy.start())
    a_buf[no_a] = jnp.zeros((tile, tile), BF16)
    b_buf[no_b] = jnp.zeros((tile, tile), BF16)
    count = {}
    for n, j in enumerate(cols_out):
        for i in range(rows):
            first = (n * rows + i) * (grid + GROUP)
            at = jnp.int32(first)
            for k in range(grid):
                order[at] = k
                at = at + (lax.shift_right_logical(used[i, j], k) & 1)
            for g in range(GROUP - 1):
                order[at + g] = grid
            count[i, j] = (at - first + GROUP - 1) // GROUP
    each(lambda copy: copy.wait())

    for n, j in enumerate(cols_out):
        out_ref = out_refs[n * n_out // wide]
        place = n % (wide // n_out)
        for i in range(rows):
            here = slice(i * tile, (i + 1) * tile), slice(place * tile, (place + 1) * tile)
            acc[...] = start_ref[here] if begun else jnp.zeros_like(acc)

            def step(m, _, i=i, n=n):
                part = None
                for g in range(GROUP):
                    k = order[(n * rows + i) * (grid + GROUP) + m * GROUP + g]
                    a_tile = a_buf[jnp.where(k < grid, i * grid + k, no_a)]
                    b_tile = b_buf[jnp.where(k < grid, n * grid + k, no_b)]
                    dot = jnp.dot(a_tile, b_tile, preferred_element_type=F32)
                    part = dot if part is None else part + dot
                acc[...] += part
                return 0

            lax.fori_loop(0, count[i, j], step, 0)
            out_ref[here] = acc[...]


def product(plan, a_units, b_units, rows, cols, cols_out, start=None):
    begun = start is not None
    tile = a_units[0].shape[0] // rows
    grid = YL * NX * (a_units[0].shape[1] // tile)
    half = jax.ShapeDtypeStruct((rows * tile, cols // NC * tile), F32)
    n_out = 1 if begun else NC
    return pl.pallas_call(
        functools.partial(product_kernel, len(a_units), len(b_units), (rows, cols, grid, tile), cols_out, begun),
        out_shape=(half,) * n_out,
        in_specs=[SMEM] + [VMEM] * begun + [ANY] * (len(a_units) + len(b_units)),
        out_specs=(VMEM,) * n_out,
        scratch_shapes=[
            pltpu.VMEM((rows * grid + 1, tile, tile), BF16),
            pltpu.VMEM((len(cols_out) * grid + 1, tile, tile), BF16),
            pltpu.VMEM((tile, tile), F32),
            pltpu.SMEM((rows * len(cols_out) * (grid + GROUP),), I32),
            pltpu.SemaphoreType.DMA((rows * grid,)),
            pltpu.SemaphoreType.DMA((len(cols_out) * grid,)),
        ],
        compiler_params=vmem_limit(26),
        cost_estimate=pl.CostEstimate(flops=10**6, bytes_accessed=2**10, transcendentals=0),
        name="finish" if begun else "begin",
    )(plan, *([start] if begun else []), *a_units, *b_units)


def tile_keep(flags):
    tile_rows, tile_cols = flags.shape
    row_ids = lax.axis_index("row") * tile_rows + jnp.arange(tile_rows, dtype=I32)
    col_ids = lax.axis_index("col") * tile_cols + jnp.arange(tile_cols, dtype=I32)
    diagonal = (row_ids[:, None] == col_ids[None, :]).astype(I32)
    return jnp.maximum(flags, diagonal)


def shards(entries, pattern, prune):
    row, col = lax.axis_index("row"), lax.axis_index("col")
    rows, cols = pattern.shape
    height, width = entries.shape
    grid = rows * lax.axis_size("row")
    c = col % NC

    keep = tile_keep(pattern)
    keep_out = tile_keep(prune)
    keep_f = keep.astype(F32)
    masked, sums = mask(keep, entries)

    left = lax.dynamic_update_slice(jnp.zeros((rows, grid), F32), keep_f, (0, col * cols)).reshape(-1)
    left = turn_sum(left, X_TURNS)
    left = left + move(left, SWAP_YL)

    flags = lax.dynamic_update_slice(jnp.zeros((grid, cols), F32), keep_f, (row * rows, 0))
    sums = jnp.concatenate([sums[0], flags.reshape(-1)])
    sums = row_sum(sums)
    colsum, right = sums[:width], sums[width:]
    a = (masked / colsum[None, :]).astype(BF16)
    a, left = lax.optimization_barrier((a, left))

    half = height // 2
    mine = lax.dynamic_slice(a, (c * half, 0), (half, width))
    theirs = lax.dynamic_slice(a, ((1 - c) * half, 0), (half, width))
    b = jnp.concatenate([mine, move(theirs, SWAP_CORE)], axis=1)
    notes = jnp.concatenate([left, right, keep_out.astype(F32).reshape(-1)])
    notes_o = move(notes, SWAP_CORE)

    xl, xr, pa = move(a, X_UP), move(a, X_DOWN), move(a, SWAP_YL)
    zl, zr = move(b, Z_UP), move(b, Z_DOWN)
    a, b, xl, xr, pa, zl, zr = lax.optimization_barrier((a, b, xl, xr, pa, zl, zr))
    pxl, pxr = move(pa, X_UP), move(pa, X_DOWN)
    zf, pb = move(zl, Z_UP), move(b, SWAP_YH)
    a, b, xl, xr, pa, zl, zr, pxl, pxr, zf, pb, notes_o, left, right = lax.optimization_barrier(
        (a, b, xl, xr, pa, zl, zr, pxl, pxr, zf, pb, notes_o, left, right)
    )
    xf, pxf = move(xl, X_UP), move(pxr, X_DOWN)
    pzl, pzr, pzf = move(pb, Z_UP), move(pb, Z_DOWN), move(zf, SWAP_YH)

    plan = planned(rows, cols, left, right, keep_out.astype(F32).reshape(-1), notes_o)
    a_units = [a, xl, xr, pa, pxl, pxr, xf, pxf]
    b_units = [b, zl, zr, zf, pb, pzl, pzr, pzf]
    wide = NC * cols
    mine, theirs = product(plan, a_units[:6], b_units[:5], rows, wide, tuple(range(wide)))
    theirs, = product(plan, a_units, b_units, rows, wide, tuple(range(cols, wide)), theirs)
    got = move(theirs, SWAP_CORE)
    mine, = product(plan, a_units, b_units, rows, wide, tuple(range(cols)), mine)
    inflated, total = squared(mine, got)
    total = row_sum(total[0])
    return rescaled(float(height * lax.axis_size("row")), inflated, total[None, :])


def solution(mesh):
    return jax.shard_map(
        shards,
        mesh=mesh,
        in_specs=(P("row", "col"), P("row", "col"), P("row", "col")),
        out_specs=P("row", "col"),
        check_vma=False,
    )
```

time: 161 us -> 136 us (0.84)
  other arithmetic: 11.9 us -> 0.59 us
  local copies, waits for them, and re-layouts: 20.7 us -> 9.91 us
  Pallas kernels: 25.1 us -> 19.8 us
  starting transfers between devices: 37.9 us -> 40.2 us
    pallas_call x3, Pallas kernels: 25.1 us -> 15.7 us  [product(): pl.pallas_call(functools.partial(product_kernel, len(a_units), len(b_unit...]
    reduce_sum x19 -> x0, other arithmetic: 5.35 us -> none  [the longest x1 2.66 us: shards(): total = row_sum(jnp.sum(inflated, axis=0))]
    another operation x55 -> x0, local copies, waits for them, and re-layouts: 4.19 us -> none  [the longest x25 1.9 us: product(): jnp.stack([lax.dynamic_slice(need_a, (0, base), (rows, deep)).reshape(-1)...]
    pallas_call x0 -> x4, Pallas kernels: none -> 4.09 us  [the longest x1 1.61 us: planned(): pl.pallas_call(functools.partial(plan_kernel, rows, cols), out_shape=jax....]
    mul x2 -> x0, other arithmetic: 3.43 us -> none  [the longest x1 3.42 us: shards(): return inflated * (order / total)[None, :]]
    dynamic_slice x28 -> x0, local copies, waits for them, and re-layouts: 2.53 us -> none  [the longest x23 2.11 us: product(): lax.dynamic_slice(need_b, (base, 0), (deep, cols)).reshape(-1)]
    unnamed x33 -> x30, local copies, waits for them, and re-layouts: 11.9 us -> 9.48 us
    ppermute x29, starting transfers between devices: 37.9 us -> 40.2 us  [move(): return lax.ppermute(value, AXES, perm)]
  transfers between devices with their start and end apart: 29 -> 29, of which waited for: 17 -> 19; matrix products, arithmetic and copies ran while one was open for 4% -> 0% of each run, Pallas kernels for 11% -> 10%
where the time goes in v3:
time: 136 us
  waiting for transfers between devices  65 us (48%)
  starting transfers between devices  40.2 us (30%)
  Pallas kernels  19.8 us (15%)
  local copies, waits for them, and re-layouts  9.91 us (7%)
    ppermute x29, waiting for transfers between devices, move(): return lax.ppermute(value, AXES, perm)  65 us
    ppermute x29, starting transfers between devices, move(): return lax.ppermute(value, AXES, perm)  40.2 us
    pallas_call x3, Pallas kernels, product(): pl.pallas_call(functools.partial(product_kernel, len(a_units), len(b_unit...  15.7 us
    unnamed x30, local copies, waits for them, and re-layouts  9.48 us
  transfers between devices with their start and end apart: 29, of which 19 were waited for; matrix products, arithmetic and copies ran while one was open for 0% of the time, Pallas kernels for 10%

profile of v3, /device:TPU:0, one launch (start us, length us, event | category | flops | bytes accessed | tf_op | source)
XLA Modules:
  0.0 135.8 jit_solution(17356380189376939053)
XLA Ops:
  0.0 0.8 copy.6
  0.8 0.8 copy.7
  1.6 0.1 reshape.19
  1.7 1.6 %copy-done.7 = f32[1024,512]{1,0:T(8,128)S(1)} copy-done((f32[1024,512]{1,0:T(8,128)S(1)}, f32[1024,512]{1,0:T(8,128)}, u32[]{:S(2)}) %copy-start.7) | copy-done | bytes 2097176
  3.3 0.8 mask.1
  4.1 4.2 %collective-permute-start.2 = (f32[576]{0:T(1024)S(1)}, f32[576]{0:T(1024)S(1)}, u32[]{:S(2)}, u32[]{:S(2)}) collective-permute-start(f32[576]{0:T(1024)S(1)} %pad_maximum_fusion.1), channel_id=1, source_target_pairs={{0,48},{1,49},{2,50},{3,51},{4,52},{5,53},{6,54},{7,55},{8,56},{9,... | collective-permute-start | bytes 6920 | tf_op jit(solution)/shard_map/ppermute | solution.py:44
  8.3 1.3 collective-permute-start
  9.6 0.1 reshape.20
  9.7 2.9 %collective-permute-start.6 = (f32[128]{0:T(128)S(1)}, f32[128]{0:T(128)S(1)}, u32[]{:S(2)}, u32[]{:S(2)}) collective-permute-start(f32[128]{0:T(128)S(1)} %reshape.20), channel_id=1, source_target_pairs={{0,6},{1,7},{2,0},{3,1},{4,2},{5,3},{6,4},{7,5},{8,14},{9,15},{10,... | collective-permute-start | bytes 1544 | tf_op jit(solution)/shard_map/ppermute | solution.py:44
  12.6 0.8 collective-permute-start.5
  13.4 0.9 collective-permute-start.4
  14.3 3.3 %collective-permute-start.3 = (f32[576]{0:T(1024)S(1)}, f32[576]{0:T(1024)S(1)}, u32[]{:S(2)}, u32[]{:S(2)}) collective-permute-start(f32[576]{0:T(1024)S(1)} %add_add_fusion), channel_id=1, source_target_pairs={{0,64},{1,65},{2,66},{3,67},{4,68},{5,69},{6,70},{7,71},{8,72},{9,... | collective-permute-start | bytes 6920 | tf_op jit(solution)/shard_map/ppermute | solution.py:44
  17.6 0.5 collective-permute-done.4
  18.2 1.6 %collective-permute-start.7 = (f32[128]{0:T(128)S(1)}, f32[128]{0:T(128)S(1)}, u32[]{:S(2)}, u32[]{:S(2)}) collective-permute-start(f32[128]{0:T(128)S(1)} %add_add_fusion.2), channel_id=1, source_target_pairs={{0,8},{1,9},{2,10},{3,11},{4,12},{5,13},{6,14},{7,15},{8,0},{9,1},... | collective-permute-start | bytes 1544 | tf_op jit(solution)/shard_map/ppermute | solution.py:44
  19.7 2.0 %collective-permute-done.7 = f32[128]{0:T(128)S(1)} collective-permute-done((f32[128]{0:T(128)S(1)}, f32[128]{0:T(128)S(1)}, u32[]{:S(2)}, u32[]{:S(2)}) %collective-permute-start.7) | collective-permute-done | bytes 544 | tf_op jit(solution)/shard_map/ppermute | solution.py:44
  21.7 0.3 divide_convert_fusion.refs_1_.refs_2_
  22.0 0.1 constant_dynamic-slice_fusion.1
  22.1 0.1 collective-permute-start.8
  22.2 1.7 %collective-permute-start.11 = (bf16[1024,512]{1,0:T(8,128)(2,1)S(1)}, bf16[1024,512]{1,0:T(8,128)(2,1)S(1)}, u32[]{:S(2)}, u32[]{:S(2)}) collective-permute-start(bf16[1024,512]{1,0:T(8,128)(2,1)S(1)} %divide_convert_fusion.refs_1_.refs_2_), channel_id=1, source_target_pairs={{0,8},{1,9},{2,10},{3,11},{4,12},{5,13},{6,14},{7,15},{8,0},{9,1},... | collective-permute-start | bytes 3145736 | tf_op jit(solution)/shard_map/ppermute | solution.py:44
  23.9 1.0 collective-permute-start.10
  24.8 1.0 collective-permute-start.9
  25.9 0.1 pad_maximum_fusion.refs_7_.refs_10_
  26.0 2.0 %collective-permute-start.13 = (bf16[512,1024]{1,0:T(8,128)(2,1)S(1)}, bf16[512,1024]{1,0:T(8,128)(2,1)S(1)}, u32[]{:S(2)}, u32[]{:S(2)}) collective-permute-start(bf16[512,1024]{1,0:T(8,128)(2,1)S(1)} %pad_maximum_fusion.refs_7_.refs_10_), channel_id=1, source_target_pairs={{0,48},{1,49},{2,50},{3,51},{4,52},{5,53},{6,54},{7,55},{8,56},{9,... | collective-permute-start | bytes 3145736 | tf_op jit(solution)/shard_map/ppermute | solution.py:44
  28.1 0.3 collective-permute-start.12
  28.4 19.4 %collective-permute-done.11.refs_4_.refs_5_ = bf16[1024,512]{1,0:T(8,128)(2,1)S(1)} collective-permute-done((bf16[1024,512]{1,0:T(8,128)(2,1)S(1)}, bf16[1024,512]{1,0:T(8,128)(2,1)S(1)}, u32[]{:S(2)}, u32[]{:S(2)}) %collective-permute-start.11) | collective-permute-done | bytes 1048608 | tf_op jit(solution)/shard_map/ppermute | solution.py:44
  47.8 1.3 collective-permute-done.10.refs_3_.refs_4_
  49.1 1.0 copy-done
  50.0 0.9 collective-permute-done.9.refs_2_.refs_3_
  51.0 0.2 collective-permute-done.13.refs_9_.refs_12_
  51.2 1.1 copy-done.5
  52.3 1.5 %collective-permute-done.12.refs_8_.refs_11_ = bf16[512,1024]{1,0:T(8,128)(2,1)} collective-permute-done((bf16[512,1024]{1,0:T(8,128)(2,1)S(1)}, bf16[512,1024]{1,0:T(8,128)(2,1)}, u32[]{:S(2)}, u32[]{:S(2)}) %collective-permute-start.12) | collective-permute-done | bytes 1048608 | tf_op jit(solution)/shard_map/ppermute | solution.py:44
  53.8 2.9 %collective-permute-start.17 = (bf16[512,1024]{1,0:T(8,128)(2,1)S(1)}, bf16[512,1024]{1,0:T(8,128)(2,1)}, u32[]{:S(2)}, u32[]{:S(2)}) collective-permute-start(bf16[512,1024]{1,0:T(8,128)(2,1)S(1)} %pad_maximum_fusion.refs_7_.refs_10_), channel_id=1, source_target_pairs={{0,64},{1,65},{2,66},{3,67},{4,68},{5,69},{6,70},{7,71},{8,72},{9,... | collective-permute-start | bytes 3145736 | tf_op jit(solution)/shard_map/ppermute | solution.py:44
  56.7 0.2 collective-permute-start.16
  56.9 1.6 %collective-permute-start.15 = (bf16[1024,512]{1,0:T(8,128)(2,1)S(1)}, bf16[1024,512]{1,0:T(8,128)(2,1)}, u32[]{:S(2)}, u32[]{:S(2)}) collective-permute-start(bf16[1024,512]{1,0:T(8,128)(2,1)S(1)} %collective-permute-done.11.refs_4_.refs_5_), channel_id=1, source_target_pairs={{0,6},{1,7},{2,0},{3,1},{4,2},{5,3},{6,4},{7,5},{8,14},{9,15},{10,... | collective-permute-start | bytes 3145736 | tf_op jit(solution)/shard_map/ppermute | solution.py:44
  58.5 0.4 collective-permute-start.14
  58.9 0.1 reshape.21.out_ref
  59.1 1.1 collective-permute-done.18.other_ref
  60.2 18.6 %collective-permute-done.17.refs_11_.refs_14_ = bf16[512,1024]{1,0:T(8,128)(2,1)} collective-permute-done((bf16[512,1024]{1,0:T(8,128)(2,1)S(1)}, bf16[512,1024]{1,0:T(8,128)(2,1)}, u32[]{:S(2)}, u32[]{:S(2)}) %collective-permute-start.17) | collective-permute-done | bytes 1048608 | tf_op jit(solution)/shard_map/ppermute | solution.py:44
  78.8 2.5 %collective-permute-done.16.refs_10_.refs_13_ = bf16[512,1024]{1,0:T(8,128)(2,1)} collective-permute-done((bf16[512,1024]{1,0:T(8,128)(2,1)}, bf16[512,1024]{1,0:T(8,128)(2,1)}, u32[]{:S(2)}, u32[]{:S(2)}) %collective-permute-start.16) | collective-permute-done | bytes 1048608 | tf_op jit(solution)/shard_map/ppermute | solution.py:44
  81.4 1.5 %collective-permute-done.14.refs_5_.refs_6_ = bf16[1024,512]{1,0:T(8,128)(2,1)} collective-permute-done((bf16[1024,512]{1,0:T(8,128)(2,1)S(1)}, bf16[1024,512]{1,0:T(8,128)(2,1)}, u32[]{:S(2)}, u32[]{:S(2)}) %collective-permute-start.14) | collective-permute-done | bytes 1048608 | tf_op jit(solution)/shard_map/ppermute | solution.py:44
  82.9 3.2 %collective-permute-start.20 = (bf16[1024,512]{1,0:T(8,128)(2,1)}, bf16[1024,512]{1,0:T(8,128)(2,1)}, u32[]{:S(2)}, u32[]{:S(2)}) collective-permute-start(bf16[1024,512]{1,0:T(8,128)(2,1)} %collective-permute-done.15.refs_6_.refs_7_), channel_id=1, source_target_pairs={{0,6},{1,7},{2,0},{3,1},{4,2},{5,3},{6,4},{7,5},{8,14},{9,15},{10,... | collective-permute-start | bytes 3145736 | tf_op jit(solution)/shard_map/ppermute | solution.py:44
  86.1 1.2 collective-permute-start.23
  87.3 2.5 %collective-permute-start.22 = (bf16[512,1024]{1,0:T(8,128)(2,1)}, bf16[512,1024]{1,0:T(8,128)(2,1)}, u32[]{:S(2)}, u32[]{:S(2)}) collective-permute-start(bf16[512,1024]{1,0:T(8,128)(2,1)} %collective-permute-done.17.refs_11_.refs_14_), channel_id=1, source_target_pairs={{0,48},{1,49},{2,50},{3,51},{4,52},{5,53},{6,54},{7,55},{8,56},{9,... | collective-permute-start | bytes 3145736 | tf_op jit(solution)/shard_map/ppermute | solution.py:44
  89.9 1.6 %plan.1.refs_0_ = s32[48]{0:T(128)} custom-call(f32[128]{0:T(128)} %copy-done.11, f32[64]{0:T(128)} %copy-done.12, f32[8]{0:T(128)} %copy-done.10, f32[200]{0:T(256)} %copy-done.13), custom_call_target="tpu_custom_call" | custom-call | tf_op jit(solution)/shard_map/plan/pallas_call | solution.py:196
  91.5 1.2 copy-done.1
  92.7 1.2 copy-done.3
  94.0 1.2 copy-done.6
  95.2 0.6 copy-done.8
  95.8 7.1 %begin.1 = (f32[1024,512]{1,0:T(8,128)S(1)}, f32[1024,512]{1,0:T(8,128)S(1)}) custom-call(s32[48]{0:T(128)S(1)} %copy-done.8, bf16[1024,512]{1,0:T(8,128)(2,1)S(1)} %divide_convert_fusion.refs_1_.refs_2_, bf16[1024,512]{1,0:T(8,128)(2,1)S(1)} %copy-done.3, bf16[1024,512]{1,0:T(8,128)(2,1)S(1)} %copy-done.1, ...), custom_call_target="tpu_custom_call" | custom-call | flops 1000000 | bytes 1024 | tf_op jit(solution)/shard_map/begin/pallas_call | solution.py:293
  103.0 3.7 %collective-permute-done.19.refs_8_ = bf16[1024,512]{1,0:T(8,128)(2,1)} collective-permute-done((bf16[1024,512]{1,0:T(8,128)(2,1)}, bf16[1024,512]{1,0:T(8,128)(2,1)}, u32[]{:S(2)}, u32[]{:S(2)}) %collective-permute-start.19) | collective-permute-done | bytes 1048608 | tf_op jit(solution)/shard_map/ppermute | solution.py:44
  106.6 3.0 %collective-permute-done.23.refs_17_ = bf16[512,1024]{1,0:T(8,128)(2,1)} collective-permute-done((bf16[512,1024]{1,0:T(8,128)(2,1)}, bf16[512,1024]{1,0:T(8,128)(2,1)}, u32[]{:S(2)}, u32[]{:S(2)}) %collective-permute-start.23) | collective-permute-done | bytes 1048608 | tf_op jit(solution)/shard_map/ppermute | solution.py:44
  109.6 2.4 %collective-permute-done.21.refs_15_ = bf16[512,1024]{1,0:T(8,128)(2,1)} collective-permute-done((bf16[512,1024]{1,0:T(8,128)(2,1)}, bf16[512,1024]{1,0:T(8,128)(2,1)}, u32[]{:S(2)}, u32[]{:S(2)}) %collective-permute-start.21) | collective-permute-done | bytes 1048608 | tf_op jit(solution)/shard_map/ppermute | solution.py:44
  112.0 4.3 %finish.3 = f32[1024,512]{1,0:T(8,128)S(1)} custom-call(s32[48]{0:T(128)S(1)} %copy-done.8, f32[1024,512]{1,0:T(8,128)S(1)} %get-tuple-element.60.refs_1_, bf16[1024,512]{1,0:T(8,128)(2,1)S(1)} %divide_convert_fusion.refs_1_.refs_2_, bf16[1024,512]{1,0:T(8,128)(2,1)S(1)} %copy-done.4, bf16[1024,512]{1,0:T(8,128)(2,1)S(1)} %copy-done.1, ...), custom_call_target="tpu_custom_call" | custom-call | flops 1000000 | bytes 1024 | tf_op jit(solution)/shard_map/finish/pallas_call | solution.py:293
  116.3 0.1 collective-permute-start.24
  116.4 4.3 %finish.2.mine_ref = f32[1024,512]{1,0:T(8,128)S(1)} custom-call(s32[48]{0:T(128)S(1)} %copy-done.9, f32[1024,512]{1,0:T(8,128)S(1)} %get-tuple-element.59.refs_1_, bf16[1024,512]{1,0:T(8,128)(2,1)S(1)} %divide_convert_fusion.refs_1_.refs_2_, bf16[1024,512]{1,0:T(8,128)(2,1)S(1)} %copy-done.4, bf16[1024,512]{1,0:T(8,128)(2,1)S(1)} %copy-done.1, ...), custom_call_target="tpu_custom_call" | custom-call | flops 1000000 | bytes 1024 | tf_op jit(solution)/shard_map/finish/pallas_call | solution.py:293
  120.7 0.2 square.1
  121.0 0.5 collective-permute-start.27
  121.4 2.3 %collective-permute-start.26 = (f32[512]{0:T(512)S(1)}, f32[512]{0:T(512)S(1)}, u32[]{:S(2)}, u32[]{:S(2)}) collective-permute-start(f32[512]{0:T(512)S(1)} %bitcast.7), channel_id=1, source_target_pairs={{0,32},{1,33},{2,34},{3,35},{4,36},{5,37},{6,38},{7,39},{8,40},{9,... | collective-permute-start | bytes 6152 | tf_op jit(solution)/shard_map/ppermute | solution.py:44
  123.7 0.9 collective-permute-done.27
  124.6 1.9 %collective-permute-done.26 = f32[512]{0:T(512)S(1)} collective-permute-done((f32[512]{0:T(512)S(1)}, f32[512]{0:T(512)S(1)}, u32[]{:S(2)}, u32[]{:S(2)}) %collective-permute-start.26) | collective-permute-done | bytes 2080 | tf_op jit(solution)/shard_map/ppermute | solution.py:44
  126.5 2.0 %collective-permute-done.25 = f32[512]{0:T(512)S(1)} collective-permute-done((f32[512]{0:T(512)S(1)}, f32[512]{0:T(512)S(1)}, u32[]{:S(2)}, u32[]{:S(2)}) %collective-permute-start.25) | collective-permute-done | bytes 2080 | tf_op jit(solution)/shard_map/ppermute | solution.py:44
  128.5 4.3 %collective-permute-start.28 = (f32[512]{0:T(512)S(1)}, f32[512]{0:T(512)S(1)}, u32[]{:S(2)}, u32[]{:S(2)}) collective-permute-start(f32[512]{0:T(512)S(1)} %add_add_fusion.1), channel_id=1, source_target_pairs={{0,64},{1,65},{2,66},{3,67},{4,68},{5,69},{6,70},{7,71},{8,72},{9,... | collective-permute-start | bytes 6152 | tf_op jit(solution)/shard_map/ppermute | solution.py:44
  132.8 1.6 %collective-permute-done.28 = f32[512]{0:T(512)S(1)} collective-permute-done((f32[512]{0:T(512)S(1)}, f32[512]{0:T(512)S(1)}, u32[]{:S(2)}, u32[]{:S(2)}) %collective-permute-start.28) | collective-permute-done | bytes 2080 | tf_op jit(solution)/shard_map/ppermute | solution.py:44
  134.3 1.5 %rescale.1 = f32[1024,512]{1,0:T(8,128)} custom-call(f32[1024,512]{1,0:T(8,128)S(1)} %get-tuple-element.61.value_ref, f32[1,512]{1,0:T(1,128)S(1)} %bitcast.3), custom_call_target="tpu_custom_call" | custom-call | tf_op jit(solution)/shard_map/rescale/pallas_call | solution.py:132
  (54 shorter events, 0.4 us)
Async XLA Ops:
  1.7 1.6 %copy-start.7 = (f32[1024,512]{1,0:T(8,128)S(1)}, f32[1024,512]{1,0:T(8,128)}, u32[]{:S(2)}) copy-start(f32[1024,512]{1,0:T(8,128)} %entries_ref.1) | copy-start | bytes 6291460
  4.1 9.3 %collective-permute-start.2 = (f32[576]{0:T(1024)S(1)}, f32[576]{0:T(1024)S(1)}, u32[]{:S(2)}, u32[]{:S(2)}) collective-permute-start(f32[576]{0:T(1024)S(1)} %pad_maximum_fusion.1), channel_id=1, source_target_pairs={{0,48},{1,49},{2,50},{3,51},{4,52},{5,53},{6,54},{7,55},{8,56},{9,... | collective-permute-start | bytes 6920 | tf_op jit(solution)/shard_map/ppermute | solution.py:44
  8.3 6.0 %collective-permute-start.1 = (f32[576]{0:T(1024)S(1)}, f32[576]{0:T(1024)S(1)}, u32[]{:S(2)}, u32[]{:S(2)}) collective-permute-start(f32[576]{0:T(1024)S(1)} %pad_maximum_fusion.1), channel_id=1, source_target_pairs={{0,32},{1,33},{2,34},{3,35},{4,36},{5,37},{6,38},{7,39},{8,40},{9,... | collective-permute-start | bytes 6920 | tf_op jit(solution)/shard_map/ppermute | solution.py:44
  8.3 6.0 %collective-permute-start = (f32[576]{0:T(1024)S(1)}, f32[576]{0:T(1024)S(1)}, u32[]{:S(2)}, u32[]{:S(2)}) collective-permute-start(f32[576]{0:T(1024)S(1)} %pad_maximum_fusion.1), channel_id=1, source_target_pairs={{0,16},{1,17},{2,18},{3,19},{4,20},{5,21},{6,22},{7,23},{8,24},{9,... | collective-permute-start | bytes 6920 | tf_op jit(solution)/shard_map/ppermute | solution.py:44
  9.7 7.9 %collective-permute-start.6 = (f32[128]{0:T(128)S(1)}, f32[128]{0:T(128)S(1)}, u32[]{:S(2)}, u32[]{:S(2)}) collective-permute-start(f32[128]{0:T(128)S(1)} %reshape.20), channel_id=1, source_target_pairs={{0,6},{1,7},{2,0},{3,1},{4,2},{5,3},{6,4},{7,5},{8,14},{9,15},{10,... | collective-permute-start | bytes 1544 | tf_op jit(solution)/shard_map/ppermute | solution.py:44
  12.6 5.0 %collective-permute-start.5 = (f32[128]{0:T(128)S(1)}, f32[128]{0:T(128)S(1)}, u32[]{:S(2)}, u32[]{:S(2)}) collective-permute-start(f32[128]{0:T(128)S(1)} %reshape.20), channel_id=1, source_target_pairs={{0,4},{1,5},{2,6},{3,7},{4,0},{5,1},{6,2},{7,3},{8,12},{9,13},{10,... | collective-permute-start | bytes 1544 | tf_op jit(solution)/shard_map/ppermute | solution.py:44
  13.4 4.8 %collective-permute-start.4 = (f32[128]{0:T(128)S(1)}, f32[128]{0:T(128)S(1)}, u32[]{:S(2)}, u32[]{:S(2)}) collective-permute-start(f32[128]{0:T(128)S(1)} %reshape.20), channel_id=1, source_target_pairs={{0,2},{1,3},{2,4},{3,5},{4,6},{5,7},{6,0},{7,1},{8,10},{9,11},{10,... | collective-permute-start | bytes 1544 | tf_op jit(solution)/shard_map/ppermute | solution.py:44
  14.3 7.4 %collective-permute-start.3 = (f32[576]{0:T(1024)S(1)}, f32[576]{0:T(1024)S(1)}, u32[]{:S(2)}, u32[]{:S(2)}) collective-permute-start(f32[576]{0:T(1024)S(1)} %add_add_fusion), channel_id=1, source_target_pairs={{0,64},{1,65},{2,66},{3,67},{4,68},{5,69},{6,70},{7,71},{8,72},{9,... | collective-permute-start | bytes 6920 | tf_op jit(solution)/shard_map/ppermute | solution.py:44
  18.2 3.5 %collective-permute-start.7 = (f32[128]{0:T(128)S(1)}, f32[128]{0:T(128)S(1)}, u32[]{:S(2)}, u32[]{:S(2)}) collective-permute-start(f32[128]{0:T(128)S(1)} %add_add_fusion.2), channel_id=1, source_target_pairs={{0,8},{1,9},{2,10},{3,11},{4,12},{5,13},{6,14},{7,15},{8,0},{9,1},... | collective-permute-start | bytes 1544 | tf_op jit(solution)/shard_map/ppermute | solution.py:44
  21.7 37.3 %copy-start.11 = (f32[128]{0:T(128)}, f32[128]{0:T(128)S(1)}, u32[]{:S(2)}) copy-start(f32[128]{0:T(128)S(1)} %add.89.left_ref) | copy-start | bytes 1540
  22.1 3.8 %collective-permute-start.8 = (bf16[512,512]{1,0:T(8,128)(2,1)S(1)}, bf16[512,512]{1,0:T(8,128)(2,1)S(1)}, u32[]{:S(2)}, u32[]{:S(2)}) collective-permute-start(bf16[512,512]{1,0:T(8,128)(2,1)S(1)} %get-tuple-element.66), channel_id=1, source_target_pairs={{0,1},{1,0},{2,3},{3,2},{4,5},{5,4},{6,7},{7,6},{8,9},{9,8},{10,11... | collective-permute-start | bytes 1572872 | tf_op jit(solution)/shard_map/ppermute | solution.py:44
  22.2 25.6 %collective-permute-start.11 = (bf16[1024,512]{1,0:T(8,128)(2,1)S(1)}, bf16[1024,512]{1,0:T(8,128)(2,1)S(1)}, u32[]{:S(2)}, u32[]{:S(2)}) collective-permute-start(bf16[1024,512]{1,0:T(8,128)(2,1)S(1)} %divide_convert_fusion.refs_1_.refs_2_), channel_id=1, source_target_pairs={{0,8},{1,9},{2,10},{3,11},{4,12},{5,13},{6,14},{7,15},{8,0},{9,1},... | collective-permute-start | bytes 3145736 | tf_op jit(solution)/shard_map/ppermute | solution.py:44
  23.9 25.2 %collective-permute-start.10 = (bf16[1024,512]{1,0:T(8,128)(2,1)S(1)}, bf16[1024,512]{1,0:T(8,128)(2,1)S(1)}, u32[]{:S(2)}, u32[]{:S(2)}) collective-permute-start(bf16[1024,512]{1,0:T(8,128)(2,1)S(1)} %divide_convert_fusion.refs_1_.refs_2_), channel_id=1, source_target_pairs={{0,6},{1,7},{2,0},{3,1},{4,2},{5,3},{6,4},{7,5},{8,14},{9,15},{10,... | collective-permute-start | bytes 3145736 | tf_op jit(solution)/shard_map/ppermute | solution.py:44
  24.8 26.1 %collective-permute-start.9 = (bf16[1024,512]{1,0:T(8,128)(2,1)S(1)}, bf16[1024,512]{1,0:T(8,128)(2,1)S(1)}, u32[]{:S(2)}, u32[]{:S(2)}) collective-permute-start(bf16[1024,512]{1,0:T(8,128)(2,1)S(1)} %divide_convert_fusion.refs_1_.refs_2_), channel_id=1, source_target_pairs={{0,2},{1,3},{2,4},{3,5},{4,6},{5,7},{6,0},{7,1},{8,10},{9,11},{10,... | collective-permute-start | bytes 3145736 | tf_op jit(solution)/shard_map/ppermute | solution.py:44
  26.0 25.2 %collective-permute-start.13 = (bf16[512,1024]{1,0:T(8,128)(2,1)S(1)}, bf16[512,1024]{1,0:T(8,128)(2,1)S(1)}, u32[]{:S(2)}, u32[]{:S(2)}) collective-permute-start(bf16[512,1024]{1,0:T(8,128)(2,1)S(1)} %pad_maximum_fusion.refs_7_.refs_10_), channel_id=1, source_target_pairs={{0,48},{1,49},{2,50},{3,51},{4,52},{5,53},{6,54},{7,55},{8,56},{9,... | collective-permute-start | bytes 3145736 | tf_op jit(solution)/shard_map/ppermute | solution.py:44
  28.1 25.7 %collective-permute-start.12 = (bf16[512,1024]{1,0:T(8,128)(2,1)S(1)}, bf16[512,1024]{1,0:T(8,128)(2,1)}, u32[]{:S(2)}, u32[]{:S(2)}) collective-permute-start(bf16[512,1024]{1,0:T(8,128)(2,1)S(1)} %pad_maximum_fusion.refs_7_.refs_10_), channel_id=1, source_target_pairs={{0,16},{1,17},{2,18},{3,19},{4,20},{5,21},{6,22},{7,23},{8,24},{9,... | collective-permute-start | bytes 3145736 | tf_op jit(solution)/shard_map/ppermute | solution.py:44
  49.1 1.0 copy-start
  51.0 5.9 %copy-start.2 = (bf16[1024,512]{1,0:T(8,128)(2,1)}, bf16[1024,512]{1,0:T(8,128)(2,1)S(1)}, u32[]{:S(2)}) copy-start(bf16[1024,512]{1,0:T(8,128)(2,1)S(1)} %collective-permute-done.9.refs_2_.refs_3_) | copy-start | bytes 3145732
  51.2 1.1 copy-start.5
  53.8 25.1 %collective-permute-start.17 = (bf16[512,1024]{1,0:T(8,128)(2,1)S(1)}, bf16[512,1024]{1,0:T(8,128)(2,1)}, u32[]{:S(2)}, u32[]{:S(2)}) collective-permute-start(bf16[512,1024]{1,0:T(8,128)(2,1)S(1)} %pad_maximum_fusion.refs_7_.refs_10_), channel_id=1, source_target_pairs={{0,64},{1,65},{2,66},{3,67},{4,68},{5,69},{6,70},{7,71},{8,72},{9,... | collective-permute-start | bytes 3145736 | tf_op jit(solution)/shard_map/ppermute | solution.py:44
  56.7 24.7 %collective-permute-start.16 = (bf16[512,1024]{1,0:T(8,128)(2,1)}, bf16[512,1024]{1,0:T(8,128)(2,1)}, u32[]{:S(2)}, u32[]{:S(2)}) collective-permute-start(bf16[512,1024]{1,0:T(8,128)(2,1)} %collective-permute-done.12.refs_8_.refs_11_), channel_id=1, source_target_pairs={{0,16},{1,17},{2,18},{3,19},{4,20},{5,21},{6,22},{7,23},{8,24},{9,... | collective-permute-start | bytes 3145736 | tf_op jit(solution)/shard_map/ppermute | solution.py:44
  56.9 24.5 %collective-permute-start.15 = (bf16[1024,512]{1,0:T(8,128)(2,1)S(1)}, bf16[1024,512]{1,0:T(8,128)(2,1)}, u32[]{:S(2)}, u32[]{:S(2)}) collective-permute-start(bf16[1024,512]{1,0:T(8,128)(2,1)S(1)} %collective-permute-done.11.refs_4_.refs_5_), channel_id=1, source_target_pairs={{0,6},{1,7},{2,0},{3,1},{4,2},{5,3},{6,4},{7,5},{8,14},{9,15},{10,... | collective-permute-start | bytes 3145736 | tf_op jit(solution)/shard_map/ppermute | solution.py:44
  58.5 24.5 %collective-permute-start.14 = (bf16[1024,512]{1,0:T(8,128)(2,1)S(1)}, bf16[1024,512]{1,0:T(8,128)(2,1)}, u32[]{:S(2)}, u32[]{:S(2)}) collective-permute-start(bf16[1024,512]{1,0:T(8,128)(2,1)S(1)} %collective-permute-done.11.refs_4_.refs_5_), channel_id=1, source_target_pairs={{0,2},{1,3},{2,4},{3,5},{4,6},{5,7},{6,0},{7,1},{8,10},{9,11},{10,... | collective-permute-start | bytes 3145736 | tf_op jit(solution)/shard_map/ppermute | solution.py:44
  59.0 30.9 %copy-start.10 = (f32[8]{0:T(128)}, f32[8]{0:T(128)S(1)}, u32[]{:S(2)}) copy-start(f32[8]{0:T(128)S(1)} %reshape.21.out_ref) | copy-start | bytes 100
  59.0 30.9 %copy-start.12 = (f32[64]{0:T(128)}, f32[64]{0:T(128)S(1)}, u32[]{:S(2)}) copy-start(f32[64]{0:T(128)S(1)} %slice.7.right_ref) | copy-start | bytes 772
  59.1 1.2 collective-permute-start.18
  60.2 29.7 %copy-start.13 = (f32[200]{0:T(256)}, f32[200]{0:T(256)S(1)}, u32[]{:S(2)}) copy-start(f32[200]{0:T(256)S(1)} %collective-permute-done.18.other_ref) | copy-start | bytes 2404
  82.9 23.7 %collective-permute-start.19 = (bf16[1024,512]{1,0:T(8,128)(2,1)}, bf16[1024,512]{1,0:T(8,128)(2,1)}, u32[]{:S(2)}, u32[]{:S(2)}) collective-permute-start(bf16[1024,512]{1,0:T(8,128)(2,1)} %copy-done.2), channel_id=1, source_target_pairs={{0,2},{1,3},{2,4},{3,5},{4,6},{5,7},{6,0},{7,1},{8,10},{9,11},{10,... | collective-permute-start | bytes 3145736 | tf_op jit(solution)/shard_map/ppermute | solution.py:44
  82.9 23.7 %collective-permute-start.20 = (bf16[1024,512]{1,0:T(8,128)(2,1)}, bf16[1024,512]{1,0:T(8,128)(2,1)}, u32[]{:S(2)}, u32[]{:S(2)}) collective-permute-start(bf16[1024,512]{1,0:T(8,128)(2,1)} %collective-permute-done.15.refs_6_.refs_7_), channel_id=1, source_target_pairs={{0,6},{1,7},{2,0},{3,1},{4,2},{5,3},{6,4},{7,5},{8,14},{9,15},{10,... | collective-permute-start | bytes 3145736 | tf_op jit(solution)/shard_map/ppermute | solution.py:44
  86.1 23.5 %collective-permute-start.23 = (bf16[512,1024]{1,0:T(8,128)(2,1)}, bf16[512,1024]{1,0:T(8,128)(2,1)}, u32[]{:S(2)}, u32[]{:S(2)}) collective-permute-start(bf16[512,1024]{1,0:T(8,128)(2,1)} %collective-permute-done.16.refs_10_.refs_13_), channel_id=1, source_target_pairs={{0,64},{1,65},{2,66},{3,67},{4,68},{5,69},{6,70},{7,71},{8,72},{9,... | collective-permute-start | bytes 3145736 | tf_op jit(solution)/shard_map/ppermute | solution.py:44
  87.3 22.3 %collective-permute-start.22 = (bf16[512,1024]{1,0:T(8,128)(2,1)}, bf16[512,1024]{1,0:T(8,128)(2,1)}, u32[]{:S(2)}, u32[]{:S(2)}) collective-permute-start(bf16[512,1024]{1,0:T(8,128)(2,1)} %collective-permute-done.17.refs_11_.refs_14_), channel_id=1, source_target_pairs={{0,48},{1,49},{2,50},{3,51},{4,52},{5,53},{6,54},{7,55},{8,56},{9,... | collective-permute-start | bytes 3145736 | tf_op jit(solution)/shard_map/ppermute | solution.py:44
  89.9 22.1 %collective-permute-start.21 = (bf16[512,1024]{1,0:T(8,128)(2,1)}, bf16[512,1024]{1,0:T(8,128)(2,1)}, u32[]{:S(2)}, u32[]{:S(2)}) collective-permute-start(bf16[512,1024]{1,0:T(8,128)(2,1)} %collective-permute-done.17.refs_11_.refs_14_), channel_id=1, source_target_pairs={{0,16},{1,17},{2,18},{3,19},{4,20},{5,21},{6,22},{7,23},{8,24},{9,... | collective-permute-start | bytes 3145736 | tf_op jit(solution)/shard_map/ppermute | solution.py:44
  91.5 1.2 copy-start.1
  92.7 1.2 copy-start.3
  94.0 1.2 copy-start.6
  95.2 0.6 copy-start.8
  95.8 16.1 %copy-start.4 = (bf16[1024,512]{1,0:T(8,128)(2,1)S(1)}, bf16[1024,512]{1,0:T(8,128)(2,1)}, u32[]{:S(2)}) copy-start(bf16[1024,512]{1,0:T(8,128)(2,1)} %copy-done.2) | copy-start | bytes 3145732
  112.0 4.4 %copy-start.9 = (s32[48]{0:T(128)S(1)}, s32[48]{0:T(128)}, u32[]{:S(2)}) copy-start(s32[48]{0:T(128)} %plan.1.refs_0_) | copy-start | bytes 580
  116.3 4.4 %collective-permute-start.24 = (f32[1024,512]{1,0:T(8,128)S(1)}, f32[1024,512]{1,0:T(8,128)S(1)}, u32[]{:S(2)}, u32[]{:S(2)}) collective-permute-start(f32[1024,512]{1,0:T(8,128)S(1)} %finish.3), channel_id=1, source_target_pairs={{0,1},{1,0},{2,3},{3,2},{4,5},{5,4},{6,7},{7,6},{8,9},{9,8},{10,11... | collective-permute-start | bytes 6291464 | tf_op jit(solution)/shard_map/ppermute | solution.py:44
  121.0 3.7 %collective-permute-start.27 = (f32[512]{0:T(512)S(1)}, f32[512]{0:T(512)S(1)}, u32[]{:S(2)}, u32[]{:S(2)}) collective-permute-start(f32[512]{0:T(512)S(1)} %bitcast.6), channel_id=1, source_target_pairs={{0,48},{1,49},{2,50},{3,51},{4,52},{5,53},{6,54},{7,55},{8,56},{9,... | collective-permute-start | bytes 6152 | tf_op jit(solution)/shard_map/ppermute | solution.py:44
  121.4 5.1 %collective-permute-start.26 = (f32[512]{0:T(512)S(1)}, f32[512]{0:T(512)S(1)}, u32[]{:S(2)}, u32[]{:S(2)}) collective-permute-start(f32[512]{0:T(512)S(1)} %bitcast.7), channel_id=1, source_target_pairs={{0,32},{1,33},{2,34},{3,35},{4,36},{5,37},{6,38},{7,39},{8,40},{9,... | collective-permute-start | bytes 6152 | tf_op jit(solution)/shard_map/ppermute | solution.py:44
  123.7 4.8 %collective-permute-start.25 = (f32[512]{0:T(512)S(1)}, f32[512]{0:T(512)S(1)}, u32[]{:S(2)}, u32[]{:S(2)}) collective-permute-start(f32[512]{0:T(512)S(1)} %bitcast.8), channel_id=1, source_target_pairs={{0,16},{1,17},{2,18},{3,19},{4,20},{5,21},{6,22},{7,23},{8,24},{9,... | collective-permute-start | bytes 6152 | tf_op jit(solution)/shard_map/ppermute | solution.py:44
  128.5 5.8 %collective-permute-start.28 = (f32[512]{0:T(512)S(1)}, f32[512]{0:T(512)S(1)}, u32[]{:S(2)}, u32[]{:S(2)}) collective-permute-start(f32[512]{0:T(512)S(1)} %add_add_fusion.1), channel_id=1, source_target_pairs={{0,64},{1,65},{2,66},{3,67},{4,68},{5,69},{6,70},{7,71},{8,72},{9,... | collective-permute-start | bytes 6152 | tf_op jit(solution)/shard_map/ppermute | solution.py:44

commit v4 on v3

--- a/solution.py
+++ b/solution.py
@@ -37,7 +37,6 @@
 SWAP_YL = pairs(lambda yh, z, yl, x, c: (yh, z, 1 - yl, x, c))
 SWAP_YH = pairs(lambda yh, z, yl, x, c: (1 - yh, z, yl, x, c))
 Z_TURNS = [pairs(lambda yh, z, yl, x, c, d=d: (yh, (z + d) % NZ, yl, x, c)) for d in range(1, NZ)]
-X_TURNS = [pairs(lambda yh, z, yl, x, c, d=d: (yh, z, yl, (x + d) % NX, c)) for d in range(1, NX)]
 
 
 def move(value, perm):
@@ -67,14 +66,14 @@
 
 
 def mask_kernel(keep_ref, entries_ref, masked_ref, sum_ref):
-    rows, cols = keep_ref.shape
+    cols, rows = keep_ref.shape
     tall, wide = entries_ref.shape[0] // rows, entries_ref.shape[1] // cols
     for j in range(cols):
         right = slice(j * wide, (j + 1) * wide)
         total = jnp.zeros((1, wide), F32)
         for i in range(rows):
             down = slice(i * tall, (i + 1) * tall)
-            masked = entries_ref[down, right] * keep_ref[i, j].astype(F32)
+            masked = entries_ref[down, right] * keep_ref[j, i].astype(F32)
             masked_ref[down, right] = masked
             total = total + jnp.sum(masked, axis=0, keepdims=True)
         sum_ref[:, right] = total
@@ -145,61 +144,81 @@
 A_LATE, B_LATE = (6, 7), (5, 6, 7)
 
 
-def plan_kernel(rows, cols, left_ref, right_ref, out_ref, other_ref, plan_ref):
+def plan_kernel(rows, cols, right_ref, out_ref, other_ref, *refs):
+    units, (plan_ref, corner, sem) = refs[:-3], refs[-3:]
     row, col = lax.axis_index("row"), lax.axis_index("col")
     yh, z = row // NZ, row % NZ
     yl, x, c = col // (NX * NC), (col // NC) % NX, col % NC
     parts = YL * NX
     grid = parts * NC * cols
-    n_left, n_right = rows * grid, grid * cols
-
-    for i in range(rows):
-        def add(q, m, i=i):
-            for j in range(cols):
-                at = i * grid + (q * NC + c) * cols + j
-                flag = ((left_ref[at] + other_ref[at]) > 0.5).astype(I32)
-                m = m + flag * (1 << (q * cols + j))
-            return m
-
-        plan_ref[PLAN_LEFT + i] = functools.reduce(lambda m, q: add(q, m), range(parts), jnp.int32(0))
-    for j in range(NC * cols):
-        m = jnp.int32(0)
-        for q in range(parts):
-            for i in range(cols):
-                at = ((q * NC + c) * cols + i) * cols + j % cols
-                flag = right_ref[at] if j < cols else other_ref[n_left + at]
-                m = m + (flag > 0.5).astype(I32) * (1 << (q * cols + i))
-        plan_ref[PLAN_RIGHT + j] = m
-    for i in range(rows):
-        for j in range(NC * cols):
-            if j < cols:
-                flag = out_ref[i * cols + j]
-            else:
-                flag = other_ref[n_left + n_right + i * cols + j - cols]
-            plan_ref[PLAN_OUT + i * NC * cols + j] = (flag > 0.5).astype(I32)
+    n_right = grid * cols
+    tall, wide = units[0].shape[0] // rows, units[0].shape[1] // cols
+
+    copies = []
+    for u, unit in enumerate(units):
+        for i in range(rows):
+            for k in range(cols):
+                n = (u * rows + i) * cols + k
+                source = unit.at[pl.ds(i * tall, corner.shape[1]), pl.ds(k * wide, corner.shape[2])]
+                copies.append(pltpu.make_async_copy(source, corner.at[n], sem.at[n]))
+    for copy in copies:
+        copy.start()
+
     late = jnp.int32(0)
+    left = [jnp.int32(0)] * rows
     whole = (1 << cols) - 1
+    bases = []
     for u, (dy, dx) in enumerate(A_PLACES):
         base = ((yl + dy) % YL * NX + (x + dx) % NX) * cols
+        bases.append(base)
         plan_ref[PLAN_A + u] = base
         if u in A_LATE:
             late = late | lax.shift_left(jnp.int32(whole), base)
+            left = [m | lax.shift_left(jnp.int32(whole), base) for m in left]
     for u, (dy, dz) in enumerate(B_PLACES):
         base = ((yh + dy) % YH * NZ + (z + dz) % NZ) * cols
         plan_ref[PLAN_B + u] = base
         if u in B_LATE:
             late = late | lax.shift_left(jnp.int32(whole), base)
     plan_ref[PLAN_LATE] = late
-
-
-def planned(rows, cols, left, right, keep_out, other):
+    for j in range(NC * cols):
+        m = jnp.int32(0)
+        for q in range(parts):
+            for i in range(cols):
+                at = j % cols * grid + (q * NC + c) * cols + i
+                flag = right_ref[at] if j < cols else other_ref[at]
+                m = m + (flag > 0.5).astype(I32) * (1 << (q * cols + i))
+        plan_ref[PLAN_RIGHT + j] = m
+    for i in range(rows):
+        for j in range(NC * cols):
+            flag = out_ref[j * rows + i] if j < cols else other_ref[n_right + (j - cols) * rows + i]
+            plan_ref[PLAN_OUT + i * NC * cols + j] = (flag > 0.5).astype(I32)
+
+    for copy in copies:
+        copy.wait()
+    for i in range(rows):
+        m = left[i]
+        for u in range(len(units)):
+            bits = jnp.int32(0)
+            for k in range(cols):
+                full = jnp.max(corner[(u * rows + i) * cols + k].astype(F32)) > 0
+                bits = bits + full.astype(I32) * (1 << k)
+            m = m | lax.shift_left(bits, bases[u])
+        plan_ref[PLAN_LEFT + i] = m
+
+
+def planned(rows, cols, right, keep_out, other, units):
+    count = len(units) * rows * cols
     return pl.pallas_call(
         functools.partial(plan_kernel, rows, cols),
         out_shape=jax.ShapeDtypeStruct((PLAN_SIZE,), I32),
-        in_specs=[SMEM] * 4,
+        in_specs=[SMEM] * 3 + [ANY] * len(units),
         out_specs=SMEM,
+        scratch_shapes=[pltpu.VMEM((count, 16, 128), BF16), pltpu.SemaphoreType.DMA((count,))],
+        compiler_params=vmem_limit(4),
+        cost_estimate=pl.CostEstimate(flops=10**6, bytes_accessed=2**10, transcendentals=0),
         name="plan",
-    )(left, right, keep_out, other)
+    )(right, keep_out, other, *units)
 
 
 def product_kernel(n_a, n_b, shape, cols_out, begun, *refs):
@@ -313,8 +332,8 @@
     tile_rows, tile_cols = flags.shape
     row_ids = lax.axis_index("row") * tile_rows + jnp.arange(tile_rows, dtype=I32)
     col_ids = lax.axis_index("col") * tile_cols + jnp.arange(tile_cols, dtype=I32)
-    diagonal = (row_ids[:, None] == col_ids[None, :]).astype(I32)
-    return jnp.maximum(flags, diagonal)
+    diagonal = (col_ids[:, None] == row_ids[None, :]).astype(I32)
+    return jnp.maximum(flags.T, diagonal)
 
 
 def shards(entries, pattern, prune):
@@ -326,40 +345,32 @@
 
     keep = tile_keep(pattern)
     keep_out = tile_keep(prune)
-    keep_f = keep.astype(F32)
     masked, sums = mask(keep, entries)
 
-    left = lax.dynamic_update_slice(jnp.zeros((rows, grid), F32), keep_f, (0, col * cols)).reshape(-1)
-    left = turn_sum(left, X_TURNS)
-    left = left + move(left, SWAP_YL)
-
-    flags = lax.dynamic_update_slice(jnp.zeros((grid, cols), F32), keep_f, (row * rows, 0))
+    flags = lax.dynamic_update_slice(jnp.zeros((cols, grid), F32), keep.astype(F32), (0, row * rows))
     sums = jnp.concatenate([sums[0], flags.reshape(-1)])
     sums = row_sum(sums)
     colsum, right = sums[:width], sums[width:]
     a = (masked / colsum[None, :]).astype(BF16)
-    a, left = lax.optimization_barrier((a, left))
 
     half = height // 2
     mine = lax.dynamic_slice(a, (c * half, 0), (half, width))
     theirs = lax.dynamic_slice(a, ((1 - c) * half, 0), (half, width))
     b = jnp.concatenate([mine, move(theirs, SWAP_CORE)], axis=1)
-    notes = jnp.concatenate([left, right, keep_out.astype(F32).reshape(-1)])
+    kept = keep_out.astype(F32).reshape(-1)
+    notes = jnp.concatenate([right, kept])
     notes_o = move(notes, SWAP_CORE)
 
     xl, xr, pa = move(a, X_UP), move(a, X_DOWN), move(a, SWAP_YL)
     zl, zr = move(b, Z_UP), move(b, Z_DOWN)
-    a, b, xl, xr, pa, zl, zr = lax.optimization_barrier((a, b, xl, xr, pa, zl, zr))
-    pxl, pxr = move(pa, X_UP), move(pa, X_DOWN)
-    zf, pb = move(zl, Z_UP), move(b, SWAP_YH)
-    a, b, xl, xr, pa, zl, zr, pxl, pxr, zf, pb, notes_o, left, right = lax.optimization_barrier(
-        (a, b, xl, xr, pa, zl, zr, pxl, pxr, zf, pb, notes_o, left, right)
-    )
-    xf, pxf = move(xl, X_UP), move(pxr, X_DOWN)
-    pzl, pzr, pzf = move(pb, Z_UP), move(pb, Z_DOWN), move(zf, SWAP_YH)
-
-    plan = planned(rows, cols, left, right, keep_out.astype(F32).reshape(-1), notes_o)
+    pxl, pxr = move(after(pa, xl), X_UP), move(after(pa, xr), X_DOWN)
+    zf, pb = move(zl, Z_UP), move(after(b, pa, zr), SWAP_YH)
+    xf, pxf = move(after(xl, pxl), X_UP), move(pxr, X_DOWN)
+    pzl, pzr, pzf = move(after(pb, zf), Z_UP), move(pb, Z_DOWN), move(after(zf, pb), SWAP_YH)
+    notes_o, right = after(notes_o, pxl, pxr, pb), after(right, pxl, pxr, pb)
+
     a_units = [a, xl, xr, pa, pxl, pxr, xf, pxf]
+    plan = planned(rows, cols, right, kept, notes_o, a_units[:6])
     b_units = [b, zl, zr, zf, pb, pzl, pzr, pzf]
     wide = NC * cols
     mine, theirs = product(plan, a_units[:6], b_units[:5], rows, wide, tuple(range(wide)))

time: 136 us -> 131 us (0.963)
  local copies, waits for them, and re-layouts: 9.91 us -> 4.14 us
    unnamed x30 -> x12, local copies, waits for them, and re-layouts: 9.48 us -> 3.79 us
    ppermute x29 -> x25, starting transfers between devices: 40.2 us -> 39.3 us  [move(): return lax.ppermute(value, AXES, perm)]
    ppermute x29 -> x25, waiting for transfers between devices: 65 us -> 65 us  [move(): return lax.ppermute(value, AXES, perm)]
  transfers between devices with their start and end apart: 29 -> 25, of which waited for: 19 -> 15; matrix products, arithmetic and copies ran while one was open for 0% -> 0% of each run, Pallas kernels for 10% -> 10%
where the time goes in v4:
time: 131 us; the launch traced here: 130 us
  waiting for transfers between devices  65 us (50%)
  starting transfers between devices  39.3 us (30%)
  Pallas kernels  20.3 us (15%)
  local copies, waits for them, and re-layouts  4.14 us (3%)
    ppermute x25, waiting for transfers between devices, move(): return lax.ppermute(value, AXES, perm)  65 us
    ppermute x25, starting transfers between devices, move(): return lax.ppermute(value, AXES, perm)  39.3 us
    pallas_call x3, Pallas kernels, product(): pl.pallas_call(functools.partial(product_kernel, len(a_units), len(b_unit...  15.2 us
    unnamed x12, local copies, waits for them, and re-layouts  3.79 us
    pallas_call x1, Pallas kernels, planned(): pl.pallas_call(functools.partial(plan_kernel, rows, cols), out_shape=jax....  2.62 us
  transfers between devices with their start and end apart: 25, of which 15 were waited for; matrix products, arithmetic and copies ran while one was open for 0% of the time, Pallas kernels for 10%

profile of v4, /device:TPU:0, one launch (start us, length us, event | category | flops | bytes accessed | tf_op | source)
XLA Modules:
  0.0 130.1 jit_solution(10296592342081646535)
XLA Ops:
  0.0 0.8 fusion.3
  0.8 0.1 dynamic_update_slice.3
  0.9 0.1 reshape.15
  1.0 1.6 %copy-done.5 = f32[1024,512]{1,0:T(8,128)S(1)} copy-done((f32[1024,512]{1,0:T(8,128)S(1)}, f32[1024,512]{1,0:T(8,128)}, u32[]{:S(2)}) %copy-start.5) | copy-done | bytes 2097176
  2.6 0.7 mask.1
  3.3 4.3 %collective-permute-start.2 = (f32[576]{0:T(1024)S(1)}, f32[576]{0:T(1024)S(1)}, u32[]{:S(2)}, u32[]{:S(2)}) collective-permute-start(f32[576]{0:T(1024)S(1)} %pad_maximum_fusion.1), channel_id=1, source_target_pairs={{0,48},{1,49},{2,50},{3,51},{4,52},{5,53},{6,54},{7,55},{8,56},{9,... | collective-permute-start | bytes 6920 | tf_op jit(solution)/shard_map/ppermute | solution.py:43
  7.6 0.0 collective-permute-start.1
  7.6 1.3 collective-permute-start
  8.9 0.1 collective-permute-done.2
  9.0 3.8 %collective-permute-done.1 = f32[576]{0:T(1024)S(1)} collective-permute-done((f32[576]{0:T(1024)S(1)}, f32[576]{0:T(1024)S(1)}, u32[]{:S(2)}, u32[]{:S(2)}) %collective-permute-start.1) | collective-permute-done | bytes 2336 | tf_op jit(solution)/shard_map/ppermute | solution.py:43
  12.7 0.0 collective-permute-done
  12.8 3.3 %collective-permute-start.3 = (f32[576]{0:T(1024)S(1)}, f32[576]{0:T(1024)S(1)}, u32[]{:S(2)}, u32[]{:S(2)}) collective-permute-start(f32[576]{0:T(1024)S(1)} %add_add_fusion), channel_id=1, source_target_pairs={{0,64},{1,65},{2,66},{3,67},{4,68},{5,69},{6,70},{7,71},{8,72},{9,... | collective-permute-start | bytes 6920 | tf_op jit(solution)/shard_map/ppermute | solution.py:43
  16.0 1.9 %collective-permute-done.3 = f32[576]{0:T(1024)S(1)} collective-permute-done((f32[576]{0:T(1024)S(1)}, f32[576]{0:T(1024)S(1)}, u32[]{:S(2)}, u32[]{:S(2)}) %collective-permute-start.3) | collective-permute-done | bytes 2336 | tf_op jit(solution)/shard_map/ppermute | solution.py:43
  18.0 0.3 divide_convert_fusion.refs_0_.refs_1_.refs_2_
  18.2 0.1 constant_dynamic-slice_fusion.1
  18.3 0.1 collective-permute-start.9
  18.4 2.8 %collective-permute-start.7 = (bf16[1024,512]{1,0:T(8,128)(2,1)S(1)}, bf16[1024,512]{1,0:T(8,128)(2,1)S(1)}, u32[]{:S(2)}, u32[]{:S(2)}) collective-permute-start(bf16[1024,512]{1,0:T(8,128)(2,1)S(1)} %divide_convert_fusion.refs_0_.refs_1_.refs_2_), channel_id=1, source_target_pairs={{0,6},{1,7},{2,0},{3,1},{4,2},{5,3},{6,4},{7,5},{8,14},{9,15},{10,... | collective-permute-start | bytes 3145736 | tf_op jit(solution)/shard_map/ppermute | solution.py:43
  21.2 0.0 collective-permute-start.5
  21.2 1.6 %collective-permute-start.4 = (bf16[1024,512]{1,0:T(8,128)(2,1)S(1)}, bf16[1024,512]{1,0:T(8,128)(2,1)}, u32[]{:S(2)}, u32[]{:S(2)}) collective-permute-start(bf16[1024,512]{1,0:T(8,128)(2,1)S(1)} %divide_convert_fusion.refs_0_.refs_1_.refs_2_), channel_id=1, source_target_pairs={{0,8},{1,9},{2,10},{3,11},{4,12},{5,13},{6,14},{7,15},{8,0},{9,1},... | collective-permute-start | bytes 3145736 | tf_op jit(solution)/shard_map/ppermute | solution.py:43
  22.8 0.0 collective-permute-done.9
  22.8 0.1 pad_maximum_fusion.refs_7_.refs_10_
  23.0 0.6 collective-permute-start.10
  23.6 1.5 %collective-permute-start.13 = (bf16[512,1024]{1,0:T(8,128)(2,1)S(1)}, bf16[512,1024]{1,0:T(8,128)(2,1)}, u32[]{:S(2)}, u32[]{:S(2)}) collective-permute-start(bf16[512,1024]{1,0:T(8,128)(2,1)S(1)} %pad_maximum_fusion.refs_7_.refs_10_), channel_id=1, source_target_pairs={{0,16},{1,17},{2,18},{3,19},{4,20},{5,21},{6,22},{7,23},{8,24},{9,... | collective-permute-start | bytes 3145736 | tf_op jit(solution)/shard_map/ppermute | solution.py:43
  25.0 19.2 %collective-permute-done.7.refs_2_.refs_3_.refs_4_ = bf16[1024,512]{1,0:T(8,128)(2,1)S(1)} collective-permute-done((bf16[1024,512]{1,0:T(8,128)(2,1)S(1)}, bf16[1024,512]{1,0:T(8,128)(2,1)S(1)}, u32[]{:S(2)}, u32[]{:S(2)}) %collective-permute-start.7) | collective-permute-done | bytes 1048608 | tf_op jit(solution)/shard_map/ppermute | solution.py:43
  44.3 2.3 %collective-permute-done.4.refs_3_.refs_4_.refs_5_ = bf16[1024,512]{1,0:T(8,128)(2,1)} collective-permute-done((bf16[1024,512]{1,0:T(8,128)(2,1)S(1)}, bf16[1024,512]{1,0:T(8,128)(2,1)}, u32[]{:S(2)}, u32[]{:S(2)}) %collective-permute-start.4) | collective-permute-done | bytes 1048608 | tf_op jit(solution)/shard_map/ppermute | solution.py:43
  46.6 1.1 collective-permute-done.5.refs_1_.refs_2_.refs_3_
  47.7 0.0 collective-permute-start.6
  47.7 3.2 %collective-permute-start.8 = (bf16[1024,512]{1,0:T(8,128)(2,1)}, bf16[1024,512]{1,0:T(8,128)(2,1)}, u32[]{:S(2)}, u32[]{:S(2)}) collective-permute-start(bf16[1024,512]{1,0:T(8,128)(2,1)} %collective-permute-done.4.refs_3_.refs_4_.refs_5_), channel_id=1, source_target_pairs={{0,6},{1,7},{2,0},{3,1},{4,2},{5,3},{6,4},{7,5},{8,14},{9,15},{10,... | collective-permute-start | bytes 3145736 | tf_op jit(solution)/shard_map/ppermute | solution.py:43
  50.9 0.0 collective-permute-done.10.refs_9_.refs_12_
  50.9 1.0 copy-done.3
  51.9 0.0 collective-permute-done.13.refs_8_.refs_11_
  51.9 3.3 %collective-permute-start.11 = (bf16[512,1024]{1,0:T(8,128)(2,1)S(1)}, bf16[512,1024]{1,0:T(8,128)(2,1)}, u32[]{:S(2)}, u32[]{:S(2)}) collective-permute-start(bf16[512,1024]{1,0:T(8,128)(2,1)S(1)} %pad_maximum_fusion.refs_7_.refs_10_), channel_id=1, source_target_pairs={{0,64},{1,65},{2,66},{3,67},{4,68},{5,69},{6,70},{7,71},{8,72},{9,... | collective-permute-start | bytes 3145736 | tf_op jit(solution)/shard_map/ppermute | solution.py:43
  55.2 0.1 reshape.16.out_ref
  55.3 0.1 pad_maximum_fusion.2
  55.3 0.0 collective-permute-start.12
  55.4 18.3 %collective-permute-done.6.refs_4_.refs_5_.refs_6_ = bf16[1024,512]{1,0:T(8,128)(2,1)} collective-permute-done((bf16[1024,512]{1,0:T(8,128)(2,1)}, bf16[1024,512]{1,0:T(8,128)(2,1)}, u32[]{:S(2)}, u32[]{:S(2)}) %collective-permute-start.6) | collective-permute-done | bytes 1048608 | tf_op jit(solution)/shard_map/ppermute | solution.py:43
  73.7 3.2 %collective-permute-start.16 = (bf16[1024,512]{1,0:T(8,128)(2,1)}, bf16[1024,512]{1,0:T(8,128)(2,1)S(1)}, u32[]{:S(2)}, u32[]{:S(2)}) collective-permute-start(bf16[1024,512]{1,0:T(8,128)(2,1)} %collective-permute-done.8.refs_5_.refs_6_.refs_7_), channel_id=1, source_target_pairs={{0,6},{1,7},{2,0},{3,1},{4,2},{5,3},{6,4},{7,5},{8,14},{9,15},{10,... | collective-permute-start | bytes 3145736 | tf_op jit(solution)/shard_map/ppermute | solution.py:43
  77.0 0.4 collective-permute-done.14.refs_10_.refs_13_
  77.4 0.2 collective-permute-done.11.refs_11_.refs_14_
  77.5 1.4 %collective-permute-start.17 = (bf16[512,1024]{1,0:T(8,128)(2,1)}, bf16[512,1024]{1,0:T(8,128)(2,1)S(1)}, u32[]{:S(2)}, u32[]{:S(2)}) collective-permute-start(bf16[512,1024]{1,0:T(8,128)(2,1)} %collective-permute-done.11.refs_11_.refs_14_), channel_id=1, source_target_pairs={{0,16},{1,17},{2,18},{3,19},{4,20},{5,21},{6,22},{7,23},{8,24},{9,... | collective-permute-start | bytes 3145736 | tf_op jit(solution)/shard_map/ppermute | solution.py:43
  79.0 3.2 %collective-permute-start.19 = (bf16[512,1024]{1,0:T(8,128)(2,1)}, bf16[512,1024]{1,0:T(8,128)(2,1)S(1)}, u32[]{:S(2)}, u32[]{:S(2)}) collective-permute-start(bf16[512,1024]{1,0:T(8,128)(2,1)} %collective-permute-done.14.refs_10_.refs_13_), channel_id=1, source_target_pairs={{0,64},{1,65},{2,66},{3,67},{4,68},{5,69},{6,70},{7,71},{8,72},{9,... | collective-permute-start | bytes 3145736 | tf_op jit(solution)/shard_map/ppermute | solution.py:43
  82.2 0.0 collective-permute-done.12.other_ref
  82.2 1.8 %collective-permute-start.18 = (bf16[512,1024]{1,0:T(8,128)(2,1)}, bf16[512,1024]{1,0:T(8,128)(2,1)S(1)}, u32[]{:S(2)}, u32[]{:S(2)}) collective-permute-start(bf16[512,1024]{1,0:T(8,128)(2,1)} %collective-permute-done.11.refs_11_.refs_14_), channel_id=1, source_target_pairs={{0,48},{1,49},{2,50},{3,51},{4,52},{5,53},{6,54},{7,55},{8,56},{9,... | collective-permute-start | bytes 3145736 | tf_op jit(solution)/shard_map/ppermute | solution.py:43
  84.0 1.2 copy-done.1
  85.2 2.6 %plan.1.refs_0_ = s32[48]{0:T(128)S(1)} custom-call(f32[64]{0:T(128)S(1)} %slice.6.right_ref, f32[8]{0:T(128)S(1)} %reshape.16.out_ref, f32[72]{0:T(128)S(1)} %collective-permute-done.12.other_ref, bf16[1024,512]{1,0:T(8,128)(2,1)S(1)} %divide_convert_fusion.refs_0_.refs_1_.refs_2_, bf16[1024,512]{1,0:T(8,128)(2,1)S(1)} %copy-done.1, ...), custom_call_target="tpu_custom_call" | custom-call | flops 1000000 | bytes 1024 | tf_op jit(solution)/shard_map/plan/pallas_call | solution.py:212
  87.8 6.2 %begin.1 = (f32[1024,512]{1,0:T(8,128)S(1)}, f32[1024,512]{1,0:T(8,128)S(1)}) custom-call(s32[48]{0:T(128)S(1)} %plan.1.refs_0_, bf16[1024,512]{1,0:T(8,128)(2,1)S(1)} %divide_convert_fusion.refs_0_.refs_1_.refs_2_, bf16[1024,512]{1,0:T(8,128)(2,1)S(1)} %copy-done.2, bf16[1024,512]{1,0:T(8,128)(2,1)S(1)} %collective-permute-done.7.refs_2_.refs_3_.refs_4_, ...), custom_call_target="tpu_custom_call" | custom-call | flops 1000000 | bytes 1024 | tf_op jit(solution)/shard_map/begin/pallas_call | solution.py:312
  94.1 4.6 %collective-permute-done.15.refs_8_ = bf16[1024,512]{1,0:T(8,128)(2,1)S(1)} collective-permute-done((bf16[1024,512]{1,0:T(8,128)(2,1)}, bf16[1024,512]{1,0:T(8,128)(2,1)S(1)}, u32[]{:S(2)}, u32[]{:S(2)}) %collective-permute-start.15) | collective-permute-done | bytes 1048608 | tf_op jit(solution)/shard_map/ppermute | solution.py:43
  98.7 0.0 collective-permute-done.16.refs_9_
  98.7 3.3 %collective-permute-done.17.refs_15_ = bf16[512,1024]{1,0:T(8,128)(2,1)S(1)} collective-permute-done((bf16[512,1024]{1,0:T(8,128)(2,1)}, bf16[512,1024]{1,0:T(8,128)(2,1)S(1)}, u32[]{:S(2)}, u32[]{:S(2)}) %collective-permute-start.17) | collective-permute-done | bytes 1048608 | tf_op jit(solution)/shard_map/ppermute | solution.py:43
  102.0 1.1 collective-permute-done.19.refs_17_
  103.0 1.4 %collective-permute-done.18.refs_16_ = bf16[512,1024]{1,0:T(8,128)(2,1)S(1)} collective-permute-done((bf16[512,1024]{1,0:T(8,128)(2,1)}, bf16[512,1024]{1,0:T(8,128)(2,1)S(1)}, u32[]{:S(2)}, u32[]{:S(2)}) %collective-permute-start.18) | collective-permute-done | bytes 1048608 | tf_op jit(solution)/shard_map/ppermute | solution.py:43
  104.4 4.4 %finish.3 = f32[1024,512]{1,0:T(8,128)S(1)} custom-call(s32[48]{0:T(128)S(1)} %plan.1.refs_0_, f32[1024,512]{1,0:T(8,128)S(1)} %get-tuple-element.30.refs_1_, bf16[1024,512]{1,0:T(8,128)(2,1)S(1)} %divide_convert_fusion.refs_0_.refs_1_.refs_2_, bf16[1024,512]{1,0:T(8,128)(2,1)S(1)} %copy-done.2, ...), custom_call_target="tpu_custom_call" | custom-call | flops 1000000 | bytes 1024 | tf_op jit(solution)/shard_map/finish/pallas_call | solution.py:312
  108.8 0.1 collective-permute-start.20
  108.9 4.6 %finish.2.mine_ref = f32[1024,512]{1,0:T(8,128)S(1)} custom-call(s32[48]{0:T(128)S(1)} %plan.1.refs_0_, f32[1024,512]{1,0:T(8,128)S(1)} %get-tuple-element.26.refs_1_, bf16[1024,512]{1,0:T(8,128)(2,1)S(1)} %divide_convert_fusion.refs_0_.refs_1_.refs_2_, bf16[1024,512]{1,0:T(8,128)(2,1)S(1)} %copy-done.2, ...), custom_call_target="tpu_custom_call" | custom-call | flops 1000000 | bytes 1024 | tf_op jit(solution)/shard_map/finish/pallas_call | solution.py:312
  113.5 0.2 square.1
  113.8 4.6 %collective-permute-start.23 = (f32[512]{0:T(512)S(1)}, f32[512]{0:T(512)S(1)}, u32[]{:S(2)}, u32[]{:S(2)}) collective-permute-start(f32[512]{0:T(512)S(1)} %bitcast.11), channel_id=1, source_target_pairs={{0,48},{1,49},{2,50},{3,51},{4,52},{5,53},{6,54},{7,55},{8,56},{9,... | collective-permute-start | bytes 6152 | tf_op jit(solution)/shard_map/ppermute | solution.py:43
  118.4 0.0 collective-permute-start.22
  118.4 1.3 collective-permute-start.21
  119.6 0.0 collective-permute-done.23
  119.7 3.8 %collective-permute-done.22 = f32[512]{0:T(512)S(1)} collective-permute-done((f32[512]{0:T(512)S(1)}, f32[512]{0:T(512)S(1)}, u32[]{:S(2)}, u32[]{:S(2)}) %collective-permute-start.22) | collective-permute-done | bytes 2080 | tf_op jit(solution)/shard_map/ppermute | solution.py:43
  123.5 0.0 collective-permute-done.21
  123.5 1.7 %collective-permute-start.24 = (f32[512]{0:T(512)S(1)}, f32[512]{0:T(512)S(1)}, u32[]{:S(2)}, u32[]{:S(2)}) collective-permute-start(f32[512]{0:T(512)S(1)} %add_add_fusion.1), channel_id=1, source_target_pairs={{0,64},{1,65},{2,66},{3,67},{4,68},{5,69},{6,70},{7,71},{8,72},{9,... | collective-permute-start | bytes 6152 | tf_op jit(solution)/shard_map/ppermute | solution.py:43
  125.2 3.4 %collective-permute-done.24 = f32[512]{0:T(512)S(1)} collective-permute-done((f32[512]{0:T(512)S(1)}, f32[512]{0:T(512)S(1)}, u32[]{:S(2)}, u32[]{:S(2)}) %collective-permute-start.24) | collective-permute-done | bytes 2080 | tf_op jit(solution)/shard_map/ppermute | solution.py:43
  128.7 1.5 %rescale.1 = f32[1024,512]{1,0:T(8,128)} custom-call(f32[1024,512]{1,0:T(8,128)S(1)} %get-tuple-element.31.value_ref, f32[1,512]{1,0:T(1,128)S(1)} %bitcast.8), custom_call_target="tpu_custom_call" | custom-call | tf_op jit(solution)/shard_map/rescale/pallas_call | solution.py:131
  (23 shorter events, 0.1 us)
Async XLA Ops:
  1.0 1.6 %copy-start.5 = (f32[1024,512]{1,0:T(8,128)S(1)}, f32[1024,512]{1,0:T(8,128)}, u32[]{:S(2)}) copy-start(f32[1024,512]{1,0:T(8,128)} %entries_ref.1) | copy-start | bytes 6291460
  3.3 5.6 %collective-permute-start.2 = (f32[576]{0:T(1024)S(1)}, f32[576]{0:T(1024)S(1)}, u32[]{:S(2)}, u32[]{:S(2)}) collective-permute-start(f32[576]{0:T(1024)S(1)} %pad_maximum_fusion.1), channel_id=1, source_target_pairs={{0,48},{1,49},{2,50},{3,51},{4,52},{5,53},{6,54},{7,55},{8,56},{9,... | collective-permute-start | bytes 6920 | tf_op jit(solution)/shard_map/ppermute | solution.py:43
  7.6 5.1 %collective-permute-start.1 = (f32[576]{0:T(1024)S(1)}, f32[576]{0:T(1024)S(1)}, u32[]{:S(2)}, u32[]{:S(2)}) collective-permute-start(f32[576]{0:T(1024)S(1)} %pad_maximum_fusion.1), channel_id=1, source_target_pairs={{0,32},{1,33},{2,34},{3,35},{4,36},{5,37},{6,38},{7,39},{8,40},{9,... | collective-permute-start | bytes 6920 | tf_op jit(solution)/shard_map/ppermute | solution.py:43
  7.6 5.1 %collective-permute-start = (f32[576]{0:T(1024)S(1)}, f32[576]{0:T(1024)S(1)}, u32[]{:S(2)}, u32[]{:S(2)}) collective-permute-start(f32[576]{0:T(1024)S(1)} %pad_maximum_fusion.1), channel_id=1, source_target_pairs={{0,16},{1,17},{2,18},{3,19},{4,20},{5,21},{6,22},{7,23},{8,24},{9,... | collective-permute-start | bytes 6920 | tf_op jit(solution)/shard_map/ppermute | solution.py:43
  12.8 5.2 %collective-permute-start.3 = (f32[576]{0:T(1024)S(1)}, f32[576]{0:T(1024)S(1)}, u32[]{:S(2)}, u32[]{:S(2)}) collective-permute-start(f32[576]{0:T(1024)S(1)} %add_add_fusion), channel_id=1, source_target_pairs={{0,64},{1,65},{2,66},{3,67},{4,68},{5,69},{6,70},{7,71},{8,72},{9,... | collective-permute-start | bytes 6920 | tf_op jit(solution)/shard_map/ppermute | solution.py:43
  18.3 4.5 %collective-permute-start.9 = (bf16[512,512]{1,0:T(8,128)(2,1)S(1)}, bf16[512,512]{1,0:T(8,128)(2,1)S(1)}, u32[]{:S(2)}, u32[]{:S(2)}) collective-permute-start(bf16[512,512]{1,0:T(8,128)(2,1)S(1)} %get-tuple-element.36), channel_id=1, source_target_pairs={{0,1},{1,0},{2,3},{3,2},{4,5},{5,4},{6,7},{7,6},{8,9},{9,8},{10,11... | collective-permute-start | bytes 1572872 | tf_op jit(solution)/shard_map/ppermute | solution.py:43
  18.4 25.9 %collective-permute-start.7 = (bf16[1024,512]{1,0:T(8,128)(2,1)S(1)}, bf16[1024,512]{1,0:T(8,128)(2,1)S(1)}, u32[]{:S(2)}, u32[]{:S(2)}) collective-permute-start(bf16[1024,512]{1,0:T(8,128)(2,1)S(1)} %divide_convert_fusion.refs_0_.refs_1_.refs_2_), channel_id=1, source_target_pairs={{0,6},{1,7},{2,0},{3,1},{4,2},{5,3},{6,4},{7,5},{8,14},{9,15},{10,... | collective-permute-start | bytes 3145736 | tf_op jit(solution)/shard_map/ppermute | solution.py:43
  21.2 26.4 %collective-permute-start.5 = (bf16[1024,512]{1,0:T(8,128)(2,1)S(1)}, bf16[1024,512]{1,0:T(8,128)(2,1)S(1)}, u32[]{:S(2)}, u32[]{:S(2)}) collective-permute-start(bf16[1024,512]{1,0:T(8,128)(2,1)S(1)} %divide_convert_fusion.refs_0_.refs_1_.refs_2_), channel_id=1, source_target_pairs={{0,2},{1,3},{2,4},{3,5},{4,6},{5,7},{6,0},{7,1},{8,10},{9,11},{10,... | collective-permute-start | bytes 3145736 | tf_op jit(solution)/shard_map/ppermute | solution.py:43
  21.2 25.3 %collective-permute-start.4 = (bf16[1024,512]{1,0:T(8,128)(2,1)S(1)}, bf16[1024,512]{1,0:T(8,128)(2,1)}, u32[]{:S(2)}, u32[]{:S(2)}) collective-permute-start(bf16[1024,512]{1,0:T(8,128)(2,1)S(1)} %divide_convert_fusion.refs_0_.refs_1_.refs_2_), channel_id=1, source_target_pairs={{0,8},{1,9},{2,10},{3,11},{4,12},{5,13},{6,14},{7,15},{8,0},{9,1},... | collective-permute-start | bytes 3145736 | tf_op jit(solution)/shard_map/ppermute | solution.py:43
  23.0 28.0 %collective-permute-start.10 = (bf16[512,1024]{1,0:T(8,128)(2,1)S(1)}, bf16[512,1024]{1,0:T(8,128)(2,1)S(1)}, u32[]{:S(2)}, u32[]{:S(2)}) collective-permute-start(bf16[512,1024]{1,0:T(8,128)(2,1)S(1)} %pad_maximum_fusion.refs_7_.refs_10_), channel_id=1, source_target_pairs={{0,48},{1,49},{2,50},{3,51},{4,52},{5,53},{6,54},{7,55},{8,56},{9,... | collective-permute-start | bytes 3145736 | tf_op jit(solution)/shard_map/ppermute | solution.py:43
  23.6 28.3 %collective-permute-start.13 = (bf16[512,1024]{1,0:T(8,128)(2,1)S(1)}, bf16[512,1024]{1,0:T(8,128)(2,1)}, u32[]{:S(2)}, u32[]{:S(2)}) collective-permute-start(bf16[512,1024]{1,0:T(8,128)(2,1)S(1)} %pad_maximum_fusion.refs_7_.refs_10_), channel_id=1, source_target_pairs={{0,16},{1,17},{2,18},{3,19},{4,20},{5,21},{6,22},{7,23},{8,24},{9,... | collective-permute-start | bytes 3145736 | tf_op jit(solution)/shard_map/ppermute | solution.py:43
  47.7 4.2 %copy-start = (bf16[1024,512]{1,0:T(8,128)(2,1)}, bf16[1024,512]{1,0:T(8,128)(2,1)S(1)}, u32[]{:S(2)}) copy-start(bf16[1024,512]{1,0:T(8,128)(2,1)S(1)} %collective-permute-done.5.refs_1_.refs_2_.refs_3_) | copy-start | bytes 3145732
  47.7 26.0 %collective-permute-start.6 = (bf16[1024,512]{1,0:T(8,128)(2,1)}, bf16[1024,512]{1,0:T(8,128)(2,1)}, u32[]{:S(2)}, u32[]{:S(2)}) collective-permute-start(bf16[1024,512]{1,0:T(8,128)(2,1)} %collective-permute-done.4.refs_3_.refs_4_.refs_5_), channel_id=1, source_target_pairs={{0,2},{1,3},{2,4},{3,5},{4,6},{5,7},{6,0},{7,1},{8,10},{9,11},{10,... | collective-permute-start | bytes 3145736 | tf_op jit(solution)/shard_map/ppermute | solution.py:43
  47.7 26.0 %collective-permute-start.8 = (bf16[1024,512]{1,0:T(8,128)(2,1)}, bf16[1024,512]{1,0:T(8,128)(2,1)}, u32[]{:S(2)}, u32[]{:S(2)}) collective-permute-start(bf16[1024,512]{1,0:T(8,128)(2,1)} %collective-permute-done.4.refs_3_.refs_4_.refs_5_), channel_id=1, source_target_pairs={{0,6},{1,7},{2,0},{3,1},{4,2},{5,3},{6,4},{7,5},{8,14},{9,15},{10,... | collective-permute-start | bytes 3145736 | tf_op jit(solution)/shard_map/ppermute | solution.py:43
  50.9 1.0 copy-start.3
  51.9 25.5 %collective-permute-start.14 = (bf16[512,1024]{1,0:T(8,128)(2,1)}, bf16[512,1024]{1,0:T(8,128)(2,1)}, u32[]{:S(2)}, u32[]{:S(2)}) collective-permute-start(bf16[512,1024]{1,0:T(8,128)(2,1)} %collective-permute-done.13.refs_8_.refs_11_), channel_id=1, source_target_pairs={{0,16},{1,17},{2,18},{3,19},{4,20},{5,21},{6,22},{7,23},{8,24},{9,... | collective-permute-start | bytes 3145736 | tf_op jit(solution)/shard_map/ppermute | solution.py:43
  51.9 25.6 %collective-permute-start.11 = (bf16[512,1024]{1,0:T(8,128)(2,1)S(1)}, bf16[512,1024]{1,0:T(8,128)(2,1)}, u32[]{:S(2)}, u32[]{:S(2)}) collective-permute-start(bf16[512,1024]{1,0:T(8,128)(2,1)S(1)} %pad_maximum_fusion.refs_7_.refs_10_), channel_id=1, source_target_pairs={{0,64},{1,65},{2,66},{3,67},{4,68},{5,69},{6,70},{7,71},{8,72},{9,... | collective-permute-start | bytes 3145736 | tf_op jit(solution)/shard_map/ppermute | solution.py:43
  55.3 26.8 %collective-permute-start.12 = (f32[72]{0:T(128)S(1)}, f32[72]{0:T(128)S(1)}, u32[]{:S(2)}, u32[]{:S(2)}) collective-permute-start(f32[72]{0:T(128)S(1)} %pad_maximum_fusion.2), channel_id=1, source_target_pairs={{0,1},{1,0},{2,3},{3,2},{4,5},{5,4},{6,7},{7,6},{8,9},{9,8},{10,11... | collective-permute-start | bytes 872 | tf_op jit(solution)/shard_map/ppermute | solution.py:43
  73.7 25.0 %collective-permute-start.15 = (bf16[1024,512]{1,0:T(8,128)(2,1)}, bf16[1024,512]{1,0:T(8,128)(2,1)S(1)}, u32[]{:S(2)}, u32[]{:S(2)}) collective-permute-start(bf16[1024,512]{1,0:T(8,128)(2,1)} %copy-done), channel_id=1, source_target_pairs={{0,2},{1,3},{2,4},{3,5},{4,6},{5,7},{6,0},{7,1},{8,10},{9,11},{10,... | collective-permute-start | bytes 3145736 | tf_op jit(solution)/shard_map/ppermute | solution.py:43
  73.7 25.0 %collective-permute-start.16 = (bf16[1024,512]{1,0:T(8,128)(2,1)}, bf16[1024,512]{1,0:T(8,128)(2,1)S(1)}, u32[]{:S(2)}, u32[]{:S(2)}) collective-permute-start(bf16[1024,512]{1,0:T(8,128)(2,1)} %collective-permute-done.8.refs_5_.refs_6_.refs_7_), channel_id=1, source_target_pairs={{0,6},{1,7},{2,0},{3,1},{4,2},{5,3},{6,4},{7,5},{8,14},{9,15},{10,... | collective-permute-start | bytes 3145736 | tf_op jit(solution)/shard_map/ppermute | solution.py:43
  77.5 24.4 %collective-permute-start.17 = (bf16[512,1024]{1,0:T(8,128)(2,1)}, bf16[512,1024]{1,0:T(8,128)(2,1)S(1)}, u32[]{:S(2)}, u32[]{:S(2)}) collective-permute-start(bf16[512,1024]{1,0:T(8,128)(2,1)} %collective-permute-done.11.refs_11_.refs_14_), channel_id=1, source_target_pairs={{0,16},{1,17},{2,18},{3,19},{4,20},{5,21},{6,22},{7,23},{8,24},{9,... | collective-permute-start | bytes 3145736 | tf_op jit(solution)/shard_map/ppermute | solution.py:43
  79.0 24.1 %collective-permute-start.19 = (bf16[512,1024]{1,0:T(8,128)(2,1)}, bf16[512,1024]{1,0:T(8,128)(2,1)S(1)}, u32[]{:S(2)}, u32[]{:S(2)}) collective-permute-start(bf16[512,1024]{1,0:T(8,128)(2,1)} %collective-permute-done.14.refs_10_.refs_13_), channel_id=1, source_target_pairs={{0,64},{1,65},{2,66},{3,67},{4,68},{5,69},{6,70},{7,71},{8,72},{9,... | collective-permute-start | bytes 3145736 | tf_op jit(solution)/shard_map/ppermute | solution.py:43
  82.2 22.3 %collective-permute-start.18 = (bf16[512,1024]{1,0:T(8,128)(2,1)}, bf16[512,1024]{1,0:T(8,128)(2,1)S(1)}, u32[]{:S(2)}, u32[]{:S(2)}) collective-permute-start(bf16[512,1024]{1,0:T(8,128)(2,1)} %collective-permute-done.11.refs_11_.refs_14_), channel_id=1, source_target_pairs={{0,48},{1,49},{2,50},{3,51},{4,52},{5,53},{6,54},{7,55},{8,56},{9,... | collective-permute-start | bytes 3145736 | tf_op jit(solution)/shard_map/ppermute | solution.py:43
  84.0 1.2 copy-start.1
  85.2 2.6 %copy-start.2 = (bf16[1024,512]{1,0:T(8,128)(2,1)S(1)}, bf16[1024,512]{1,0:T(8,128)(2,1)}, u32[]{:S(2)}) copy-start(bf16[1024,512]{1,0:T(8,128)(2,1)} %copy-done) | copy-start | bytes 3145732
  85.2 2.6 %copy-start.4 = (bf16[512,1024]{1,0:T(8,128)(2,1)S(1)}, bf16[512,1024]{1,0:T(8,128)(2,1)}, u32[]{:S(2)}) copy-start(bf16[512,1024]{1,0:T(8,128)(2,1)} %copy-done.3) | copy-start | bytes 3145732
  108.8 4.7 %collective-permute-start.20 = (f32[1024,512]{1,0:T(8,128)S(1)}, f32[1024,512]{1,0:T(8,128)S(1)}, u32[]{:S(2)}, u32[]{:S(2)}) collective-permute-start(f32[1024,512]{1,0:T(8,128)S(1)} %finish.3), channel_id=1, source_target_pairs={{0,1},{1,0},{2,3},{3,2},{4,5},{5,4},{6,7},{7,6},{8,9},{9,8},{10,11... | collective-permute-start | bytes 6291464 | tf_op jit(solution)/shard_map/ppermute | solution.py:43
  113.8 5.9 %collective-permute-start.23 = (f32[512]{0:T(512)S(1)}, f32[512]{0:T(512)S(1)}, u32[]{:S(2)}, u32[]{:S(2)}) collective-permute-start(f32[512]{0:T(512)S(1)} %bitcast.11), channel_id=1, source_target_pairs={{0,48},{1,49},{2,50},{3,51},{4,52},{5,53},{6,54},{7,55},{8,56},{9,... | collective-permute-start | bytes 6152 | tf_op jit(solution)/shard_map/ppermute | solution.py:43
  118.4 5.1 %collective-permute-start.22 = (f32[512]{0:T(512)S(1)}, f32[512]{0:T(512)S(1)}, u32[]{:S(2)}, u32[]{:S(2)}) collective-permute-start(f32[512]{0:T(512)S(1)} %bitcast.12), channel_id=1, source_target_pairs={{0,32},{1,33},{2,34},{3,35},{4,36},{5,37},{6,38},{7,39},{8,40},{9,... | collective-permute-start | bytes 6152 | tf_op jit(solution)/shard_map/ppermute | solution.py:43
  118.4 5.1 %collective-permute-start.21 = (f32[512]{0:T(512)S(1)}, f32[512]{0:T(512)S(1)}, u32[]{:S(2)}, u32[]{:S(2)}) collective-permute-start(f32[512]{0:T(512)S(1)} %bitcast.13), channel_id=1, source_target_pairs={{0,16},{1,17},{2,18},{3,19},{4,20},{5,21},{6,22},{7,23},{8,24},{9,... | collective-permute-start | bytes 6152 | tf_op jit(solution)/shard_map/ppermute | solution.py:43
  123.5 5.2 %collective-permute-start.24 = (f32[512]{0:T(512)S(1)}, f32[512]{0:T(512)S(1)}, u32[]{:S(2)}, u32[]{:S(2)}) collective-permute-start(f32[512]{0:T(512)S(1)} %add_add_fusion.1), channel_id=1, source_target_pairs={{0,64},{1,65},{2,66},{3,67},{4,68},{5,69},{6,70},{7,71},{8,72},{9,... | collective-permute-start | bytes 6152 | tf_op jit(solution)/shard_map/ppermute | solution.py:43

commit v5 on v4

--- a/solution.py
+++ b/solution.py
@@ -11,21 +11,21 @@
 F32 = jnp.float32
 BF16 = jnp.bfloat16
 I32 = jnp.int32
-GROUP = 2
+GROUP = 4
 
 
 def place(yh, z, yl, x, c):
     return (yh * NZ + z) * (YL * NX * NC) + (yl * NX + x) * NC + c
 
 
-def pairs(step):
+def pairs(step, cores=range(NC)):
     return [
         (place(yh, z, yl, x, c), place(*step(yh, z, yl, x, c)))
         for yh in range(YH)
         for z in range(NZ)
         for yl in range(YL)
         for x in range(NX)
-        for c in range(NC)
+        for c in cores
     ]
 
 
@@ -36,6 +36,10 @@
 SWAP_CORE = pairs(lambda yh, z, yl, x, c: (yh, z, yl, x, 1 - c))
 SWAP_YL = pairs(lambda yh, z, yl, x, c: (yh, z, 1 - yl, x, c))
 SWAP_YH = pairs(lambda yh, z, yl, x, c: (1 - yh, z, yl, x, c))
+FAR_1 = [
+    pairs(lambda yh, z, yl, x, c, dy=dy: (yh, z, (yl + dy) % YL, (x + 2) % NX, c), cores=(1,))
+    for dy in (0, 1)
+]
 Z_TURNS = [pairs(lambda yh, z, yl, x, c, d=d: (yh, (z + d) % NZ, yl, x, c)) for d in range(1, NZ)]
 
 
@@ -65,32 +69,64 @@
 ANY = pl.BlockSpec(memory_space=pl.ANY)
 
 
-def mask_kernel(keep_ref, entries_ref, masked_ref, sum_ref):
-    cols, rows = keep_ref.shape
+LANES = 128
+
+
+def mask_kernel(pattern_in, entries_in, masked_ref, message_ref, flags_ref, pattern_ref, entries_ref, sem):
+    cols, rows = pattern_ref.shape
     tall, wide = entries_ref.shape[0] // rows, entries_ref.shape[1] // cols
+    small = pltpu.make_async_copy(pattern_in, pattern_ref, sem.at[rows])
+    strips = [
+        pltpu.make_async_copy(
+            entries_in.at[pl.ds(i * tall, tall)], entries_ref.at[pl.ds(i * tall, tall)], sem.at[i]
+        )
+        for i in range(rows)
+    ]
+    for copy in [small] + strips:
+        copy.start()
+    row, col = lax.axis_index("row"), lax.axis_index("col")
+    grid = lax.axis_size("row") * rows
+    lane = lax.broadcasted_iota(I32, (1, LANES), 1)
+    column_flags = jnp.zeros((1, LANES), F32)
+    flags = jnp.zeros((1, LANES), F32)
+    totals = [jnp.zeros((1, wide), F32) for _ in range(cols)]
+    small.wait()
+    for i in range(rows):
+        strips[i].wait()
+        down = slice(i * tall, (i + 1) * tall)
+        for j in range(cols):
+            right = slice(j * wide, (j + 1) * wide)
+            diagonal = (row * rows + i == col * cols + j).astype(I32)
+            keep = jnp.maximum(pattern_ref[j, i], diagonal).astype(F32)
+            masked = entries_ref[down, right] * keep
+            masked_ref[down, right] = masked
+            totals[j] = totals[j] + jnp.sum(masked, axis=0, keepdims=True)
+            column_flags = jnp.where(lane == j * grid + row * rows + i, keep, column_flags)
+            flags = jnp.where(lane == j * rows + i, keep, flags)
     for j in range(cols):
-        right = slice(j * wide, (j + 1) * wide)
-        total = jnp.zeros((1, wide), F32)
-        for i in range(rows):
-            down = slice(i * tall, (i + 1) * tall)
-            masked = entries_ref[down, right] * keep_ref[j, i].astype(F32)
-            masked_ref[down, right] = masked
-            total = total + jnp.sum(masked, axis=0, keepdims=True)
-        sum_ref[:, right] = total
-
-
-def mask(keep, entries):
+        message_ref[:, j * wide:(j + 1) * wide] = totals[j]
+    message_ref[:, cols * wide:] = column_flags
+    flags_ref[...] = flags
+
+
+def mask(pattern, entries):
     return pl.pallas_call(
         mask_kernel,
         out_shape=(
             jax.ShapeDtypeStruct(entries.shape, F32),
-            jax.ShapeDtypeStruct((1, entries.shape[1]), F32),
+            jax.ShapeDtypeStruct((1, entries.shape[1] + LANES), F32),
+            jax.ShapeDtypeStruct((1, LANES), F32),
         ),
-        in_specs=[SMEM, VMEM],
-        out_specs=(VMEM, VMEM),
+        in_specs=[ANY] * 2,
+        out_specs=(VMEM, VMEM, VMEM),
+        scratch_shapes=[
+            pltpu.SMEM(pattern.shape[::-1], I32),
+            pltpu.VMEM(entries.shape, F32),
+            pltpu.SemaphoreType.DMA((pattern.shape[0] + 1,)),
+        ],
         compiler_params=vmem_limit(16),
         name="mask",
-    )(keep, entries)
+    )(pattern.T, entries)
 
 
 def square_kernel(mine_ref, got_ref, out_ref, sum_ref):
@@ -144,7 +180,7 @@
 A_LATE, B_LATE = (6, 7), (5, 6, 7)
 
 
-def plan_kernel(rows, cols, right_ref, out_ref, other_ref, *refs):
+def plan_kernel(rows, cols, far_ref, right_ref, out_ref, other_ref, *refs):
     units, (plan_ref, corner, sem) = refs[:-3], refs[-3:]
     row, col = lax.axis_index("row"), lax.axis_index("col")
     yh, z = row // NZ, row % NZ
@@ -152,6 +188,7 @@
     parts = YL * NX
     grid = parts * NC * cols
     n_right = grid * cols
+    n_other = n_right + rows * cols
     tall, wide = units[0].shape[0] // rows, units[0].shape[1] // cols
 
     copies = []
@@ -174,7 +211,17 @@
         plan_ref[PLAN_A + u] = base
         if u in A_LATE:
             late = late | lax.shift_left(jnp.int32(whole), base)
-            left = [m | lax.shift_left(jnp.int32(whole), base) for m in left]
+            first = (A_LATE.index(u) + len(FAR_1) - len(A_LATE)) * NC * rows * cols
+            for i in range(rows):
+                bits = jnp.int32(0)
+                for k in range(cols):
+                    if first < 0:
+                        bits = jnp.int32(whole)
+                    else:
+                        at = first + k * rows + i
+                        flag = jnp.where(c == 1, far_ref[at], other_ref[n_other + rows * cols + at])
+                        bits = bits + (flag > 0.5).astype(I32) * (1 << k)
+                left[i] = left[i] | lax.shift_left(bits, base)
     for u, (dy, dz) in enumerate(B_PLACES):
         base = ((yh + dy) % YH * NZ + (z + dz) % NZ) * cols
         plan_ref[PLAN_B + u] = base
@@ -207,28 +254,27 @@
         plan_ref[PLAN_LEFT + i] = m
 
 
-def planned(rows, cols, right, keep_out, other, units):
+def planned(rows, cols, far, right, keep_out, other, units):
     count = len(units) * rows * cols
     return pl.pallas_call(
         functools.partial(plan_kernel, rows, cols),
         out_shape=jax.ShapeDtypeStruct((PLAN_SIZE,), I32),
-        in_specs=[SMEM] * 3 + [ANY] * len(units),
+        in_specs=[SMEM] * 4 + [ANY] * len(units),
         out_specs=SMEM,
         scratch_shapes=[pltpu.VMEM((count, 16, 128), BF16), pltpu.SemaphoreType.DMA((count,))],
         compiler_params=vmem_limit(4),
         cost_estimate=pl.CostEstimate(flops=10**6, bytes_accessed=2**10, transcendentals=0),
         name="plan",
-    )(right, keep_out, other, *units)
+    )(far, right, keep_out, other, *units)
 
 
 def product_kernel(n_a, n_b, shape, cols_out, begun, *refs):
     rows, cols, grid, tile = shape
     plan, refs = refs[0], refs[1:]
-    if begun:
-        start_ref, refs = refs[0], refs[1:]
+    refs = refs[begun:]
     a_in, b_in, refs = refs[:n_a], refs[n_a:n_a + n_b], refs[n_a + n_b:]
     n_out = 1 if begun else 2
-    out_refs, (a_buf, b_buf, acc, order, a_sem, b_sem) = refs[:n_out], refs[n_out:]
+    out_refs, (a_buf, b_buf, order, a_sem, b_sem) = refs[:n_out], refs[n_out:]
     wide = len(cols_out)
     no_a, no_b = rows * grid, wide * grid
     deep = a_in[0].shape[1] // tile
@@ -248,22 +294,28 @@
     def each(act):
         for u in range(n_a):
             base = plan[PLAN_A + u]
-            for i in range(rows):
-                bits = lax.shift_right_logical(need_a[i], base)
-                for k in range(deep):
-                    @pl.when(bits & (1 << k) > 0)
-                    def _(u=u, i=i, k=k, base=base):
-                        slot = i * grid + base + k
-                        act(pltpu.make_async_copy(tile_at(a_in[u], i, k), a_buf.at[slot], a_sem.at[slot]))
+            bits = [lax.shift_right_logical(m, base) & ((1 << deep) - 1) for m in need_a]
+
+            @pl.when(functools.reduce(jnp.bitwise_or, bits) > 0)
+            def _(u=u, base=base, bits=bits):
+                for i in range(rows):
+                    for k in range(deep):
+                        @pl.when(bits[i] & (1 << k) > 0)
+                        def _(i=i, k=k):
+                            slot = i * grid + base + k
+                            act(pltpu.make_async_copy(tile_at(a_in[u], i, k), a_buf.at[slot], a_sem.at[slot]))
         for u in range(n_b):
             base = plan[PLAN_B + u]
-            for n, j in enumerate(cols_out):
-                bits = lax.shift_right_logical(need_b[n], base)
-                for k in range(deep):
-                    @pl.when(bits & (1 << k) > 0)
-                    def _(u=u, n=n, j=j, k=k, base=base):
-                        slot = n * grid + base + k
-                        act(pltpu.make_async_copy(tile_at(b_in[u], k, j), b_buf.at[slot], b_sem.at[slot]))
+            bits = [lax.shift_right_logical(m, base) & ((1 << deep) - 1) for m in need_b]
+
+            @pl.when(functools.reduce(jnp.bitwise_or, bits) > 0)
+            def _(u=u, base=base, bits=bits):
+                for n, j in enumerate(cols_out):
+                    for k in range(deep):
+                        @pl.when(bits[n] & (1 << k) > 0)
+                        def _(n=n, j=j, k=k):
+                            slot = n * grid + base + k
+                            act(pltpu.make_async_copy(tile_at(b_in[u], k, j), b_buf.at[slot], b_sem.at[slot]))
 
     each(lambda copy: copy.start())
     a_buf[no_a] = jnp.zeros((tile, tile), BF16)
@@ -286,9 +338,10 @@
         place = n % (wide // n_out)
         for i in range(rows):
             here = slice(i * tile, (i + 1) * tile), slice(place * tile, (place + 1) * tile)
-            acc[...] = start_ref[here] if begun else jnp.zeros_like(acc)
-
-            def step(m, _, i=i, n=n):
+            if not begun:
+                out_ref[here] = jnp.zeros((tile, tile), F32)
+
+            def step(m, _, i=i, n=n, here=here, out_ref=out_ref):
                 part = None
                 for g in range(GROUP):
                     k = order[(n * rows + i) * (grid + GROUP) + m * GROUP + g]
@@ -296,11 +349,10 @@
                     b_tile = b_buf[jnp.where(k < grid, n * grid + k, no_b)]
                     dot = jnp.dot(a_tile, b_tile, preferred_element_type=F32)
                     part = dot if part is None else part + dot
-                acc[...] += part
+                out_ref[here] += part
                 return 0
 
             lax.fori_loop(0, count[i, j], step, 0)
-            out_ref[here] = acc[...]
 
 
 def product(plan, a_units, b_units, rows, cols, cols_out, start=None):
@@ -317,49 +369,44 @@
         scratch_shapes=[
             pltpu.VMEM((rows * grid + 1, tile, tile), BF16),
             pltpu.VMEM((len(cols_out) * grid + 1, tile, tile), BF16),
-            pltpu.VMEM((tile, tile), F32),
             pltpu.SMEM((rows * len(cols_out) * (grid + GROUP),), I32),
             pltpu.SemaphoreType.DMA((rows * grid,)),
             pltpu.SemaphoreType.DMA((len(cols_out) * grid,)),
         ],
         compiler_params=vmem_limit(26),
         cost_estimate=pl.CostEstimate(flops=10**6, bytes_accessed=2**10, transcendentals=0),
+        input_output_aliases={1: 0} if begun else {},
         name="finish" if begun else "begin",
     )(plan, *([start] if begun else []), *a_units, *b_units)
 
 
-def tile_keep(flags):
-    tile_rows, tile_cols = flags.shape
-    row_ids = lax.axis_index("row") * tile_rows + jnp.arange(tile_rows, dtype=I32)
-    col_ids = lax.axis_index("col") * tile_cols + jnp.arange(tile_cols, dtype=I32)
-    diagonal = (col_ids[:, None] == row_ids[None, :]).astype(I32)
-    return jnp.maximum(flags.T, diagonal)
-
-
 def shards(entries, pattern, prune):
-    row, col = lax.axis_index("row"), lax.axis_index("col")
+    col = lax.axis_index("col")
     rows, cols = pattern.shape
     height, width = entries.shape
     grid = rows * lax.axis_size("row")
     c = col % NC
 
-    keep = tile_keep(pattern)
-    keep_out = tile_keep(prune)
-    masked, sums = mask(keep, entries)
-
-    flags = lax.dynamic_update_slice(jnp.zeros((cols, grid), F32), keep.astype(F32), (0, row * rows))
-    sums = jnp.concatenate([sums[0], flags.reshape(-1)])
-    sums = row_sum(sums)
-    colsum, right = sums[:width], sums[width:]
-    a = (masked / colsum[None, :]).astype(BF16)
+    masked, message, flags = mask(pattern, entries)
+    flags = flags[0, :rows * cols]
+    row_ids = lax.axis_index("row") * rows + jnp.arange(rows, dtype=I32)
+    col_ids = col * cols + jnp.arange(cols, dtype=I32)
+    diagonal = (col_ids[:, None] == row_ids[None, :]).astype(I32)
+    kept = jnp.maximum(prune.T, diagonal).astype(F32).reshape(-1)
+
+    message = row_sum(message)
+    colsum, right = message[:, :width], message[0, width:width + grid * cols]
+    a = (masked / colsum).astype(BF16)
 
     half = height // 2
     mine = lax.dynamic_slice(a, (c * half, 0), (half, width))
     theirs = lax.dynamic_slice(a, ((1 - c) * half, 0), (half, width))
     b = jnp.concatenate([mine, move(theirs, SWAP_CORE)], axis=1)
-    kept = keep_out.astype(F32).reshape(-1)
-    notes = jnp.concatenate([right, kept])
-    notes_o = move(notes, SWAP_CORE)
+
+    flags = after(jnp.concatenate([flags, move(flags, SWAP_CORE)]), b)
+    far = jnp.concatenate([move(flags, far) for far in FAR_1])
+    a, b, far = lax.optimization_barrier((a, b, far))
+    notes_o = move(jnp.concatenate([right, kept, far]), SWAP_CORE)
 
     xl, xr, pa = move(a, X_UP), move(a, X_DOWN), move(a, SWAP_YL)
     zl, zr = move(b, Z_UP), move(b, Z_DOWN)
@@ -367,10 +414,10 @@
     zf, pb = move(zl, Z_UP), move(after(b, pa, zr), SWAP_YH)
     xf, pxf = move(after(xl, pxl), X_UP), move(pxr, X_DOWN)
     pzl, pzr, pzf = move(after(pb, zf), Z_UP), move(pb, Z_DOWN), move(after(zf, pb), SWAP_YH)
-    notes_o, right = after(notes_o, pxl, pxr, pb), after(right, pxl, pxr, pb)
+    notes_o, far, right = after(notes_o, pxl, pxr, pb), after(far, pxl, pxr, pb), after(right, pxl, pxr, pb)
 
     a_units = [a, xl, xr, pa, pxl, pxr, xf, pxf]
-    plan = planned(rows, cols, right, kept, notes_o, a_units[:6])
+    plan = planned(rows, cols, far, right, kept, notes_o, a_units[:6])
     b_units = [b, zl, zr, zf, pb, pzl, pzr, pzf]
     wide = NC * cols
     mine, theirs = product(plan, a_units[:6], b_units[:5], rows, wide, tuple(range(wide)))
@@ -378,8 +425,8 @@
     got = move(theirs, SWAP_CORE)
     mine, = product(plan, a_units, b_units, rows, wide, tuple(range(cols)), mine)
     inflated, total = squared(mine, got)
-    total = row_sum(total[0])
-    return rescaled(float(height * lax.axis_size("row")), inflated, total[None, :])
+    total = row_sum(total)
+    return rescaled(float(height * lax.axis_size("row")), inflated, total)
 
 
 def solution(mesh):

time: 131 us -> 125 us (0.954)
  waiting for transfers between devices: 65 us -> 40.9 us
  starting transfers between devices: 39.3 us -> 57.7 us
  local copies, waits for them, and re-layouts: 4.14 us -> 5.61 us
    ppermute x25 -> x28, waiting for transfers between devices: 65 us -> 40.9 us  [move(): return lax.ppermute(value, AXES, perm)]
    ppermute x25 -> x28, starting transfers between devices: 39.3 us -> 57.7 us  [move(): return lax.ppermute(value, AXES, perm)]
    unnamed x12 -> x16, local copies, waits for them, and re-layouts: 3.79 us -> 5.44 us
  transfers between devices with their start and end apart: 25 -> 28, of which waited for: 15 -> 16; matrix products, arithmetic and copies ran while one was open for 0% -> 0% of each run, Pallas kernels for 10% -> 10%
where the time goes in v5:
time: 125 us
  starting transfers between devices  57.7 us (46%)
  waiting for transfers between devices  40.9 us (33%)
  Pallas kernels  19.6 us (16%)
  local copies, waits for them, and re-layouts  5.61 us (4%)
    ppermute x28, starting transfers between devices, move(): return lax.ppermute(value, AXES, perm)  57.7 us
    ppermute x28, waiting for transfers between devices, move(): return lax.ppermute(value, AXES, perm)  40.9 us
    pallas_call x3, Pallas kernels, product(): pl.pallas_call(functools.partial(product_kernel, len(a_units), len(b_unit...  14.2 us
    unnamed x16, local copies, waits for them, and re-layouts  5.44 us
    pallas_call x1, Pallas kernels, planned(): pl.pallas_call(functools.partial(plan_kernel, rows, cols), out_shape=jax....  2.64 us
  transfers between devices with their start and end apart: 28, of which 16 were waited for; matrix products, arithmetic and copies ran while one was open for 0% of the time, Pallas kernels for 10%

profile of v5, /device:TPU:0, one launch (start us, length us, event | category | flops | bytes accessed | tf_op | source)
XLA Modules:
  0.0 124.7 jit_solution(11256423621377279601)
XLA Ops:
  0.0 1.6 %copy-done.5 = f32[1024,512]{1,0:T(8,128)S(1)} copy-done((f32[1024,512]{1,0:T(8,128)S(1)}, f32[1024,512]{1,0:T(8,128)}, u32[]{:S(2)}) %copy-start.5) | copy-done | bytes 2097176
  1.6 0.7 copy-done.6
  2.3 0.9 mask.1
  3.2 4.2 %collective-permute-start.2 = (f32[1,640]{1,0:T(1,128)S(1)}, f32[1,640]{1,0:T(1,128)S(1)}, u32[]{:S(2)}, u32[]{:S(2)}) collective-permute-start(f32[1,640]{1,0:T(1,128)S(1)} %get-tuple-element.26), channel_id=1, source_target_pairs={{0,48},{1,49},{2,50},{3,51},{4,52},{5,53},{6,54},{7,55},{8,56},{9,... | collective-permute-start | bytes 7688 | tf_op jit(solution)/shard_map/ppermute | solution.py:47
  7.3 1.3 %collective-permute-start = (f32[1,640]{1,0:T(1,128)S(1)}, f32[1,640]{1,0:T(1,128)S(1)}, u32[]{:S(2)}, u32[]{:S(2)}) collective-permute-start(f32[1,640]{1,0:T(1,128)S(1)} %get-tuple-element.26), channel_id=1, source_target_pairs={{0,16},{1,17},{2,18},{3,19},{4,20},{5,21},{6,22},{7,23},{8,24},{9,... | collective-permute-start | bytes 7688 | tf_op jit(solution)/shard_map/ppermute | solution.py:47
  8.6 0.1 collective-permute-done.2
  8.7 3.8 %collective-permute-done.1 = f32[1,640]{1,0:T(1,128)S(1)} collective-permute-done((f32[1,640]{1,0:T(1,128)S(1)}, f32[1,640]{1,0:T(1,128)S(1)}, u32[]{:S(2)}, u32[]{:S(2)}) %collective-permute-start.1) | collective-permute-done | bytes 2592 | tf_op jit(solution)/shard_map/ppermute | solution.py:47
  12.5 3.3 %collective-permute-start.3 = (f32[1,640]{1,0:T(1,128)S(1)}, f32[1,640]{1,0:T(1,128)S(1)}, u32[]{:S(2)}, u32[]{:S(2)}) collective-permute-start(f32[1,640]{1,0:T(1,128)S(1)} %add_add_fusion), channel_id=1, source_target_pairs={{0,64},{1,65},{2,66},{3,67},{4,68},{5,69},{6,70},{7,71},{8,72},{9,... | collective-permute-start | bytes 7688 | tf_op jit(solution)/shard_map/ppermute | solution.py:47
  15.7 1.9 %collective-permute-done.3 = f32[1,640]{1,0:T(1,128)S(1)} collective-permute-done((f32[1,640]{1,0:T(1,128)S(1)}, f32[1,640]{1,0:T(1,128)S(1)}, u32[]{:S(2)}, u32[]{:S(2)}) %collective-permute-start.3) | collective-permute-done | bytes 2592 | tf_op jit(solution)/shard_map/ppermute | solution.py:47
  17.6 0.3 divide_convert_fusion.refs_0_.refs_1_.refs_2_
  17.9 0.0 copy-start.7
  17.9 0.1 constant_dynamic-slice_fusion.1
  18.0 0.1 collective-permute-start.4
  18.1 0.5 collective-permute-start.5
  18.6 1.4 %collective-permute-done.5 = f32[8]{0:T(128)S(1)} collective-permute-done((f32[8]{0:T(128)S(1)}, f32[8]{0:T(128)S(1)}, u32[]{:S(2)}, u32[]{:S(2)}) %collective-permute-start.5) | collective-permute-done | bytes 64 | tf_op jit(solution)/shard_map/ppermute | solution.py:47
  20.0 0.1 pad_maximum_fusion.1
  20.1 0.1 pad_maximum_fusion.refs_7_.refs_10_
  20.2 0.7 collective-permute-start.7
  20.9 0.7 collective-permute-start.6
  21.6 0.1 pad_maximum_fusion.2.far_ref
  21.7 1.5 %collective-permute-start.9 = (bf16[1024,512]{1,0:T(8,128)(2,1)S(1)}, bf16[1024,512]{1,0:T(8,128)(2,1)S(1)}, u32[]{:S(2)}, u32[]{:S(2)}) collective-permute-start(bf16[1024,512]{1,0:T(8,128)(2,1)S(1)} %divide_convert_fusion.refs_0_.refs_1_.refs_2_), channel_id=1, source_target_pairs={{0,2},{1,3},{2,4},{3,5},{4,6},{5,7},{6,0},{7,1},{8,10},{9,11},{10,... | collective-permute-start | bytes 3145736 | tf_op jit(solution)/shard_map/ppermute | solution.py:47
  23.2 1.6 %collective-permute-start.8 = (bf16[1024,512]{1,0:T(8,128)(2,1)S(1)}, bf16[1024,512]{1,0:T(8,128)(2,1)}, u32[]{:S(2)}, u32[]{:S(2)}) collective-permute-start(bf16[1024,512]{1,0:T(8,128)(2,1)S(1)} %divide_convert_fusion.refs_0_.refs_1_.refs_2_), channel_id=1, source_target_pairs={{0,8},{1,9},{2,10},{3,11},{4,12},{5,13},{6,14},{7,15},{8,0},{9,1},... | collective-permute-start | bytes 3145736 | tf_op jit(solution)/shard_map/ppermute | solution.py:47
  24.7 0.6 collective-permute-start.13
  25.3 1.4 %collective-permute-start.16 = (bf16[512,1024]{1,0:T(8,128)(2,1)S(1)}, bf16[512,1024]{1,0:T(8,128)(2,1)}, u32[]{:S(2)}, u32[]{:S(2)}) collective-permute-start(bf16[512,1024]{1,0:T(8,128)(2,1)S(1)} %pad_maximum_fusion.refs_7_.refs_10_), channel_id=1, source_target_pairs={{0,16},{1,17},{2,18},{3,19},{4,20},{5,21},{6,22},{7,23},{8,24},{9,... | collective-permute-start | bytes 3145736 | tf_op jit(solution)/shard_map/ppermute | solution.py:47
  26.8 1.7 %collective-permute-start.11 = (bf16[1024,512]{1,0:T(8,128)(2,1)S(1)}, bf16[1024,512]{1,0:T(8,128)(2,1)S(1)}, u32[]{:S(2)}, u32[]{:S(2)}) collective-permute-start(bf16[1024,512]{1,0:T(8,128)(2,1)S(1)} %divide_convert_fusion.refs_0_.refs_1_.refs_2_), channel_id=1, source_target_pairs={{0,6},{1,7},{2,0},{3,1},{4,2},{5,3},{6,4},{7,5},{8,14},{9,15},{10,... | collective-permute-start | bytes 3145736 | tf_op jit(solution)/shard_map/ppermute | solution.py:47
  28.5 11.0 %collective-permute-done.9.refs_1_.refs_2_.refs_3_ = bf16[1024,512]{1,0:T(8,128)(2,1)S(1)} collective-permute-done((bf16[1024,512]{1,0:T(8,128)(2,1)S(1)}, bf16[1024,512]{1,0:T(8,128)(2,1)S(1)}, u32[]{:S(2)}, u32[]{:S(2)}) %collective-permute-start.9) | collective-permute-done | bytes 1048608 | tf_op jit(solution)/shard_map/ppermute | solution.py:47
  39.5 1.3 %collective-permute-done.8.refs_3_.refs_4_.refs_5_ = bf16[1024,512]{1,0:T(8,128)(2,1)} collective-permute-done((bf16[1024,512]{1,0:T(8,128)(2,1)S(1)}, bf16[1024,512]{1,0:T(8,128)(2,1)}, u32[]{:S(2)}, u32[]{:S(2)}) %collective-permute-start.8) | collective-permute-done | bytes 1048608 | tf_op jit(solution)/shard_map/ppermute | solution.py:47
  40.9 2.6 %collective-permute-start.10 = (bf16[1024,512]{1,0:T(8,128)(2,1)}, bf16[1024,512]{1,0:T(8,128)(2,1)}, u32[]{:S(2)}, u32[]{:S(2)}) collective-permute-start(bf16[1024,512]{1,0:T(8,128)(2,1)} %collective-permute-done.8.refs_3_.refs_4_.refs_5_), channel_id=1, source_target_pairs={{0,2},{1,3},{2,4},{3,5},{4,6},{5,7},{6,0},{7,1},{8,10},{9,11},{10,... | collective-permute-start | bytes 3145736 | tf_op jit(solution)/shard_map/ppermute | solution.py:47
  43.5 0.1 collective-permute-done.13.refs_9_.refs_12_
  43.6 1.0 copy-done.3
  44.6 1.3 %collective-permute-done.16.refs_8_.refs_11_ = bf16[512,1024]{1,0:T(8,128)(2,1)} collective-permute-done((bf16[512,1024]{1,0:T(8,128)(2,1)S(1)}, bf16[512,1024]{1,0:T(8,128)(2,1)}, u32[]{:S(2)}, u32[]{:S(2)}) %collective-permute-start.16) | collective-permute-done | bytes 1048608 | tf_op jit(solution)/shard_map/ppermute | solution.py:47
  45.9 0.1 collective-permute-start.17
  46.0 2.6 %collective-permute-start.14 = (bf16[512,1024]{1,0:T(8,128)(2,1)S(1)}, bf16[512,1024]{1,0:T(8,128)(2,1)}, u32[]{:S(2)}, u32[]{:S(2)}) collective-permute-start(bf16[512,1024]{1,0:T(8,128)(2,1)S(1)} %pad_maximum_fusion.refs_7_.refs_10_), channel_id=1, source_target_pairs={{0,64},{1,65},{2,66},{3,67},{4,68},{5,69},{6,70},{7,71},{8,72},{9,... | collective-permute-start | bytes 3145736 | tf_op jit(solution)/shard_map/ppermute | solution.py:47
  48.7 1.0 copy-done
  49.6 1.2 collective-permute-start.12
  50.8 0.1 fusion.1
  50.9 0.1 reshape.11.out_ref
  51.0 0.1 pad_maximum_fusion.3
  51.1 10.8 %collective-permute-start.15 = (f32[104]{0:T(128)S(1)}, f32[104]{0:T(128)S(1)}, u32[]{:S(2)}, u32[]{:S(2)}) collective-permute-start(f32[104]{0:T(128)S(1)} %pad_maximum_fusion.3), channel_id=1, source_target_pairs={{0,1},{1,0},{2,3},{3,2},{4,5},{5,4},{6,7},{7,6},{8,9},{9,8},{10,11... | collective-permute-start | bytes 1256 | tf_op jit(solution)/shard_map/ppermute | solution.py:47
  61.9 2.3 %collective-permute-done.10.refs_4_.refs_5_.refs_6_ = bf16[1024,512]{1,0:T(8,128)(2,1)} collective-permute-done((bf16[1024,512]{1,0:T(8,128)(2,1)}, bf16[1024,512]{1,0:T(8,128)(2,1)}, u32[]{:S(2)}, u32[]{:S(2)}) %collective-permute-start.10) | collective-permute-done | bytes 1048608 | tf_op jit(solution)/shard_map/ppermute | solution.py:47
  64.2 1.5 %collective-permute-start.18 = (bf16[1024,512]{1,0:T(8,128)(2,1)S(1)}, bf16[1024,512]{1,0:T(8,128)(2,1)S(1)}, u32[]{:S(2)}, u32[]{:S(2)}) collective-permute-start(bf16[1024,512]{1,0:T(8,128)(2,1)S(1)} %collective-permute-done.9.refs_1_.refs_2_.refs_3_), channel_id=1, source_target_pairs={{0,2},{1,3},{2,4},{3,5},{4,6},{5,7},{6,0},{7,1},{8,10},{9,11},{10,... | collective-permute-start | bytes 3145736 | tf_op jit(solution)/shard_map/ppermute | solution.py:47
  65.7 3.6 %collective-permute-done.17.refs_10_.refs_13_ = bf16[512,1024]{1,0:T(8,128)(2,1)} collective-permute-done((bf16[512,1024]{1,0:T(8,128)(2,1)}, bf16[512,1024]{1,0:T(8,128)(2,1)}, u32[]{:S(2)}, u32[]{:S(2)}) %collective-permute-start.17) | collective-permute-done | bytes 1048608 | tf_op jit(solution)/shard_map/ppermute | solution.py:47
  69.2 0.1 collective-permute-start.20
  69.4 1.3 %collective-permute-start.19 = (bf16[1024,512]{1,0:T(8,128)(2,1)}, bf16[1024,512]{1,0:T(8,128)(2,1)S(1)}, u32[]{:S(2)}, u32[]{:S(2)}) collective-permute-start(bf16[1024,512]{1,0:T(8,128)(2,1)} %collective-permute-done.12.refs_5_.refs_6_.refs_7_), channel_id=1, source_target_pairs={{0,6},{1,7},{2,0},{3,1},{4,2},{5,3},{6,4},{7,5},{8,14},{9,15},{10,... | collective-permute-start | bytes 3145736 | tf_op jit(solution)/shard_map/ppermute | solution.py:47
  70.7 2.9 %collective-permute-start.22 = (bf16[512,1024]{1,0:T(8,128)(2,1)}, bf16[512,1024]{1,0:T(8,128)(2,1)S(1)}, u32[]{:S(2)}, u32[]{:S(2)}) collective-permute-start(bf16[512,1024]{1,0:T(8,128)(2,1)} %collective-permute-done.17.refs_10_.refs_13_), channel_id=1, source_target_pairs={{0,64},{1,65},{2,66},{3,67},{4,68},{5,69},{6,70},{7,71},{8,72},{9,... | collective-permute-start | bytes 3145736 | tf_op jit(solution)/shard_map/ppermute | solution.py:47
  73.6 2.8 %collective-permute-start.21 = (bf16[512,1024]{1,0:T(8,128)(2,1)}, bf16[512,1024]{1,0:T(8,128)(2,1)S(1)}, u32[]{:S(2)}, u32[]{:S(2)}) collective-permute-start(bf16[512,1024]{1,0:T(8,128)(2,1)} %collective-permute-done.14.refs_11_.refs_14_), channel_id=1, source_target_pairs={{0,48},{1,49},{2,50},{3,51},{4,52},{5,53},{6,54},{7,55},{8,56},{9,... | collective-permute-start | bytes 3145736 | tf_op jit(solution)/shard_map/ppermute | solution.py:47
  76.4 1.2 copy-done.1
  77.7 2.6 %plan.1.refs_0_ = s32[48]{0:T(128)S(1)} custom-call(f32[32]{0:T(128)S(1)} %pad_maximum_fusion.2.far_ref, f32[64]{0:T(128)S(1)} %slice_bitcast_fusion.right_ref, f32[8]{0:T(128)S(1)} %reshape.11.out_ref, f32[104]{0:T(128)S(1)} %collective-permute-done.15.other_ref, bf16[1024,512]{1,0:T(8,128)(2,1)S(1)} %divide_convert_fusion.refs_0_.refs_1_.refs_2_, ...), custom_call_target="tpu_custom_call" | custom-call | flops 1000000 | bytes 1024 | tf_op jit(solution)/shard_map/plan/pallas_call | solution.py:259
  80.3 6.5 %begin.1 = (f32[1024,512]{1,0:T(8,128)S(1)}, f32[1024,512]{1,0:T(8,128)S(1)}) custom-call(s32[48]{0:T(128)S(1)} %plan.1.refs_0_, bf16[1024,512]{1,0:T(8,128)(2,1)S(1)} %divide_convert_fusion.refs_0_.refs_1_.refs_2_, bf16[1024,512]{1,0:T(8,128)(2,1)S(1)} %collective-permute-done.9.refs_1_.refs_2_.refs_3_, bf16[1024,512]{1,0:T(8,128)(2,1)S(1)} %copy-done.2, ...), custom_call_target="tpu_custom_call" | custom-call | flops 1000000 | bytes 1024 | tf_op jit(solution)/shard_map/begin/pallas_call | solution.py:364
  86.8 0.7 collective-permute-done.18.refs_8_
  87.5 5.5 %collective-permute-done.19.refs_9_ = bf16[1024,512]{1,0:T(8,128)(2,1)S(1)} collective-permute-done((bf16[1024,512]{1,0:T(8,128)(2,1)}, bf16[1024,512]{1,0:T(8,128)(2,1)S(1)}, u32[]{:S(2)}, u32[]{:S(2)}) %collective-permute-start.19) | collective-permute-done | bytes 1048608 | tf_op jit(solution)/shard_map/ppermute | solution.py:47
  93.0 0.7 collective-permute-done.21.refs_16_
  93.7 4.0 %finish.3 = f32[1024,512]{1,0:T(8,128)S(1)} custom-call(s32[48]{0:T(128)S(1)} %plan.1.refs_0_, f32[1024,512]{1,0:T(8,128)S(1)} %get-tuple-element.42.refs_1_, bf16[1024,512]{1,0:T(8,128)(2,1)S(1)} %divide_convert_fusion.refs_0_.refs_1_.refs_2_, bf16[1024,512]{1,0:T(8,128)(2,1)S(1)} %collective-permute-done.9.refs_1_.refs_2_.refs_3_, ...), custom_call_target="tpu_custom_call", output_to_operand_aliasing={{}: (1, {})} | custom-call | flops 1000000 | bytes 1024 | tf_op jit(solution)/shard_map/finish/pallas_call | solution.py:364
  97.7 6.2 %collective-permute-start.23 = (f32[1024,512]{1,0:T(8,128)S(1)}, f32[1024,512]{1,0:T(8,128)S(1)}, u32[]{:S(2)}, u32[]{:S(2)}) collective-permute-start(f32[1024,512]{1,0:T(8,128)S(1)} %finish.3), channel_id=1, source_target_pairs={{0,1},{1,0},{2,3},{3,2},{4,5},{5,4},{6,7},{7,6},{8,9},{9,8},{10,11... | collective-permute-start | bytes 6291464 | tf_op jit(solution)/shard_map/ppermute | solution.py:47
  103.8 3.8 %finish.2.mine_ref = f32[1024,512]{1,0:T(8,128)S(1)} custom-call(s32[48]{0:T(128)S(1)} %plan.1.refs_0_, f32[1024,512]{1,0:T(8,128)S(1)} %get-tuple-element.38.refs_1_, bf16[1024,512]{1,0:T(8,128)(2,1)S(1)} %divide_convert_fusion.refs_0_.refs_1_.refs_2_, ...), custom_call_target="tpu_custom_call", output_to_operand_aliasing={{}: (1, {})} | custom-call | flops 1000000 | bytes 1024 | tf_op jit(solution)/shard_map/finish/pallas_call | solution.py:364
  107.6 0.0 collective-permute-done.23.got_ref
  107.6 0.3 square.1
  108.0 4.9 %collective-permute-start.26 = (f32[1,512]{1,0:T(1,128)S(1)}, f32[1,512]{1,0:T(1,128)S(1)}, u32[]{:S(2)}, u32[]{:S(2)}) collective-permute-start(f32[1,512]{1,0:T(1,128)S(1)} %get-tuple-element.44), channel_id=1, source_target_pairs={{0,48},{1,49},{2,50},{3,51},{4,52},{5,53},{6,54},{7,55},{8,56},{9,... | collective-permute-start | bytes 6152 | tf_op jit(solution)/shard_map/ppermute | solution.py:47
  112.9 0.9 collective-permute-start.24
  113.9 0.4 collective-permute-done.26
  114.2 3.8 %collective-permute-done.25 = f32[1,512]{1,0:T(1,128)S(1)} collective-permute-done((f32[1,512]{1,0:T(1,128)S(1)}, f32[1,512]{1,0:T(1,128)S(1)}, u32[]{:S(2)}, u32[]{:S(2)}) %collective-permute-start.25) | collective-permute-done | bytes 2080 | tf_op jit(solution)/shard_map/ppermute | solution.py:47
  118.0 2.2 %collective-permute-start.27 = (f32[1,512]{1,0:T(1,128)S(1)}, f32[1,512]{1,0:T(1,128)S(1)}, u32[]{:S(2)}, u32[]{:S(2)}) collective-permute-start(f32[1,512]{1,0:T(1,128)S(1)} %add_add_fusion.1), channel_id=1, source_target_pairs={{0,64},{1,65},{2,66},{3,67},{4,68},{5,69},{6,70},{7,71},{8,72},{9,... | collective-permute-start | bytes 6152 | tf_op jit(solution)/shard_map/ppermute | solution.py:47
  120.2 3.0 %collective-permute-done.27 = f32[1,512]{1,0:T(1,128)S(1)} collective-permute-done((f32[1,512]{1,0:T(1,128)S(1)}, f32[1,512]{1,0:T(1,128)S(1)}, u32[]{:S(2)}, u32[]{:S(2)}) %collective-permute-start.27) | collective-permute-done | bytes 2080 | tf_op jit(solution)/shard_map/ppermute | solution.py:47
  123.2 1.5 %rescale.1 = f32[1024,512]{1,0:T(8,128)} custom-call(f32[1024,512]{1,0:T(8,128)S(1)} %get-tuple-element.43.value_ref, f32[1,512]{1,0:T(1,128)S(1)} %add.68.total_ref), custom_call_target="tpu_custom_call" | custom-call | tf_op jit(solution)/shard_map/rescale/pallas_call | solution.py:167
  (32 shorter events, 0.1 us)
Async XLA Ops:
  0.0 1.6 %copy-start.5 = (f32[1024,512]{1,0:T(8,128)S(1)}, f32[1024,512]{1,0:T(8,128)}, u32[]{:S(2)}) copy-start(f32[1024,512]{1,0:T(8,128)} %entries_in.1) | copy-start | bytes 6291460
  1.6 0.7 copy-start.6
  3.2 5.5 %collective-permute-start.2 = (f32[1,640]{1,0:T(1,128)S(1)}, f32[1,640]{1,0:T(1,128)S(1)}, u32[]{:S(2)}, u32[]{:S(2)}) collective-permute-start(f32[1,640]{1,0:T(1,128)S(1)} %get-tuple-element.26), channel_id=1, source_target_pairs={{0,48},{1,49},{2,50},{3,51},{4,52},{5,53},{6,54},{7,55},{8,56},{9,... | collective-permute-start | bytes 7688 | tf_op jit(solution)/shard_map/ppermute | solution.py:47
  7.3 5.1 %collective-permute-start.1 = (f32[1,640]{1,0:T(1,128)S(1)}, f32[1,640]{1,0:T(1,128)S(1)}, u32[]{:S(2)}, u32[]{:S(2)}) collective-permute-start(f32[1,640]{1,0:T(1,128)S(1)} %get-tuple-element.26), channel_id=1, source_target_pairs={{0,32},{1,33},{2,34},{3,35},{4,36},{5,37},{6,38},{7,39},{8,40},{9,... | collective-permute-start | bytes 7688 | tf_op jit(solution)/shard_map/ppermute | solution.py:47
  7.3 5.1 %collective-permute-start = (f32[1,640]{1,0:T(1,128)S(1)}, f32[1,640]{1,0:T(1,128)S(1)}, u32[]{:S(2)}, u32[]{:S(2)}) collective-permute-start(f32[1,640]{1,0:T(1,128)S(1)} %get-tuple-element.26), channel_id=1, source_target_pairs={{0,16},{1,17},{2,18},{3,19},{4,20},{5,21},{6,22},{7,23},{8,24},{9,... | collective-permute-start | bytes 7688 | tf_op jit(solution)/shard_map/ppermute | solution.py:47
  12.5 5.2 %collective-permute-start.3 = (f32[1,640]{1,0:T(1,128)S(1)}, f32[1,640]{1,0:T(1,128)S(1)}, u32[]{:S(2)}, u32[]{:S(2)}) collective-permute-start(f32[1,640]{1,0:T(1,128)S(1)} %add_add_fusion), channel_id=1, source_target_pairs={{0,64},{1,65},{2,66},{3,67},{4,68},{5,69},{6,70},{7,71},{8,72},{9,... | collective-permute-start | bytes 7688 | tf_op jit(solution)/shard_map/ppermute | solution.py:47
  17.9 32.9 %copy-start.7 = (s32[4,2]{0,1:T(2,128)S(1)}, s32[4,2]{0,1:T(2,128)}, u32[]{:S(2)}) copy-start(s32[4,2]{0,1:T(2,128)} %param.5) | copy-start | bytes 100
  18.0 2.1 %collective-permute-start.4 = (bf16[512,512]{1,0:T(8,128)(2,1)S(1)}, bf16[512,512]{1,0:T(8,128)(2,1)S(1)}, u32[]{:S(2)}, u32[]{:S(2)}) collective-permute-start(bf16[512,512]{1,0:T(8,128)(2,1)S(1)} %get-tuple-element.46), channel_id=1, source_target_pairs={{0,1},{1,0},{2,3},{3,2},{4,5},{5,4},{6,7},{7,6},{8,9},{9,8},{10,11... | collective-permute-start | bytes 1572872 | tf_op jit(solution)/shard_map/ppermute | solution.py:47
  18.1 1.9 %collective-permute-start.5 = (f32[8]{0:T(128)S(1)}, f32[8]{0:T(128)S(1)}, u32[]{:S(2)}, u32[]{:S(2)}) collective-permute-start(f32[8]{0:T(128)S(1)} %slice_bitcast_fusion.1), channel_id=1, source_target_pairs={{0,1},{1,0},{2,3},{3,2},{4,5},{5,4},{6,7},{7,6},{8,9},{9,8},{10,11... | collective-permute-start | bytes 104 | tf_op jit(solution)/shard_map/ppermute | solution.py:47
  20.2 1.3 %collective-permute-start.7 = (f32[16]{0:T(128)S(1)}, f32[16]{0:T(128)S(1)}, u32[]{:S(2)}, u32[]{:S(2)}) collective-permute-start(f32[16]{0:T(128)S(1)} %pad_maximum_fusion.1), channel_id=1, source_target_pairs={{1,13},{3,15},{5,9},{7,11},{9,5},{11,7},{13,1},{15,3},{17,29},{19,... | collective-permute-start | bytes 200 | tf_op jit(solution)/shard_map/ppermute | solution.py:47
  20.9 0.7 collective-permute-start.6
  21.7 17.9 %collective-permute-start.9 = (bf16[1024,512]{1,0:T(8,128)(2,1)S(1)}, bf16[1024,512]{1,0:T(8,128)(2,1)S(1)}, u32[]{:S(2)}, u32[]{:S(2)}) collective-permute-start(bf16[1024,512]{1,0:T(8,128)(2,1)S(1)} %divide_convert_fusion.refs_0_.refs_1_.refs_2_), channel_id=1, source_target_pairs={{0,2},{1,3},{2,4},{3,5},{4,6},{5,7},{6,0},{7,1},{8,10},{9,11},{10,... | collective-permute-start | bytes 3145736 | tf_op jit(solution)/shard_map/ppermute | solution.py:47
  23.2 17.7 %collective-permute-start.8 = (bf16[1024,512]{1,0:T(8,128)(2,1)S(1)}, bf16[1024,512]{1,0:T(8,128)(2,1)}, u32[]{:S(2)}, u32[]{:S(2)}) collective-permute-start(bf16[1024,512]{1,0:T(8,128)(2,1)S(1)} %divide_convert_fusion.refs_0_.refs_1_.refs_2_), channel_id=1, source_target_pairs={{0,8},{1,9},{2,10},{3,11},{4,12},{5,13},{6,14},{7,15},{8,0},{9,1},... | collective-permute-start | bytes 3145736 | tf_op jit(solution)/shard_map/ppermute | solution.py:47
  24.7 18.9 %collective-permute-start.13 = (bf16[512,1024]{1,0:T(8,128)(2,1)S(1)}, bf16[512,1024]{1,0:T(8,128)(2,1)S(1)}, u32[]{:S(2)}, u32[]{:S(2)}) collective-permute-start(bf16[512,1024]{1,0:T(8,128)(2,1)S(1)} %pad_maximum_fusion.refs_7_.refs_10_), channel_id=1, source_target_pairs={{0,48},{1,49},{2,50},{3,51},{4,52},{5,53},{6,54},{7,55},{8,56},{9,... | collective-permute-start | bytes 3145736 | tf_op jit(solution)/shard_map/ppermute | solution.py:47
  25.3 20.6 %collective-permute-start.16 = (bf16[512,1024]{1,0:T(8,128)(2,1)S(1)}, bf16[512,1024]{1,0:T(8,128)(2,1)}, u32[]{:S(2)}, u32[]{:S(2)}) collective-permute-start(bf16[512,1024]{1,0:T(8,128)(2,1)S(1)} %pad_maximum_fusion.refs_7_.refs_10_), channel_id=1, source_target_pairs={{0,16},{1,17},{2,18},{3,19},{4,20},{5,21},{6,22},{7,23},{8,24},{9,... | collective-permute-start | bytes 3145736 | tf_op jit(solution)/shard_map/ppermute | solution.py:47
  26.8 21.9 %collective-permute-start.11 = (bf16[1024,512]{1,0:T(8,128)(2,1)S(1)}, bf16[1024,512]{1,0:T(8,128)(2,1)S(1)}, u32[]{:S(2)}, u32[]{:S(2)}) collective-permute-start(bf16[1024,512]{1,0:T(8,128)(2,1)S(1)} %divide_convert_fusion.refs_0_.refs_1_.refs_2_), channel_id=1, source_target_pairs={{0,6},{1,7},{2,0},{3,1},{4,2},{5,3},{6,4},{7,5},{8,14},{9,15},{10,... | collective-permute-start | bytes 3145736 | tf_op jit(solution)/shard_map/ppermute | solution.py:47
  40.9 23.3 %collective-permute-start.10 = (bf16[1024,512]{1,0:T(8,128)(2,1)}, bf16[1024,512]{1,0:T(8,128)(2,1)}, u32[]{:S(2)}, u32[]{:S(2)}) collective-permute-start(bf16[1024,512]{1,0:T(8,128)(2,1)} %collective-permute-done.8.refs_3_.refs_4_.refs_5_), channel_id=1, source_target_pairs={{0,2},{1,3},{2,4},{3,5},{4,6},{5,7},{6,0},{7,1},{8,10},{9,11},{10,... | collective-permute-start | bytes 3145736 | tf_op jit(solution)/shard_map/ppermute | solution.py:47
  43.6 1.0 copy-start.3
  45.9 23.3 %collective-permute-start.17 = (bf16[512,1024]{1,0:T(8,128)(2,1)}, bf16[512,1024]{1,0:T(8,128)(2,1)}, u32[]{:S(2)}, u32[]{:S(2)}) collective-permute-start(bf16[512,1024]{1,0:T(8,128)(2,1)} %collective-permute-done.16.refs_8_.refs_11_), channel_id=1, source_target_pairs={{0,16},{1,17},{2,18},{3,19},{4,20},{5,21},{6,22},{7,23},{8,24},{9,... | collective-permute-start | bytes 3145736 | tf_op jit(solution)/shard_map/ppermute | solution.py:47
  46.0 23.2 %collective-permute-start.14 = (bf16[512,1024]{1,0:T(8,128)(2,1)S(1)}, bf16[512,1024]{1,0:T(8,128)(2,1)}, u32[]{:S(2)}, u32[]{:S(2)}) collective-permute-start(bf16[512,1024]{1,0:T(8,128)(2,1)S(1)} %pad_maximum_fusion.refs_7_.refs_10_), channel_id=1, source_target_pairs={{0,64},{1,65},{2,66},{3,67},{4,68},{5,69},{6,70},{7,71},{8,72},{9,... | collective-permute-start | bytes 3145736 | tf_op jit(solution)/shard_map/ppermute | solution.py:47
  48.6 1.0 copy-start
  49.6 19.7 %collective-permute-start.12 = (bf16[1024,512]{1,0:T(8,128)(2,1)}, bf16[1024,512]{1,0:T(8,128)(2,1)}, u32[]{:S(2)}, u32[]{:S(2)}) collective-permute-start(bf16[1024,512]{1,0:T(8,128)(2,1)} %collective-permute-done.8.refs_3_.refs_4_.refs_5_), channel_id=1, source_target_pairs={{0,6},{1,7},{2,0},{3,1},{4,2},{5,3},{6,4},{7,5},{8,14},{9,15},{10,... | collective-permute-start | bytes 3145736 | tf_op jit(solution)/shard_map/ppermute | solution.py:47
  51.1 22.6 %collective-permute-start.15 = (f32[104]{0:T(128)S(1)}, f32[104]{0:T(128)S(1)}, u32[]{:S(2)}, u32[]{:S(2)}) collective-permute-start(f32[104]{0:T(128)S(1)} %pad_maximum_fusion.3), channel_id=1, source_target_pairs={{0,1},{1,0},{2,3},{3,2},{4,5},{5,4},{6,7},{7,6},{8,9},{9,8},{10,11... | collective-permute-start | bytes 1256 | tf_op jit(solution)/shard_map/ppermute | solution.py:47
  64.2 23.3 %collective-permute-start.18 = (bf16[1024,512]{1,0:T(8,128)(2,1)S(1)}, bf16[1024,512]{1,0:T(8,128)(2,1)S(1)}, u32[]{:S(2)}, u32[]{:S(2)}) collective-permute-start(bf16[1024,512]{1,0:T(8,128)(2,1)S(1)} %collective-permute-done.9.refs_1_.refs_2_.refs_3_), channel_id=1, source_target_pairs={{0,2},{1,3},{2,4},{3,5},{4,6},{5,7},{6,0},{7,1},{8,10},{9,11},{10,... | collective-permute-start | bytes 3145736 | tf_op jit(solution)/shard_map/ppermute | solution.py:47
  69.2 23.8 %collective-permute-start.20 = (bf16[512,1024]{1,0:T(8,128)(2,1)}, bf16[512,1024]{1,0:T(8,128)(2,1)S(1)}, u32[]{:S(2)}, u32[]{:S(2)}) collective-permute-start(bf16[512,1024]{1,0:T(8,128)(2,1)} %collective-permute-done.14.refs_11_.refs_14_), channel_id=1, source_target_pairs={{0,16},{1,17},{2,18},{3,19},{4,20},{5,21},{6,22},{7,23},{8,24},{9,... | collective-permute-start | bytes 3145736 | tf_op jit(solution)/shard_map/ppermute | solution.py:47
  69.4 23.6 %collective-permute-start.19 = (bf16[1024,512]{1,0:T(8,128)(2,1)}, bf16[1024,512]{1,0:T(8,128)(2,1)S(1)}, u32[]{:S(2)}, u32[]{:S(2)}) collective-permute-start(bf16[1024,512]{1,0:T(8,128)(2,1)} %collective-permute-done.12.refs_5_.refs_6_.refs_7_), channel_id=1, source_target_pairs={{0,6},{1,7},{2,0},{3,1},{4,2},{5,3},{6,4},{7,5},{8,14},{9,15},{10,... | collective-permute-start | bytes 3145736 | tf_op jit(solution)/shard_map/ppermute | solution.py:47
  70.7 22.3 %collective-permute-start.22 = (bf16[512,1024]{1,0:T(8,128)(2,1)}, bf16[512,1024]{1,0:T(8,128)(2,1)S(1)}, u32[]{:S(2)}, u32[]{:S(2)}) collective-permute-start(bf16[512,1024]{1,0:T(8,128)(2,1)} %collective-permute-done.17.refs_10_.refs_13_), channel_id=1, source_target_pairs={{0,64},{1,65},{2,66},{3,67},{4,68},{5,69},{6,70},{7,71},{8,72},{9,... | collective-permute-start | bytes 3145736 | tf_op jit(solution)/shard_map/ppermute | solution.py:47
  73.6 20.1 %collective-permute-start.21 = (bf16[512,1024]{1,0:T(8,128)(2,1)}, bf16[512,1024]{1,0:T(8,128)(2,1)S(1)}, u32[]{:S(2)}, u32[]{:S(2)}) collective-permute-start(bf16[512,1024]{1,0:T(8,128)(2,1)} %collective-permute-done.14.refs_11_.refs_14_), channel_id=1, source_target_pairs={{0,48},{1,49},{2,50},{3,51},{4,52},{5,53},{6,54},{7,55},{8,56},{9,... | collective-permute-start | bytes 3145736 | tf_op jit(solution)/shard_map/ppermute | solution.py:47
  76.4 1.2 copy-start.1
  77.7 2.7 %copy-start.2 = (bf16[1024,512]{1,0:T(8,128)(2,1)S(1)}, bf16[1024,512]{1,0:T(8,128)(2,1)}, u32[]{:S(2)}) copy-start(bf16[1024,512]{1,0:T(8,128)(2,1)} %copy-done) | copy-start | bytes 3145732
  77.7 2.7 %copy-start.4 = (bf16[512,1024]{1,0:T(8,128)(2,1)S(1)}, bf16[512,1024]{1,0:T(8,128)(2,1)}, u32[]{:S(2)}) copy-start(bf16[512,1024]{1,0:T(8,128)(2,1)} %copy-done.3) | copy-start | bytes 3145732
  97.7 10.0 %collective-permute-start.23 = (f32[1024,512]{1,0:T(8,128)S(1)}, f32[1024,512]{1,0:T(8,128)S(1)}, u32[]{:S(2)}, u32[]{:S(2)}) collective-permute-start(f32[1024,512]{1,0:T(8,128)S(1)} %finish.3), channel_id=1, source_target_pairs={{0,1},{1,0},{2,3},{3,2},{4,5},{5,4},{6,7},{7,6},{8,9},{9,8},{10,11... | collective-permute-start | bytes 6291464 | tf_op jit(solution)/shard_map/ppermute | solution.py:47
  108.0 6.2 %collective-permute-start.26 = (f32[1,512]{1,0:T(1,128)S(1)}, f32[1,512]{1,0:T(1,128)S(1)}, u32[]{:S(2)}, u32[]{:S(2)}) collective-permute-start(f32[1,512]{1,0:T(1,128)S(1)} %get-tuple-element.44), channel_id=1, source_target_pairs={{0,48},{1,49},{2,50},{3,51},{4,52},{5,53},{6,54},{7,55},{8,56},{9,... | collective-permute-start | bytes 6152 | tf_op jit(solution)/shard_map/ppermute | solution.py:47
  112.9 5.1 %collective-permute-start.25 = (f32[1,512]{1,0:T(1,128)S(1)}, f32[1,512]{1,0:T(1,128)S(1)}, u32[]{:S(2)}, u32[]{:S(2)}) collective-permute-start(f32[1,512]{1,0:T(1,128)S(1)} %get-tuple-element.44), channel_id=1, source_target_pairs={{0,32},{1,33},{2,34},{3,35},{4,36},{5,37},{6,38},{7,39},{8,40},{9,... | collective-permute-start | bytes 6152 | tf_op jit(solution)/shard_map/ppermute | solution.py:47
  112.9 5.1 %collective-permute-start.24 = (f32[1,512]{1,0:T(1,128)S(1)}, f32[1,512]{1,0:T(1,128)S(1)}, u32[]{:S(2)}, u32[]{:S(2)}) collective-permute-start(f32[1,512]{1,0:T(1,128)S(1)} %get-tuple-element.44), channel_id=1, source_target_pairs={{0,16},{1,17},{2,18},{3,19},{4,20},{5,21},{6,22},{7,23},{8,24},{9,... | collective-permute-start | bytes 6152 | tf_op jit(solution)/shard_map/ppermute | solution.py:47
  118.0 5.2 %collective-permute-start.27 = (f32[1,512]{1,0:T(1,128)S(1)}, f32[1,512]{1,0:T(1,128)S(1)}, u32[]{:S(2)}, u32[]{:S(2)}) collective-permute-start(f32[1,512]{1,0:T(1,128)S(1)} %add_add_fusion.1), channel_id=1, source_target_pairs={{0,64},{1,65},{2,66},{3,67},{4,68},{5,69},{6,70},{7,71},{8,72},{9,... | collective-permute-start | bytes 6152 | tf_op jit(solution)/shard_map/ppermute | solution.py:47

commit v6 on v5

--- a/solution.py
+++ b/solution.py
@@ -51,8 +51,10 @@
     return value + sum(move(value, turn) for turn in turns)
 
 
-def row_sum(value):
+def row_sum(value, *beside):
     value = turn_sum(value, Z_TURNS)
+    if beside:
+        value = after(value, *beside)
     return value + move(value, SWAP_YH)
 
 
@@ -394,7 +396,8 @@
     diagonal = (col_ids[:, None] == row_ids[None, :]).astype(I32)
     kept = jnp.maximum(prune.T, diagonal).astype(F32).reshape(-1)
 
-    message = row_sum(message)
+    flags = jnp.concatenate([flags, move(flags, SWAP_CORE)])
+    message = row_sum(message, flags)
     colsum, right = message[:, :width], message[0, width:width + grid * cols]
     a = (masked / colsum).astype(BF16)
 
@@ -403,15 +406,15 @@
     theirs = lax.dynamic_slice(a, ((1 - c) * half, 0), (half, width))
     b = jnp.concatenate([mine, move(theirs, SWAP_CORE)], axis=1)
 
-    flags = after(jnp.concatenate([flags, move(flags, SWAP_CORE)]), b)
+    flags = after(flags, a)
     far = jnp.concatenate([move(flags, far) for far in FAR_1])
-    a, b, far = lax.optimization_barrier((a, b, far))
+    a, far = lax.optimization_barrier((a, far))
     notes_o = move(jnp.concatenate([right, kept, far]), SWAP_CORE)
 
     xl, xr, pa = move(a, X_UP), move(a, X_DOWN), move(a, SWAP_YL)
-    zl, zr = move(b, Z_UP), move(b, Z_DOWN)
+    zl, zr = move(after(b, far), Z_UP), move(b, Z_DOWN)
     pxl, pxr = move(after(pa, xl), X_UP), move(after(pa, xr), X_DOWN)
-    zf, pb = move(zl, Z_UP), move(after(b, pa, zr), SWAP_YH)
+    zf, pb = move(after(zl, zr), Z_UP), move(after(b, pa), SWAP_YH)
     xf, pxf = move(after(xl, pxl), X_UP), move(pxr, X_DOWN)
     pzl, pzr, pzf = move(after(pb, zf), Z_UP), move(pb, Z_DOWN), move(after(zf, pb), SWAP_YH)
     notes_o, far, right = after(notes_o, pxl, pxr, pb), after(far, pxl, pxr, pb), after(right, pxl, pxr, pb)

time: 125 us -> 123 us (0.984)
  Pallas kernels: 19.6 us -> 23 us
  starting transfers between devices: 57.7 us -> 54.8 us
  waiting for transfers between devices: 40.9 us -> 38.3 us
    pallas_call x3, Pallas kernels: 14.2 us -> 17.7 us  [product(): pl.pallas_call(functools.partial(product_kernel, len(a_units), len(b_unit...]
    ppermute x28, starting transfers between devices: 57.7 us -> 54.8 us  [move(): return lax.ppermute(value, AXES, perm)]
    ppermute x28, waiting for transfers between devices: 40.9 us -> 38.3 us  [move(): return lax.ppermute(value, AXES, perm)]
  transfers between devices with their start and end apart: 28 -> 28, of which waited for: 16 -> 12; matrix products, arithmetic and copies ran while one was open for 0% -> 0% of each run, Pallas kernels for 10% -> 13%
where the time goes in v6:
time: 123 us; the launch traced here: 122 us
  starting transfers between devices  54.8 us (45%)
  waiting for transfers between devices  38.3 us (31%)
  Pallas kernels  23 us (19%)
  local copies, waits for them, and re-layouts  4.64 us (4%)
    ppermute x28, starting transfers between devices, move(): return lax.ppermute(value, AXES, perm)  54.8 us
    ppermute x28, waiting for transfers between devices, move(): return lax.ppermute(value, AXES, perm)  38.3 us
    pallas_call x3, Pallas kernels, product(): pl.pallas_call(functools.partial(product_kernel, len(a_units), len(b_unit...  17.7 us
    unnamed x16, local copies, waits for them, and re-layouts  4.47 us
    pallas_call x1, Pallas kernels, planned(): pl.pallas_call(functools.partial(plan_kernel, rows, cols), out_shape=jax....  2.64 us
  transfers between devices with their start and end apart: 28, of which 12 were waited for; matrix products, arithmetic and copies ran while one was open for 0% of the time, Pallas kernels for 13%

profile of v6, /device:TPU:0, one launch (start us, length us, event | category | flops | bytes accessed | tf_op | source)
XLA Modules:
  0.0 121.6 jit_solution(631638187437231504)
XLA Ops:
  0.0 1.6 %copy-done.5 = f32[1024,512]{1,0:T(8,128)S(1)} copy-done((f32[1024,512]{1,0:T(8,128)S(1)}, f32[1024,512]{1,0:T(8,128)}, u32[]{:S(2)}) %copy-start.5) | copy-done | bytes 2097176
  1.6 0.7 copy-done.6
  2.3 0.9 mask.1
  3.2 4.2 %collective-permute-start.2 = (f32[1,640]{1,0:T(1,128)S(1)}, f32[1,640]{1,0:T(1,128)S(1)}, u32[]{:S(2)}, u32[]{:S(2)}) collective-permute-start(f32[1,640]{1,0:T(1,128)S(1)} %get-tuple-element.28), channel_id=1, source_target_pairs={{0,48},{1,49},{2,50},{3,51},{4,52},{5,53},{6,54},{7,55},{8,56},{9,... | collective-permute-start | bytes 7688 | tf_op jit(solution)/shard_map/ppermute | solution.py:47
  7.3 0.0 collective-permute-start.1
  7.3 1.3 %collective-permute-start = (f32[1,640]{1,0:T(1,128)S(1)}, f32[1,640]{1,0:T(1,128)S(1)}, u32[]{:S(2)}, u32[]{:S(2)}) collective-permute-start(f32[1,640]{1,0:T(1,128)S(1)} %get-tuple-element.28), channel_id=1, source_target_pairs={{0,16},{1,17},{2,18},{3,19},{4,20},{5,21},{6,22},{7,23},{8,24},{9,... | collective-permute-start | bytes 7688 | tf_op jit(solution)/shard_map/ppermute | solution.py:47
  8.6 0.0 collective-permute-start.3
  8.6 1.1 collective-permute-done.3
  9.7 0.1 pad_maximum_fusion.1
  9.8 0.0 collective-permute-done.2
  9.8 2.6 %collective-permute-done.1 = f32[1,640]{1,0:T(1,128)S(1)} collective-permute-done((f32[1,640]{1,0:T(1,128)S(1)}, f32[1,640]{1,0:T(1,128)S(1)}, u32[]{:S(2)}, u32[]{:S(2)}) %collective-permute-start.1) | collective-permute-done | bytes 2592 | tf_op jit(solution)/shard_map/ppermute | solution.py:47
  12.4 0.0 collective-permute-done
  12.5 3.3 %collective-permute-start.4 = (f32[1,640]{1,0:T(1,128)S(1)}, f32[1,640]{1,0:T(1,128)S(1)}, u32[]{:S(2)}, u32[]{:S(2)}) collective-permute-start(f32[1,640]{1,0:T(1,128)S(1)} %add_add_fusion), channel_id=1, source_target_pairs={{0,64},{1,65},{2,66},{3,67},{4,68},{5,69},{6,70},{7,71},{8,72},{9,... | collective-permute-start | bytes 7688 | tf_op jit(solution)/shard_map/ppermute | solution.py:47
  15.7 1.9 %collective-permute-done.4 = f32[1,640]{1,0:T(1,128)S(1)} collective-permute-done((f32[1,640]{1,0:T(1,128)S(1)}, f32[1,640]{1,0:T(1,128)S(1)}, u32[]{:S(2)}, u32[]{:S(2)}) %collective-permute-start.4) | collective-permute-done | bytes 2592 | tf_op jit(solution)/shard_map/ppermute | solution.py:47
  17.6 0.3 divide_convert_fusion.refs_0_.refs_1_.refs_2_
  17.9 0.0 copy-start.7
  17.9 0.1 constant_dynamic-slice_fusion.1
  18.0 0.1 collective-permute-start.12
  18.1 0.7 collective-permute-start.6
  18.8 0.7 collective-permute-start.5
  19.5 0.0 collective-permute-done.6
  19.5 0.0 collective-permute-done.5
  19.5 0.1 pad_maximum_fusion.2.far_ref
  19.6 2.8 %collective-permute-start.10 = (bf16[1024,512]{1,0:T(8,128)(2,1)S(1)}, bf16[1024,512]{1,0:T(8,128)(2,1)S(1)}, u32[]{:S(2)}, u32[]{:S(2)}) collective-permute-start(bf16[1024,512]{1,0:T(8,128)(2,1)S(1)} %divide_convert_fusion.refs_0_.refs_1_.refs_2_), channel_id=1, source_target_pairs={{0,6},{1,7},{2,0},{3,1},{4,2},{5,3},{6,4},{7,5},{8,14},{9,15},{10,... | collective-permute-start | bytes 3145736 | tf_op jit(solution)/shard_map/ppermute | solution.py:47
  22.3 1.6 %collective-permute-start.7 = (bf16[1024,512]{1,0:T(8,128)(2,1)S(1)}, bf16[1024,512]{1,0:T(8,128)(2,1)}, u32[]{:S(2)}, u32[]{:S(2)}) collective-permute-start(bf16[1024,512]{1,0:T(8,128)(2,1)S(1)} %divide_convert_fusion.refs_0_.refs_1_.refs_2_), channel_id=1, source_target_pairs={{0,8},{1,9},{2,10},{3,11},{4,12},{5,13},{6,14},{7,15},{8,0},{9,1},... | collective-permute-start | bytes 3145736 | tf_op jit(solution)/shard_map/ppermute | solution.py:47
  23.9 0.1 pad_maximum_fusion.refs_7_.refs_10_
  24.0 0.1 collective-permute-start.15
  24.1 3.2 %collective-permute-start.16 = (bf16[512,1024]{1,0:T(8,128)(2,1)S(1)}, bf16[512,1024]{1,0:T(8,128)(2,1)S(1)}, u32[]{:S(2)}, u32[]{:S(2)}) collective-permute-start(bf16[512,1024]{1,0:T(8,128)(2,1)S(1)} %pad_maximum_fusion.refs_7_.refs_10_), channel_id=1, source_target_pairs={{0,48},{1,49},{2,50},{3,51},{4,52},{5,53},{6,54},{7,55},{8,56},{9,... | collective-permute-start | bytes 3145736 | tf_op jit(solution)/shard_map/ppermute | solution.py:47
  27.3 12.8 %collective-permute-done.7.refs_3_.refs_4_.refs_5_ = bf16[1024,512]{1,0:T(8,128)(2,1)} collective-permute-done((bf16[1024,512]{1,0:T(8,128)(2,1)S(1)}, bf16[1024,512]{1,0:T(8,128)(2,1)}, u32[]{:S(2)}, u32[]{:S(2)}) %collective-permute-start.7) | collective-permute-done | bytes 1048608 | tf_op jit(solution)/shard_map/ppermute | solution.py:47
  40.1 1.6 %collective-permute-done.8.refs_1_.refs_2_.refs_3_ = bf16[1024,512]{1,0:T(8,128)(2,1)S(1)} collective-permute-done((bf16[1024,512]{1,0:T(8,128)(2,1)S(1)}, bf16[1024,512]{1,0:T(8,128)(2,1)S(1)}, u32[]{:S(2)}, u32[]{:S(2)}) %collective-permute-start.8) | collective-permute-done | bytes 1048608 | tf_op jit(solution)/shard_map/ppermute | solution.py:47
  41.7 0.0 collective-permute-start.9
  41.7 3.2 %collective-permute-start.11 = (bf16[1024,512]{1,0:T(8,128)(2,1)}, bf16[1024,512]{1,0:T(8,128)(2,1)}, u32[]{:S(2)}, u32[]{:S(2)}) collective-permute-start(bf16[1024,512]{1,0:T(8,128)(2,1)} %collective-permute-done.7.refs_3_.refs_4_.refs_5_), channel_id=1, source_target_pairs={{0,6},{1,7},{2,0},{3,1},{4,2},{5,3},{6,4},{7,5},{8,14},{9,15},{10,... | collective-permute-start | bytes 3145736 | tf_op jit(solution)/shard_map/ppermute | solution.py:47
  45.0 3.5 %collective-permute-start.13 = (bf16[512,1024]{1,0:T(8,128)(2,1)S(1)}, bf16[512,1024]{1,0:T(8,128)(2,1)}, u32[]{:S(2)}, u32[]{:S(2)}) collective-permute-start(bf16[512,1024]{1,0:T(8,128)(2,1)S(1)} %pad_maximum_fusion.refs_7_.refs_10_), channel_id=1, source_target_pairs={{0,64},{1,65},{2,66},{3,67},{4,68},{5,69},{6,70},{7,71},{8,72},{9,... | collective-permute-start | bytes 3145736 | tf_op jit(solution)/shard_map/ppermute | solution.py:47
  48.5 1.0 copy-done.3
  49.5 0.1 fusion.1
  49.5 0.1 reshape.11.out_ref
  49.6 0.1 pad_maximum_fusion.3
  49.7 9.4 %collective-permute-start.14 = (f32[104]{0:T(128)S(1)}, f32[104]{0:T(128)S(1)}, u32[]{:S(2)}, u32[]{:S(2)}) collective-permute-start(f32[104]{0:T(128)S(1)} %pad_maximum_fusion.3), channel_id=1, source_target_pairs={{0,1},{1,0},{2,3},{3,2},{4,5},{5,4},{6,7},{7,6},{8,9},{9,8},{10,11... | collective-permute-start | bytes 1256 | tf_op jit(solution)/shard_map/ppermute | solution.py:47
  59.1 5.9 %collective-permute-done.9.refs_4_.refs_5_.refs_6_ = bf16[1024,512]{1,0:T(8,128)(2,1)} collective-permute-done((bf16[1024,512]{1,0:T(8,128)(2,1)}, bf16[1024,512]{1,0:T(8,128)(2,1)}, u32[]{:S(2)}, u32[]{:S(2)}) %collective-permute-start.9) | collective-permute-done | bytes 1048608 | tf_op jit(solution)/shard_map/ppermute | solution.py:47
  65.1 0.0 collective-permute-done.11.refs_5_.refs_6_.refs_7_
  65.1 3.2 %collective-permute-start.19 = (bf16[1024,512]{1,0:T(8,128)(2,1)}, bf16[1024,512]{1,0:T(8,128)(2,1)S(1)}, u32[]{:S(2)}, u32[]{:S(2)}) collective-permute-start(bf16[1024,512]{1,0:T(8,128)(2,1)} %collective-permute-done.11.refs_5_.refs_6_.refs_7_), channel_id=1, source_target_pairs={{0,6},{1,7},{2,0},{3,1},{4,2},{5,3},{6,4},{7,5},{8,14},{9,15},{10,... | collective-permute-start | bytes 3145736 | tf_op jit(solution)/shard_map/ppermute | solution.py:47
  68.3 0.0 collective-permute-done.13.refs_11_.refs_14_
  68.3 0.6 collective-permute-start.21
  68.9 1.4 %collective-permute-start.20 = (bf16[512,1024]{1,0:T(8,128)(2,1)}, bf16[512,1024]{1,0:T(8,128)(2,1)S(1)}, u32[]{:S(2)}, u32[]{:S(2)}) collective-permute-start(bf16[512,1024]{1,0:T(8,128)(2,1)} %collective-permute-done.13.refs_11_.refs_14_), channel_id=1, source_target_pairs={{0,16},{1,17},{2,18},{3,19},{4,20},{5,21},{6,22},{7,23},{8,24},{9,... | collective-permute-start | bytes 3145736 | tf_op jit(solution)/shard_map/ppermute | solution.py:47
  70.3 3.5 %collective-permute-start.22 = (bf16[512,1024]{1,0:T(8,128)(2,1)}, bf16[512,1024]{1,0:T(8,128)(2,1)S(1)}, u32[]{:S(2)}, u32[]{:S(2)}) collective-permute-start(bf16[512,1024]{1,0:T(8,128)(2,1)} %collective-permute-done.17.refs_10_.refs_13_), channel_id=1, source_target_pairs={{0,64},{1,65},{2,66},{3,67},{4,68},{5,69},{6,70},{7,71},{8,72},{9,... | collective-permute-start | bytes 3145736 | tf_op jit(solution)/shard_map/ppermute | solution.py:47
  73.8 1.2 %copy-done.1 = bf16[1024,512]{1,0:T(8,128)(2,1)S(1)} copy-done((bf16[1024,512]{1,0:T(8,128)(2,1)S(1)}, bf16[1024,512]{1,0:T(8,128)(2,1)}, u32[]{:S(2)}) %copy-start.1) | copy-done | bytes 1048600
  75.1 2.6 %plan.1.refs_0_ = s32[48]{0:T(128)S(1)} custom-call(f32[32]{0:T(128)S(1)} %pad_maximum_fusion.2.far_ref, f32[64]{0:T(128)S(1)} %slice_bitcast_fusion.right_ref, f32[8]{0:T(128)S(1)} %reshape.11.out_ref, f32[104]{0:T(128)S(1)} %collective-permute-done.14.other_ref, bf16[1024,512]{1,0:T(8,128)(2,1)S(1)} %divide_convert_fusion.refs_0_.refs_1_.refs_2_, ...), custom_call_target="tpu_custom_call" | custom-call | flops 1000000 | bytes 1024 | tf_op jit(solution)/shard_map/plan/pallas_call | solution.py:261
  77.7 8.3 %begin.1 = (f32[1024,512]{1,0:T(8,128)S(1)}, f32[1024,512]{1,0:T(8,128)S(1)}) custom-call(s32[48]{0:T(128)S(1)} %plan.1.refs_0_, bf16[1024,512]{1,0:T(8,128)(2,1)S(1)} %divide_convert_fusion.refs_0_.refs_1_.refs_2_, bf16[1024,512]{1,0:T(8,128)(2,1)S(1)} %copy-done.2, bf16[1024,512]{1,0:T(8,128)(2,1)S(1)} %collective-permute-done.10.refs_2_.refs_3_.refs_4_, ...), custom_call_target="tpu_custom_call" | custom-call | flops 1000000 | bytes 1024 | tf_op jit(solution)/shard_map/begin/pallas_call | solution.py:366
  86.1 2.3 %collective-permute-done.18.refs_8_ = bf16[1024,512]{1,0:T(8,128)(2,1)S(1)} collective-permute-done((bf16[1024,512]{1,0:T(8,128)(2,1)}, bf16[1024,512]{1,0:T(8,128)(2,1)S(1)}, u32[]{:S(2)}, u32[]{:S(2)}) %collective-permute-start.18) | collective-permute-done | bytes 1048608 | tf_op jit(solution)/shard_map/ppermute | solution.py:47
  88.4 3.8 %collective-permute-done.20.refs_15_ = bf16[512,1024]{1,0:T(8,128)(2,1)S(1)} collective-permute-done((bf16[512,1024]{1,0:T(8,128)(2,1)}, bf16[512,1024]{1,0:T(8,128)(2,1)S(1)}, u32[]{:S(2)}, u32[]{:S(2)}) %collective-permute-start.20) | collective-permute-done | bytes 1048608 | tf_op jit(solution)/shard_map/ppermute | solution.py:47
  92.2 4.6 %finish.3 = f32[1024,512]{1,0:T(8,128)S(1)} custom-call(s32[48]{0:T(128)S(1)} %plan.1.refs_0_, f32[1024,512]{1,0:T(8,128)S(1)} %get-tuple-element.46.refs_1_, bf16[1024,512]{1,0:T(8,128)(2,1)S(1)} %divide_convert_fusion.refs_0_.refs_1_.refs_2_, bf16[1024,512]{1,0:T(8,128)(2,1)S(1)} %copy-done.2, ...), custom_call_target="tpu_custom_call", output_to_operand_aliasing={{}: (1, {})} | custom-call | flops 1000000 | bytes 1024 | tf_op jit(solution)/shard_map/finish/pallas_call | solution.py:366
  96.9 6.8 %collective-permute-start.23 = (f32[1024,512]{1,0:T(8,128)S(1)}, f32[1024,512]{1,0:T(8,128)S(1)}, u32[]{:S(2)}, u32[]{:S(2)}) collective-permute-start(f32[1024,512]{1,0:T(8,128)S(1)} %finish.3), channel_id=1, source_target_pairs={{0,1},{1,0},{2,3},{3,2},{4,5},{5,4},{6,7},{7,6},{8,9},{9,8},{10,11... | collective-permute-start | bytes 6291464 | tf_op jit(solution)/shard_map/ppermute | solution.py:47
  103.7 4.7 %finish.2.mine_ref = f32[1024,512]{1,0:T(8,128)S(1)} custom-call(s32[48]{0:T(128)S(1)} %plan.1.refs_0_, f32[1024,512]{1,0:T(8,128)S(1)} %get-tuple-element.42.refs_1_, bf16[1024,512]{1,0:T(8,128)(2,1)S(1)} %divide_convert_fusion.refs_0_.refs_1_.refs_2_, bf16[1024,512]{1,0:T(8,128)(2,1)S(1)} %copy-done.2, ...), custom_call_target="tpu_custom_call", output_to_operand_aliasing={{}: (1, {})} | custom-call | flops 1000000 | bytes 1024 | tf_op jit(solution)/shard_map/finish/pallas_call | solution.py:366
  108.4 0.0 collective-permute-done.23.got_ref
  108.4 0.3 square.1
  108.7 0.1 collective-permute-start.26
  108.8 1.4 %collective-permute-start.25 = (f32[1,512]{1,0:T(1,128)S(1)}, f32[1,512]{1,0:T(1,128)S(1)}, u32[]{:S(2)}, u32[]{:S(2)}) collective-permute-start(f32[1,512]{1,0:T(1,128)S(1)} %get-tuple-element.48), channel_id=1, source_target_pairs={{0,32},{1,33},{2,34},{3,35},{4,36},{5,37},{6,38},{7,39},{8,40},{9,... | collective-permute-start | bytes 6152 | tf_op jit(solution)/shard_map/ppermute | solution.py:47
  110.2 1.3 %collective-permute-start.24 = (f32[1,512]{1,0:T(1,128)S(1)}, f32[1,512]{1,0:T(1,128)S(1)}, u32[]{:S(2)}, u32[]{:S(2)}) collective-permute-start(f32[1,512]{1,0:T(1,128)S(1)} %get-tuple-element.48), channel_id=1, source_target_pairs={{0,16},{1,17},{2,18},{3,19},{4,20},{5,21},{6,22},{7,23},{8,24},{9,... | collective-permute-start | bytes 6152 | tf_op jit(solution)/shard_map/ppermute | solution.py:47
  111.5 0.8 collective-permute-done.26
  112.4 1.6 %collective-permute-done.25 = f32[1,512]{1,0:T(1,128)S(1)} collective-permute-done((f32[1,512]{1,0:T(1,128)S(1)}, f32[1,512]{1,0:T(1,128)S(1)}, u32[]{:S(2)}, u32[]{:S(2)}) %collective-permute-start.25) | collective-permute-done | bytes 2080 | tf_op jit(solution)/shard_map/ppermute | solution.py:47
  114.0 1.1 collective-permute-done.24
  115.0 2.5 %collective-permute-start.27 = (f32[1,512]{1,0:T(1,128)S(1)}, f32[1,512]{1,0:T(1,128)S(1)}, u32[]{:S(2)}, u32[]{:S(2)}) collective-permute-start(f32[1,512]{1,0:T(1,128)S(1)} %add_add_fusion.1), channel_id=1, source_target_pairs={{0,64},{1,65},{2,66},{3,67},{4,68},{5,69},{6,70},{7,71},{8,72},{9,... | collective-permute-start | bytes 6152 | tf_op jit(solution)/shard_map/ppermute | solution.py:47
  117.5 2.6 %collective-permute-done.27 = f32[1,512]{1,0:T(1,128)S(1)} collective-permute-done((f32[1,512]{1,0:T(1,128)S(1)}, f32[1,512]{1,0:T(1,128)S(1)}, u32[]{:S(2)}, u32[]{:S(2)}) %collective-permute-start.27) | collective-permute-done | bytes 2080 | tf_op jit(solution)/shard_map/ppermute | solution.py:47
  120.1 1.5 %rescale.1 = f32[1024,512]{1,0:T(8,128)} custom-call(f32[1024,512]{1,0:T(8,128)S(1)} %get-tuple-element.47.value_ref, f32[1,512]{1,0:T(1,128)S(1)} %add.68.total_ref), custom_call_target="tpu_custom_call" | custom-call | tf_op jit(solution)/shard_map/rescale/pallas_call | solution.py:169
  (32 shorter events, 0.1 us)
Async XLA Ops:
  0.0 1.6 %copy-start.5 = (f32[1024,512]{1,0:T(8,128)S(1)}, f32[1024,512]{1,0:T(8,128)}, u32[]{:S(2)}) copy-start(f32[1024,512]{1,0:T(8,128)} %entries_in.1) | copy-start | bytes 6291460
  1.6 0.7 copy-start.6
  3.2 6.7 %collective-permute-start.2 = (f32[1,640]{1,0:T(1,128)S(1)}, f32[1,640]{1,0:T(1,128)S(1)}, u32[]{:S(2)}, u32[]{:S(2)}) collective-permute-start(f32[1,640]{1,0:T(1,128)S(1)} %get-tuple-element.28), channel_id=1, source_target_pairs={{0,48},{1,49},{2,50},{3,51},{4,52},{5,53},{6,54},{7,55},{8,56},{9,... | collective-permute-start | bytes 7688 | tf_op jit(solution)/shard_map/ppermute | solution.py:47
  7.3 5.1 %collective-permute-start.1 = (f32[1,640]{1,0:T(1,128)S(1)}, f32[1,640]{1,0:T(1,128)S(1)}, u32[]{:S(2)}, u32[]{:S(2)}) collective-permute-start(f32[1,640]{1,0:T(1,128)S(1)} %get-tuple-element.28), channel_id=1, source_target_pairs={{0,32},{1,33},{2,34},{3,35},{4,36},{5,37},{6,38},{7,39},{8,40},{9,... | collective-permute-start | bytes 7688 | tf_op jit(solution)/shard_map/ppermute | solution.py:47
  7.3 5.1 %collective-permute-start = (f32[1,640]{1,0:T(1,128)S(1)}, f32[1,640]{1,0:T(1,128)S(1)}, u32[]{:S(2)}, u32[]{:S(2)}) collective-permute-start(f32[1,640]{1,0:T(1,128)S(1)} %get-tuple-element.28), channel_id=1, source_target_pairs={{0,16},{1,17},{2,18},{3,19},{4,20},{5,21},{6,22},{7,23},{8,24},{9,... | collective-permute-start | bytes 7688 | tf_op jit(solution)/shard_map/ppermute | solution.py:47
  8.6 1.1 collective-permute-start.3
  12.5 5.2 %collective-permute-start.4 = (f32[1,640]{1,0:T(1,128)S(1)}, f32[1,640]{1,0:T(1,128)S(1)}, u32[]{:S(2)}, u32[]{:S(2)}) collective-permute-start(f32[1,640]{1,0:T(1,128)S(1)} %add_add_fusion), channel_id=1, source_target_pairs={{0,64},{1,65},{2,66},{3,67},{4,68},{5,69},{6,70},{7,71},{8,72},{9,... | collective-permute-start | bytes 7688 | tf_op jit(solution)/shard_map/ppermute | solution.py:47
  17.9 31.5 %copy-start.7 = (s32[4,2]{0,1:T(2,128)S(1)}, s32[4,2]{0,1:T(2,128)}, u32[]{:S(2)}) copy-start(s32[4,2]{0,1:T(2,128)} %param.5) | copy-start | bytes 100
  18.0 5.9 %collective-permute-start.12 = (bf16[512,512]{1,0:T(8,128)(2,1)S(1)}, bf16[512,512]{1,0:T(8,128)(2,1)S(1)}, u32[]{:S(2)}, u32[]{:S(2)}) collective-permute-start(bf16[512,512]{1,0:T(8,128)(2,1)S(1)} %get-tuple-element.50), channel_id=1, source_target_pairs={{0,1},{1,0},{2,3},{3,2},{4,5},{5,4},{6,7},{7,6},{8,9},{9,8},{10,11... | collective-permute-start | bytes 1572872 | tf_op jit(solution)/shard_map/ppermute | solution.py:47
  18.1 1.3 %collective-permute-start.6 = (f32[16]{0:T(128)S(1)}, f32[16]{0:T(128)S(1)}, u32[]{:S(2)}, u32[]{:S(2)}) collective-permute-start(f32[16]{0:T(128)S(1)} %pad_maximum_fusion.1), channel_id=1, source_target_pairs={{1,13},{3,15},{5,9},{7,11},{9,5},{11,7},{13,1},{15,3},{17,29},{19,... | collective-permute-start | bytes 200 | tf_op jit(solution)/shard_map/ppermute | solution.py:47
  18.8 0.7 collective-permute-start.5
  19.6 20.6 %collective-permute-start.10 = (bf16[1024,512]{1,0:T(8,128)(2,1)S(1)}, bf16[1024,512]{1,0:T(8,128)(2,1)S(1)}, u32[]{:S(2)}, u32[]{:S(2)}) collective-permute-start(bf16[1024,512]{1,0:T(8,128)(2,1)S(1)} %divide_convert_fusion.refs_0_.refs_1_.refs_2_), channel_id=1, source_target_pairs={{0,6},{1,7},{2,0},{3,1},{4,2},{5,3},{6,4},{7,5},{8,14},{9,15},{10,... | collective-permute-start | bytes 3145736 | tf_op jit(solution)/shard_map/ppermute | solution.py:47
  22.3 19.4 %collective-permute-start.8 = (bf16[1024,512]{1,0:T(8,128)(2,1)S(1)}, bf16[1024,512]{1,0:T(8,128)(2,1)S(1)}, u32[]{:S(2)}, u32[]{:S(2)}) collective-permute-start(bf16[1024,512]{1,0:T(8,128)(2,1)S(1)} %divide_convert_fusion.refs_0_.refs_1_.refs_2_), channel_id=1, source_target_pairs={{0,2},{1,3},{2,4},{3,5},{4,6},{5,7},{6,0},{7,1},{8,10},{9,11},{10,... | collective-permute-start | bytes 3145736 | tf_op jit(solution)/shard_map/ppermute | solution.py:47
  22.3 17.8 %collective-permute-start.7 = (bf16[1024,512]{1,0:T(8,128)(2,1)S(1)}, bf16[1024,512]{1,0:T(8,128)(2,1)}, u32[]{:S(2)}, u32[]{:S(2)}) collective-permute-start(bf16[1024,512]{1,0:T(8,128)(2,1)S(1)} %divide_convert_fusion.refs_0_.refs_1_.refs_2_), channel_id=1, source_target_pairs={{0,8},{1,9},{2,10},{3,11},{4,12},{5,13},{6,14},{7,15},{8,0},{9,1},... | collective-permute-start | bytes 3145736 | tf_op jit(solution)/shard_map/ppermute | solution.py:47
  24.0 24.4 %collective-permute-start.15 = (bf16[512,1024]{1,0:T(8,128)(2,1)S(1)}, bf16[512,1024]{1,0:T(8,128)(2,1)}, u32[]{:S(2)}, u32[]{:S(2)}) collective-permute-start(bf16[512,1024]{1,0:T(8,128)(2,1)S(1)} %pad_maximum_fusion.refs_7_.refs_10_), channel_id=1, source_target_pairs={{0,16},{1,17},{2,18},{3,19},{4,20},{5,21},{6,22},{7,23},{8,24},{9,... | collective-permute-start | bytes 3145736 | tf_op jit(solution)/shard_map/ppermute | solution.py:47
  24.1 24.4 %collective-permute-start.16 = (bf16[512,1024]{1,0:T(8,128)(2,1)S(1)}, bf16[512,1024]{1,0:T(8,128)(2,1)S(1)}, u32[]{:S(2)}, u32[]{:S(2)}) collective-permute-start(bf16[512,1024]{1,0:T(8,128)(2,1)S(1)} %pad_maximum_fusion.refs_7_.refs_10_), channel_id=1, source_target_pairs={{0,48},{1,49},{2,50},{3,51},{4,52},{5,53},{6,54},{7,55},{8,56},{9,... | collective-permute-start | bytes 3145736 | tf_op jit(solution)/shard_map/ppermute | solution.py:47
  41.7 6.7 %copy-start = (bf16[1024,512]{1,0:T(8,128)(2,1)}, bf16[1024,512]{1,0:T(8,128)(2,1)S(1)}, u32[]{:S(2)}) copy-start(bf16[1024,512]{1,0:T(8,128)(2,1)S(1)} %collective-permute-done.8.refs_1_.refs_2_.refs_3_) | copy-start | bytes 3145732
  41.7 23.3 %collective-permute-start.9 = (bf16[1024,512]{1,0:T(8,128)(2,1)}, bf16[1024,512]{1,0:T(8,128)(2,1)}, u32[]{:S(2)}, u32[]{:S(2)}) collective-permute-start(bf16[1024,512]{1,0:T(8,128)(2,1)} %collective-permute-done.7.refs_3_.refs_4_.refs_5_), channel_id=1, source_target_pairs={{0,2},{1,3},{2,4},{3,5},{4,6},{5,7},{6,0},{7,1},{8,10},{9,11},{10,... | collective-permute-start | bytes 3145736 | tf_op jit(solution)/shard_map/ppermute | solution.py:47
  41.7 23.3 %collective-permute-start.11 = (bf16[1024,512]{1,0:T(8,128)(2,1)}, bf16[1024,512]{1,0:T(8,128)(2,1)}, u32[]{:S(2)}, u32[]{:S(2)}) collective-permute-start(bf16[1024,512]{1,0:T(8,128)(2,1)} %collective-permute-done.7.refs_3_.refs_4_.refs_5_), channel_id=1, source_target_pairs={{0,6},{1,7},{2,0},{3,1},{4,2},{5,3},{6,4},{7,5},{8,14},{9,15},{10,... | collective-permute-start | bytes 3145736 | tf_op jit(solution)/shard_map/ppermute | solution.py:47
  45.0 23.3 %collective-permute-start.13 = (bf16[512,1024]{1,0:T(8,128)(2,1)S(1)}, bf16[512,1024]{1,0:T(8,128)(2,1)}, u32[]{:S(2)}, u32[]{:S(2)}) collective-permute-start(bf16[512,1024]{1,0:T(8,128)(2,1)S(1)} %pad_maximum_fusion.refs_7_.refs_10_), channel_id=1, source_target_pairs={{0,64},{1,65},{2,66},{3,67},{4,68},{5,69},{6,70},{7,71},{8,72},{9,... | collective-permute-start | bytes 3145736 | tf_op jit(solution)/shard_map/ppermute | solution.py:47
  48.5 1.0 copy-start.3
  49.4 19.5 %collective-permute-start.17 = (bf16[512,1024]{1,0:T(8,128)(2,1)}, bf16[512,1024]{1,0:T(8,128)(2,1)}, u32[]{:S(2)}, u32[]{:S(2)}) collective-permute-start(bf16[512,1024]{1,0:T(8,128)(2,1)} %collective-permute-done.15.refs_8_.refs_11_), channel_id=1, source_target_pairs={{0,16},{1,17},{2,18},{3,19},{4,20},{5,21},{6,22},{7,23},{8,24},{9,... | collective-permute-start | bytes 3145736 | tf_op jit(solution)/shard_map/ppermute | solution.py:47
  49.7 20.6 %collective-permute-start.14 = (f32[104]{0:T(128)S(1)}, f32[104]{0:T(128)S(1)}, u32[]{:S(2)}, u32[]{:S(2)}) collective-permute-start(f32[104]{0:T(128)S(1)} %pad_maximum_fusion.3), channel_id=1, source_target_pairs={{0,1},{1,0},{2,3},{3,2},{4,5},{5,4},{6,7},{7,6},{8,9},{9,8},{10,11... | collective-permute-start | bytes 1256 | tf_op jit(solution)/shard_map/ppermute | solution.py:47
  65.0 23.3 %collective-permute-start.18 = (bf16[1024,512]{1,0:T(8,128)(2,1)}, bf16[1024,512]{1,0:T(8,128)(2,1)S(1)}, u32[]{:S(2)}, u32[]{:S(2)}) collective-permute-start(bf16[1024,512]{1,0:T(8,128)(2,1)} %copy-done), channel_id=1, source_target_pairs={{0,2},{1,3},{2,4},{3,5},{4,6},{5,7},{6,0},{7,1},{8,10},{9,11},{10,... | collective-permute-start | bytes 3145736 | tf_op jit(solution)/shard_map/ppermute | solution.py:47
  65.1 23.3 %collective-permute-start.19 = (bf16[1024,512]{1,0:T(8,128)(2,1)}, bf16[1024,512]{1,0:T(8,128)(2,1)S(1)}, u32[]{:S(2)}, u32[]{:S(2)}) collective-permute-start(bf16[1024,512]{1,0:T(8,128)(2,1)} %collective-permute-done.11.refs_5_.refs_6_.refs_7_), channel_id=1, source_target_pairs={{0,6},{1,7},{2,0},{3,1},{4,2},{5,3},{6,4},{7,5},{8,14},{9,15},{10,... | collective-permute-start | bytes 3145736 | tf_op jit(solution)/shard_map/ppermute | solution.py:47
  68.3 20.1 %collective-permute-start.21 = (bf16[512,1024]{1,0:T(8,128)(2,1)}, bf16[512,1024]{1,0:T(8,128)(2,1)S(1)}, u32[]{:S(2)}, u32[]{:S(2)}) collective-permute-start(bf16[512,1024]{1,0:T(8,128)(2,1)} %collective-permute-done.13.refs_11_.refs_14_), channel_id=1, source_target_pairs={{0,48},{1,49},{2,50},{3,51},{4,52},{5,53},{6,54},{7,55},{8,56},{9,... | collective-permute-start | bytes 3145736 | tf_op jit(solution)/shard_map/ppermute | solution.py:47
  68.9 23.3 %collective-permute-start.20 = (bf16[512,1024]{1,0:T(8,128)(2,1)}, bf16[512,1024]{1,0:T(8,128)(2,1)S(1)}, u32[]{:S(2)}, u32[]{:S(2)}) collective-permute-start(bf16[512,1024]{1,0:T(8,128)(2,1)} %collective-permute-done.13.refs_11_.refs_14_), channel_id=1, source_target_pairs={{0,16},{1,17},{2,18},{3,19},{4,20},{5,21},{6,22},{7,23},{8,24},{9,... | collective-permute-start | bytes 3145736 | tf_op jit(solution)/shard_map/ppermute | solution.py:47
  70.3 21.9 %collective-permute-start.22 = (bf16[512,1024]{1,0:T(8,128)(2,1)}, bf16[512,1024]{1,0:T(8,128)(2,1)S(1)}, u32[]{:S(2)}, u32[]{:S(2)}) collective-permute-start(bf16[512,1024]{1,0:T(8,128)(2,1)} %collective-permute-done.17.refs_10_.refs_13_), channel_id=1, source_target_pairs={{0,64},{1,65},{2,66},{3,67},{4,68},{5,69},{6,70},{7,71},{8,72},{9,... | collective-permute-start | bytes 3145736 | tf_op jit(solution)/shard_map/ppermute | solution.py:47
  73.8 1.2 %copy-start.1 = (bf16[1024,512]{1,0:T(8,128)(2,1)S(1)}, bf16[1024,512]{1,0:T(8,128)(2,1)}, u32[]{:S(2)}) copy-start(bf16[1024,512]{1,0:T(8,128)(2,1)} %copy-done) | copy-start | bytes 3145732
  75.0 2.7 %copy-start.2 = (bf16[1024,512]{1,0:T(8,128)(2,1)S(1)}, bf16[1024,512]{1,0:T(8,128)(2,1)}, u32[]{:S(2)}) copy-start(bf16[1024,512]{1,0:T(8,128)(2,1)} %copy-done) | copy-start | bytes 3145732
  75.1 2.7 %copy-start.4 = (bf16[512,1024]{1,0:T(8,128)(2,1)S(1)}, bf16[512,1024]{1,0:T(8,128)(2,1)}, u32[]{:S(2)}) copy-start(bf16[512,1024]{1,0:T(8,128)(2,1)} %copy-done.3) | copy-start | bytes 3145732
  96.9 11.5 %collective-permute-start.23 = (f32[1024,512]{1,0:T(8,128)S(1)}, f32[1024,512]{1,0:T(8,128)S(1)}, u32[]{:S(2)}, u32[]{:S(2)}) collective-permute-start(f32[1024,512]{1,0:T(8,128)S(1)} %finish.3), channel_id=1, source_target_pairs={{0,1},{1,0},{2,3},{3,2},{4,5},{5,4},{6,7},{7,6},{8,9},{9,8},{10,11... | collective-permute-start | bytes 6291464 | tf_op jit(solution)/shard_map/ppermute | solution.py:47
  108.7 3.7 %collective-permute-start.26 = (f32[1,512]{1,0:T(1,128)S(1)}, f32[1,512]{1,0:T(1,128)S(1)}, u32[]{:S(2)}, u32[]{:S(2)}) collective-permute-start(f32[1,512]{1,0:T(1,128)S(1)} %get-tuple-element.48), channel_id=1, source_target_pairs={{0,48},{1,49},{2,50},{3,51},{4,52},{5,53},{6,54},{7,55},{8,56},{9,... | collective-permute-start | bytes 6152 | tf_op jit(solution)/shard_map/ppermute | solution.py:47
  108.8 5.2 %collective-permute-start.25 = (f32[1,512]{1,0:T(1,128)S(1)}, f32[1,512]{1,0:T(1,128)S(1)}, u32[]{:S(2)}, u32[]{:S(2)}) collective-permute-start(f32[1,512]{1,0:T(1,128)S(1)} %get-tuple-element.48), channel_id=1, source_target_pairs={{0,32},{1,33},{2,34},{3,35},{4,36},{5,37},{6,38},{7,39},{8,40},{9,... | collective-permute-start | bytes 6152 | tf_op jit(solution)/shard_map/ppermute | solution.py:47
  110.2 4.9 %collective-permute-start.24 = (f32[1,512]{1,0:T(1,128)S(1)}, f32[1,512]{1,0:T(1,128)S(1)}, u32[]{:S(2)}, u32[]{:S(2)}) collective-permute-start(f32[1,512]{1,0:T(1,128)S(1)} %get-tuple-element.48), channel_id=1, source_target_pairs={{0,16},{1,17},{2,18},{3,19},{4,20},{5,21},{6,22},{7,23},{8,24},{9,... | collective-permute-start | bytes 6152 | tf_op jit(solution)/shard_map/ppermute | solution.py:47
  115.0 5.1 %collective-permute-start.27 = (f32[1,512]{1,0:T(1,128)S(1)}, f32[1,512]{1,0:T(1,128)S(1)}, u32[]{:S(2)}, u32[]{:S(2)}) collective-permute-start(f32[1,512]{1,0:T(1,128)S(1)} %add_add_fusion.1), channel_id=1, source_target_pairs={{0,64},{1,65},{2,66},{3,67},{4,68},{5,69},{6,70},{7,71},{8,72},{9,... | collective-permute-start | bytes 6152 | tf_op jit(solution)/shard_map/ppermute | solution.py:47

commit v7 on v6

--- a/solution.py
+++ b/solution.py
@@ -413,8 +413,8 @@
 
     xl, xr, pa = move(a, X_UP), move(a, X_DOWN), move(a, SWAP_YL)
     zl, zr = move(after(b, far), Z_UP), move(b, Z_DOWN)
-    pxl, pxr = move(after(pa, xl), X_UP), move(after(pa, xr), X_DOWN)
-    zf, pb = move(after(zl, zr), Z_UP), move(after(b, pa), SWAP_YH)
+    pxl, pxr = move(after(pa, xl), X_UP), move(after(pa, xr, zl, zr), X_DOWN)
+    zf, pb = move(after(zl, zr), Z_UP), move(after(b, pa, xl), SWAP_YH)
     xf, pxf = move(after(xl, pxl), X_UP), move(pxr, X_DOWN)
     pzl, pzr, pzf = move(after(pb, zf), Z_UP), move(pb, Z_DOWN), move(after(zf, pb), SWAP_YH)
     notes_o, far, right = after(notes_o, pxl, pxr, pb), after(far, pxl, pxr, pb), after(right, pxl, pxr, pb)

time: 123 us -> 121 us (0.984)
  Pallas kernels: 23 us -> 18.8 us
  starting transfers between devices: 54.8 us -> 56.5 us
    pallas_call x3, Pallas kernels: 17.7 us -> 13.5 us  [product(): pl.pallas_call(functools.partial(product_kernel, len(a_units), len(b_unit...]
    ppermute x28, starting transfers between devices: 54.8 us -> 56.5 us  [move(): return lax.ppermute(value, AXES, perm)]
  transfers between devices with their start and end apart: 28 -> 28, of which waited for: 12 -> 14; matrix products, arithmetic and copies ran while one was open for 0% -> 0% of each run, Pallas kernels for 13% -> 10%
where the time goes in v7:
time: 121 us
  starting transfers between devices  56.5 us (47%)
  waiting for transfers between devices  38.9 us (32%)
  Pallas kernels  18.8 us (16%)
  local copies, waits for them, and re-layouts  5.61 us (5%)
    ppermute x28, starting transfers between devices, move(): return lax.ppermute(value, AXES, perm)  56.5 us
    ppermute x28, waiting for transfers between devices, move(): return lax.ppermute(value, AXES, perm)  38.9 us
    pallas_call x3, Pallas kernels, product(): pl.pallas_call(functools.partial(product_kernel, len(a_units), len(b_unit...  13.5 us
    unnamed x16, local copies, waits for them, and re-layouts  5.44 us
    pallas_call x1, Pallas kernels, planned(): pl.pallas_call(functools.partial(plan_kernel, rows, cols), out_shape=jax....  2.64 us
  transfers between devices with their start and end apart: 28, of which 14 were waited for; matrix products, arithmetic and copies ran while one was open for 0% of the time, Pallas kernels for 10%

profile of v7, /device:TPU:0, one launch (start us, length us, event | category | flops | bytes accessed | tf_op | source)
XLA Modules:
  0.0 120.7 jit_solution(4501110847948440382)
XLA Ops:
  0.0 1.6 %copy-done.5 = f32[1024,512]{1,0:T(8,128)S(1)} copy-done((f32[1024,512]{1,0:T(8,128)S(1)}, f32[1024,512]{1,0:T(8,128)}, u32[]{:S(2)}) %copy-start.5) | copy-done | bytes 2097176
  1.6 0.7 copy-done.6
  2.3 0.9 mask.1
  3.2 4.2 %collective-permute-start.2 = (f32[1,640]{1,0:T(1,128)S(1)}, f32[1,640]{1,0:T(1,128)S(1)}, u32[]{:S(2)}, u32[]{:S(2)}) collective-permute-start(f32[1,640]{1,0:T(1,128)S(1)} %get-tuple-element.28), channel_id=1, source_target_pairs={{0,48},{1,49},{2,50},{3,51},{4,52},{5,53},{6,54},{7,55},{8,56},{9,... | collective-permute-start | bytes 7688 | tf_op jit(solution)/shard_map/ppermute | solution.py:47
  7.3 0.0 collective-permute-start.1
  7.3 1.3 %collective-permute-start = (f32[1,640]{1,0:T(1,128)S(1)}, f32[1,640]{1,0:T(1,128)S(1)}, u32[]{:S(2)}, u32[]{:S(2)}) collective-permute-start(f32[1,640]{1,0:T(1,128)S(1)} %get-tuple-element.28), channel_id=1, source_target_pairs={{0,16},{1,17},{2,18},{3,19},{4,20},{5,21},{6,22},{7,23},{8,24},{9,... | collective-permute-start | bytes 7688 | tf_op jit(solution)/shard_map/ppermute | solution.py:47
  8.6 0.0 collective-permute-start.3
  8.6 1.1 collective-permute-done.3
  9.7 0.1 pad_maximum_fusion.1
  9.8 2.6 %collective-permute-done.1 = f32[1,640]{1,0:T(1,128)S(1)} collective-permute-done((f32[1,640]{1,0:T(1,128)S(1)}, f32[1,640]{1,0:T(1,128)S(1)}, u32[]{:S(2)}, u32[]{:S(2)}) %collective-permute-start.1) | collective-permute-done | bytes 2592 | tf_op jit(solution)/shard_map/ppermute | solution.py:47
  12.5 3.3 %collective-permute-start.4 = (f32[1,640]{1,0:T(1,128)S(1)}, f32[1,640]{1,0:T(1,128)S(1)}, u32[]{:S(2)}, u32[]{:S(2)}) collective-permute-start(f32[1,640]{1,0:T(1,128)S(1)} %add_add_fusion), channel_id=1, source_target_pairs={{0,64},{1,65},{2,66},{3,67},{4,68},{5,69},{6,70},{7,71},{8,72},{9,... | collective-permute-start | bytes 7688 | tf_op jit(solution)/shard_map/ppermute | solution.py:47
  15.7 1.9 %collective-permute-done.4 = f32[1,640]{1,0:T(1,128)S(1)} collective-permute-done((f32[1,640]{1,0:T(1,128)S(1)}, f32[1,640]{1,0:T(1,128)S(1)}, u32[]{:S(2)}, u32[]{:S(2)}) %collective-permute-start.4) | collective-permute-done | bytes 2592 | tf_op jit(solution)/shard_map/ppermute | solution.py:47
  17.6 0.3 divide_convert_fusion.refs_0_.refs_1_.refs_2_
  17.9 0.0 copy-start.7
  17.9 0.1 constant_dynamic-slice_fusion.1
  18.0 0.1 collective-permute-start.11
  18.1 0.7 collective-permute-start.6
  18.8 0.7 collective-permute-start.5
  19.5 0.0 collective-permute-done.5
  19.5 0.1 pad_maximum_fusion.2.far_ref
  19.6 1.5 %collective-permute-start.8 = (bf16[1024,512]{1,0:T(8,128)(2,1)S(1)}, bf16[1024,512]{1,0:T(8,128)(2,1)S(1)}, u32[]{:S(2)}, u32[]{:S(2)}) collective-permute-start(bf16[1024,512]{1,0:T(8,128)(2,1)S(1)} %divide_convert_fusion.refs_0_.refs_1_.refs_2_), channel_id=1, source_target_pairs={{0,2},{1,3},{2,4},{3,5},{4,6},{5,7},{6,0},{7,1},{8,10},{9,11},{10,... | collective-permute-start | bytes 3145736 | tf_op jit(solution)/shard_map/ppermute | solution.py:47
  21.1 1.6 %collective-permute-start.7 = (bf16[1024,512]{1,0:T(8,128)(2,1)S(1)}, bf16[1024,512]{1,0:T(8,128)(2,1)}, u32[]{:S(2)}, u32[]{:S(2)}) collective-permute-start(bf16[1024,512]{1,0:T(8,128)(2,1)S(1)} %divide_convert_fusion.refs_0_.refs_1_.refs_2_), channel_id=1, source_target_pairs={{0,8},{1,9},{2,10},{3,11},{4,12},{5,13},{6,14},{7,15},{8,0},{9,1},... | collective-permute-start | bytes 3145736 | tf_op jit(solution)/shard_map/ppermute | solution.py:47
  22.6 0.1 pad_maximum_fusion.refs_7_.refs_10_
  22.8 0.1 collective-permute-start.12
  22.8 3.2 %collective-permute-start.13 = (bf16[512,1024]{1,0:T(8,128)(2,1)S(1)}, bf16[512,1024]{1,0:T(8,128)(2,1)S(1)}, u32[]{:S(2)}, u32[]{:S(2)}) collective-permute-start(bf16[512,1024]{1,0:T(8,128)(2,1)S(1)} %pad_maximum_fusion.refs_7_.refs_10_), channel_id=1, source_target_pairs={{0,48},{1,49},{2,50},{3,51},{4,52},{5,53},{6,54},{7,55},{8,56},{9,... | collective-permute-start | bytes 3145736 | tf_op jit(solution)/shard_map/ppermute | solution.py:47
  26.1 1.7 %collective-permute-start.10 = (bf16[1024,512]{1,0:T(8,128)(2,1)S(1)}, bf16[1024,512]{1,0:T(8,128)(2,1)S(1)}, u32[]{:S(2)}, u32[]{:S(2)}) collective-permute-start(bf16[1024,512]{1,0:T(8,128)(2,1)S(1)} %divide_convert_fusion.refs_0_.refs_1_.refs_2_), channel_id=1, source_target_pairs={{0,6},{1,7},{2,0},{3,1},{4,2},{5,3},{6,4},{7,5},{8,14},{9,15},{10,... | collective-permute-start | bytes 3145736 | tf_op jit(solution)/shard_map/ppermute | solution.py:47
  27.8 9.3 %collective-permute-done.8.refs_1_.refs_2_.refs_3_ = bf16[1024,512]{1,0:T(8,128)(2,1)S(1)} collective-permute-done((bf16[1024,512]{1,0:T(8,128)(2,1)S(1)}, bf16[1024,512]{1,0:T(8,128)(2,1)S(1)}, u32[]{:S(2)}, u32[]{:S(2)}) %collective-permute-start.8) | collective-permute-done | bytes 1048608 | tf_op jit(solution)/shard_map/ppermute | solution.py:47
  37.1 1.3 %collective-permute-done.7.refs_3_.refs_4_.refs_5_ = bf16[1024,512]{1,0:T(8,128)(2,1)} collective-permute-done((bf16[1024,512]{1,0:T(8,128)(2,1)S(1)}, bf16[1024,512]{1,0:T(8,128)(2,1)}, u32[]{:S(2)}, u32[]{:S(2)}) %collective-permute-start.7) | collective-permute-done | bytes 1048608 | tf_op jit(solution)/shard_map/ppermute | solution.py:47
  38.4 2.6 %collective-permute-start.9 = (bf16[1024,512]{1,0:T(8,128)(2,1)}, bf16[1024,512]{1,0:T(8,128)(2,1)}, u32[]{:S(2)}, u32[]{:S(2)}) collective-permute-start(bf16[1024,512]{1,0:T(8,128)(2,1)} %collective-permute-done.7.refs_3_.refs_4_.refs_5_), channel_id=1, source_target_pairs={{0,2},{1,3},{2,4},{3,5},{4,6},{5,7},{6,0},{7,1},{8,10},{9,11},{10,... | collective-permute-start | bytes 3145736 | tf_op jit(solution)/shard_map/ppermute | solution.py:47
  41.0 3.4 %collective-permute-start.15 = (bf16[512,1024]{1,0:T(8,128)(2,1)S(1)}, bf16[512,1024]{1,0:T(8,128)(2,1)}, u32[]{:S(2)}, u32[]{:S(2)}) collective-permute-start(bf16[512,1024]{1,0:T(8,128)(2,1)S(1)} %pad_maximum_fusion.refs_7_.refs_10_), channel_id=1, source_target_pairs={{0,64},{1,65},{2,66},{3,67},{4,68},{5,69},{6,70},{7,71},{8,72},{9,... | collective-permute-start | bytes 3145736 | tf_op jit(solution)/shard_map/ppermute | solution.py:47
  44.4 1.0 copy-done.3
  45.4 0.1 collective-permute-start.17
  45.5 1.0 copy-done
  46.5 2.0 %collective-permute-start.14 = (bf16[1024,512]{1,0:T(8,128)(2,1)}, bf16[1024,512]{1,0:T(8,128)(2,1)}, u32[]{:S(2)}, u32[]{:S(2)}) collective-permute-start(bf16[1024,512]{1,0:T(8,128)(2,1)} %collective-permute-done.7.refs_3_.refs_4_.refs_5_), channel_id=1, source_target_pairs={{0,6},{1,7},{2,0},{3,1},{4,2},{5,3},{6,4},{7,5},{8,14},{9,15},{10,... | collective-permute-start | bytes 3145736 | tf_op jit(solution)/shard_map/ppermute | solution.py:47
  48.5 0.1 fusion.1
  48.6 0.1 reshape.11.out_ref
  48.7 0.1 pad_maximum_fusion.3
  48.8 9.2 %collective-permute-start.16 = (f32[104]{0:T(128)S(1)}, f32[104]{0:T(128)S(1)}, u32[]{:S(2)}, u32[]{:S(2)}) collective-permute-start(f32[104]{0:T(128)S(1)} %pad_maximum_fusion.3), channel_id=1, source_target_pairs={{0,1},{1,0},{2,3},{3,2},{4,5},{5,4},{6,7},{7,6},{8,9},{9,8},{10,11... | collective-permute-start | bytes 1256 | tf_op jit(solution)/shard_map/ppermute | solution.py:47
  58.0 3.7 %collective-permute-done.9.refs_4_.refs_5_.refs_6_ = bf16[1024,512]{1,0:T(8,128)(2,1)} collective-permute-done((bf16[1024,512]{1,0:T(8,128)(2,1)}, bf16[1024,512]{1,0:T(8,128)(2,1)}, u32[]{:S(2)}, u32[]{:S(2)}) %collective-permute-start.9) | collective-permute-done | bytes 1048608 | tf_op jit(solution)/shard_map/ppermute | solution.py:47
  61.7 1.5 %collective-permute-start.18 = (bf16[1024,512]{1,0:T(8,128)(2,1)S(1)}, bf16[1024,512]{1,0:T(8,128)(2,1)S(1)}, u32[]{:S(2)}, u32[]{:S(2)}) collective-permute-start(bf16[1024,512]{1,0:T(8,128)(2,1)S(1)} %collective-permute-done.8.refs_1_.refs_2_.refs_3_), channel_id=1, source_target_pairs={{0,2},{1,3},{2,4},{3,5},{4,6},{5,7},{6,0},{7,1},{8,10},{9,11},{10,... | collective-permute-start | bytes 3145736 | tf_op jit(solution)/shard_map/ppermute | solution.py:47
  63.2 3.4 %collective-permute-done.15.refs_11_.refs_14_ = bf16[512,1024]{1,0:T(8,128)(2,1)} collective-permute-done((bf16[512,1024]{1,0:T(8,128)(2,1)S(1)}, bf16[512,1024]{1,0:T(8,128)(2,1)}, u32[]{:S(2)}, u32[]{:S(2)}) %collective-permute-start.15) | collective-permute-done | bytes 1048608 | tf_op jit(solution)/shard_map/ppermute | solution.py:47
  66.7 0.6 collective-permute-start.21
  67.2 1.4 %collective-permute-start.20 = (bf16[512,1024]{1,0:T(8,128)(2,1)}, bf16[512,1024]{1,0:T(8,128)(2,1)S(1)}, u32[]{:S(2)}, u32[]{:S(2)}) collective-permute-start(bf16[512,1024]{1,0:T(8,128)(2,1)} %collective-permute-done.15.refs_11_.refs_14_), channel_id=1, source_target_pairs={{0,16},{1,17},{2,18},{3,19},{4,20},{5,21},{6,22},{7,23},{8,24},{9,... | collective-permute-start | bytes 3145736 | tf_op jit(solution)/shard_map/ppermute | solution.py:47
  68.7 1.9 %collective-permute-start.19 = (bf16[1024,512]{1,0:T(8,128)(2,1)}, bf16[1024,512]{1,0:T(8,128)(2,1)S(1)}, u32[]{:S(2)}, u32[]{:S(2)}) collective-permute-start(bf16[1024,512]{1,0:T(8,128)(2,1)} %collective-permute-done.14.refs_5_.refs_6_.refs_7_), channel_id=1, source_target_pairs={{0,6},{1,7},{2,0},{3,1},{4,2},{5,3},{6,4},{7,5},{8,14},{9,15},{10,... | collective-permute-start | bytes 3145736 | tf_op jit(solution)/shard_map/ppermute | solution.py:47
  70.6 2.9 %collective-permute-start.22 = (bf16[512,1024]{1,0:T(8,128)(2,1)}, bf16[512,1024]{1,0:T(8,128)(2,1)S(1)}, u32[]{:S(2)}, u32[]{:S(2)}) collective-permute-start(bf16[512,1024]{1,0:T(8,128)(2,1)} %collective-permute-done.17.refs_10_.refs_13_), channel_id=1, source_target_pairs={{0,64},{1,65},{2,66},{3,67},{4,68},{5,69},{6,70},{7,71},{8,72},{9,... | collective-permute-start | bytes 3145736 | tf_op jit(solution)/shard_map/ppermute | solution.py:47
  73.5 1.2 %copy-done.1 = bf16[1024,512]{1,0:T(8,128)(2,1)S(1)} copy-done((bf16[1024,512]{1,0:T(8,128)(2,1)S(1)}, bf16[1024,512]{1,0:T(8,128)(2,1)}, u32[]{:S(2)}) %copy-start.1) | copy-done | bytes 1048600
  74.7 2.6 %plan.1.refs_0_ = s32[48]{0:T(128)S(1)} custom-call(f32[32]{0:T(128)S(1)} %pad_maximum_fusion.2.far_ref, f32[64]{0:T(128)S(1)} %slice_bitcast_fusion.right_ref, f32[8]{0:T(128)S(1)} %reshape.11.out_ref, f32[104]{0:T(128)S(1)} %collective-permute-done.16.other_ref, bf16[1024,512]{1,0:T(8,128)(2,1)S(1)} %divide_convert_fusion.refs_0_.refs_1_.refs_2_, ...), custom_call_target="tpu_custom_call" | custom-call | flops 1000000 | bytes 1024 | tf_op jit(solution)/shard_map/plan/pallas_call | solution.py:261
  77.4 6.1 %begin.1 = (f32[1024,512]{1,0:T(8,128)S(1)}, f32[1024,512]{1,0:T(8,128)S(1)}) custom-call(s32[48]{0:T(128)S(1)} %plan.1.refs_0_, bf16[1024,512]{1,0:T(8,128)(2,1)S(1)} %divide_convert_fusion.refs_0_.refs_1_.refs_2_, bf16[1024,512]{1,0:T(8,128)(2,1)S(1)} %collective-permute-done.8.refs_1_.refs_2_.refs_3_, bf16[1024,512]{1,0:T(8,128)(2,1)S(1)} %copy-done.2, ...), custom_call_target="tpu_custom_call" | custom-call | flops 1000000 | bytes 1024 | tf_op jit(solution)/shard_map/begin/pallas_call | solution.py:366
  83.5 1.6 %collective-permute-done.18.refs_8_ = bf16[1024,512]{1,0:T(8,128)(2,1)S(1)} collective-permute-done((bf16[1024,512]{1,0:T(8,128)(2,1)S(1)}, bf16[1024,512]{1,0:T(8,128)(2,1)S(1)}, u32[]{:S(2)}, u32[]{:S(2)}) %collective-permute-start.18) | collective-permute-done | bytes 1048608 | tf_op jit(solution)/shard_map/ppermute | solution.py:47
  85.1 3.3 %collective-permute-done.21.refs_16_ = bf16[512,1024]{1,0:T(8,128)(2,1)S(1)} collective-permute-done((bf16[512,1024]{1,0:T(8,128)(2,1)}, bf16[512,1024]{1,0:T(8,128)(2,1)S(1)}, u32[]{:S(2)}, u32[]{:S(2)}) %collective-permute-start.21) | collective-permute-done | bytes 1048608 | tf_op jit(solution)/shard_map/ppermute | solution.py:47
  88.3 3.1 %collective-permute-done.19.refs_9_ = bf16[1024,512]{1,0:T(8,128)(2,1)S(1)} collective-permute-done((bf16[1024,512]{1,0:T(8,128)(2,1)}, bf16[1024,512]{1,0:T(8,128)(2,1)S(1)}, u32[]{:S(2)}, u32[]{:S(2)}) %collective-permute-start.19) | collective-permute-done | bytes 1048608 | tf_op jit(solution)/shard_map/ppermute | solution.py:47
  91.5 3.7 %finish.3 = f32[1024,512]{1,0:T(8,128)S(1)} custom-call(s32[48]{0:T(128)S(1)} %plan.1.refs_0_, f32[1024,512]{1,0:T(8,128)S(1)} %get-tuple-element.46.refs_1_, bf16[1024,512]{1,0:T(8,128)(2,1)S(1)} %divide_convert_fusion.refs_0_.refs_1_.refs_2_, bf16[1024,512]{1,0:T(8,128)(2,1)S(1)} %collective-permute-done.8.refs_1_.refs_2_.refs_3_, ...), custom_call_target="tpu_custom_call", output_to_operand_aliasing={{}: (1, {})} | custom-call | flops 1000000 | bytes 1024 | tf_op jit(solution)/shard_map/finish/pallas_call | solution.py:366
  95.2 5.3 %collective-permute-start.23 = (f32[1024,512]{1,0:T(8,128)S(1)}, f32[1024,512]{1,0:T(8,128)S(1)}, u32[]{:S(2)}, u32[]{:S(2)}) collective-permute-start(f32[1024,512]{1,0:T(8,128)S(1)} %finish.3), channel_id=1, source_target_pairs={{0,1},{1,0},{2,3},{3,2},{4,5},{5,4},{6,7},{7,6},{8,9},{9,8},{10,11... | collective-permute-start | bytes 6291464 | tf_op jit(solution)/shard_map/ppermute | solution.py:47
  100.5 3.7 %finish.2.mine_ref = f32[1024,512]{1,0:T(8,128)S(1)} custom-call(s32[48]{0:T(128)S(1)} %plan.1.refs_0_, f32[1024,512]{1,0:T(8,128)S(1)} %get-tuple-element.42.refs_1_, bf16[1024,512]{1,0:T(8,128)(2,1)S(1)} %divide_convert_fusion.refs_0_.refs_1_.refs_2_, ...), custom_call_target="tpu_custom_call", output_to_operand_aliasing={{}: (1, {})} | custom-call | flops 1000000 | bytes 1024 | tf_op jit(solution)/shard_map/finish/pallas_call | solution.py:366
  104.2 0.1 collective-permute-done.23.got_ref
  104.3 0.3 square.1
  104.6 4.3 %collective-permute-start.26 = (f32[1,512]{1,0:T(1,128)S(1)}, f32[1,512]{1,0:T(1,128)S(1)}, u32[]{:S(2)}, u32[]{:S(2)}) collective-permute-start(f32[1,512]{1,0:T(1,128)S(1)} %get-tuple-element.48), channel_id=1, source_target_pairs={{0,48},{1,49},{2,50},{3,51},{4,52},{5,53},{6,54},{7,55},{8,56},{9,... | collective-permute-start | bytes 6152 | tf_op jit(solution)/shard_map/ppermute | solution.py:47
  108.9 0.4 collective-permute-start.25
  109.3 1.3 %collective-permute-start.24 = (f32[1,512]{1,0:T(1,128)S(1)}, f32[1,512]{1,0:T(1,128)S(1)}, u32[]{:S(2)}, u32[]{:S(2)}) collective-permute-start(f32[1,512]{1,0:T(1,128)S(1)} %get-tuple-element.48), channel_id=1, source_target_pairs={{0,16},{1,17},{2,18},{3,19},{4,20},{5,21},{6,22},{7,23},{8,24},{9,... | collective-permute-start | bytes 6152 | tf_op jit(solution)/shard_map/ppermute | solution.py:47
  110.6 3.4 %collective-permute-done.25 = f32[1,512]{1,0:T(1,128)S(1)} collective-permute-done((f32[1,512]{1,0:T(1,128)S(1)}, f32[1,512]{1,0:T(1,128)S(1)}, u32[]{:S(2)}, u32[]{:S(2)}) %collective-permute-start.25) | collective-permute-done | bytes 2080 | tf_op jit(solution)/shard_map/ppermute | solution.py:47
  114.0 0.1 collective-permute-done.24
  114.1 1.2 %collective-permute-start.27 = (f32[1,512]{1,0:T(1,128)S(1)}, f32[1,512]{1,0:T(1,128)S(1)}, u32[]{:S(2)}, u32[]{:S(2)}) collective-permute-start(f32[1,512]{1,0:T(1,128)S(1)} %add_add_fusion.1), channel_id=1, source_target_pairs={{0,64},{1,65},{2,66},{3,67},{4,68},{5,69},{6,70},{7,71},{8,72},{9,... | collective-permute-start | bytes 6152 | tf_op jit(solution)/shard_map/ppermute | solution.py:47
  115.3 3.9 %collective-permute-done.27 = f32[1,512]{1,0:T(1,128)S(1)} collective-permute-done((f32[1,512]{1,0:T(1,128)S(1)}, f32[1,512]{1,0:T(1,128)S(1)}, u32[]{:S(2)}, u32[]{:S(2)}) %collective-permute-start.27) | collective-permute-done | bytes 2080 | tf_op jit(solution)/shard_map/ppermute | solution.py:47
  119.2 1.5 %rescale.1 = f32[1024,512]{1,0:T(8,128)} custom-call(f32[1024,512]{1,0:T(8,128)S(1)} %get-tuple-element.47.value_ref, f32[1,512]{1,0:T(1,128)S(1)} %add.68.total_ref), custom_call_target="tpu_custom_call" | custom-call | tf_op jit(solution)/shard_map/rescale/pallas_call | solution.py:169
  (32 shorter events, 0.1 us)
Async XLA Ops:
  0.0 1.6 %copy-start.5 = (f32[1024,512]{1,0:T(8,128)S(1)}, f32[1024,512]{1,0:T(8,128)}, u32[]{:S(2)}) copy-start(f32[1024,512]{1,0:T(8,128)} %entries_in.1) | copy-start | bytes 6291460
  1.6 0.7 copy-start.6
  3.2 6.7 %collective-permute-start.2 = (f32[1,640]{1,0:T(1,128)S(1)}, f32[1,640]{1,0:T(1,128)S(1)}, u32[]{:S(2)}, u32[]{:S(2)}) collective-permute-start(f32[1,640]{1,0:T(1,128)S(1)} %get-tuple-element.28), channel_id=1, source_target_pairs={{0,48},{1,49},{2,50},{3,51},{4,52},{5,53},{6,54},{7,55},{8,56},{9,... | collective-permute-start | bytes 7688 | tf_op jit(solution)/shard_map/ppermute | solution.py:47
  7.3 5.1 %collective-permute-start.1 = (f32[1,640]{1,0:T(1,128)S(1)}, f32[1,640]{1,0:T(1,128)S(1)}, u32[]{:S(2)}, u32[]{:S(2)}) collective-permute-start(f32[1,640]{1,0:T(1,128)S(1)} %get-tuple-element.28), channel_id=1, source_target_pairs={{0,32},{1,33},{2,34},{3,35},{4,36},{5,37},{6,38},{7,39},{8,40},{9,... | collective-permute-start | bytes 7688 | tf_op jit(solution)/shard_map/ppermute | solution.py:47
  7.3 5.1 %collective-permute-start = (f32[1,640]{1,0:T(1,128)S(1)}, f32[1,640]{1,0:T(1,128)S(1)}, u32[]{:S(2)}, u32[]{:S(2)}) collective-permute-start(f32[1,640]{1,0:T(1,128)S(1)} %get-tuple-element.28), channel_id=1, source_target_pairs={{0,16},{1,17},{2,18},{3,19},{4,20},{5,21},{6,22},{7,23},{8,24},{9,... | collective-permute-start | bytes 7688 | tf_op jit(solution)/shard_map/ppermute | solution.py:47
  8.6 1.1 collective-permute-start.3
  12.5 5.2 %collective-permute-start.4 = (f32[1,640]{1,0:T(1,128)S(1)}, f32[1,640]{1,0:T(1,128)S(1)}, u32[]{:S(2)}, u32[]{:S(2)}) collective-permute-start(f32[1,640]{1,0:T(1,128)S(1)} %add_add_fusion), channel_id=1, source_target_pairs={{0,64},{1,65},{2,66},{3,67},{4,68},{5,69},{6,70},{7,71},{8,72},{9,... | collective-permute-start | bytes 7688 | tf_op jit(solution)/shard_map/ppermute | solution.py:47
  17.9 30.6 %copy-start.7 = (s32[4,2]{0,1:T(2,128)S(1)}, s32[4,2]{0,1:T(2,128)}, u32[]{:S(2)}) copy-start(s32[4,2]{0,1:T(2,128)} %param.5) | copy-start | bytes 100
  18.0 4.6 %collective-permute-start.11 = (bf16[512,512]{1,0:T(8,128)(2,1)S(1)}, bf16[512,512]{1,0:T(8,128)(2,1)S(1)}, u32[]{:S(2)}, u32[]{:S(2)}) collective-permute-start(bf16[512,512]{1,0:T(8,128)(2,1)S(1)} %get-tuple-element.50), channel_id=1, source_target_pairs={{0,1},{1,0},{2,3},{3,2},{4,5},{5,4},{6,7},{7,6},{8,9},{9,8},{10,11... | collective-permute-start | bytes 1572872 | tf_op jit(solution)/shard_map/ppermute | solution.py:47
  18.1 1.3 %collective-permute-start.6 = (f32[16]{0:T(128)S(1)}, f32[16]{0:T(128)S(1)}, u32[]{:S(2)}, u32[]{:S(2)}) collective-permute-start(f32[16]{0:T(128)S(1)} %pad_maximum_fusion.1), channel_id=1, source_target_pairs={{1,13},{3,15},{5,9},{7,11},{9,5},{11,7},{13,1},{15,3},{17,29},{19,... | collective-permute-start | bytes 200 | tf_op jit(solution)/shard_map/ppermute | solution.py:47
  18.8 0.7 collective-permute-start.5
  19.6 17.5 %collective-permute-start.8 = (bf16[1024,512]{1,0:T(8,128)(2,1)S(1)}, bf16[1024,512]{1,0:T(8,128)(2,1)S(1)}, u32[]{:S(2)}, u32[]{:S(2)}) collective-permute-start(bf16[1024,512]{1,0:T(8,128)(2,1)S(1)} %divide_convert_fusion.refs_0_.refs_1_.refs_2_), channel_id=1, source_target_pairs={{0,2},{1,3},{2,4},{3,5},{4,6},{5,7},{6,0},{7,1},{8,10},{9,11},{10,... | collective-permute-start | bytes 3145736 | tf_op jit(solution)/shard_map/ppermute | solution.py:47
  21.1 17.4 %collective-permute-start.7 = (bf16[1024,512]{1,0:T(8,128)(2,1)S(1)}, bf16[1024,512]{1,0:T(8,128)(2,1)}, u32[]{:S(2)}, u32[]{:S(2)}) collective-permute-start(bf16[1024,512]{1,0:T(8,128)(2,1)S(1)} %divide_convert_fusion.refs_0_.refs_1_.refs_2_), channel_id=1, source_target_pairs={{0,8},{1,9},{2,10},{3,11},{4,12},{5,13},{6,14},{7,15},{8,0},{9,1},... | collective-permute-start | bytes 3145736 | tf_op jit(solution)/shard_map/ppermute | solution.py:47
  22.8 21.6 %collective-permute-start.12 = (bf16[512,1024]{1,0:T(8,128)(2,1)S(1)}, bf16[512,1024]{1,0:T(8,128)(2,1)}, u32[]{:S(2)}, u32[]{:S(2)}) collective-permute-start(bf16[512,1024]{1,0:T(8,128)(2,1)S(1)} %pad_maximum_fusion.refs_7_.refs_10_), channel_id=1, source_target_pairs={{0,16},{1,17},{2,18},{3,19},{4,20},{5,21},{6,22},{7,23},{8,24},{9,... | collective-permute-start | bytes 3145736 | tf_op jit(solution)/shard_map/ppermute | solution.py:47
  22.8 21.6 %collective-permute-start.13 = (bf16[512,1024]{1,0:T(8,128)(2,1)S(1)}, bf16[512,1024]{1,0:T(8,128)(2,1)S(1)}, u32[]{:S(2)}, u32[]{:S(2)}) collective-permute-start(bf16[512,1024]{1,0:T(8,128)(2,1)S(1)} %pad_maximum_fusion.refs_7_.refs_10_), channel_id=1, source_target_pairs={{0,48},{1,49},{2,50},{3,51},{4,52},{5,53},{6,54},{7,55},{8,56},{9,... | collective-permute-start | bytes 3145736 | tf_op jit(solution)/shard_map/ppermute | solution.py:47
  26.1 19.5 %collective-permute-start.10 = (bf16[1024,512]{1,0:T(8,128)(2,1)S(1)}, bf16[1024,512]{1,0:T(8,128)(2,1)S(1)}, u32[]{:S(2)}, u32[]{:S(2)}) collective-permute-start(bf16[1024,512]{1,0:T(8,128)(2,1)S(1)} %divide_convert_fusion.refs_0_.refs_1_.refs_2_), channel_id=1, source_target_pairs={{0,6},{1,7},{2,0},{3,1},{4,2},{5,3},{6,4},{7,5},{8,14},{9,15},{10,... | collective-permute-start | bytes 3145736 | tf_op jit(solution)/shard_map/ppermute | solution.py:47
  38.4 23.3 %collective-permute-start.9 = (bf16[1024,512]{1,0:T(8,128)(2,1)}, bf16[1024,512]{1,0:T(8,128)(2,1)}, u32[]{:S(2)}, u32[]{:S(2)}) collective-permute-start(bf16[1024,512]{1,0:T(8,128)(2,1)} %collective-permute-done.7.refs_3_.refs_4_.refs_5_), channel_id=1, source_target_pairs={{0,2},{1,3},{2,4},{3,5},{4,6},{5,7},{6,0},{7,1},{8,10},{9,11},{10,... | collective-permute-start | bytes 3145736 | tf_op jit(solution)/shard_map/ppermute | solution.py:47
  41.0 25.6 %collective-permute-start.15 = (bf16[512,1024]{1,0:T(8,128)(2,1)S(1)}, bf16[512,1024]{1,0:T(8,128)(2,1)}, u32[]{:S(2)}, u32[]{:S(2)}) collective-permute-start(bf16[512,1024]{1,0:T(8,128)(2,1)S(1)} %pad_maximum_fusion.refs_7_.refs_10_), channel_id=1, source_target_pairs={{0,64},{1,65},{2,66},{3,67},{4,68},{5,69},{6,70},{7,71},{8,72},{9,... | collective-permute-start | bytes 3145736 | tf_op jit(solution)/shard_map/ppermute | solution.py:47
  44.4 1.0 copy-start.3
  45.4 21.9 %collective-permute-start.17 = (bf16[512,1024]{1,0:T(8,128)(2,1)}, bf16[512,1024]{1,0:T(8,128)(2,1)}, u32[]{:S(2)}, u32[]{:S(2)}) collective-permute-start(bf16[512,1024]{1,0:T(8,128)(2,1)} %collective-permute-done.12.refs_8_.refs_11_), channel_id=1, source_target_pairs={{0,16},{1,17},{2,18},{3,19},{4,20},{5,21},{6,22},{7,23},{8,24},{9,... | collective-permute-start | bytes 3145736 | tf_op jit(solution)/shard_map/ppermute | solution.py:47
  45.5 1.0 copy-start
  46.5 22.2 %collective-permute-start.14 = (bf16[1024,512]{1,0:T(8,128)(2,1)}, bf16[1024,512]{1,0:T(8,128)(2,1)}, u32[]{:S(2)}, u32[]{:S(2)}) collective-permute-start(bf16[1024,512]{1,0:T(8,128)(2,1)} %collective-permute-done.7.refs_3_.refs_4_.refs_5_), channel_id=1, source_target_pairs={{0,6},{1,7},{2,0},{3,1},{4,2},{5,3},{6,4},{7,5},{8,14},{9,15},{10,... | collective-permute-start | bytes 3145736 | tf_op jit(solution)/shard_map/ppermute | solution.py:47
  48.8 21.8 %collective-permute-start.16 = (f32[104]{0:T(128)S(1)}, f32[104]{0:T(128)S(1)}, u32[]{:S(2)}, u32[]{:S(2)}) collective-permute-start(f32[104]{0:T(128)S(1)} %pad_maximum_fusion.3), channel_id=1, source_target_pairs={{0,1},{1,0},{2,3},{3,2},{4,5},{5,4},{6,7},{7,6},{8,9},{9,8},{10,11... | collective-permute-start | bytes 1256 | tf_op jit(solution)/shard_map/ppermute | solution.py:47
  61.7 23.3 %collective-permute-start.18 = (bf16[1024,512]{1,0:T(8,128)(2,1)S(1)}, bf16[1024,512]{1,0:T(8,128)(2,1)S(1)}, u32[]{:S(2)}, u32[]{:S(2)}) collective-permute-start(bf16[1024,512]{1,0:T(8,128)(2,1)S(1)} %collective-permute-done.8.refs_1_.refs_2_.refs_3_), channel_id=1, source_target_pairs={{0,2},{1,3},{2,4},{3,5},{4,6},{5,7},{6,0},{7,1},{8,10},{9,11},{10,... | collective-permute-start | bytes 3145736 | tf_op jit(solution)/shard_map/ppermute | solution.py:47
  66.7 21.7 %collective-permute-start.21 = (bf16[512,1024]{1,0:T(8,128)(2,1)}, bf16[512,1024]{1,0:T(8,128)(2,1)S(1)}, u32[]{:S(2)}, u32[]{:S(2)}) collective-permute-start(bf16[512,1024]{1,0:T(8,128)(2,1)} %collective-permute-done.15.refs_11_.refs_14_), channel_id=1, source_target_pairs={{0,48},{1,49},{2,50},{3,51},{4,52},{5,53},{6,54},{7,55},{8,56},{9,... | collective-permute-start | bytes 3145736 | tf_op jit(solution)/shard_map/ppermute | solution.py:47
  67.2 24.2 %collective-permute-start.20 = (bf16[512,1024]{1,0:T(8,128)(2,1)}, bf16[512,1024]{1,0:T(8,128)(2,1)S(1)}, u32[]{:S(2)}, u32[]{:S(2)}) collective-permute-start(bf16[512,1024]{1,0:T(8,128)(2,1)} %collective-permute-done.15.refs_11_.refs_14_), channel_id=1, source_target_pairs={{0,16},{1,17},{2,18},{3,19},{4,20},{5,21},{6,22},{7,23},{8,24},{9,... | collective-permute-start | bytes 3145736 | tf_op jit(solution)/shard_map/ppermute | solution.py:47
  68.7 22.8 %collective-permute-start.19 = (bf16[1024,512]{1,0:T(8,128)(2,1)}, bf16[1024,512]{1,0:T(8,128)(2,1)S(1)}, u32[]{:S(2)}, u32[]{:S(2)}) collective-permute-start(bf16[1024,512]{1,0:T(8,128)(2,1)} %collective-permute-done.14.refs_5_.refs_6_.refs_7_), channel_id=1, source_target_pairs={{0,6},{1,7},{2,0},{3,1},{4,2},{5,3},{6,4},{7,5},{8,14},{9,15},{10,... | collective-permute-start | bytes 3145736 | tf_op jit(solution)/shard_map/ppermute | solution.py:47
  70.6 20.9 %collective-permute-start.22 = (bf16[512,1024]{1,0:T(8,128)(2,1)}, bf16[512,1024]{1,0:T(8,128)(2,1)S(1)}, u32[]{:S(2)}, u32[]{:S(2)}) collective-permute-start(bf16[512,1024]{1,0:T(8,128)(2,1)} %collective-permute-done.17.refs_10_.refs_13_), channel_id=1, source_target_pairs={{0,64},{1,65},{2,66},{3,67},{4,68},{5,69},{6,70},{7,71},{8,72},{9,... | collective-permute-start | bytes 3145736 | tf_op jit(solution)/shard_map/ppermute | solution.py:47
  73.5 1.2 %copy-start.1 = (bf16[1024,512]{1,0:T(8,128)(2,1)S(1)}, bf16[1024,512]{1,0:T(8,128)(2,1)}, u32[]{:S(2)}) copy-start(bf16[1024,512]{1,0:T(8,128)(2,1)} %copy-done) | copy-start | bytes 3145732
  74.7 2.6 %copy-start.2 = (bf16[1024,512]{1,0:T(8,128)(2,1)S(1)}, bf16[1024,512]{1,0:T(8,128)(2,1)}, u32[]{:S(2)}) copy-start(bf16[1024,512]{1,0:T(8,128)(2,1)} %copy-done) | copy-start | bytes 3145732
  74.7 2.7 %copy-start.4 = (bf16[512,1024]{1,0:T(8,128)(2,1)S(1)}, bf16[512,1024]{1,0:T(8,128)(2,1)}, u32[]{:S(2)}) copy-start(bf16[512,1024]{1,0:T(8,128)(2,1)} %copy-done.3) | copy-start | bytes 3145732
  95.2 9.1 %collective-permute-start.23 = (f32[1024,512]{1,0:T(8,128)S(1)}, f32[1024,512]{1,0:T(8,128)S(1)}, u32[]{:S(2)}, u32[]{:S(2)}) collective-permute-start(f32[1024,512]{1,0:T(8,128)S(1)} %finish.3), channel_id=1, source_target_pairs={{0,1},{1,0},{2,3},{3,2},{4,5},{5,4},{6,7},{7,6},{8,9},{9,8},{10,11... | collective-permute-start | bytes 6291464 | tf_op jit(solution)/shard_map/ppermute | solution.py:47
  104.6 6.0 %collective-permute-start.26 = (f32[1,512]{1,0:T(1,128)S(1)}, f32[1,512]{1,0:T(1,128)S(1)}, u32[]{:S(2)}, u32[]{:S(2)}) collective-permute-start(f32[1,512]{1,0:T(1,128)S(1)} %get-tuple-element.48), channel_id=1, source_target_pairs={{0,48},{1,49},{2,50},{3,51},{4,52},{5,53},{6,54},{7,55},{8,56},{9,... | collective-permute-start | bytes 6152 | tf_op jit(solution)/shard_map/ppermute | solution.py:47
  108.9 5.1 %collective-permute-start.25 = (f32[1,512]{1,0:T(1,128)S(1)}, f32[1,512]{1,0:T(1,128)S(1)}, u32[]{:S(2)}, u32[]{:S(2)}) collective-permute-start(f32[1,512]{1,0:T(1,128)S(1)} %get-tuple-element.48), channel_id=1, source_target_pairs={{0,32},{1,33},{2,34},{3,35},{4,36},{5,37},{6,38},{7,39},{8,40},{9,... | collective-permute-start | bytes 6152 | tf_op jit(solution)/shard_map/ppermute | solution.py:47
  109.3 4.8 %collective-permute-start.24 = (f32[1,512]{1,0:T(1,128)S(1)}, f32[1,512]{1,0:T(1,128)S(1)}, u32[]{:S(2)}, u32[]{:S(2)}) collective-permute-start(f32[1,512]{1,0:T(1,128)S(1)} %get-tuple-element.48), channel_id=1, source_target_pairs={{0,16},{1,17},{2,18},{3,19},{4,20},{5,21},{6,22},{7,23},{8,24},{9,... | collective-permute-start | bytes 6152 | tf_op jit(solution)/shard_map/ppermute | solution.py:47
  114.1 5.1 %collective-permute-start.27 = (f32[1,512]{1,0:T(1,128)S(1)}, f32[1,512]{1,0:T(1,128)S(1)}, u32[]{:S(2)}, u32[]{:S(2)}) collective-permute-start(f32[1,512]{1,0:T(1,128)S(1)} %add_add_fusion.1), channel_id=1, source_target_pairs={{0,64},{1,65},{2,66},{3,67},{4,68},{5,69},{6,70},{7,71},{8,72},{9,... | collective-permute-start | bytes 6152 | tf_op jit(solution)/shard_map/ppermute | solution.py:47

commit v8 on v7

--- a/solution.py
+++ b/solution.py
@@ -40,7 +40,7 @@
     pairs(lambda yh, z, yl, x, c, dy=dy: (yh, z, (yl + dy) % YL, (x + 2) % NX, c), cores=(1,))
     for dy in (0, 1)
 ]
-Z_TURNS = [pairs(lambda yh, z, yl, x, c, d=d: (yh, (z + d) % NZ, yl, x, c)) for d in range(1, NZ)]
+Z_TURNS = [pairs(lambda yh, z, yl, x, c, d=d: (yh, (z + d) % NZ, yl, x, c)) for d in (1, 3, 2)]
 
 
 def move(value, perm):
@@ -157,20 +157,30 @@
     )(mine, got)
 
 
-def rescale_kernel(order, value_ref, total_ref, out_ref):
+def rescale_kernel(order, value_ref, total_ref, out_ref, strips, sem):
     factor = order / total_ref[...]
-    rows = out_ref.shape[0]
-    step = rows // 4
-    for r in range(0, rows, step):
-        out_ref[r:r + step, :] = value_ref[r:r + step, :] * factor
+    n, step = strips.shape[:2]
+    copies = []
+    for r in range(n):
+        strips[r] = value_ref[r * step:(r + 1) * step, :] * factor
+        copies.append(pltpu.make_async_copy(strips.at[r], out_ref.at[pl.ds(r * step, step)], sem.at[r]))
+        copies[r].start()
+    for copy in copies:
+        copy.wait()
 
 
 def rescaled(order, value, total):
+    rows, cols = value.shape
+    strips = 8
     return pl.pallas_call(
         functools.partial(rescale_kernel, order),
         out_shape=jax.ShapeDtypeStruct(value.shape, F32),
         in_specs=[VMEM, VMEM],
-        out_specs=VMEM,
+        out_specs=ANY,
+        scratch_shapes=[
+            pltpu.VMEM((strips, rows // strips, cols), F32),
+            pltpu.SemaphoreType.DMA((strips,)),
+        ],
         compiler_params=vmem_limit(16),
         name="rescale",
     )(value, total)

time: 121 us -> 123 us (1.017)
  waiting for transfers between devices: 38.9 us -> 35.4 us
  Pallas kernels: 18.8 us -> 21.6 us
  starting transfers between devices: 56.5 us -> 58 us
    ppermute x28, waiting for transfers between devices: 38.9 us -> 35.4 us  [move(): return lax.ppermute(value, AXES, perm)]
    pallas_call x3, Pallas kernels: 13.5 us -> 16.3 us  [product(): pl.pallas_call(functools.partial(product_kernel, len(a_units), len(b_unit...]
    ppermute x28, starting transfers between devices: 56.5 us -> 58 us  [move(): return lax.ppermute(value, AXES, perm)]
  transfers between devices with their start and end apart: 28 -> 28, of which waited for: 14 -> 13; matrix products, arithmetic and copies ran while one was open for 0% -> 0% of each run, Pallas kernels for 10% -> 12%
where the time goes in v8:
time: 123 us; the launch traced here: 122 us
  starting transfers between devices  58 us (47%)
  waiting for transfers between devices  35.4 us (29%)
  Pallas kernels  21.6 us (18%)
  local copies, waits for them, and re-layouts  5.61 us (5%)
    ppermute x28, starting transfers between devices, move(): return lax.ppermute(value, AXES, perm)  58 us
    ppermute x28, waiting for transfers between devices, move(): return lax.ppermute(value, AXES, perm)  35.4 us
    pallas_call x3, Pallas kernels, product(): pl.pallas_call(functools.partial(product_kernel, len(a_units), len(b_unit...  16.3 us
    unnamed x16, local copies, waits for them, and re-layouts  5.44 us
    pallas_call x1, Pallas kernels, planned(): pl.pallas_call(functools.partial(plan_kernel, rows, cols), out_shape=jax....  2.64 us
  transfers between devices with their start and end apart: 28, of which 13 were waited for; matrix products, arithmetic and copies ran while one was open for 0% of the time, Pallas kernels for 12%

profile of v8, /device:TPU:0, one launch (start us, length us, event | category | flops | bytes accessed | tf_op | source)
XLA Modules:
  0.0 121.6 jit_solution(14530433741381034671)
XLA Ops:
  0.0 1.6 %copy-done.5 = f32[1024,512]{1,0:T(8,128)S(1)} copy-done((f32[1024,512]{1,0:T(8,128)S(1)}, f32[1024,512]{1,0:T(8,128)}, u32[]{:S(2)}) %copy-start.5) | copy-done | bytes 2097176
  1.6 0.7 copy-done.6
  2.3 0.9 mask.1
  3.2 4.0 %collective-permute-start.2 = (f32[1,640]{1,0:T(1,128)S(1)}, f32[1,640]{1,0:T(1,128)S(1)}, u32[]{:S(2)}, u32[]{:S(2)}) collective-permute-start(f32[1,640]{1,0:T(1,128)S(1)} %get-tuple-element.28), channel_id=1, source_target_pairs={{0,32},{1,33},{2,34},{3,35},{4,36},{5,37},{6,38},{7,39},{8,40},{9,... | collective-permute-start | bytes 7688 | tf_op jit(solution)/shard_map/ppermute | solution.py:47
  7.2 0.7 collective-permute-start.1
  7.9 1.3 %collective-permute-start = (f32[1,640]{1,0:T(1,128)S(1)}, f32[1,640]{1,0:T(1,128)S(1)}, u32[]{:S(2)}, u32[]{:S(2)}) collective-permute-start(f32[1,640]{1,0:T(1,128)S(1)} %get-tuple-element.28), channel_id=1, source_target_pairs={{0,16},{1,17},{2,18},{3,19},{4,20},{5,21},{6,22},{7,23},{8,24},{9,... | collective-permute-start | bytes 7688 | tf_op jit(solution)/shard_map/ppermute | solution.py:47
  9.2 1.1 collective-permute-done.3
  10.3 0.1 pad_maximum_fusion.1
  10.4 0.0 collective-permute-done.2
  10.4 0.4 collective-permute-done.1
  10.8 1.9 %collective-permute-done = f32[1,640]{1,0:T(1,128)S(1)} collective-permute-done((f32[1,640]{1,0:T(1,128)S(1)}, f32[1,640]{1,0:T(1,128)S(1)}, u32[]{:S(2)}, u32[]{:S(2)}) %collective-permute-start) | collective-permute-done | bytes 2592 | tf_op jit(solution)/shard_map/ppermute | solution.py:47
  12.7 3.3 %collective-permute-start.4 = (f32[1,640]{1,0:T(1,128)S(1)}, f32[1,640]{1,0:T(1,128)S(1)}, u32[]{:S(2)}, u32[]{:S(2)}) collective-permute-start(f32[1,640]{1,0:T(1,128)S(1)} %add_add_fusion), channel_id=1, source_target_pairs={{0,64},{1,65},{2,66},{3,67},{4,68},{5,69},{6,70},{7,71},{8,72},{9,... | collective-permute-start | bytes 7688 | tf_op jit(solution)/shard_map/ppermute | solution.py:47
  16.0 1.9 %collective-permute-done.4 = f32[1,640]{1,0:T(1,128)S(1)} collective-permute-done((f32[1,640]{1,0:T(1,128)S(1)}, f32[1,640]{1,0:T(1,128)S(1)}, u32[]{:S(2)}, u32[]{:S(2)}) %collective-permute-start.4) | collective-permute-done | bytes 2592 | tf_op jit(solution)/shard_map/ppermute | solution.py:47
  17.9 0.3 divide_convert_fusion.refs_0_.refs_1_.refs_2_
  18.2 0.0 copy-start.7
  18.2 0.1 constant_dynamic-slice_fusion.1
  18.3 0.1 collective-permute-start.11
  18.4 0.7 collective-permute-start.6
  19.1 0.7 collective-permute-start.5
  19.7 0.0 collective-permute-done.5
  19.7 0.1 pad_maximum_fusion.2.far_ref
  19.8 1.5 %collective-permute-start.8 = (bf16[1024,512]{1,0:T(8,128)(2,1)S(1)}, bf16[1024,512]{1,0:T(8,128)(2,1)S(1)}, u32[]{:S(2)}, u32[]{:S(2)}) collective-permute-start(bf16[1024,512]{1,0:T(8,128)(2,1)S(1)} %divide_convert_fusion.refs_0_.refs_1_.refs_2_), channel_id=1, source_target_pairs={{0,2},{1,3},{2,4},{3,5},{4,6},{5,7},{6,0},{7,1},{8,10},{9,11},{10,... | collective-permute-start | bytes 3145736 | tf_op jit(solution)/shard_map/ppermute | solution.py:47
  21.3 1.6 %collective-permute-start.7 = (bf16[1024,512]{1,0:T(8,128)(2,1)S(1)}, bf16[1024,512]{1,0:T(8,128)(2,1)}, u32[]{:S(2)}, u32[]{:S(2)}) collective-permute-start(bf16[1024,512]{1,0:T(8,128)(2,1)S(1)} %divide_convert_fusion.refs_0_.refs_1_.refs_2_), channel_id=1, source_target_pairs={{0,8},{1,9},{2,10},{3,11},{4,12},{5,13},{6,14},{7,15},{8,0},{9,1},... | collective-permute-start | bytes 3145736 | tf_op jit(solution)/shard_map/ppermute | solution.py:47
  22.9 0.1 pad_maximum_fusion.refs_7_.refs_10_
  23.0 0.2 collective-permute-start.12
  23.2 3.1 %collective-permute-start.13 = (bf16[512,1024]{1,0:T(8,128)(2,1)S(1)}, bf16[512,1024]{1,0:T(8,128)(2,1)S(1)}, u32[]{:S(2)}, u32[]{:S(2)}) collective-permute-start(bf16[512,1024]{1,0:T(8,128)(2,1)S(1)} %pad_maximum_fusion.refs_7_.refs_10_), channel_id=1, source_target_pairs={{0,48},{1,49},{2,50},{3,51},{4,52},{5,53},{6,54},{7,55},{8,56},{9,... | collective-permute-start | bytes 3145736 | tf_op jit(solution)/shard_map/ppermute | solution.py:47
  26.3 1.7 %collective-permute-start.10 = (bf16[1024,512]{1,0:T(8,128)(2,1)S(1)}, bf16[1024,512]{1,0:T(8,128)(2,1)S(1)}, u32[]{:S(2)}, u32[]{:S(2)}) collective-permute-start(bf16[1024,512]{1,0:T(8,128)(2,1)S(1)} %divide_convert_fusion.refs_0_.refs_1_.refs_2_), channel_id=1, source_target_pairs={{0,6},{1,7},{2,0},{3,1},{4,2},{5,3},{6,4},{7,5},{8,14},{9,15},{10,... | collective-permute-start | bytes 3145736 | tf_op jit(solution)/shard_map/ppermute | solution.py:47
  28.1 9.3 %collective-permute-done.8.refs_1_.refs_2_.refs_3_ = bf16[1024,512]{1,0:T(8,128)(2,1)S(1)} collective-permute-done((bf16[1024,512]{1,0:T(8,128)(2,1)S(1)}, bf16[1024,512]{1,0:T(8,128)(2,1)S(1)}, u32[]{:S(2)}, u32[]{:S(2)}) %collective-permute-start.8) | collective-permute-done | bytes 1048608 | tf_op jit(solution)/shard_map/ppermute | solution.py:47
  37.3 1.3 %collective-permute-done.7.refs_3_.refs_4_.refs_5_ = bf16[1024,512]{1,0:T(8,128)(2,1)} collective-permute-done((bf16[1024,512]{1,0:T(8,128)(2,1)S(1)}, bf16[1024,512]{1,0:T(8,128)(2,1)}, u32[]{:S(2)}, u32[]{:S(2)}) %collective-permute-start.7) | collective-permute-done | bytes 1048608 | tf_op jit(solution)/shard_map/ppermute | solution.py:47
  38.7 2.6 %collective-permute-start.9 = (bf16[1024,512]{1,0:T(8,128)(2,1)}, bf16[1024,512]{1,0:T(8,128)(2,1)}, u32[]{:S(2)}, u32[]{:S(2)}) collective-permute-start(bf16[1024,512]{1,0:T(8,128)(2,1)} %collective-permute-done.7.refs_3_.refs_4_.refs_5_), channel_id=1, source_target_pairs={{0,2},{1,3},{2,4},{3,5},{4,6},{5,7},{6,0},{7,1},{8,10},{9,11},{10,... | collective-permute-start | bytes 3145736 | tf_op jit(solution)/shard_map/ppermute | solution.py:47
  41.3 3.4 %collective-permute-start.15 = (bf16[512,1024]{1,0:T(8,128)(2,1)S(1)}, bf16[512,1024]{1,0:T(8,128)(2,1)}, u32[]{:S(2)}, u32[]{:S(2)}) collective-permute-start(bf16[512,1024]{1,0:T(8,128)(2,1)S(1)} %pad_maximum_fusion.refs_7_.refs_10_), channel_id=1, source_target_pairs={{0,64},{1,65},{2,66},{3,67},{4,68},{5,69},{6,70},{7,71},{8,72},{9,... | collective-permute-start | bytes 3145736 | tf_op jit(solution)/shard_map/ppermute | solution.py:47
  44.7 1.0 copy-done.3
  45.6 0.5 collective-permute-start.17
  46.1 0.0 collective-permute-done.10.refs_2_.refs_3_.refs_4_
  46.1 1.0 copy-done
  47.1 1.7 %collective-permute-start.14 = (bf16[1024,512]{1,0:T(8,128)(2,1)}, bf16[1024,512]{1,0:T(8,128)(2,1)}, u32[]{:S(2)}, u32[]{:S(2)}) collective-permute-start(bf16[1024,512]{1,0:T(8,128)(2,1)} %collective-permute-done.7.refs_3_.refs_4_.refs_5_), channel_id=1, source_target_pairs={{0,6},{1,7},{2,0},{3,1},{4,2},{5,3},{6,4},{7,5},{8,14},{9,15},{10,... | collective-permute-start | bytes 3145736 | tf_op jit(solution)/shard_map/ppermute | solution.py:47
  48.8 0.1 fusion.1
  48.9 0.1 reshape.11.out_ref
  49.0 0.1 pad_maximum_fusion.3
  49.0 9.2 %collective-permute-start.16 = (f32[104]{0:T(128)S(1)}, f32[104]{0:T(128)S(1)}, u32[]{:S(2)}, u32[]{:S(2)}) collective-permute-start(f32[104]{0:T(128)S(1)} %pad_maximum_fusion.3), channel_id=1, source_target_pairs={{0,1},{1,0},{2,3},{3,2},{4,5},{5,4},{6,7},{7,6},{8,9},{9,8},{10,11... | collective-permute-start | bytes 1256 | tf_op jit(solution)/shard_map/ppermute | solution.py:47
  58.3 3.7 %collective-permute-done.9.refs_4_.refs_5_.refs_6_ = bf16[1024,512]{1,0:T(8,128)(2,1)} collective-permute-done((bf16[1024,512]{1,0:T(8,128)(2,1)}, bf16[1024,512]{1,0:T(8,128)(2,1)}, u32[]{:S(2)}, u32[]{:S(2)}) %collective-permute-start.9) | collective-permute-done | bytes 1048608 | tf_op jit(solution)/shard_map/ppermute | solution.py:47
  62.0 1.5 %collective-permute-start.18 = (bf16[1024,512]{1,0:T(8,128)(2,1)S(1)}, bf16[1024,512]{1,0:T(8,128)(2,1)S(1)}, u32[]{:S(2)}, u32[]{:S(2)}) collective-permute-start(bf16[1024,512]{1,0:T(8,128)(2,1)S(1)} %collective-permute-done.8.refs_1_.refs_2_.refs_3_), channel_id=1, source_target_pairs={{0,2},{1,3},{2,4},{3,5},{4,6},{5,7},{6,0},{7,1},{8,10},{9,11},{10,... | collective-permute-start | bytes 3145736 | tf_op jit(solution)/shard_map/ppermute | solution.py:47
  63.5 3.4 %collective-permute-done.15.refs_11_.refs_14_ = bf16[512,1024]{1,0:T(8,128)(2,1)} collective-permute-done((bf16[512,1024]{1,0:T(8,128)(2,1)S(1)}, bf16[512,1024]{1,0:T(8,128)(2,1)}, u32[]{:S(2)}, u32[]{:S(2)}) %collective-permute-start.15) | collective-permute-done | bytes 1048608 | tf_op jit(solution)/shard_map/ppermute | solution.py:47
  66.9 0.0 collective-permute-start.21
  66.9 2.0 %collective-permute-start.20 = (bf16[512,1024]{1,0:T(8,128)(2,1)}, bf16[512,1024]{1,0:T(8,128)(2,1)S(1)}, u32[]{:S(2)}, u32[]{:S(2)}) collective-permute-start(bf16[512,1024]{1,0:T(8,128)(2,1)} %collective-permute-done.15.refs_11_.refs_14_), channel_id=1, source_target_pairs={{0,16},{1,17},{2,18},{3,19},{4,20},{5,21},{6,22},{7,23},{8,24},{9,... | collective-permute-start | bytes 3145736 | tf_op jit(solution)/shard_map/ppermute | solution.py:47
  69.0 1.9 %collective-permute-start.19 = (bf16[1024,512]{1,0:T(8,128)(2,1)}, bf16[1024,512]{1,0:T(8,128)(2,1)S(1)}, u32[]{:S(2)}, u32[]{:S(2)}) collective-permute-start(bf16[1024,512]{1,0:T(8,128)(2,1)} %collective-permute-done.14.refs_5_.refs_6_.refs_7_), channel_id=1, source_target_pairs={{0,6},{1,7},{2,0},{3,1},{4,2},{5,3},{6,4},{7,5},{8,14},{9,15},{10,... | collective-permute-start | bytes 3145736 | tf_op jit(solution)/shard_map/ppermute | solution.py:47
  70.8 0.0 collective-permute-done.16.other_ref
  70.8 2.9 %collective-permute-start.22 = (bf16[512,1024]{1,0:T(8,128)(2,1)}, bf16[512,1024]{1,0:T(8,128)(2,1)S(1)}, u32[]{:S(2)}, u32[]{:S(2)}) collective-permute-start(bf16[512,1024]{1,0:T(8,128)(2,1)} %collective-permute-done.17.refs_10_.refs_13_), channel_id=1, source_target_pairs={{0,64},{1,65},{2,66},{3,67},{4,68},{5,69},{6,70},{7,71},{8,72},{9,... | collective-permute-start | bytes 3145736 | tf_op jit(solution)/shard_map/ppermute | solution.py:47
  73.8 1.2 %copy-done.1 = bf16[1024,512]{1,0:T(8,128)(2,1)S(1)} copy-done((bf16[1024,512]{1,0:T(8,128)(2,1)S(1)}, bf16[1024,512]{1,0:T(8,128)(2,1)}, u32[]{:S(2)}) %copy-start.1) | copy-done | bytes 1048600
  75.0 2.6 %plan.1.refs_0_ = s32[48]{0:T(128)S(1)} custom-call(f32[32]{0:T(128)S(1)} %pad_maximum_fusion.2.far_ref, f32[64]{0:T(128)S(1)} %slice_bitcast_fusion.right_ref, f32[8]{0:T(128)S(1)} %reshape.11.out_ref, f32[104]{0:T(128)S(1)} %collective-permute-done.16.other_ref, bf16[1024,512]{1,0:T(8,128)(2,1)S(1)} %divide_convert_fusion.refs_0_.refs_1_.refs_2_, ...), custom_call_target="tpu_custom_call" | custom-call | flops 1000000 | bytes 1024 | tf_op jit(solution)/shard_map/plan/pallas_call | solution.py:271
  77.6 7.7 %begin.1 = (f32[1024,512]{1,0:T(8,128)S(1)}, f32[1024,512]{1,0:T(8,128)S(1)}) custom-call(s32[48]{0:T(128)S(1)} %plan.1.refs_0_, bf16[1024,512]{1,0:T(8,128)(2,1)S(1)} %divide_convert_fusion.refs_0_.refs_1_.refs_2_, bf16[1024,512]{1,0:T(8,128)(2,1)S(1)} %collective-permute-done.8.refs_1_.refs_2_.refs_3_, bf16[1024,512]{1,0:T(8,128)(2,1)S(1)} %copy-done.2, ...), custom_call_target="tpu_custom_call" | custom-call | flops 1000000 | bytes 1024 | tf_op jit(solution)/shard_map/begin/pallas_call | solution.py:376
  85.4 3.3 %collective-permute-done.21.refs_16_ = bf16[512,1024]{1,0:T(8,128)(2,1)S(1)} collective-permute-done((bf16[512,1024]{1,0:T(8,128)(2,1)}, bf16[512,1024]{1,0:T(8,128)(2,1)S(1)}, u32[]{:S(2)}, u32[]{:S(2)}) %collective-permute-start.21) | collective-permute-done | bytes 1048608 | tf_op jit(solution)/shard_map/ppermute | solution.py:47
  88.6 3.1 %collective-permute-done.19.refs_9_ = bf16[1024,512]{1,0:T(8,128)(2,1)S(1)} collective-permute-done((bf16[1024,512]{1,0:T(8,128)(2,1)}, bf16[1024,512]{1,0:T(8,128)(2,1)S(1)}, u32[]{:S(2)}, u32[]{:S(2)}) %collective-permute-start.19) | collective-permute-done | bytes 1048608 | tf_op jit(solution)/shard_map/ppermute | solution.py:47
  91.7 4.4 %finish.3 = f32[1024,512]{1,0:T(8,128)S(1)} custom-call(s32[48]{0:T(128)S(1)} %plan.1.refs_0_, f32[1024,512]{1,0:T(8,128)S(1)} %get-tuple-element.46.refs_1_, bf16[1024,512]{1,0:T(8,128)(2,1)S(1)} %divide_convert_fusion.refs_0_.refs_1_.refs_2_, bf16[1024,512]{1,0:T(8,128)(2,1)S(1)} %collective-permute-done.8.refs_1_.refs_2_.refs_3_, ...), custom_call_target="tpu_custom_call", output_to_operand_aliasing={{}: (1, {})} | custom-call | flops 1000000 | bytes 1024 | tf_op jit(solution)/shard_map/finish/pallas_call | solution.py:376
  96.1 8.5 %collective-permute-start.23 = (f32[1024,512]{1,0:T(8,128)S(1)}, f32[1024,512]{1,0:T(8,128)S(1)}, u32[]{:S(2)}, u32[]{:S(2)}) collective-permute-start(f32[1024,512]{1,0:T(8,128)S(1)} %finish.3), channel_id=1, source_target_pairs={{0,1},{1,0},{2,3},{3,2},{4,5},{5,4},{6,7},{7,6},{8,9},{9,8},{10,11... | collective-permute-start | bytes 6291464 | tf_op jit(solution)/shard_map/ppermute | solution.py:47
  104.6 4.2 %finish.2.mine_ref = f32[1024,512]{1,0:T(8,128)S(1)} custom-call(s32[48]{0:T(128)S(1)} %plan.1.refs_0_, f32[1024,512]{1,0:T(8,128)S(1)} %get-tuple-element.42.refs_1_, bf16[1024,512]{1,0:T(8,128)(2,1)S(1)} %divide_convert_fusion.refs_0_.refs_1_.refs_2_, ...), custom_call_target="tpu_custom_call", output_to_operand_aliasing={{}: (1, {})} | custom-call | flops 1000000 | bytes 1024 | tf_op jit(solution)/shard_map/finish/pallas_call | solution.py:376
  108.9 0.3 square.1
  109.2 0.4 collective-permute-start.26
  109.6 2.0 %collective-permute-start.24 = (f32[1,512]{1,0:T(1,128)S(1)}, f32[1,512]{1,0:T(1,128)S(1)}, u32[]{:S(2)}, u32[]{:S(2)}) collective-permute-start(f32[1,512]{1,0:T(1,128)S(1)} %get-tuple-element.48), channel_id=1, source_target_pairs={{0,16},{1,17},{2,18},{3,19},{4,20},{5,21},{6,22},{7,23},{8,24},{9,... | collective-permute-start | bytes 6152 | tf_op jit(solution)/shard_map/ppermute | solution.py:47
  111.6 2.8 %collective-permute-done.26 = f32[1,512]{1,0:T(1,128)S(1)} collective-permute-done((f32[1,512]{1,0:T(1,128)S(1)}, f32[1,512]{1,0:T(1,128)S(1)}, u32[]{:S(2)}, u32[]{:S(2)}) %collective-permute-start.26) | collective-permute-done | bytes 2080 | tf_op jit(solution)/shard_map/ppermute | solution.py:47
  114.4 0.6 collective-permute-done.24
  115.0 2.5 %collective-permute-start.27 = (f32[1,512]{1,0:T(1,128)S(1)}, f32[1,512]{1,0:T(1,128)S(1)}, u32[]{:S(2)}, u32[]{:S(2)}) collective-permute-start(f32[1,512]{1,0:T(1,128)S(1)} %add_add_fusion.1), channel_id=1, source_target_pairs={{0,64},{1,65},{2,66},{3,67},{4,68},{5,69},{6,70},{7,71},{8,72},{9,... | collective-permute-start | bytes 6152 | tf_op jit(solution)/shard_map/ppermute | solution.py:47
  117.5 2.6 %collective-permute-done.27 = f32[1,512]{1,0:T(1,128)S(1)} collective-permute-done((f32[1,512]{1,0:T(1,128)S(1)}, f32[1,512]{1,0:T(1,128)S(1)}, u32[]{:S(2)}, u32[]{:S(2)}) %collective-permute-start.27) | collective-permute-done | bytes 2080 | tf_op jit(solution)/shard_map/ppermute | solution.py:47
  120.1 1.4 %rescale.1 = f32[1024,512]{1,0:T(8,128)} custom-call(f32[1024,512]{1,0:T(8,128)S(1)} %get-tuple-element.47.value_ref, f32[1,512]{1,0:T(1,128)S(1)} %add.68.total_ref), custom_call_target="tpu_custom_call" | custom-call | tf_op jit(solution)/shard_map/rescale/pallas_call | solution.py:175
  (32 shorter events, 0.1 us)
Async XLA Ops:
  0.0 1.6 %copy-start.5 = (f32[1024,512]{1,0:T(8,128)S(1)}, f32[1024,512]{1,0:T(8,128)}, u32[]{:S(2)}) copy-start(f32[1024,512]{1,0:T(8,128)} %entries_in.1) | copy-start | bytes 6291460
  1.6 0.7 copy-start.6
  3.2 7.3 %collective-permute-start.2 = (f32[1,640]{1,0:T(1,128)S(1)}, f32[1,640]{1,0:T(1,128)S(1)}, u32[]{:S(2)}, u32[]{:S(2)}) collective-permute-start(f32[1,640]{1,0:T(1,128)S(1)} %get-tuple-element.28), channel_id=1, source_target_pairs={{0,32},{1,33},{2,34},{3,35},{4,36},{5,37},{6,38},{7,39},{8,40},{9,... | collective-permute-start | bytes 7688 | tf_op jit(solution)/shard_map/ppermute | solution.py:47
  7.2 3.6 %collective-permute-start.1 = (f32[1,640]{1,0:T(1,128)S(1)}, f32[1,640]{1,0:T(1,128)S(1)}, u32[]{:S(2)}, u32[]{:S(2)}) collective-permute-start(f32[1,640]{1,0:T(1,128)S(1)} %get-tuple-element.28), channel_id=1, source_target_pairs={{0,48},{1,49},{2,50},{3,51},{4,52},{5,53},{6,54},{7,55},{8,56},{9,... | collective-permute-start | bytes 7688 | tf_op jit(solution)/shard_map/ppermute | solution.py:47
  7.9 4.8 %collective-permute-start = (f32[1,640]{1,0:T(1,128)S(1)}, f32[1,640]{1,0:T(1,128)S(1)}, u32[]{:S(2)}, u32[]{:S(2)}) collective-permute-start(f32[1,640]{1,0:T(1,128)S(1)} %get-tuple-element.28), channel_id=1, source_target_pairs={{0,16},{1,17},{2,18},{3,19},{4,20},{5,21},{6,22},{7,23},{8,24},{9,... | collective-permute-start | bytes 7688 | tf_op jit(solution)/shard_map/ppermute | solution.py:47
  9.2 1.1 collective-permute-start.3
  12.7 5.2 %collective-permute-start.4 = (f32[1,640]{1,0:T(1,128)S(1)}, f32[1,640]{1,0:T(1,128)S(1)}, u32[]{:S(2)}, u32[]{:S(2)}) collective-permute-start(f32[1,640]{1,0:T(1,128)S(1)} %add_add_fusion), channel_id=1, source_target_pairs={{0,64},{1,65},{2,66},{3,67},{4,68},{5,69},{6,70},{7,71},{8,72},{9,... | collective-permute-start | bytes 7688 | tf_op jit(solution)/shard_map/ppermute | solution.py:47
  18.2 30.6 %copy-start.7 = (s32[4,2]{0,1:T(2,128)S(1)}, s32[4,2]{0,1:T(2,128)}, u32[]{:S(2)}) copy-start(s32[4,2]{0,1:T(2,128)} %param.5) | copy-start | bytes 100
  18.3 4.6 %collective-permute-start.11 = (bf16[512,512]{1,0:T(8,128)(2,1)S(1)}, bf16[512,512]{1,0:T(8,128)(2,1)S(1)}, u32[]{:S(2)}, u32[]{:S(2)}) collective-permute-start(bf16[512,512]{1,0:T(8,128)(2,1)S(1)} %get-tuple-element.50), channel_id=1, source_target_pairs={{0,1},{1,0},{2,3},{3,2},{4,5},{5,4},{6,7},{7,6},{8,9},{9,8},{10,11... | collective-permute-start | bytes 1572872 | tf_op jit(solution)/shard_map/ppermute | solution.py:47
  18.4 1.3 %collective-permute-start.6 = (f32[16]{0:T(128)S(1)}, f32[16]{0:T(128)S(1)}, u32[]{:S(2)}, u32[]{:S(2)}) collective-permute-start(f32[16]{0:T(128)S(1)} %pad_maximum_fusion.1), channel_id=1, source_target_pairs={{1,13},{3,15},{5,9},{7,11},{9,5},{11,7},{13,1},{15,3},{17,29},{19,... | collective-permute-start | bytes 200 | tf_op jit(solution)/shard_map/ppermute | solution.py:47
  19.1 0.7 collective-permute-start.5
  19.8 17.5 %collective-permute-start.8 = (bf16[1024,512]{1,0:T(8,128)(2,1)S(1)}, bf16[1024,512]{1,0:T(8,128)(2,1)S(1)}, u32[]{:S(2)}, u32[]{:S(2)}) collective-permute-start(bf16[1024,512]{1,0:T(8,128)(2,1)S(1)} %divide_convert_fusion.refs_0_.refs_1_.refs_2_), channel_id=1, source_target_pairs={{0,2},{1,3},{2,4},{3,5},{4,6},{5,7},{6,0},{7,1},{8,10},{9,11},{10,... | collective-permute-start | bytes 3145736 | tf_op jit(solution)/shard_map/ppermute | solution.py:47
  21.3 17.4 %collective-permute-start.7 = (bf16[1024,512]{1,0:T(8,128)(2,1)S(1)}, bf16[1024,512]{1,0:T(8,128)(2,1)}, u32[]{:S(2)}, u32[]{:S(2)}) collective-permute-start(bf16[1024,512]{1,0:T(8,128)(2,1)S(1)} %divide_convert_fusion.refs_0_.refs_1_.refs_2_), channel_id=1, source_target_pairs={{0,8},{1,9},{2,10},{3,11},{4,12},{5,13},{6,14},{7,15},{8,0},{9,1},... | collective-permute-start | bytes 3145736 | tf_op jit(solution)/shard_map/ppermute | solution.py:47
  23.0 21.6 %collective-permute-start.12 = (bf16[512,1024]{1,0:T(8,128)(2,1)S(1)}, bf16[512,1024]{1,0:T(8,128)(2,1)}, u32[]{:S(2)}, u32[]{:S(2)}) collective-permute-start(bf16[512,1024]{1,0:T(8,128)(2,1)S(1)} %pad_maximum_fusion.refs_7_.refs_10_), channel_id=1, source_target_pairs={{0,16},{1,17},{2,18},{3,19},{4,20},{5,21},{6,22},{7,23},{8,24},{9,... | collective-permute-start | bytes 3145736 | tf_op jit(solution)/shard_map/ppermute | solution.py:47
  23.2 21.5 %collective-permute-start.13 = (bf16[512,1024]{1,0:T(8,128)(2,1)S(1)}, bf16[512,1024]{1,0:T(8,128)(2,1)S(1)}, u32[]{:S(2)}, u32[]{:S(2)}) collective-permute-start(bf16[512,1024]{1,0:T(8,128)(2,1)S(1)} %pad_maximum_fusion.refs_7_.refs_10_), channel_id=1, source_target_pairs={{0,48},{1,49},{2,50},{3,51},{4,52},{5,53},{6,54},{7,55},{8,56},{9,... | collective-permute-start | bytes 3145736 | tf_op jit(solution)/shard_map/ppermute | solution.py:47
  26.3 19.8 %collective-permute-start.10 = (bf16[1024,512]{1,0:T(8,128)(2,1)S(1)}, bf16[1024,512]{1,0:T(8,128)(2,1)S(1)}, u32[]{:S(2)}, u32[]{:S(2)}) collective-permute-start(bf16[1024,512]{1,0:T(8,128)(2,1)S(1)} %divide_convert_fusion.refs_0_.refs_1_.refs_2_), channel_id=1, source_target_pairs={{0,6},{1,7},{2,0},{3,1},{4,2},{5,3},{6,4},{7,5},{8,14},{9,15},{10,... | collective-permute-start | bytes 3145736 | tf_op jit(solution)/shard_map/ppermute | solution.py:47
  38.7 23.3 %collective-permute-start.9 = (bf16[1024,512]{1,0:T(8,128)(2,1)}, bf16[1024,512]{1,0:T(8,128)(2,1)}, u32[]{:S(2)}, u32[]{:S(2)}) collective-permute-start(bf16[1024,512]{1,0:T(8,128)(2,1)} %collective-permute-done.7.refs_3_.refs_4_.refs_5_), channel_id=1, source_target_pairs={{0,2},{1,3},{2,4},{3,5},{4,6},{5,7},{6,0},{7,1},{8,10},{9,11},{10,... | collective-permute-start | bytes 3145736 | tf_op jit(solution)/shard_map/ppermute | solution.py:47
  41.3 25.6 %collective-permute-start.15 = (bf16[512,1024]{1,0:T(8,128)(2,1)S(1)}, bf16[512,1024]{1,0:T(8,128)(2,1)}, u32[]{:S(2)}, u32[]{:S(2)}) collective-permute-start(bf16[512,1024]{1,0:T(8,128)(2,1)S(1)} %pad_maximum_fusion.refs_7_.refs_10_), channel_id=1, source_target_pairs={{0,64},{1,65},{2,66},{3,67},{4,68},{5,69},{6,70},{7,71},{8,72},{9,... | collective-permute-start | bytes 3145736 | tf_op jit(solution)/shard_map/ppermute | solution.py:47
  44.7 1.0 copy-start.3
  45.6 21.3 %collective-permute-start.17 = (bf16[512,1024]{1,0:T(8,128)(2,1)}, bf16[512,1024]{1,0:T(8,128)(2,1)}, u32[]{:S(2)}, u32[]{:S(2)}) collective-permute-start(bf16[512,1024]{1,0:T(8,128)(2,1)} %collective-permute-done.12.refs_8_.refs_11_), channel_id=1, source_target_pairs={{0,16},{1,17},{2,18},{3,19},{4,20},{5,21},{6,22},{7,23},{8,24},{9,... | collective-permute-start | bytes 3145736 | tf_op jit(solution)/shard_map/ppermute | solution.py:47
  46.1 1.0 copy-start
  47.1 21.9 %collective-permute-start.14 = (bf16[1024,512]{1,0:T(8,128)(2,1)}, bf16[1024,512]{1,0:T(8,128)(2,1)}, u32[]{:S(2)}, u32[]{:S(2)}) collective-permute-start(bf16[1024,512]{1,0:T(8,128)(2,1)} %collective-permute-done.7.refs_3_.refs_4_.refs_5_), channel_id=1, source_target_pairs={{0,6},{1,7},{2,0},{3,1},{4,2},{5,3},{6,4},{7,5},{8,14},{9,15},{10,... | collective-permute-start | bytes 3145736 | tf_op jit(solution)/shard_map/ppermute | solution.py:47
  49.0 21.8 %collective-permute-start.16 = (f32[104]{0:T(128)S(1)}, f32[104]{0:T(128)S(1)}, u32[]{:S(2)}, u32[]{:S(2)}) collective-permute-start(f32[104]{0:T(128)S(1)} %pad_maximum_fusion.3), channel_id=1, source_target_pairs={{0,1},{1,0},{2,3},{3,2},{4,5},{5,4},{6,7},{7,6},{8,9},{9,8},{10,11... | collective-permute-start | bytes 1256 | tf_op jit(solution)/shard_map/ppermute | solution.py:47
  62.0 23.3 %collective-permute-start.18 = (bf16[1024,512]{1,0:T(8,128)(2,1)S(1)}, bf16[1024,512]{1,0:T(8,128)(2,1)S(1)}, u32[]{:S(2)}, u32[]{:S(2)}) collective-permute-start(bf16[1024,512]{1,0:T(8,128)(2,1)S(1)} %collective-permute-done.8.refs_1_.refs_2_.refs_3_), channel_id=1, source_target_pairs={{0,2},{1,3},{2,4},{3,5},{4,6},{5,7},{6,0},{7,1},{8,10},{9,11},{10,... | collective-permute-start | bytes 3145736 | tf_op jit(solution)/shard_map/ppermute | solution.py:47
  66.9 21.7 %collective-permute-start.21 = (bf16[512,1024]{1,0:T(8,128)(2,1)}, bf16[512,1024]{1,0:T(8,128)(2,1)S(1)}, u32[]{:S(2)}, u32[]{:S(2)}) collective-permute-start(bf16[512,1024]{1,0:T(8,128)(2,1)} %collective-permute-done.15.refs_11_.refs_14_), channel_id=1, source_target_pairs={{0,48},{1,49},{2,50},{3,51},{4,52},{5,53},{6,54},{7,55},{8,56},{9,... | collective-permute-start | bytes 3145736 | tf_op jit(solution)/shard_map/ppermute | solution.py:47
  66.9 24.8 %collective-permute-start.20 = (bf16[512,1024]{1,0:T(8,128)(2,1)}, bf16[512,1024]{1,0:T(8,128)(2,1)S(1)}, u32[]{:S(2)}, u32[]{:S(2)}) collective-permute-start(bf16[512,1024]{1,0:T(8,128)(2,1)} %collective-permute-done.15.refs_11_.refs_14_), channel_id=1, source_target_pairs={{0,16},{1,17},{2,18},{3,19},{4,20},{5,21},{6,22},{7,23},{8,24},{9,... | collective-permute-start | bytes 3145736 | tf_op jit(solution)/shard_map/ppermute | solution.py:47
  69.0 22.8 %collective-permute-start.19 = (bf16[1024,512]{1,0:T(8,128)(2,1)}, bf16[1024,512]{1,0:T(8,128)(2,1)S(1)}, u32[]{:S(2)}, u32[]{:S(2)}) collective-permute-start(bf16[1024,512]{1,0:T(8,128)(2,1)} %collective-permute-done.14.refs_5_.refs_6_.refs_7_), channel_id=1, source_target_pairs={{0,6},{1,7},{2,0},{3,1},{4,2},{5,3},{6,4},{7,5},{8,14},{9,15},{10,... | collective-permute-start | bytes 3145736 | tf_op jit(solution)/shard_map/ppermute | solution.py:47
  70.8 20.9 %collective-permute-start.22 = (bf16[512,1024]{1,0:T(8,128)(2,1)}, bf16[512,1024]{1,0:T(8,128)(2,1)S(1)}, u32[]{:S(2)}, u32[]{:S(2)}) collective-permute-start(bf16[512,1024]{1,0:T(8,128)(2,1)} %collective-permute-done.17.refs_10_.refs_13_), channel_id=1, source_target_pairs={{0,64},{1,65},{2,66},{3,67},{4,68},{5,69},{6,70},{7,71},{8,72},{9,... | collective-permute-start | bytes 3145736 | tf_op jit(solution)/shard_map/ppermute | solution.py:47
  73.8 1.2 %copy-start.1 = (bf16[1024,512]{1,0:T(8,128)(2,1)S(1)}, bf16[1024,512]{1,0:T(8,128)(2,1)}, u32[]{:S(2)}) copy-start(bf16[1024,512]{1,0:T(8,128)(2,1)} %copy-done) | copy-start | bytes 3145732
  75.0 2.6 %copy-start.2 = (bf16[1024,512]{1,0:T(8,128)(2,1)S(1)}, bf16[1024,512]{1,0:T(8,128)(2,1)}, u32[]{:S(2)}) copy-start(bf16[1024,512]{1,0:T(8,128)(2,1)} %copy-done) | copy-start | bytes 3145732
  75.0 2.7 %copy-start.4 = (bf16[512,1024]{1,0:T(8,128)(2,1)S(1)}, bf16[512,1024]{1,0:T(8,128)(2,1)}, u32[]{:S(2)}) copy-start(bf16[512,1024]{1,0:T(8,128)(2,1)} %copy-done.3) | copy-start | bytes 3145732
  96.1 12.7 %collective-permute-start.23 = (f32[1024,512]{1,0:T(8,128)S(1)}, f32[1024,512]{1,0:T(8,128)S(1)}, u32[]{:S(2)}, u32[]{:S(2)}) collective-permute-start(f32[1024,512]{1,0:T(8,128)S(1)} %finish.3), channel_id=1, source_target_pairs={{0,1},{1,0},{2,3},{3,2},{4,5},{5,4},{6,7},{7,6},{8,9},{9,8},{10,11... | collective-permute-start | bytes 6291464 | tf_op jit(solution)/shard_map/ppermute | solution.py:47
  109.2 5.2 %collective-permute-start.26 = (f32[1,512]{1,0:T(1,128)S(1)}, f32[1,512]{1,0:T(1,128)S(1)}, u32[]{:S(2)}, u32[]{:S(2)}) collective-permute-start(f32[1,512]{1,0:T(1,128)S(1)} %get-tuple-element.48), channel_id=1, source_target_pairs={{0,32},{1,33},{2,34},{3,35},{4,36},{5,37},{6,38},{7,39},{8,40},{9,... | collective-permute-start | bytes 6152 | tf_op jit(solution)/shard_map/ppermute | solution.py:47
  109.6 4.8 %collective-permute-start.25 = (f32[1,512]{1,0:T(1,128)S(1)}, f32[1,512]{1,0:T(1,128)S(1)}, u32[]{:S(2)}, u32[]{:S(2)}) collective-permute-start(f32[1,512]{1,0:T(1,128)S(1)} %get-tuple-element.48), channel_id=1, source_target_pairs={{0,48},{1,49},{2,50},{3,51},{4,52},{5,53},{6,54},{7,55},{8,56},{9,... | collective-permute-start | bytes 6152 | tf_op jit(solution)/shard_map/ppermute | solution.py:47
  109.6 5.4 %collective-permute-start.24 = (f32[1,512]{1,0:T(1,128)S(1)}, f32[1,512]{1,0:T(1,128)S(1)}, u32[]{:S(2)}, u32[]{:S(2)}) collective-permute-start(f32[1,512]{1,0:T(1,128)S(1)} %get-tuple-element.48), channel_id=1, source_target_pairs={{0,16},{1,17},{2,18},{3,19},{4,20},{5,21},{6,22},{7,23},{8,24},{9,... | collective-permute-start | bytes 6152 | tf_op jit(solution)/shard_map/ppermute | solution.py:47
  115.0 5.1 %collective-permute-start.27 = (f32[1,512]{1,0:T(1,128)S(1)}, f32[1,512]{1,0:T(1,128)S(1)}, u32[]{:S(2)}, u32[]{:S(2)}) collective-permute-start(f32[1,512]{1,0:T(1,128)S(1)} %add_add_fusion.1), channel_id=1, source_target_pairs={{0,64},{1,65},{2,66},{3,67},{4,68},{5,69},{6,70},{7,71},{8,72},{9,... | collective-permute-start | bytes 6152 | tf_op jit(solution)/shard_map/ppermute | solution.py:47

commit v9 on v7

--- a/solution.py
+++ b/solution.py
@@ -12,6 +12,7 @@
 BF16 = jnp.bfloat16
 I32 = jnp.int32
 GROUP = 4
+PAIR = 2
 
 
 def place(yh, z, yl, x, c):
@@ -328,33 +329,39 @@
             first = (n * rows + i) * (grid + GROUP)
             at = jnp.int32(first)
             for k in range(grid):
+                order[first + k] = grid
+            for k in range(grid):
                 order[at] = k
                 at = at + (lax.shift_right_logical(used[i, j], k) & 1)
-            for g in range(GROUP - 1):
-                order[at + g] = grid
+            order[at] = grid
             count[i, j] = (at - first + GROUP - 1) // GROUP
     each(lambda copy: copy.wait())
 
-    for n, j in enumerate(cols_out):
-        out_ref = out_refs[n * n_out // wide]
-        place = n % (wide // n_out)
+    for n in range(0, wide, PAIR):
         for i in range(rows):
-            here = slice(i * tile, (i + 1) * tile), slice(place * tile, (place + 1) * tile)
+            outs = []
+            for p in range(PAIR):
+                place = (n + p) % (wide // n_out)
+                here = slice(i * tile, (i + 1) * tile), slice(place * tile, (place + 1) * tile)
+                outs.append((out_refs[(n + p) * n_out // wide], here))
             if not begun:
-                out_ref[here] = jnp.zeros((tile, tile), F32)
-
-            def step(m, _, i=i, n=n, here=here, out_ref=out_ref):
-                part = None
-                for g in range(GROUP):
-                    k = order[(n * rows + i) * (grid + GROUP) + m * GROUP + g]
-                    a_tile = a_buf[jnp.where(k < grid, i * grid + k, no_a)]
-                    b_tile = b_buf[jnp.where(k < grid, n * grid + k, no_b)]
-                    dot = jnp.dot(a_tile, b_tile, preferred_element_type=F32)
-                    part = dot if part is None else part + dot
-                out_ref[here] += part
+                for out_ref, here in outs:
+                    out_ref[here] = jnp.zeros((tile, tile), F32)
+
+            def step(m, _, i=i, n=n, outs=outs):
+                for p, (out_ref, here) in enumerate(outs):
+                    part = None
+                    for g in range(GROUP):
+                        k = order[((n + p) * rows + i) * (grid + GROUP) + m * GROUP + g]
+                        a_tile = a_buf[jnp.where(k < grid, i * grid + k, no_a)]
+                        b_tile = b_buf[jnp.where(k < grid, (n + p) * grid + k, no_b)]
+                        dot = jnp.dot(a_tile, b_tile, preferred_element_type=F32)
+                        part = dot if part is None else part + dot
+                    out_ref[here] += part
                 return 0
 
-            lax.fori_loop(0, count[i, j], step, 0)
+            steps = [count[i, cols_out[n + p]] for p in range(PAIR)]
+            lax.fori_loop(0, functools.reduce(jnp.maximum, steps), step, 0)
 
 
 def product(plan, a_units, b_units, rows, cols, cols_out, start=None):

time: 121 us -> 121 us (level)
  waiting for transfers between devices: 38.9 us -> 36.5 us
  Pallas kernels: 18.8 us -> 21.1 us
    ppermute x28, waiting for transfers between devices: 38.9 us -> 36.5 us  [move(): return lax.ppermute(value, AXES, perm)]
    pallas_call x3, Pallas kernels: 13.5 us -> 15.8 us  [product(): pl.pallas_call(functools.partial(product_kernel, len(a_units), len(b_unit...]
  transfers between devices with their start and end apart: 28 -> 28, of which waited for: 14 -> 13; matrix products, arithmetic and copies ran while one was open for 0% -> 0% of each run, Pallas kernels for 10% -> 11%
where the time goes in v9:
time: 121 us; the launch traced here: 120 us
  starting transfers between devices  56.1 us (46%)
  waiting for transfers between devices  36.5 us (30%)
  Pallas kernels  21.1 us (17%)
  local copies, waits for them, and re-layouts  5.61 us (5%)
    ppermute x28, starting transfers between devices, move(): return lax.ppermute(value, AXES, perm)  56.1 us
    ppermute x28, waiting for transfers between devices, move(): return lax.ppermute(value, AXES, perm)  36.5 us
    pallas_call x3, Pallas kernels, product(): pl.pallas_call(functools.partial(product_kernel, len(a_units), len(b_unit...  15.8 us
    unnamed x16, local copies, waits for them, and re-layouts  5.44 us
    pallas_call x1, Pallas kernels, planned(): pl.pallas_call(functools.partial(plan_kernel, rows, cols), out_shape=jax....  2.64 us
  transfers between devices with their start and end apart: 28, of which 13 were waited for; matrix products, arithmetic and copies ran while one was open for 0% of the time, Pallas kernels for 11%

profile of v9, /device:TPU:0, one launch (start us, length us, event | category | flops | bytes accessed | tf_op | source)
XLA Modules:
  0.0 120.3 jit_solution(13471294787548642819)
XLA Ops:
  0.0 1.6 %copy-done.5 = f32[1024,512]{1,0:T(8,128)S(1)} copy-done((f32[1024,512]{1,0:T(8,128)S(1)}, f32[1024,512]{1,0:T(8,128)}, u32[]{:S(2)}) %copy-start.5) | copy-done | bytes 2097176
  1.6 0.7 copy-done.6
  2.3 0.9 mask.1
  3.2 4.2 %collective-permute-start.2 = (f32[1,640]{1,0:T(1,128)S(1)}, f32[1,640]{1,0:T(1,128)S(1)}, u32[]{:S(2)}, u32[]{:S(2)}) collective-permute-start(f32[1,640]{1,0:T(1,128)S(1)} %get-tuple-element.28), channel_id=1, source_target_pairs={{0,48},{1,49},{2,50},{3,51},{4,52},{5,53},{6,54},{7,55},{8,56},{9,... | collective-permute-start | bytes 7688 | tf_op jit(solution)/shard_map/ppermute | solution.py:48
  7.3 0.0 collective-permute-start.1
  7.3 1.3 %collective-permute-start = (f32[1,640]{1,0:T(1,128)S(1)}, f32[1,640]{1,0:T(1,128)S(1)}, u32[]{:S(2)}, u32[]{:S(2)}) collective-permute-start(f32[1,640]{1,0:T(1,128)S(1)} %get-tuple-element.28), channel_id=1, source_target_pairs={{0,16},{1,17},{2,18},{3,19},{4,20},{5,21},{6,22},{7,23},{8,24},{9,... | collective-permute-start | bytes 7688 | tf_op jit(solution)/shard_map/ppermute | solution.py:48
  8.6 0.0 collective-permute-start.3
  8.6 1.1 collective-permute-done.3
  9.7 0.1 pad_maximum_fusion.1
  9.8 2.6 %collective-permute-done.1 = f32[1,640]{1,0:T(1,128)S(1)} collective-permute-done((f32[1,640]{1,0:T(1,128)S(1)}, f32[1,640]{1,0:T(1,128)S(1)}, u32[]{:S(2)}, u32[]{:S(2)}) %collective-permute-start.1) | collective-permute-done | bytes 2592 | tf_op jit(solution)/shard_map/ppermute | solution.py:48
  12.5 3.3 %collective-permute-start.4 = (f32[1,640]{1,0:T(1,128)S(1)}, f32[1,640]{1,0:T(1,128)S(1)}, u32[]{:S(2)}, u32[]{:S(2)}) collective-permute-start(f32[1,640]{1,0:T(1,128)S(1)} %add_add_fusion), channel_id=1, source_target_pairs={{0,64},{1,65},{2,66},{3,67},{4,68},{5,69},{6,70},{7,71},{8,72},{9,... | collective-permute-start | bytes 7688 | tf_op jit(solution)/shard_map/ppermute | solution.py:48
  15.7 1.9 %collective-permute-done.4 = f32[1,640]{1,0:T(1,128)S(1)} collective-permute-done((f32[1,640]{1,0:T(1,128)S(1)}, f32[1,640]{1,0:T(1,128)S(1)}, u32[]{:S(2)}, u32[]{:S(2)}) %collective-permute-start.4) | collective-permute-done | bytes 2592 | tf_op jit(solution)/shard_map/ppermute | solution.py:48
  17.6 0.3 divide_convert_fusion.refs_0_.refs_1_.refs_2_
  17.9 0.0 copy-start.7
  17.9 0.1 constant_dynamic-slice_fusion.1
  18.0 0.1 collective-permute-start.11
  18.1 0.7 collective-permute-start.6
  18.8 0.7 collective-permute-start.5
  19.5 0.0 collective-permute-done.5
  19.5 0.1 pad_maximum_fusion.2.far_ref
  19.6 1.5 %collective-permute-start.8 = (bf16[1024,512]{1,0:T(8,128)(2,1)S(1)}, bf16[1024,512]{1,0:T(8,128)(2,1)S(1)}, u32[]{:S(2)}, u32[]{:S(2)}) collective-permute-start(bf16[1024,512]{1,0:T(8,128)(2,1)S(1)} %divide_convert_fusion.refs_0_.refs_1_.refs_2_), channel_id=1, source_target_pairs={{0,2},{1,3},{2,4},{3,5},{4,6},{5,7},{6,0},{7,1},{8,10},{9,11},{10,... | collective-permute-start | bytes 3145736 | tf_op jit(solution)/shard_map/ppermute | solution.py:48
  21.1 1.6 %collective-permute-start.7 = (bf16[1024,512]{1,0:T(8,128)(2,1)S(1)}, bf16[1024,512]{1,0:T(8,128)(2,1)}, u32[]{:S(2)}, u32[]{:S(2)}) collective-permute-start(bf16[1024,512]{1,0:T(8,128)(2,1)S(1)} %divide_convert_fusion.refs_0_.refs_1_.refs_2_), channel_id=1, source_target_pairs={{0,8},{1,9},{2,10},{3,11},{4,12},{5,13},{6,14},{7,15},{8,0},{9,1},... | collective-permute-start | bytes 3145736 | tf_op jit(solution)/shard_map/ppermute | solution.py:48
  22.6 0.0 collective-permute-done.11
  22.6 0.1 pad_maximum_fusion.refs_7_.refs_10_
  22.8 0.1 collective-permute-start.12
  22.8 3.2 %collective-permute-start.13 = (bf16[512,1024]{1,0:T(8,128)(2,1)S(1)}, bf16[512,1024]{1,0:T(8,128)(2,1)S(1)}, u32[]{:S(2)}, u32[]{:S(2)}) collective-permute-start(bf16[512,1024]{1,0:T(8,128)(2,1)S(1)} %pad_maximum_fusion.refs_7_.refs_10_), channel_id=1, source_target_pairs={{0,48},{1,49},{2,50},{3,51},{4,52},{5,53},{6,54},{7,55},{8,56},{9,... | collective-permute-start | bytes 3145736 | tf_op jit(solution)/shard_map/ppermute | solution.py:48
  26.1 1.7 %collective-permute-start.10 = (bf16[1024,512]{1,0:T(8,128)(2,1)S(1)}, bf16[1024,512]{1,0:T(8,128)(2,1)S(1)}, u32[]{:S(2)}, u32[]{:S(2)}) collective-permute-start(bf16[1024,512]{1,0:T(8,128)(2,1)S(1)} %divide_convert_fusion.refs_0_.refs_1_.refs_2_), channel_id=1, source_target_pairs={{0,6},{1,7},{2,0},{3,1},{4,2},{5,3},{6,4},{7,5},{8,14},{9,15},{10,... | collective-permute-start | bytes 3145736 | tf_op jit(solution)/shard_map/ppermute | solution.py:48
  27.8 9.3 %collective-permute-done.8.refs_1_.refs_2_.refs_3_ = bf16[1024,512]{1,0:T(8,128)(2,1)S(1)} collective-permute-done((bf16[1024,512]{1,0:T(8,128)(2,1)S(1)}, bf16[1024,512]{1,0:T(8,128)(2,1)S(1)}, u32[]{:S(2)}, u32[]{:S(2)}) %collective-permute-start.8) | collective-permute-done | bytes 1048608 | tf_op jit(solution)/shard_map/ppermute | solution.py:48
  37.1 1.3 %collective-permute-done.7.refs_3_.refs_4_.refs_5_ = bf16[1024,512]{1,0:T(8,128)(2,1)} collective-permute-done((bf16[1024,512]{1,0:T(8,128)(2,1)S(1)}, bf16[1024,512]{1,0:T(8,128)(2,1)}, u32[]{:S(2)}, u32[]{:S(2)}) %collective-permute-start.7) | collective-permute-done | bytes 1048608 | tf_op jit(solution)/shard_map/ppermute | solution.py:48
  38.4 2.6 %collective-permute-start.9 = (bf16[1024,512]{1,0:T(8,128)(2,1)}, bf16[1024,512]{1,0:T(8,128)(2,1)}, u32[]{:S(2)}, u32[]{:S(2)}) collective-permute-start(bf16[1024,512]{1,0:T(8,128)(2,1)} %collective-permute-done.7.refs_3_.refs_4_.refs_5_), channel_id=1, source_target_pairs={{0,2},{1,3},{2,4},{3,5},{4,6},{5,7},{6,0},{7,1},{8,10},{9,11},{10,... | collective-permute-start | bytes 3145736 | tf_op jit(solution)/shard_map/ppermute | solution.py:48
  41.0 3.4 %collective-permute-start.15 = (bf16[512,1024]{1,0:T(8,128)(2,1)S(1)}, bf16[512,1024]{1,0:T(8,128)(2,1)}, u32[]{:S(2)}, u32[]{:S(2)}) collective-permute-start(bf16[512,1024]{1,0:T(8,128)(2,1)S(1)} %pad_maximum_fusion.refs_7_.refs_10_), channel_id=1, source_target_pairs={{0,64},{1,65},{2,66},{3,67},{4,68},{5,69},{6,70},{7,71},{8,72},{9,... | collective-permute-start | bytes 3145736 | tf_op jit(solution)/shard_map/ppermute | solution.py:48
  44.4 1.0 copy-done.3
  45.4 0.1 collective-permute-start.17
  45.5 0.0 collective-permute-done.10.refs_2_.refs_3_.refs_4_
  45.5 1.0 copy-done
  46.5 2.0 %collective-permute-start.14 = (bf16[1024,512]{1,0:T(8,128)(2,1)}, bf16[1024,512]{1,0:T(8,128)(2,1)}, u32[]{:S(2)}, u32[]{:S(2)}) collective-permute-start(bf16[1024,512]{1,0:T(8,128)(2,1)} %collective-permute-done.7.refs_3_.refs_4_.refs_5_), channel_id=1, source_target_pairs={{0,6},{1,7},{2,0},{3,1},{4,2},{5,3},{6,4},{7,5},{8,14},{9,15},{10,... | collective-permute-start | bytes 3145736 | tf_op jit(solution)/shard_map/ppermute | solution.py:48
  48.5 0.1 fusion.1
  48.6 0.1 reshape.11.out_ref
  48.7 0.1 pad_maximum_fusion.3
  48.8 9.2 %collective-permute-start.16 = (f32[104]{0:T(128)S(1)}, f32[104]{0:T(128)S(1)}, u32[]{:S(2)}, u32[]{:S(2)}) collective-permute-start(f32[104]{0:T(128)S(1)} %pad_maximum_fusion.3), channel_id=1, source_target_pairs={{0,1},{1,0},{2,3},{3,2},{4,5},{5,4},{6,7},{7,6},{8,9},{9,8},{10,11... | collective-permute-start | bytes 1256 | tf_op jit(solution)/shard_map/ppermute | solution.py:48
  58.0 3.7 %collective-permute-done.9.refs_4_.refs_5_.refs_6_ = bf16[1024,512]{1,0:T(8,128)(2,1)} collective-permute-done((bf16[1024,512]{1,0:T(8,128)(2,1)}, bf16[1024,512]{1,0:T(8,128)(2,1)}, u32[]{:S(2)}, u32[]{:S(2)}) %collective-permute-start.9) | collective-permute-done | bytes 1048608 | tf_op jit(solution)/shard_map/ppermute | solution.py:48
  61.7 1.5 %collective-permute-start.18 = (bf16[1024,512]{1,0:T(8,128)(2,1)S(1)}, bf16[1024,512]{1,0:T(8,128)(2,1)S(1)}, u32[]{:S(2)}, u32[]{:S(2)}) collective-permute-start(bf16[1024,512]{1,0:T(8,128)(2,1)S(1)} %collective-permute-done.8.refs_1_.refs_2_.refs_3_), channel_id=1, source_target_pairs={{0,2},{1,3},{2,4},{3,5},{4,6},{5,7},{6,0},{7,1},{8,10},{9,11},{10,... | collective-permute-start | bytes 3145736 | tf_op jit(solution)/shard_map/ppermute | solution.py:48
  63.2 3.4 %collective-permute-done.15.refs_11_.refs_14_ = bf16[512,1024]{1,0:T(8,128)(2,1)} collective-permute-done((bf16[512,1024]{1,0:T(8,128)(2,1)S(1)}, bf16[512,1024]{1,0:T(8,128)(2,1)}, u32[]{:S(2)}, u32[]{:S(2)}) %collective-permute-start.15) | collective-permute-done | bytes 1048608 | tf_op jit(solution)/shard_map/ppermute | solution.py:48
  66.7 0.6 collective-permute-start.21
  67.2 1.4 %collective-permute-start.20 = (bf16[512,1024]{1,0:T(8,128)(2,1)}, bf16[512,1024]{1,0:T(8,128)(2,1)S(1)}, u32[]{:S(2)}, u32[]{:S(2)}) collective-permute-start(bf16[512,1024]{1,0:T(8,128)(2,1)} %collective-permute-done.15.refs_11_.refs_14_), channel_id=1, source_target_pairs={{0,16},{1,17},{2,18},{3,19},{4,20},{5,21},{6,22},{7,23},{8,24},{9,... | collective-permute-start | bytes 3145736 | tf_op jit(solution)/shard_map/ppermute | solution.py:48
  68.7 1.9 %collective-permute-start.19 = (bf16[1024,512]{1,0:T(8,128)(2,1)}, bf16[1024,512]{1,0:T(8,128)(2,1)S(1)}, u32[]{:S(2)}, u32[]{:S(2)}) collective-permute-start(bf16[1024,512]{1,0:T(8,128)(2,1)} %collective-permute-done.14.refs_5_.refs_6_.refs_7_), channel_id=1, source_target_pairs={{0,6},{1,7},{2,0},{3,1},{4,2},{5,3},{6,4},{7,5},{8,14},{9,15},{10,... | collective-permute-start | bytes 3145736 | tf_op jit(solution)/shard_map/ppermute | solution.py:48
  70.6 2.9 %collective-permute-start.22 = (bf16[512,1024]{1,0:T(8,128)(2,1)}, bf16[512,1024]{1,0:T(8,128)(2,1)S(1)}, u32[]{:S(2)}, u32[]{:S(2)}) collective-permute-start(bf16[512,1024]{1,0:T(8,128)(2,1)} %collective-permute-done.17.refs_10_.refs_13_), channel_id=1, source_target_pairs={{0,64},{1,65},{2,66},{3,67},{4,68},{5,69},{6,70},{7,71},{8,72},{9,... | collective-permute-start | bytes 3145736 | tf_op jit(solution)/shard_map/ppermute | solution.py:48
  73.5 1.2 %copy-done.1 = bf16[1024,512]{1,0:T(8,128)(2,1)S(1)} copy-done((bf16[1024,512]{1,0:T(8,128)(2,1)S(1)}, bf16[1024,512]{1,0:T(8,128)(2,1)}, u32[]{:S(2)}) %copy-start.1) | copy-done | bytes 1048600
  74.7 2.6 %plan.1.refs_0_ = s32[48]{0:T(128)S(1)} custom-call(f32[32]{0:T(128)S(1)} %pad_maximum_fusion.2.far_ref, f32[64]{0:T(128)S(1)} %slice_bitcast_fusion.right_ref, f32[8]{0:T(128)S(1)} %reshape.11.out_ref, f32[104]{0:T(128)S(1)} %collective-permute-done.16.other_ref, bf16[1024,512]{1,0:T(8,128)(2,1)S(1)} %divide_convert_fusion.refs_0_.refs_1_.refs_2_, ...), custom_call_target="tpu_custom_call" | custom-call | flops 1000000 | bytes 1024 | tf_op jit(solution)/shard_map/plan/pallas_call | solution.py:262
  77.4 7.1 %begin.1 = (f32[1024,512]{1,0:T(8,128)S(1)}, f32[1024,512]{1,0:T(8,128)S(1)}) custom-call(s32[48]{0:T(128)S(1)} %plan.1.refs_0_, bf16[1024,512]{1,0:T(8,128)(2,1)S(1)} %divide_convert_fusion.refs_0_.refs_1_.refs_2_, bf16[1024,512]{1,0:T(8,128)(2,1)S(1)} %collective-permute-done.8.refs_1_.refs_2_.refs_3_, bf16[1024,512]{1,0:T(8,128)(2,1)S(1)} %copy-done.2, ...), custom_call_target="tpu_custom_call" | custom-call | flops 1000000 | bytes 1024 | tf_op jit(solution)/shard_map/begin/pallas_call | solution.py:373
  84.5 0.6 collective-permute-done.18.refs_8_
  85.1 3.3 %collective-permute-done.21.refs_16_ = bf16[512,1024]{1,0:T(8,128)(2,1)S(1)} collective-permute-done((bf16[512,1024]{1,0:T(8,128)(2,1)}, bf16[512,1024]{1,0:T(8,128)(2,1)S(1)}, u32[]{:S(2)}, u32[]{:S(2)}) %collective-permute-start.21) | collective-permute-done | bytes 1048608 | tf_op jit(solution)/shard_map/ppermute | solution.py:48
  88.3 3.1 %collective-permute-done.19.refs_9_ = bf16[1024,512]{1,0:T(8,128)(2,1)S(1)} collective-permute-done((bf16[1024,512]{1,0:T(8,128)(2,1)}, bf16[1024,512]{1,0:T(8,128)(2,1)S(1)}, u32[]{:S(2)}, u32[]{:S(2)}) %collective-permute-start.19) | collective-permute-done | bytes 1048608 | tf_op jit(solution)/shard_map/ppermute | solution.py:48
  91.5 4.6 %finish.3 = f32[1024,512]{1,0:T(8,128)S(1)} custom-call(s32[48]{0:T(128)S(1)} %plan.1.refs_0_, f32[1024,512]{1,0:T(8,128)S(1)} %get-tuple-element.46.refs_1_, bf16[1024,512]{1,0:T(8,128)(2,1)S(1)} %divide_convert_fusion.refs_0_.refs_1_.refs_2_, bf16[1024,512]{1,0:T(8,128)(2,1)S(1)} %collective-permute-done.8.refs_1_.refs_2_.refs_3_, ...), custom_call_target="tpu_custom_call", output_to_operand_aliasing={{}: (1, {})} | custom-call | flops 1000000 | bytes 1024 | tf_op jit(solution)/shard_map/finish/pallas_call | solution.py:373
  96.1 6.2 %collective-permute-start.23 = (f32[1024,512]{1,0:T(8,128)S(1)}, f32[1024,512]{1,0:T(8,128)S(1)}, u32[]{:S(2)}, u32[]{:S(2)}) collective-permute-start(f32[1024,512]{1,0:T(8,128)S(1)} %finish.3), channel_id=1, source_target_pairs={{0,1},{1,0},{2,3},{3,2},{4,5},{5,4},{6,7},{7,6},{8,9},{9,8},{10,11... | collective-permute-start | bytes 6291464 | tf_op jit(solution)/shard_map/ppermute | solution.py:48
  102.3 4.1 %finish.2.mine_ref = f32[1024,512]{1,0:T(8,128)S(1)} custom-call(s32[48]{0:T(128)S(1)} %plan.1.refs_0_, f32[1024,512]{1,0:T(8,128)S(1)} %get-tuple-element.42.refs_1_, bf16[1024,512]{1,0:T(8,128)(2,1)S(1)} %divide_convert_fusion.refs_0_.refs_1_.refs_2_, ...), custom_call_target="tpu_custom_call", output_to_operand_aliasing={{}: (1, {})} | custom-call | flops 1000000 | bytes 1024 | tf_op jit(solution)/shard_map/finish/pallas_call | solution.py:373
  106.4 0.3 square.1
  106.8 1.8 %collective-permute-start.26 = (f32[1,512]{1,0:T(1,128)S(1)}, f32[1,512]{1,0:T(1,128)S(1)}, u32[]{:S(2)}, u32[]{:S(2)}) collective-permute-start(f32[1,512]{1,0:T(1,128)S(1)} %get-tuple-element.48), channel_id=1, source_target_pairs={{0,48},{1,49},{2,50},{3,51},{4,52},{5,53},{6,54},{7,55},{8,56},{9,... | collective-permute-start | bytes 6152 | tf_op jit(solution)/shard_map/ppermute | solution.py:48
  108.5 0.9 collective-permute-start.24
  109.5 0.9 collective-permute-done.26
  110.4 3.2 %collective-permute-done.25 = f32[1,512]{1,0:T(1,128)S(1)} collective-permute-done((f32[1,512]{1,0:T(1,128)S(1)}, f32[1,512]{1,0:T(1,128)S(1)}, u32[]{:S(2)}, u32[]{:S(2)}) %collective-permute-start.25) | collective-permute-done | bytes 2080 | tf_op jit(solution)/shard_map/ppermute | solution.py:48
  113.6 3.3 %collective-permute-start.27 = (f32[1,512]{1,0:T(1,128)S(1)}, f32[1,512]{1,0:T(1,128)S(1)}, u32[]{:S(2)}, u32[]{:S(2)}) collective-permute-start(f32[1,512]{1,0:T(1,128)S(1)} %add_add_fusion.1), channel_id=1, source_target_pairs={{0,64},{1,65},{2,66},{3,67},{4,68},{5,69},{6,70},{7,71},{8,72},{9,... | collective-permute-start | bytes 6152 | tf_op jit(solution)/shard_map/ppermute | solution.py:48
  116.9 1.9 %collective-permute-done.27 = f32[1,512]{1,0:T(1,128)S(1)} collective-permute-done((f32[1,512]{1,0:T(1,128)S(1)}, f32[1,512]{1,0:T(1,128)S(1)}, u32[]{:S(2)}, u32[]{:S(2)}) %collective-permute-start.27) | collective-permute-done | bytes 2080 | tf_op jit(solution)/shard_map/ppermute | solution.py:48
  118.8 1.5 %rescale.1 = f32[1024,512]{1,0:T(8,128)} custom-call(f32[1024,512]{1,0:T(8,128)S(1)} %get-tuple-element.47.value_ref, f32[1,512]{1,0:T(1,128)S(1)} %add.68.total_ref), custom_call_target="tpu_custom_call" | custom-call | tf_op jit(solution)/shard_map/rescale/pallas_call | solution.py:170
  (32 shorter events, 0.1 us)
Async XLA Ops:
  0.0 1.6 %copy-start.5 = (f32[1024,512]{1,0:T(8,128)S(1)}, f32[1024,512]{1,0:T(8,128)}, u32[]{:S(2)}) copy-start(f32[1024,512]{1,0:T(8,128)} %entries_in.1) | copy-start | bytes 6291460
  1.6 0.7 copy-start.6
  3.2 6.7 %collective-permute-start.2 = (f32[1,640]{1,0:T(1,128)S(1)}, f32[1,640]{1,0:T(1,128)S(1)}, u32[]{:S(2)}, u32[]{:S(2)}) collective-permute-start(f32[1,640]{1,0:T(1,128)S(1)} %get-tuple-element.28), channel_id=1, source_target_pairs={{0,48},{1,49},{2,50},{3,51},{4,52},{5,53},{6,54},{7,55},{8,56},{9,... | collective-permute-start | bytes 7688 | tf_op jit(solution)/shard_map/ppermute | solution.py:48
  7.3 5.1 %collective-permute-start.1 = (f32[1,640]{1,0:T(1,128)S(1)}, f32[1,640]{1,0:T(1,128)S(1)}, u32[]{:S(2)}, u32[]{:S(2)}) collective-permute-start(f32[1,640]{1,0:T(1,128)S(1)} %get-tuple-element.28), channel_id=1, source_target_pairs={{0,32},{1,33},{2,34},{3,35},{4,36},{5,37},{6,38},{7,39},{8,40},{9,... | collective-permute-start | bytes 7688 | tf_op jit(solution)/shard_map/ppermute | solution.py:48
  7.3 5.1 %collective-permute-start = (f32[1,640]{1,0:T(1,128)S(1)}, f32[1,640]{1,0:T(1,128)S(1)}, u32[]{:S(2)}, u32[]{:S(2)}) collective-permute-start(f32[1,640]{1,0:T(1,128)S(1)} %get-tuple-element.28), channel_id=1, source_target_pairs={{0,16},{1,17},{2,18},{3,19},{4,20},{5,21},{6,22},{7,23},{8,24},{9,... | collective-permute-start | bytes 7688 | tf_op jit(solution)/shard_map/ppermute | solution.py:48
  8.6 1.1 collective-permute-start.3
  12.5 5.2 %collective-permute-start.4 = (f32[1,640]{1,0:T(1,128)S(1)}, f32[1,640]{1,0:T(1,128)S(1)}, u32[]{:S(2)}, u32[]{:S(2)}) collective-permute-start(f32[1,640]{1,0:T(1,128)S(1)} %add_add_fusion), channel_id=1, source_target_pairs={{0,64},{1,65},{2,66},{3,67},{4,68},{5,69},{6,70},{7,71},{8,72},{9,... | collective-permute-start | bytes 7688 | tf_op jit(solution)/shard_map/ppermute | solution.py:48
  17.9 30.6 %copy-start.7 = (s32[4,2]{0,1:T(2,128)S(1)}, s32[4,2]{0,1:T(2,128)}, u32[]{:S(2)}) copy-start(s32[4,2]{0,1:T(2,128)} %param.5) | copy-start | bytes 100
  18.0 4.6 %collective-permute-start.11 = (bf16[512,512]{1,0:T(8,128)(2,1)S(1)}, bf16[512,512]{1,0:T(8,128)(2,1)S(1)}, u32[]{:S(2)}, u32[]{:S(2)}) collective-permute-start(bf16[512,512]{1,0:T(8,128)(2,1)S(1)} %get-tuple-element.50), channel_id=1, source_target_pairs={{0,1},{1,0},{2,3},{3,2},{4,5},{5,4},{6,7},{7,6},{8,9},{9,8},{10,11... | collective-permute-start | bytes 1572872 | tf_op jit(solution)/shard_map/ppermute | solution.py:48
  18.1 1.3 %collective-permute-start.6 = (f32[16]{0:T(128)S(1)}, f32[16]{0:T(128)S(1)}, u32[]{:S(2)}, u32[]{:S(2)}) collective-permute-start(f32[16]{0:T(128)S(1)} %pad_maximum_fusion.1), channel_id=1, source_target_pairs={{1,13},{3,15},{5,9},{7,11},{9,5},{11,7},{13,1},{15,3},{17,29},{19,... | collective-permute-start | bytes 200 | tf_op jit(solution)/shard_map/ppermute | solution.py:48
  18.8 0.7 collective-permute-start.5
  19.6 17.5 %collective-permute-start.8 = (bf16[1024,512]{1,0:T(8,128)(2,1)S(1)}, bf16[1024,512]{1,0:T(8,128)(2,1)S(1)}, u32[]{:S(2)}, u32[]{:S(2)}) collective-permute-start(bf16[1024,512]{1,0:T(8,128)(2,1)S(1)} %divide_convert_fusion.refs_0_.refs_1_.refs_2_), channel_id=1, source_target_pairs={{0,2},{1,3},{2,4},{3,5},{4,6},{5,7},{6,0},{7,1},{8,10},{9,11},{10,... | collective-permute-start | bytes 3145736 | tf_op jit(solution)/shard_map/ppermute | solution.py:48
  21.1 17.4 %collective-permute-start.7 = (bf16[1024,512]{1,0:T(8,128)(2,1)S(1)}, bf16[1024,512]{1,0:T(8,128)(2,1)}, u32[]{:S(2)}, u32[]{:S(2)}) collective-permute-start(bf16[1024,512]{1,0:T(8,128)(2,1)S(1)} %divide_convert_fusion.refs_0_.refs_1_.refs_2_), channel_id=1, source_target_pairs={{0,8},{1,9},{2,10},{3,11},{4,12},{5,13},{6,14},{7,15},{8,0},{9,1},... | collective-permute-start | bytes 3145736 | tf_op jit(solution)/shard_map/ppermute | solution.py:48
  22.8 21.6 %collective-permute-start.12 = (bf16[512,1024]{1,0:T(8,128)(2,1)S(1)}, bf16[512,1024]{1,0:T(8,128)(2,1)}, u32[]{:S(2)}, u32[]{:S(2)}) collective-permute-start(bf16[512,1024]{1,0:T(8,128)(2,1)S(1)} %pad_maximum_fusion.refs_7_.refs_10_), channel_id=1, source_target_pairs={{0,16},{1,17},{2,18},{3,19},{4,20},{5,21},{6,22},{7,23},{8,24},{9,... | collective-permute-start | bytes 3145736 | tf_op jit(solution)/shard_map/ppermute | solution.py:48
  22.8 21.6 %collective-permute-start.13 = (bf16[512,1024]{1,0:T(8,128)(2,1)S(1)}, bf16[512,1024]{1,0:T(8,128)(2,1)S(1)}, u32[]{:S(2)}, u32[]{:S(2)}) collective-permute-start(bf16[512,1024]{1,0:T(8,128)(2,1)S(1)} %pad_maximum_fusion.refs_7_.refs_10_), channel_id=1, source_target_pairs={{0,48},{1,49},{2,50},{3,51},{4,52},{5,53},{6,54},{7,55},{8,56},{9,... | collective-permute-start | bytes 3145736 | tf_op jit(solution)/shard_map/ppermute | solution.py:48
  26.1 19.5 %collective-permute-start.10 = (bf16[1024,512]{1,0:T(8,128)(2,1)S(1)}, bf16[1024,512]{1,0:T(8,128)(2,1)S(1)}, u32[]{:S(2)}, u32[]{:S(2)}) collective-permute-start(bf16[1024,512]{1,0:T(8,128)(2,1)S(1)} %divide_convert_fusion.refs_0_.refs_1_.refs_2_), channel_id=1, source_target_pairs={{0,6},{1,7},{2,0},{3,1},{4,2},{5,3},{6,4},{7,5},{8,14},{9,15},{10,... | collective-permute-start | bytes 3145736 | tf_op jit(solution)/shard_map/ppermute | solution.py:48
  38.4 23.3 %collective-permute-start.9 = (bf16[1024,512]{1,0:T(8,128)(2,1)}, bf16[1024,512]{1,0:T(8,128)(2,1)}, u32[]{:S(2)}, u32[]{:S(2)}) collective-permute-start(bf16[1024,512]{1,0:T(8,128)(2,1)} %collective-permute-done.7.refs_3_.refs_4_.refs_5_), channel_id=1, source_target_pairs={{0,2},{1,3},{2,4},{3,5},{4,6},{5,7},{6,0},{7,1},{8,10},{9,11},{10,... | collective-permute-start | bytes 3145736 | tf_op jit(solution)/shard_map/ppermute | solution.py:48
  41.0 25.6 %collective-permute-start.15 = (bf16[512,1024]{1,0:T(8,128)(2,1)S(1)}, bf16[512,1024]{1,0:T(8,128)(2,1)}, u32[]{:S(2)}, u32[]{:S(2)}) collective-permute-start(bf16[512,1024]{1,0:T(8,128)(2,1)S(1)} %pad_maximum_fusion.refs_7_.refs_10_), channel_id=1, source_target_pairs={{0,64},{1,65},{2,66},{3,67},{4,68},{5,69},{6,70},{7,71},{8,72},{9,... | collective-permute-start | bytes 3145736 | tf_op jit(solution)/shard_map/ppermute | solution.py:48
  44.4 1.0 copy-start.3
  45.4 21.9 %collective-permute-start.17 = (bf16[512,1024]{1,0:T(8,128)(2,1)}, bf16[512,1024]{1,0:T(8,128)(2,1)}, u32[]{:S(2)}, u32[]{:S(2)}) collective-permute-start(bf16[512,1024]{1,0:T(8,128)(2,1)} %collective-permute-done.12.refs_8_.refs_11_), channel_id=1, source_target_pairs={{0,16},{1,17},{2,18},{3,19},{4,20},{5,21},{6,22},{7,23},{8,24},{9,... | collective-permute-start | bytes 3145736 | tf_op jit(solution)/shard_map/ppermute | solution.py:48
  45.5 1.0 copy-start
  46.5 22.2 %collective-permute-start.14 = (bf16[1024,512]{1,0:T(8,128)(2,1)}, bf16[1024,512]{1,0:T(8,128)(2,1)}, u32[]{:S(2)}, u32[]{:S(2)}) collective-permute-start(bf16[1024,512]{1,0:T(8,128)(2,1)} %collective-permute-done.7.refs_3_.refs_4_.refs_5_), channel_id=1, source_target_pairs={{0,6},{1,7},{2,0},{3,1},{4,2},{5,3},{6,4},{7,5},{8,14},{9,15},{10,... | collective-permute-start | bytes 3145736 | tf_op jit(solution)/shard_map/ppermute | solution.py:48
  48.8 21.8 %collective-permute-start.16 = (f32[104]{0:T(128)S(1)}, f32[104]{0:T(128)S(1)}, u32[]{:S(2)}, u32[]{:S(2)}) collective-permute-start(f32[104]{0:T(128)S(1)} %pad_maximum_fusion.3), channel_id=1, source_target_pairs={{0,1},{1,0},{2,3},{3,2},{4,5},{5,4},{6,7},{7,6},{8,9},{9,8},{10,11... | collective-permute-start | bytes 1256 | tf_op jit(solution)/shard_map/ppermute | solution.py:48
  61.7 23.3 %collective-permute-start.18 = (bf16[1024,512]{1,0:T(8,128)(2,1)S(1)}, bf16[1024,512]{1,0:T(8,128)(2,1)S(1)}, u32[]{:S(2)}, u32[]{:S(2)}) collective-permute-start(bf16[1024,512]{1,0:T(8,128)(2,1)S(1)} %collective-permute-done.8.refs_1_.refs_2_.refs_3_), channel_id=1, source_target_pairs={{0,2},{1,3},{2,4},{3,5},{4,6},{5,7},{6,0},{7,1},{8,10},{9,11},{10,... | collective-permute-start | bytes 3145736 | tf_op jit(solution)/shard_map/ppermute | solution.py:48
  66.7 21.7 %collective-permute-start.21 = (bf16[512,1024]{1,0:T(8,128)(2,1)}, bf16[512,1024]{1,0:T(8,128)(2,1)S(1)}, u32[]{:S(2)}, u32[]{:S(2)}) collective-permute-start(bf16[512,1024]{1,0:T(8,128)(2,1)} %collective-permute-done.15.refs_11_.refs_14_), channel_id=1, source_target_pairs={{0,48},{1,49},{2,50},{3,51},{4,52},{5,53},{6,54},{7,55},{8,56},{9,... | collective-permute-start | bytes 3145736 | tf_op jit(solution)/shard_map/ppermute | solution.py:48
  67.2 24.2 %collective-permute-start.20 = (bf16[512,1024]{1,0:T(8,128)(2,1)}, bf16[512,1024]{1,0:T(8,128)(2,1)S(1)}, u32[]{:S(2)}, u32[]{:S(2)}) collective-permute-start(bf16[512,1024]{1,0:T(8,128)(2,1)} %collective-permute-done.15.refs_11_.refs_14_), channel_id=1, source_target_pairs={{0,16},{1,17},{2,18},{3,19},{4,20},{5,21},{6,22},{7,23},{8,24},{9,... | collective-permute-start | bytes 3145736 | tf_op jit(solution)/shard_map/ppermute | solution.py:48
  68.7 22.8 %collective-permute-start.19 = (bf16[1024,512]{1,0:T(8,128)(2,1)}, bf16[1024,512]{1,0:T(8,128)(2,1)S(1)}, u32[]{:S(2)}, u32[]{:S(2)}) collective-permute-start(bf16[1024,512]{1,0:T(8,128)(2,1)} %collective-permute-done.14.refs_5_.refs_6_.refs_7_), channel_id=1, source_target_pairs={{0,6},{1,7},{2,0},{3,1},{4,2},{5,3},{6,4},{7,5},{8,14},{9,15},{10,... | collective-permute-start | bytes 3145736 | tf_op jit(solution)/shard_map/ppermute | solution.py:48
  70.6 20.9 %collective-permute-start.22 = (bf16[512,1024]{1,0:T(8,128)(2,1)}, bf16[512,1024]{1,0:T(8,128)(2,1)S(1)}, u32[]{:S(2)}, u32[]{:S(2)}) collective-permute-start(bf16[512,1024]{1,0:T(8,128)(2,1)} %collective-permute-done.17.refs_10_.refs_13_), channel_id=1, source_target_pairs={{0,64},{1,65},{2,66},{3,67},{4,68},{5,69},{6,70},{7,71},{8,72},{9,... | collective-permute-start | bytes 3145736 | tf_op jit(solution)/shard_map/ppermute | solution.py:48
  73.5 1.2 %copy-start.1 = (bf16[1024,512]{1,0:T(8,128)(2,1)S(1)}, bf16[1024,512]{1,0:T(8,128)(2,1)}, u32[]{:S(2)}) copy-start(bf16[1024,512]{1,0:T(8,128)(2,1)} %copy-done) | copy-start | bytes 3145732
  74.7 2.6 %copy-start.2 = (bf16[1024,512]{1,0:T(8,128)(2,1)S(1)}, bf16[1024,512]{1,0:T(8,128)(2,1)}, u32[]{:S(2)}) copy-start(bf16[1024,512]{1,0:T(8,128)(2,1)} %copy-done) | copy-start | bytes 3145732
  74.7 2.7 %copy-start.4 = (bf16[512,1024]{1,0:T(8,128)(2,1)S(1)}, bf16[512,1024]{1,0:T(8,128)(2,1)}, u32[]{:S(2)}) copy-start(bf16[512,1024]{1,0:T(8,128)(2,1)} %copy-done.3) | copy-start | bytes 3145732
  96.1 10.3 %collective-permute-start.23 = (f32[1024,512]{1,0:T(8,128)S(1)}, f32[1024,512]{1,0:T(8,128)S(1)}, u32[]{:S(2)}, u32[]{:S(2)}) collective-permute-start(f32[1024,512]{1,0:T(8,128)S(1)} %finish.3), channel_id=1, source_target_pairs={{0,1},{1,0},{2,3},{3,2},{4,5},{5,4},{6,7},{7,6},{8,9},{9,8},{10,11... | collective-permute-start | bytes 6291464 | tf_op jit(solution)/shard_map/ppermute | solution.py:48
  106.8 3.7 %collective-permute-start.26 = (f32[1,512]{1,0:T(1,128)S(1)}, f32[1,512]{1,0:T(1,128)S(1)}, u32[]{:S(2)}, u32[]{:S(2)}) collective-permute-start(f32[1,512]{1,0:T(1,128)S(1)} %get-tuple-element.48), channel_id=1, source_target_pairs={{0,48},{1,49},{2,50},{3,51},{4,52},{5,53},{6,54},{7,55},{8,56},{9,... | collective-permute-start | bytes 6152 | tf_op jit(solution)/shard_map/ppermute | solution.py:48
  108.5 5.1 %collective-permute-start.25 = (f32[1,512]{1,0:T(1,128)S(1)}, f32[1,512]{1,0:T(1,128)S(1)}, u32[]{:S(2)}, u32[]{:S(2)}) collective-permute-start(f32[1,512]{1,0:T(1,128)S(1)} %get-tuple-element.48), channel_id=1, source_target_pairs={{0,32},{1,33},{2,34},{3,35},{4,36},{5,37},{6,38},{7,39},{8,40},{9,... | collective-permute-start | bytes 6152 | tf_op jit(solution)/shard_map/ppermute | solution.py:48
  108.5 5.1 %collective-permute-start.24 = (f32[1,512]{1,0:T(1,128)S(1)}, f32[1,512]{1,0:T(1,128)S(1)}, u32[]{:S(2)}, u32[]{:S(2)}) collective-permute-start(f32[1,512]{1,0:T(1,128)S(1)} %get-tuple-element.48), channel_id=1, source_target_pairs={{0,16},{1,17},{2,18},{3,19},{4,20},{5,21},{6,22},{7,23},{8,24},{9,... | collective-permute-start | bytes 6152 | tf_op jit(solution)/shard_map/ppermute | solution.py:48
  113.6 5.2 %collective-permute-start.27 = (f32[1,512]{1,0:T(1,128)S(1)}, f32[1,512]{1,0:T(1,128)S(1)}, u32[]{:S(2)}, u32[]{:S(2)}) collective-permute-start(f32[1,512]{1,0:T(1,128)S(1)} %add_add_fusion.1), channel_id=1, source_target_pairs={{0,64},{1,65},{2,66},{3,67},{4,68},{5,69},{6,70},{7,71},{8,72},{9,... | collective-permute-start | bytes 6152 | tf_op jit(solution)/shard_map/ppermute | solution.py:48
